TPU v7x, 32 devices: a whole 2x2x4 slice. The times are simulated.
32 devices in a mesh: dp: 16 (over z, x, core), tensor: 2 (over y).
Axes of the slice: x: 2, y: 2, z: 4, core: 2. Of those that a mesh axis runs over, the one named last changes fastest.
Arguments:
- tokens: bfloat16 [4096, 768], P(('dp', 'tensor')), may hold values from -6 to 6
- gain_one: bfloat16 [768], replicated, may hold values from 0.5 to 1.5
- w_query: bfloat16 [768, 768], P('dp', 'tensor'), may hold values from -0.21875 to 0.21875
- w_key: bfloat16 [768, 768], P('dp', 'tensor'), may hold values from -0.21875 to 0.21875
- w_value: bfloat16 [768, 768], P('dp', 'tensor'), may hold values from -0.21875 to 0.21875
- w_out: bfloat16 [768, 768], P('dp', 'tensor'), may hold values from -0.875 to 0.875
- bias_table: float32 [32, 12], replicated, may hold values from -4 to 4
- gain_two: bfloat16 [768], replicated, may hold values from 0.5 to 1.5
- w_router: bfloat16 [768, 8], replicated, may hold values from -0.15625 to 0.15625
- w_up: bfloat16 [768, 24576], P(None, ('dp', 'tensor')), may hold values from -0.21875 to 0.21875
- w_down: bfloat16 [768, 24576], P(None, ('dp', 'tensor')), may hold values from -0.875 to 0.875
- routes: int32 [4096, 1], P('dp'), may hold values from 0 to 7; in each aligned block of 256 rows (0 to 255, 256 to 511, ...) at most 40 rows name the same one
- doc_lengths: int32 [8, 8], replicated, may hold values from 1 to 385, as said below
- buckets: int32 [1023], replicated, may hold values from 0 to 31
- cotangent: bfloat16 [4096, 768], P('dp'), may hold values from -6 to 6
Outputs:
- activations: bfloat16 [4096, 768], P(('dp', 'tensor'))
- input_grad: float32 [4096, 768], P(('dp', 'tensor'))
- grad_gain_one: float32 [768], replicated
- grad_w_query: float32 [768, 768], P('dp', 'tensor')
- grad_w_key: float32 [768, 768], P('dp', 'tensor')
- grad_w_value: float32 [768, 768], P('dp', 'tensor')
- grad_w_out: float32 [768, 768], P('dp', 'tensor')
- grad_bias: float32 [32, 12], replicated
- grad_gain_two: float32 [768], replicated
- grad_w_router: float32 [768, 8], replicated
- grad_w_up: float32 [768, 24576], P(None, ('dp', 'tensor'))
- grad_w_down: float32 [768, 24576], P(None, ('dp', 'tensor'))
Inputs may be any that keep to these rules, and one draw needn't show every extreme that they name: `routes`: in each aligned block of 256 rows no expert is named by more than 40 rows; in every draw some block has an expert named by exactly 40 rows. `doc_lengths`: each row holds the lengths of the 8 documents of one sequence in order; they sum to 512, and exactly one of them has 385 tokens.
All inputs are finite; a program needn't handle non-finite values.
Results may differ from a plain program's by a relative error of at most 0.014.
Values may be sent and summed in bfloat16 or wider, within the bound.
No kernel may reach another device: no remote copies, remote signals or barrier semaphores. Data moves between devices by JAX's collectives and lax.ppermute only.
A program may use at most 128 MiB of HBM per device.

v0:
```python
import jax
import jax.numpy as jnp
from jax import lax
from jax.sharding import PartitionSpec as P

HD = 64
GROUP = 2


norm_eps = 1e-06
masked_value = -1e30
exact = lax.Precision.HIGHEST


def from_partner(shard, axis, bit):
    return lax.ppermute(shard, axis, [(i, i ^ 1 << bit) for i in range(lax.axis_size(axis))])


def rms_scale(values, gain):
    return values * lax.rsqrt(jnp.mean(values * values, axis=-1, keepdims=True) + norm_eps) * gain


def spread_rows(vector, row_total, column_total):
    span = row_total + column_total - 1
    tiled = jnp.broadcast_to(vector[None, :], (row_total, span)).reshape(-1)
    tiled = jnp.concatenate([tiled, jnp.zeros((row_total,), vector.dtype)])
    return tiled.reshape(row_total, span + 1)[:, :column_total][::-1]


def fold_rows(grid):
    row_total, column_total = grid.shape
    span = row_total + column_total - 1
    padded = jnp.concatenate([grid[::-1], jnp.zeros((row_total, row_total), grid.dtype)], axis=1)
    return jnp.sum(padded.reshape(-1)[: row_total * span].reshape(row_total, span), axis=0)


def head_scores(query_head, key_head, bias_row, same_doc, score_scale):
    raw_scores = (
        jnp.einsum("qd,kd->qk", query_head, key_head, preferred_element_type=jnp.float32)
        * score_scale
    )
    raw_scores = raw_scores + spread_rows(bias_row, query_head.shape[0], key_head.shape[0])
    return jnp.where(same_doc, raw_scores, masked_value)


def fetch_attention(w_query, w_key, w_value, w_out):
    return (
        lax.all_gather(w_query, "dp", axis=0, tiled=True),
        lax.all_gather(w_key, "dp", axis=0, tiled=True),
        lax.all_gather(w_value, "dp", axis=0, tiled=True),
        lax.all_gather(w_out, "dp", axis=0, tiled=True),
    )


def per_device(
    tokens,
    gain_one,
    w_query,
    w_key,
    w_value,
    w_out,
    bias_table,
    gain_two,
    w_router,
    w_up,
    w_down,
    routes,
    doc_lengths,
    buckets,
    cotangent,
):
    own_rows, width = tokens.shape
    block_rows = routes.shape[0]
    seq_length = block_rows * GROUP
    levels = GROUP.bit_length() - 1
    local_width = w_query.shape[1]
    heads_here = local_width // HD
    score_scale = HD ** (-0.5)
    experts = w_router.shape[1]
    capacity = max(2, (5 * block_rows + 4 * experts - 1) // (4 * experts))
    pair_count = lax.axis_size("dp") // experts
    tensor_at = lax.axis_index("tensor")
    dp_index = lax.axis_index("dp")
    within = dp_index % GROUP
    first_place = within * block_rows
    own_start = tensor_at * own_rows
    x_own = tokens.astype(jnp.float32)
    gain_first = gain_one.astype(jnp.float32)
    gain_second = gain_two.astype(jnp.float32)
    normed_own = rms_scale(x_own, gain_first).astype(jnp.bfloat16)
    normed = lax.all_gather(normed_own, "tensor", axis=0, tiled=True)
    weight_query, weight_key, weight_value, weight_out = fetch_attention(
        w_query, w_key, w_value, w_out
    )
    query = jnp.dot(normed, weight_query, preferred_element_type=jnp.float32).astype(jnp.bfloat16)
    key_local = jnp.dot(normed, weight_key, preferred_element_type=jnp.float32).astype(jnp.bfloat16)
    value_local = jnp.dot(normed, weight_value, preferred_element_type=jnp.float32).astype(
        jnp.bfloat16
    )
    key_all, value_all = (key_local, value_local)
    level = 0
    other_key, other_value = from_partner((key_all, value_all), "dp", level)
    lower_half = within // (1 << level) % 2 == 0
    key_all = jnp.where(
        lower_half, jnp.concatenate([key_all, other_key]), jnp.concatenate([other_key, key_all])
    )
    value_all = jnp.where(
        lower_half,
        jnp.concatenate([value_all, other_value]),
        jnp.concatenate([other_value, value_all]),
    )
    lengths_row = lax.dynamic_slice_in_dim(doc_lengths, dp_index // GROUP, 1, 0)[0]
    ends = jnp.cumsum(lengths_row)
    places = jnp.arange(seq_length, dtype=jnp.int32)
    key_docs = jnp.sum((ends[None, :] <= places[:, None]).astype(jnp.int32), axis=1)
    query_docs = lax.dynamic_slice_in_dim(key_docs, first_place, block_rows)
    same_doc = query_docs[:, None] == key_docs[None, :]
    offset_count = block_rows + seq_length - 1
    bucket_run = lax.dynamic_slice_in_dim(
        buckets, seq_length - block_rows - first_place, offset_count
    )
    bucket_count = bias_table.shape[0]
    bucket_hot = (bucket_run[:, None] == jnp.arange(bucket_count, dtype=jnp.int32)[None, :]).astype(
        jnp.float32
    )
    bias_here = lax.dynamic_slice_in_dim(bias_table, tensor_at * heads_here, heads_here, 1)
    bias_rows = jnp.dot(bucket_hot, bias_here, precision=exact).T

    def split_heads(matrix):
        return matrix.reshape(matrix.shape[0], heads_here, HD).transpose(1, 0, 2)

    def merge_heads(stacked):
        return stacked.transpose(1, 0, 2).reshape(stacked.shape[1], local_width)

    query_heads = split_heads(query)
    key_heads = split_heads(key_all)
    value_heads = split_heads(value_all)

    def attend(items):
        query_head, key_head, value_head, bias_row = items
        scores = head_scores(query_head, key_head, bias_row, same_doc, score_scale)
        peak = jnp.max(scores, axis=1, keepdims=True)
        exp_scores = jnp.exp(scores - peak)
        totals = jnp.sum(exp_scores, axis=1, keepdims=True)
        probs_low = (exp_scores / totals).astype(jnp.bfloat16)
        mixed_head = jnp.dot(probs_low, value_head, preferred_element_type=jnp.float32).astype(
            jnp.bfloat16
        )
        return (mixed_head, (peak + jnp.log(totals))[:, 0])

    mixed_heads, log_totals = lax.map(attend, (query_heads, key_heads, value_heads, bias_rows))
    mixed = merge_heads(mixed_heads)
    attended = lax.psum_scatter(
        jnp.einsum("tj,dj->td", mixed, weight_out, preferred_element_type=jnp.float32),
        "tensor",
        scatter_dimension=0,
        tiled=True,
    )
    hidden = x_own + attended
    normed_two_own = rms_scale(hidden, gain_second).astype(jnp.bfloat16)
    normed_two = lax.all_gather(normed_two_own, "tensor", axis=0, tiled=True)
    logits = jnp.dot(normed_two, w_router, preferred_element_type=jnp.float32)
    gates = jax.nn.softmax(logits, axis=-1)
    expert_ids = routes[:, 0]
    choose = expert_ids[:, None] == jnp.arange(experts, dtype=jnp.int32)[None, :]
    chosen = jnp.sum(jnp.where(choose, gates, 0.0), axis=1)
    pick_counts = choose.astype(jnp.int32)
    slot_index = jnp.sum((jnp.cumsum(pick_counts, axis=0) - 1) * pick_counts, axis=1)
    target = expert_ids * capacity + slot_index
    table = (target[None, :] == jnp.arange(experts * capacity, dtype=jnp.int32)[:, None]).astype(
        jnp.bfloat16
    )
    dispatched = jnp.dot(table, normed_two, preferred_element_type=jnp.float32).astype(jnp.bfloat16)
    grad_rows = cotangent.astype(jnp.float32)
    scaled_grad = (chosen[:, None] * grad_rows).astype(jnp.bfloat16)
    grad_expert = jnp.dot(table, scaled_grad, preferred_element_type=jnp.float32).astype(
        jnp.bfloat16
    )

    def to_owners(slot_rows):
        spread = jnp.broadcast_to(
            slot_rows.reshape(experts, 1, capacity, width), (experts, pair_count, capacity, width)
        )
        return spread.reshape(experts * pair_count, capacity, width)

    slots_in, grads_in = (
        lax.all_to_all(to_owners(dispatched), "dp", split_axis=0, concat_axis=0, tiled=True),
        lax.all_to_all(to_owners(grad_expert), "dp", split_axis=0, concat_axis=0, tiled=True),
    )
    slots_in = slots_in.reshape(-1, width)
    grads_in = grads_in.reshape(-1, width)
    upward = jnp.dot(slots_in, w_up, preferred_element_type=jnp.float32)
    active = jax.nn.gelu(upward).astype(jnp.bfloat16)
    expert_part = jnp.einsum("sf,df->sd", active, w_down, preferred_element_type=jnp.float32)
    grad_active = jnp.dot(grads_in, w_down, preferred_element_type=jnp.float32)
    gelu_value, gelu_pull = jax.vjp(jax.nn.gelu, upward)
    grad_upward = gelu_pull(grad_active)[0].astype(jnp.bfloat16)
    grad_w_up_here = jnp.einsum(
        "sd,sf->df", slots_in, grad_upward, preferred_element_type=jnp.float32
    )
    grad_w_down_here = jnp.einsum("sd,sf->df", grads_in, active, preferred_element_type=jnp.float32)
    grad_part = jnp.einsum("sf,df->sd", grad_upward, w_up, preferred_element_type=jnp.float32)
    back_out, back_grad = (
        lax.all_to_all(
            expert_part.reshape(-1, capacity, width), "dp", split_axis=0, concat_axis=0, tiled=True
        ),
        lax.all_to_all(
            grad_part.reshape(-1, capacity, width), "dp", split_axis=0, concat_axis=0, tiled=True
        ),
    )
    slot_out = jnp.sum(back_out.reshape(experts, pair_count, capacity, width), axis=1).reshape(
        experts * capacity, width
    )
    slot_grad = jnp.sum(back_grad.reshape(experts, pair_count, capacity, width), axis=1).reshape(
        experts * capacity, width
    )
    combined = lax.psum_scatter(
        jnp.concatenate(
            [jnp.take(slot_out, target, axis=0), jnp.take(slot_grad, target, axis=0)], axis=1
        ),
        "tensor",
        scatter_dimension=0,
        tiled=True,
    )
    returned = combined[:, :width]
    grad_normed_two = combined[:, width:]
    gates_own = lax.dynamic_slice_in_dim(gates, own_start, own_rows, 0)
    choose_own = lax.dynamic_slice_in_dim(choose, own_start, own_rows, 0)
    chosen_own = lax.dynamic_slice_in_dim(chosen, own_start, own_rows, 0)
    activations = (hidden + chosen_own[:, None] * returned).astype(jnp.bfloat16)
    grad_own = lax.dynamic_slice_in_dim(grad_rows, own_start, own_rows, 0)
    grad_chosen = jnp.sum(grad_own * returned, axis=1)
    grad_gates = jnp.where(choose_own, grad_chosen[:, None], 0.0)
    grad_logits = (gates_own * (grad_gates - chosen_own[:, None] * grad_chosen[:, None])).astype(
        jnp.bfloat16
    )
    grad_normed_two = grad_normed_two + jnp.einsum(
        "te,de->td", grad_logits, w_router, preferred_element_type=jnp.float32
    )
    grad_router_part = jnp.einsum(
        "td,te->de", normed_two_own, grad_logits, preferred_element_type=jnp.float32
    )
    norm_value, norm_pull_two = jax.vjp(rms_scale, hidden, gain_second)
    grad_hidden_part, grad_gain_second = norm_pull_two(grad_normed_two)
    grad_hidden = grad_own + grad_hidden_part
    grad_attended = lax.all_gather(grad_hidden.astype(jnp.bfloat16), "tensor", axis=0, tiled=True)
    weight_query, weight_key, weight_value, weight_out = fetch_attention(
        w_query, w_key, w_value, w_out
    )
    grad_mixed = jnp.dot(grad_attended, weight_out, preferred_element_type=jnp.float32).astype(
        jnp.bfloat16
    )

    def attend_back(items):
        query_head, key_head, value_head, bias_row, grad_head, log_total = items
        scores = head_scores(query_head, key_head, bias_row, same_doc, score_scale)
        probs = jnp.exp(scores - log_total[:, None])
        grad_probs = jnp.einsum(
            "qd,kd->qk", grad_head, value_head, preferred_element_type=jnp.float32
        )
        inner = jnp.sum(probs * grad_probs, axis=1, keepdims=True)
        grad_scores = (probs * (grad_probs - inner)).astype(jnp.bfloat16)
        grad_query_head = (
            jnp.dot(grad_scores, key_head, preferred_element_type=jnp.float32) * score_scale
        )
        grad_key_head = (
            jnp.einsum("qk,qd->kd", grad_scores, query_head, preferred_element_type=jnp.float32)
            * score_scale
        )
        grad_value_head = jnp.einsum(
            "qk,qd->kd", probs.astype(jnp.bfloat16), grad_head, preferred_element_type=jnp.float32
        )
        return (
            grad_query_head,
            grad_key_head,
            grad_value_head,
            fold_rows(grad_scores.astype(jnp.float32)),
        )

    grad_query_heads, grad_key_heads, grad_value_heads, grad_bias_rows = lax.map(
        attend_back,
        (query_heads, key_heads, value_heads, bias_rows, split_heads(grad_mixed), log_totals),
    )
    grad_query = merge_heads(grad_query_heads).astype(jnp.bfloat16)
    grad_keys = jnp.stack([merge_heads(grad_key_heads), merge_heads(grad_value_heads)])
    for level in reversed(range(levels)):
        half_rows = grad_keys.shape[1] // 2
        lower_rows = grad_keys[:, :half_rows]
        upper_rows = grad_keys[:, half_rows:]
        lower_half = within // (1 << level) % 2 == 0
        outgoing = jnp.where(lower_half, upper_rows, lower_rows)
        staying = jnp.where(lower_half, lower_rows, upper_rows)
        grad_keys = staying + from_partner(outgoing.astype(jnp.bfloat16), "dp", level).astype(
            outgoing.dtype
        )
    grad_key = grad_keys[0].astype(jnp.bfloat16)
    grad_value = grad_keys[1].astype(jnp.bfloat16)
    pieces = [
        jnp.einsum("td,tj->dj", normed, grad_query, preferred_element_type=jnp.float32),
        jnp.einsum("td,tj->dj", normed, grad_key, preferred_element_type=jnp.float32),
        jnp.einsum("td,tj->dj", normed, grad_value, preferred_element_type=jnp.float32),
        jnp.einsum("td,tj->dj", grad_attended, mixed, preferred_element_type=jnp.float32),
    ]
    attention_sums = lax.psum_scatter(
        jnp.stack(pieces, axis=1), "dp", scatter_dimension=0, tiled=True
    )
    total = jnp.einsum("tj,dj->td", grad_query, weight_query, preferred_element_type=jnp.float32)
    total = total + jnp.einsum(
        "tj,dj->td", grad_key, weight_key, preferred_element_type=jnp.float32
    )
    grad_normed = lax.psum_scatter(
        (
            total
            + jnp.einsum("tj,dj->td", grad_value, weight_value, preferred_element_type=jnp.float32)
        ).astype(jnp.bfloat16),
        "tensor",
        scatter_dimension=0,
        tiled=True,
    ).astype(jnp.float32)
    norm_first, norm_pull_one = jax.vjp(rms_scale, x_own, gain_first)
    grad_x_part, grad_gain_first = norm_pull_one(grad_normed)
    input_grad = grad_hidden + grad_x_part
    bias_part = jnp.dot(grad_bias_rows, bucket_hot, precision=exact).T
    bias_full = jnp.zeros((bucket_count, bias_table.shape[1]), jnp.float32)
    bias_full = lax.dynamic_update_slice(
        bias_full, bias_part, (jnp.int32(0), tensor_at * heads_here)
    )
    summed_gain_one, summed_gain_two, summed_router, summed_bias = lax.psum(
        (grad_gain_first, grad_gain_second, grad_router_part, bias_full), ("dp", "tensor")
    )
    return (
        activations,
        input_grad,
        summed_gain_one,
        attention_sums[:, 0],
        attention_sums[:, 1],
        attention_sums[:, 2],
        attention_sums[:, 3],
        summed_bias,
        summed_gain_two,
        summed_router,
        grad_w_up_here,
        grad_w_down_here,
    )


def solution(mesh):
    in_specs = (
        P(("dp", "tensor"), None),
        P(),
        P("dp", "tensor"),
        P("dp", "tensor"),
        P("dp", "tensor"),
        P("dp", "tensor"),
        P(),
        P(),
        P(),
        P(None, ("dp", "tensor")),
        P(None, ("dp", "tensor")),
        P("dp", None),
        P(),
        P(),
        P("dp", None),
    )
    out_specs = (
        P(("dp", "tensor"), None),
        P(("dp", "tensor"), None),
        P(),
        P("dp", "tensor"),
        P("dp", "tensor"),
        P("dp", "tensor"),
        P("dp", "tensor"),
        P(),
        P(),
        P(),
        P(None, ("dp", "tensor")),
        P(None, ("dp", "tensor")),
    )
    return jax.shard_map(
        per_device, mesh=mesh, in_specs=in_specs, out_specs=out_specs, check_vma=False
    )
```

profile of v0, /device:TPU:0, one launch (start us, length us, event | category | flops | bytes accessed | tf_op | source)
XLA Modules:
  0.0 577.7 jit_solution(6335690837938057828)
XLA Ops:
  10.1 8.5 %all_gather.25 = bf16[256,768]{1,0:T(8,128)(2,1)S(1)} all-gather(bf16[128,768]{1,0:T(8,128)(2,1)S(1)} %fusion.58), channel_id=1, replica_groups=mesh['dp'=16,'tensor'=2] {'tensor'}, dimensions={0}, use_global_device_ids=true | all-gather | bytes 589824 | tf_op jit(solution)/shard_map/all_gather | solution.py:91
  18.7 23.9 %all_gather.27 = bf16[768,384]{1,0:T(8,128)(2,1)S(1)} all-gather(bf16[48,384]{1,0:T(8,128)(2,1)} %param.24), channel_id=1, replica_groups=mesh['dp'=16,'tensor'=2] {'dp'}, dimensions={0}, use_global_device_ids=true | all-gather | bytes 626688 | tf_op jit(solution)/shard_map/all_gather | solution.py:49
  44.2 18.9 %all_gather.28 = bf16[768,384]{1,0:T(8,128)(2,1)S(1)} all-gather(bf16[48,384]{1,0:T(8,128)(2,1)S(1)} %copy-done.28), channel_id=1, replica_groups=mesh['dp'=16,'tensor'=2] {'dp'}, dimensions={0}, use_global_device_ids=true | all-gather | bytes 626688 | tf_op jit(solution)/shard_map/all_gather | solution.py:50
  65.1 20.6 %all_gather.26 = bf16[768,384]{1,0:T(8,128)(2,1)S(1)} all-gather(bf16[48,384]{1,0:T(8,128)(2,1)S(1)} %copy-done.29), channel_id=1, replica_groups=mesh['dp'=16,'tensor'=2] {'dp'}, dimensions={0}, use_global_device_ids=true | all-gather | bytes 626688 | tf_op jit(solution)/shard_map/all_gather | solution.py:48
  88.3 20.4 %all_gather.29 = bf16[768,384]{1,0:T(8,128)(2,1)} all-gather(bf16[48,384]{1,0:T(8,128)(2,1)S(1)} %copy-done.30), channel_id=1, replica_groups=mesh['dp'=16,'tensor'=2] {'dp'}, dimensions={0}, use_global_device_ids=true | all-gather | bytes 626688 | tf_op jit(solution)/shard_map/all_gather | solution.py:51
  113.7 39.9 %while.30 = (s32[]{:T(128)}, bf16[6,256,64]{1,2,0:T(8,128)(2,1)}, f32[6,256]{1,0:T(8,128)}, bf16[6,256,64]{2,1,0:T(8,128)(2,1)S(1)}, bf16[6,512,64]{2,1,0:T(8,12...) while((s32[]{:T(128)}, bf16[6,256,64]{1,2,0:T(8,128)(2,1)}, ...), condition=%wide.region_6.7_spmd.clone, body=%wide.region_3.6_spmd.clone.sunk | while | flops 34881280 | bytes 10080381 | solution.py:151
  117.2 1.8 fusion.154
  123.9 1.8 fusion.154
  130.5 1.8 fusion.154
  137.2 1.8 fusion.154
  143.8 1.8 fusion.154
  150.5 1.8 fusion.154
  153.6 2.6 fusion.92
  157.8 14.6 %reduce-scatter.5.cloned.1.call-done = f32[128,768]{1,0:T(8,128)} async-done(((f32[256,768]{1,0:T(8,128)}), f32[128,768]{1,0:T(8,128)}) %reduce-scatter.5.cloned.1.call-update) | async-done | bytes 393232 | tf_op jit(solution)/shard_map/reduce_scatter | solution.py:153
  174.5 7.3 %all_gather.30 = bf16[256,768]{1,0:T(8,128)(2,1)S(1)} all-gather(bf16[128,768]{1,0:T(8,128)(2,1)S(1)} %multiply_convert_fusion.4), channel_id=1, replica_groups=mesh['dp'=16,'tensor'=2] {'tensor'}, dimensions={0}, use_global_device_ids=true | all-gather | bytes 589824 | tf_op jit(solution)/shard_map/all_gather | solution.py:161
  184.1 5.6 all-to-all-start.2
  190.0 21.6 %all-to-all-done.2 = bf16[16,40,768]{2,1,0:T(8,128)(2,1)S(1)} async-done(((bf16[16,40,768]{2,1,0:T(8,128)(2,1)}), bf16[16,40,768]{2,1,0:T(8,128)(2,1)S(1)}, u32[]{:S(2)}, u32[]{:S(2)}) %all-to-all-start.2) | async-done | bytes 983072 | tf_op jit(solution)/shard_map/all_to_all | solution.py:188
  212.7 6.6 %all-to-all-start = ((bf16[16,40,768]{2,1,0:T(8,128)(2,1)}), bf16[16,40,768]{2,1,0:T(8,128)(2,1)}, u32[]{:S(2)}, u32[]{:S(2)}) async-start(bf16[16,40,768]{2,1,0:T(8,128)(2,1)} %bitcast.17), calls=%async_computation.1 | async-start | bytes 1966080 | tf_op jit(solution)/shard_map/all_to_all | solution.py:187
  219.3 3.5 fusion.93
  222.7 18.5 %all-to-all-done = bf16[16,40,768]{2,1,0:T(8,128)(2,1)} async-done(((bf16[16,40,768]{2,1,0:T(8,128)(2,1)}), bf16[16,40,768]{2,1,0:T(8,128)(2,1)}, u32[]{:S(2)}, u32[]{:S(2)}) %all-to-all-start) | async-done | bytes 983072 | tf_op jit(solution)/shard_map/all_to_all | solution.py:187
  241.2 4.8 fusion.53
  246.0 2.6 fusion.84
  248.6 6.5 %all-to-all-start.1 = ((f32[16,40,768]{2,1,0:T(8,128)}), f32[16,40,768]{2,1,0:T(8,128)S(1)}, u32[]{:S(2)}, u32[]{:S(2)}) async-start(f32[16,40,768]{2,1,0:T(8,128)} %bitcast.216), calls=%async_computation.2 | async-start | bytes 3932160 | tf_op jit(solution)/shard_map/all_to_all | solution.py:204
  255.1 3.4 fusion.94
  258.6 35.4 %all-to-all-done.1 = f32[16,40,768]{2,1,0:T(8,128)S(1)} async-done(((f32[16,40,768]{2,1,0:T(8,128)}), f32[16,40,768]{2,1,0:T(8,128)S(1)}, u32[]{:S(2)}, u32[]{:S(2)}) %all-to-all-start.1) | async-done | bytes 1966112 | tf_op jit(solution)/shard_map/all_to_all | solution.py:204
  294.0 10.9 %all-to-all-start.3 = ((f32[16,40,768]{2,1,0:T(8,128)}), f32[16,40,768]{2,1,0:T(8,128)}, u32[]{:S(2)}, u32[]{:S(2)}) async-start(f32[16,40,768]{2,1,0:T(8,128)} %bitcast.215), calls=%async_computation.4 | async-start | bytes 3932160 | tf_op jit(solution)/shard_map/all_to_all | solution.py:207
  306.1 37.6 %all-to-all-done.3 = f32[16,40,768]{2,1,0:T(8,128)} async-done(((f32[16,40,768]{2,1,0:T(8,128)}), f32[16,40,768]{2,1,0:T(8,128)}, u32[]{:S(2)}, u32[]{:S(2)}) %all-to-all-start.3) | async-done | bytes 1966112 | tf_op jit(solution)/shard_map/all_to_all | solution.py:207
  343.7 1.8 bitcast_reduce_fusion
  348.8 30.7 %reduce-scatter.7.cloned.1.call-done = f32[128,1536]{1,0:T(8,128)} async-done(((f32[256,1536]{1,0:T(8,128)}), f32[128,1536]{1,0:T(8,128)}) %reduce-scatter.7.cloned.1.call-update) | async-done | bytes 786448 | tf_op jit(solution)/shard_map/reduce_scatter | solution.py:217
  380.8 2.0 multiply_reduce_fusion.1
  383.9 7.3 %all_gather.31 = bf16[256,768]{1,0:T(8,128)(2,1)S(1)} all-gather(bf16[128,768]{1,0:T(8,128)(2,1)S(1)} %get-tuple-element.275), channel_id=1, replica_groups=mesh['dp'=16,'tensor'=2] {'tensor'}, dimensions={0}, use_global_device_ids=true | all-gather | bytes 589824 | tf_op jit(solution)/shard_map/all_gather | solution.py:246
  392.4 78.0 %while.31 = (s32[]{:T(128)}, bf16[6,256,64]{1,2,0:T(8,128)(2,1)}, f32[6,512,64]{1,2,0:T(8,128)}, f32[6,512,64]{1,2,0:T(8,128)}, f32[6,767]{1,0:T(8,128)}, /*inde...) while((s32[]{:T(128)}, bf16[6,256,64]{1,2,0:T(8,128)(2,1)}, ...), condition=%wide.region_23.25_spmd.clone, body=%wide.region_20.24_spmd.clone.sunk | while | flops 85572352 | bytes 19036308 | solution.py:280
  397.8 1.7 fusion.164
  399.5 1.7 fusion.165
  401.2 1.6 fusion.166
  404.0 1.4 dynamic_update_slice.48
  410.8 1.7 fusion.164
  412.5 1.7 fusion.165
  414.2 1.6 fusion.166
  417.0 1.4 dynamic_update_slice.48
  423.8 1.7 fusion.164
  425.5 1.7 fusion.165
  427.2 1.6 fusion.166
  430.0 1.4 dynamic_update_slice.48
  436.8 1.7 fusion.164
  438.5 1.7 fusion.165
  440.2 1.6 fusion.166
  449.8 1.7 fusion.164
  451.5 1.7 fusion.165
  453.2 1.6 fusion.166
  456.0 1.4 dynamic_update_slice.48
  462.8 1.7 fusion.164
  464.5 1.7 fusion.165
  466.3 1.6 fusion.166
  469.1 1.4 dynamic_update_slice.48
  470.4 1.6 select_convert_fusion
  472.1 1.4 fusion.95
  477.7 2.4 pad_maximum_fusion
  481.3 3.9 fusion.96
  485.4 2.7 fusion.83
  490.3 40.5 %all-reduce.3 = (f32[768]{0:T(1024)}, f32[32,12]{0,1:T(8,128)}, f32[768]{0:T(1024)}, f32[768,8]{0,1:T(8,128)}) all-reduce(f32[768]{0:T(1024)S(1)} %get-tuple-element.225, f32[32,12]{0,1:T(8,128)S(1)} %dynamic_update_slice.26, f32[768]{0:T(1024)S(1)} %copy-done.35, ...), channel_id=1, replica_groups=mesh['dp'=16,'tensor'=2] {'dp','tensor'}, use_global_device_ids=true, to_apply=%region_27.29 | all-reduce | flops 8064 | bytes 64512 | tf_op jit(solution)/shard_map/psum | solution.py:328
  530.8 1.8 fusion.61
  532.6 36.9 %reduce-scatter.11.cloned.1.call-done = f32[48,4,384]{2,0,1:T(8,128)} async-done(((f32[768,4,384]{2,0,1:T(8,128)}), f32[48,4,384]{2,0,1:T(8,128)}) %reduce-scatter.11.cloned.1.call-update) | async-done | bytes 294928 | tf_op jit(solution)/shard_map/reduce_scatter | solution.py:304
  569.5 1.7 slice_bitcast_fusion.6
  (390 shorter events, 105.6 us)
Async XLA Ops:
  7.2 234.0 %copy-start = (bf16[768,768]{1,0:T(8,128)(2,1)S(1)}, bf16[768,768]{1,0:T(8,128)(2,1)}, u32[]{:S(2)}) copy-start(bf16[768,768]{1,0:T(8,128)(2,1)} %param.30) | copy-start | bytes 3538948
  7.2 37.0 %copy-start.28 = (bf16[48,384]{1,0:T(8,128)(2,1)S(1)}, bf16[48,384]{1,0:T(8,128)(2,1)}, u32[]{:S(2)}) copy-start(bf16[48,384]{1,0:T(8,128)(2,1)} %param.25) | copy-start | bytes 110596
  7.2 165.2 %reduce-scatter.5.cloned.1.call-start = ((), (), s32[]{:S(2)}) async-start(), calls=%async_computation.8 | async-start | bytes 1179648 | tf_op jit(solution)/shard_map/reduce_scatter | solution.py:153
  9.1 55.2 %copy-start.58 = (f32[128]{0:T(128)}, f32[128]{0:T(128)S(1)}, u32[]{:S(2)}) copy-start(f32[128]{0:T(128)S(1)} %fusion.62) | copy-start | bytes 1540
  9.1 55.2 %copy-start.47 = (f32[128]{0:T(128)}, f32[128]{0:T(128)S(1)}, u32[]{:S(2)}) copy-start(f32[128]{0:T(128)S(1)} %fusion.81) | copy-start | bytes 1540
  43.4 21.7 %copy-start.29 = (bf16[48,384]{1,0:T(8,128)(2,1)S(1)}, bf16[48,384]{1,0:T(8,128)(2,1)}, u32[]{:S(2)}) copy-start(bf16[48,384]{1,0:T(8,128)(2,1)} %param.23) | copy-start | bytes 110596
  43.8 66.2 %collective-permute-start = (bf16[256,384]{1,0:T(8,128)(2,1)S(1)}, bf16[256,384]{1,0:T(8,128)(2,1)S(1)}, u32[]{:S(2)}, u32[]{:S(2)}) collective-permute-start(bf16[256,384]{1,0:T(8,128)(2,1)S(1)} %convolution_convert_fusion.5), channel_id=1, source_target_pairs={{0,2},{2,0},{4,6},{6,4},{8,10},{10,8},{12,14},{14,12},{16,18},{18,... | collective-permute-start | bytes 589832 | tf_op jit(solution)/shard_map/ppermute | solution.py:16
  64.3 24.0 %copy-start.30 = (bf16[48,384]{1,0:T(8,128)(2,1)S(1)}, bf16[48,384]{1,0:T(8,128)(2,1)}, u32[]{:S(2)}) copy-start(bf16[48,384]{1,0:T(8,128)(2,1)} %param.26) | copy-start | bytes 110596
  64.3 45.8 %collective-permute-start.1 = (bf16[256,384]{1,0:T(8,128)(2,1)S(1)}, bf16[256,384]{1,0:T(8,128)(2,1)}, u32[]{:S(2)}, u32[]{:S(2)}) collective-permute-start(bf16[256,384]{1,0:T(8,128)(2,1)S(1)} %convolution_convert_fusion.4), channel_id=1, source_target_pairs={{0,2},{2,0},{4,6},{6,4},{8,10},{10,8},{12,14},{14,12},{16,18},{18,... | collective-permute-start | bytes 589832 | tf_op jit(solution)/shard_map/ppermute | solution.py:16
  64.9 43.9 %copy-start.51 = (s32[1023]{0:T(1024)S(1)}, s32[1023]{0:T(1024)}, u32[]{:S(2)}) copy-start(s32[1023]{0:T(1024)} %param.34) | copy-start | bytes 12280
  64.9 44.0 %copy-start.62 = (f32[32,12]{0,1:T(8,128)S(1)}, f32[32,12]{0,1:T(8,128)}, u32[]{:S(2)}) copy-start(f32[32,12]{0,1:T(8,128)} %param.27) | copy-start | bytes 4612
  153.6 20.8 %copy-start.13 = (bf16[6,256,64]{2,1,0:T(8,128)(2,1)}, bf16[6,256,64]{2,1,0:T(8,128)(2,1)S(1)}, u32[]{:S(2)}) copy-start(bf16[6,256,64]{2,1,0:T(8,128)(2,1)S(1)} %get-tuple-element.539) | copy-start | bytes 589828
  153.6 2.7 copy-start.54
  153.6 2.7 copy-start.33
  153.6 18.8 %copy-start.11 = (bf16[128,768]{1,0:T(8,128)(2,1)S(1)}, bf16[128,768]{1,0:T(8,128)(2,1)}, u32[]{:S(2)}) copy-start(bf16[128,768]{1,0:T(8,128)(2,1)} %param.21) | copy-start | bytes 589828
  153.6 28.2 %copy-start.26 = (bf16[768,8]{0,1:T(8,128)(2,1)S(1)}, bf16[768,8]{0,1:T(8,128)(2,1)}, u32[]{:S(2)}) copy-start(bf16[768,8]{0,1:T(8,128)(2,1)} %param.29) | copy-start | bytes 36868
  156.3 26.4 %copy-start.19 = (bf16[256,768]{1,0:T(8,128)(2,1)S(1)}, bf16[256,768]{1,0:T(8,128)(2,1)}, u32[]{:S(2)}) copy-start(bf16[256,768]{1,0:T(8,128)(2,1)} %param.35) | copy-start | bytes 1179652
  157.8 26.3 %copy-start.36 = (s32[256]{0:T(256)}, s32[256]{0:T(256)S(1)}, u32[]{:S(2)}) copy-start(s32[256]{0:T(256)S(1)} %get-tuple-element.280) | copy-start | bytes 3076
  174.4 9.7 %copy-start.17 = (bf16[128,768]{1,0:T(8,128)(2,1)}, bf16[128,768]{1,0:T(8,128)(2,1)S(1)}, u32[]{:S(2)}) copy-start(bf16[128,768]{1,0:T(8,128)(2,1)S(1)} %multiply_convert_fusion.4) | copy-start | bytes 589828
  184.1 5.6 copy-start.37
  184.1 27.5 %all-to-all-start.2 = ((bf16[16,40,768]{2,1,0:T(8,128)(2,1)}), bf16[16,40,768]{2,1,0:T(8,128)(2,1)S(1)}, u32[]{:S(2)}, u32[]{:S(2)}) async-start(bf16[16,40,768]{2,1,0:T(8,128)(2,1)} %bitcast.23), calls=%async_computation.3 | async-start | bytes 1966080 | tf_op jit(solution)/shard_map/all_to_all | solution.py:188
  211.6 11.1 %copy-start.22 = (bf16[16,40,768]{2,1,0:T(8,128)(2,1)}, bf16[16,40,768]{2,1,0:T(8,128)(2,1)S(1)}, u32[]{:S(2)}) copy-start(bf16[16,40,768]{2,1,0:T(8,128)(2,1)S(1)} %all-to-all-done.2) | copy-start | bytes 2949124
  212.7 28.5 %all-to-all-start = ((bf16[16,40,768]{2,1,0:T(8,128)(2,1)}), bf16[16,40,768]{2,1,0:T(8,128)(2,1)}, u32[]{:S(2)}, u32[]{:S(2)}) async-start(bf16[16,40,768]{2,1,0:T(8,128)(2,1)} %bitcast.17), calls=%async_computation.1 | async-start | bytes 1966080 | tf_op jit(solution)/shard_map/all_to_all | solution.py:187
  241.2 4.8 copy-start.60
  246.0 2.6 copy-start.64
  248.6 45.4 %all-to-all-start.1 = ((f32[16,40,768]{2,1,0:T(8,128)}), f32[16,40,768]{2,1,0:T(8,128)S(1)}, u32[]{:S(2)}, u32[]{:S(2)}) async-start(f32[16,40,768]{2,1,0:T(8,128)} %bitcast.216), calls=%async_computation.2 | async-start | bytes 3932160 | tf_op jit(solution)/shard_map/all_to_all | solution.py:204
  294.0 10.9 %copy-start.38 = (s32[256]{0:T(256)S(1)}, s32[256]{0:T(256)}, u32[]{:S(2)}) copy-start(s32[256]{0:T(256)} %copy-done.36) | copy-start | bytes 3076
  294.0 49.8 %all-to-all-start.3 = ((f32[16,40,768]{2,1,0:T(8,128)}), f32[16,40,768]{2,1,0:T(8,128)}, u32[]{:S(2)}, u32[]{:S(2)}) async-start(f32[16,40,768]{2,1,0:T(8,128)} %bitcast.215), calls=%async_computation.4 | async-start | bytes 3932160 | tf_op jit(solution)/shard_map/all_to_all | solution.py:207
  304.8 74.7 %reduce-scatter.7.cloned.1.call-start = ((), (), s32[]{:S(2)}) async-start(), calls=%async_computation.9 | async-start | bytes 2359296 | tf_op jit(solution)/shard_map/reduce_scatter | solution.py:217
  348.1 32.6 %copy-start.44 = (f32[256]{0:T(256)S(1)}, f32[256]{0:T(256)}, u32[]{:S(2)}) copy-start(f32[256]{0:T(256)} %copy-done.43) | copy-start | bytes 3076
  348.1 32.6 %copy-start.3 = (f32[128,768]{1,0:T(8,128)S(1)}, f32[128,768]{1,0:T(8,128)}, u32[]{:S(2)}) copy-start(f32[128,768]{1,0:T(8,128)} %copy-done.2) | copy-start | bytes 1179652
  348.1 32.6 %copy-start.27 = (bf16[768,8]{0,1:T(8,128)(2,1)S(1)}, bf16[768,8]{0,1:T(8,128)(2,1)}, u32[]{:S(2)}) copy-start(bf16[768,8]{0,1:T(8,128)(2,1)} %param.29) | copy-start | bytes 36868
  348.2 32.6 %copy-start.31 = (f32[256,8]{0,1:T(8,128)S(1)}, f32[256,8]{0,1:T(8,128)}, u32[]{:S(2)}) copy-start(f32[256,8]{0,1:T(8,128)} %get-tuple-element.282) | copy-start | bytes 24580
  348.2 32.6 %copy-start.50 = (f32[128]{0:T(128)S(1)}, f32[128]{0:T(128)}, u32[]{:S(2)}) copy-start(f32[128]{0:T(128)} %copy-done.49) | copy-start | bytes 1540
  348.2 34.6 %copy-start.57 = (f32[128]{0:T(128)S(1)}, f32[128]{0:T(128)}, u32[]{:S(2)}) copy-start(f32[128]{0:T(128)} %copy-done.56) | copy-start | bytes 1540
  348.2 140.9 %reduce-scatter.9.cloned.1.call-start = ((), (), s32[]{:S(2)}) async-start(), calls=%async_computation.10 | async-start | bytes 589824 | tf_op jit(solution)/shard_map/reduce_scatter | solution.py:311
  348.8 34.0 %copy-start.41 = (pred[256,8]{0,1:T(8,128)(4,1)}, pred[256,8]{0,1:T(8,128)(4,1)S(1)}, u32[]{:S(2)}) copy-start(pred[256,8]{0,1:T(8,128)(4,1)S(1)} %iota_compare_fusion.8) | copy-start | bytes 6148
  379.5 3.4 copy-start.16
  380.7 2.2 copy-start.39
  380.8 2.1 copy-start.45
  380.8 10.4 %copy-start.6 = (bf16[768,384]{1,0:T(8,128)(2,1)S(1)}, bf16[768,384]{1,0:T(8,128)(2,1)}, u32[]{:S(2)}) copy-start(bf16[768,384]{1,0:T(8,128)(2,1)} %all_gather.29) | copy-start | bytes 1769476
  470.4 1.7 copy-start.5
  470.4 3.4 copy-start.14
  470.4 3.4 copy-start.15
  472.0 1.8 collective-permute-start.2
  472.1 1.9 copy-start.8
  474.0 2.1 copy-start.24
  474.6 1.9 copy-start.25
  475.8 93.7 %reduce-scatter.11.cloned.1.call-start = ((), (), s32[]{:S(2)}) async-start(), calls=%async_computation.11 | async-start | bytes 5013504 | tf_op jit(solution)/shard_map/reduce_scatter | solution.py:304
  481.3 3.9 copy-start.23
  481.3 3.9 copy-start.65
  485.2 2.8 copy-start.53
  485.2 2.8 copy-start.61
  485.2 3.3 copy-start.18
  485.3 3.3 copy-start.32
  485.3 3.3 copy-start.40
  485.3 3.3 copy-start.42
  485.3 3.3 copy-start.46
  485.3 3.8 copy-start.12
  485.3 3.8 copy-start.48
  485.3 5.0 copy-start.35
  485.3 45.4 %copy-start.59 = (f32[128]{0:T(128)S(1)}, f32[128]{0:T(128)}, u32[]{:S(2)}) copy-start(f32[128]{0:T(128)} %copy-done.58) | copy-start | bytes 1540
  485.3 45.4 %copy-start.21 = (f32[128,768]{1,0:T(8,128)S(1)}, f32[128,768]{1,0:T(8,128)}, u32[]{:S(2)}) copy-start(f32[128,768]{1,0:T(8,128)} %get-tuple-element.276) | copy-start | bytes 1179652
  485.4 85.8 %copy-start.1 = (bf16[768,768]{1,0:T(8,128)(2,1)S(1)}, bf16[768,768]{1,0:T(8,128)(2,1)}, u32[]{:S(2)}) copy-start(bf16[768,768]{1,0:T(8,128)(2,1)} %param.30) | copy-start | bytes 3538948
  (13 other events, 12.9 us)
Sparse Core Ops, SparseCore 0:
  156.4 15.9 reduce-scatter.4
  348.3 31.1 reduce-scatter.6
  475.9 13.2 reduce-scatter.8
  493.4 76.0 reduce-scatter.10
where the time goes:
time: 582 us; the launch traced here: 578 us
  waiting for transfers between devices  196 us (34%)
  blocking collectives  148 us (25%)
  matrix products  97.6 us (17%)
  local copies, waits for them, and re-layouts  68.3 us (12%)
  starting transfers between devices  30.9 us (5%)
  other arithmetic  21.8 us (4%)
  between operations  14.7 us (3%)
    psum x1, blocking collectives, per_device(): lax.psum((grad_gain_first, grad_gain_second, grad_router_part, bias_full)...  40.5 us
    all_to_all x1, waiting for transfers between devices, per_device(): lax.all_to_all(grad_part.reshape(-1, capacity, width), 'dp', split_axis=0...  37.6 us
    reduce_scatter x1, waiting for transfers between devices, per_device(): lax.psum_scatter(jnp.stack(pieces, axis=1), 'dp', scatter_dimension=0, ti...  36.9 us
    all_to_all x1, waiting for transfers between devices, per_device(): lax.all_to_all(expert_part.reshape(-1, capacity, width), 'dp', split_axis...  35.4 us
    reduce_scatter x1, waiting for transfers between devices, per_device(): lax.psum_scatter(jnp.concatenate([jnp.take(slot_out, target, axis=0), jnp...  30.7 us
    all_gather x1, blocking collectives, fetch_attention(): lax.all_gather(w_key, 'dp', axis=0, tiled=True)  23.9 us
    all_to_all x1, waiting for transfers between devices, per_device(): lax.all_to_all(to_owners(grad_expert), 'dp', split_axis=0, concat_axis=0,...  21.6 us
    all_gather x1, blocking collectives, fetch_attention(): lax.all_gather(w_query, 'dp', axis=0, tiled=True)  20.6 us
  transfers between devices with their start and end apart: 11, of which 9 were waited for; matrix products, arithmetic and copies ran while one was open for 5% of the time, Pallas kernels for 0%

commit v1 on v0

v1 whole, which is shorter than its diff:
```python
import functools

import jax
import jax.numpy as jnp
from jax import lax
from jax.experimental import pallas as pl
from jax.experimental.pallas import tpu as pltpu
from jax.sharding import Mesh, PartitionSpec as P

HD = 64
GROUP = 2
DIRECT = 8
TILE = 128

norm_eps = 1e-06
masked_value = -1e30
exact = lax.Precision.HIGHEST
bf16 = jnp.bfloat16
f32 = jnp.float32

VMEM = pl.BlockSpec(memory_space=pltpu.VMEM)
SMEM = pl.BlockSpec(memory_space=pltpu.SMEM)


def across(shard, axis, bits):
    return lax.ppermute(shard, axis, [(i, i ^ bits) for i in range(lax.axis_size(axis))])


def call(body, name, outs, args, smem=0, scratch=(), flops=0, limit=40):
    moved = sum(a.size * a.dtype.itemsize for a in args) + sum(
        o.size * jnp.dtype(o.dtype).itemsize for o in outs
    )
    return pl.pallas_call(
        body,
        name=name,
        out_shape=outs,
        in_specs=[SMEM] * smem + [VMEM] * (len(args) - smem),
        out_specs=[VMEM] * len(outs),
        scratch_shapes=scratch,
        compiler_params=pltpu.CompilerParams(vmem_limit_bytes=limit * 1024 * 1024),
        cost_estimate=pl.CostEstimate(flops=flops, bytes_accessed=moved, transcendentals=0),
    )(*args)


def out(shape, dtype):
    return jax.ShapeDtypeStruct(shape, dtype)


def mm(a, b):
    return jnp.dot(a, b, preferred_element_type=f32)


def mm_bt(a, b):
    return lax.dot_general(a, b, (((1,), (1,)), ((), ())), preferred_element_type=f32)


def mm_at(a, b):
    return lax.dot_general(a, b, (((0,), (0,)), ((), ())), preferred_element_type=f32)


def project_kernel(parts, ids, own_ref, other_ref, *refs):
    pieces = refs[:parts]
    wqkv_ref, wo_ref, seq_ref, qkv_ref = refs[parts:]
    core = ids[0]
    me = ids[1]
    rows = pieces[0].shape[0]
    cols = wqkv_ref.shape[1]
    half = own_ref.shape[0]
    seq_ref[pl.ds(pl.multiple_of(core * half, half), half), :] = own_ref[...]
    seq_ref[pl.ds(pl.multiple_of((1 - core) * half, half), half), :] = other_ref[...]
    for i, piece in enumerate(pieces):
        start = 0 if parts == 1 else pl.multiple_of((me ^ i) * rows, rows)
        wqkv_ref[pl.ds(start, rows), :] = piece[:, :cols]
        wo_ref[pl.ds(start, rows), :] = piece[:, cols:]
    for i in range(0, 2 * half, 256):
        qkv_ref[i : i + 256, :] = mm(seq_ref[i : i + 256, :], wqkv_ref[...]).astype(bf16)


def attend_kernel(heads, ids, qkv_ref, vec_ref, row_docs, col_docs, *refs):
    probs_ref, mixed_ref, keep_ref, send_ref = refs
    core = ids[0]
    seq = qkv_ref.shape[0]
    width = heads * HD
    half = seq // GROUP
    span = seq + TILE
    for h in range(heads):
        at = h * HD
        key = qkv_ref[:, width + at : width + at + HD]
        value = qkv_ref[:, 2 * width + at : 2 * width + at + HD]
        for i in range(0, seq, TILE):
            base = seq - TILE - i
            seg = jnp.broadcast_to(vec_ref[h : h + 1, base : base + span], (TILE, span))
            bias = pltpu.roll(seg, span - TILE + 1, 1, stride=1, stride_axis=0)[:, :seq]
            scores = mm_bt(qkv_ref[i : i + TILE, at : at + HD], key) * HD**-0.5 + bias
            scores = jnp.where(row_docs[i : i + TILE, :] == col_docs[...], scores, masked_value)
            peak = jnp.max(scores, axis=1, keepdims=True)
            exp_scores = jnp.exp(scores - peak)
            probs = exp_scores / jnp.sum(exp_scores, axis=1, keepdims=True)
            probs_ref[h, i : i + TILE, :] = probs
            mixed_ref[i : i + TILE, at : at + HD] = mm(probs.astype(bf16), value).astype(bf16)
    keep_ref[...] = mixed_ref[pl.ds(pl.multiple_of(core * half, half), half), :]
    send_ref[...] = mixed_ref[pl.ds(pl.multiple_of((1 - core) * half, half), half), :]


def attended_kernel(keep_ref, got_ref, wo_ref, wo_other_ref, out_ref):
    total = mm_bt(keep_ref[...], wo_ref[...]) + mm_bt(got_ref[...], wo_other_ref[...])
    out_ref[...] = total.astype(bf16)


def dispatch_kernel(x_ref, own_ref, got_ref, gain_ref, table_ref, hidden_ref, *blocks):
    hidden = x_ref[...].astype(f32) + (own_ref[...].astype(f32) + got_ref[...].astype(f32))
    hidden_ref[...] = hidden
    scale = lax.rsqrt(jnp.mean(hidden * hidden, axis=1, keepdims=True) + norm_eps)
    normed = (hidden * scale * gain_ref[...]).astype(bf16)
    slots = mm(table_ref[...], normed)
    rows = blocks[0].shape[0]
    for i, block in enumerate(blocks):
        block[...] = slots[i * rows : (i + 1) * rows, :].astype(bf16)


def expert_kernel(ids, own_ref, other_ref, h_ref, wup_ref, wr_ref, *refs):
    active_ref, gup_ref, chosen_ref, keep_ref, send_ref, router_ref = refs
    rows = own_ref.shape[0]
    step = rows // 2
    router = jnp.zeros(router_ref.shape, f32)
    root = 0.7978845608028654
    for i in range(0, 2 * rows, step):
        src = own_ref if i < rows else other_ref
        at = i % rows
        slots = src[at : at + step, :]
        logits = mm(slots, wr_ref[...])
        peak = jnp.max(logits, axis=1, keepdims=True)
        exp_logits = jnp.exp(logits - peak)
        gates = exp_logits / jnp.sum(exp_logits, axis=1, keepdims=True)
        mine = lax.broadcasted_iota(jnp.int32, gates.shape, 1) == ids[1]
        chosen = jnp.sum(jnp.where(mine, gates, 0.0), axis=1, keepdims=True)
        chosen_ref[i : i + step, :] = chosen
        up = mm(slots, wup_ref[...])
        square = up * up
        bent = jnp.tanh(root * (up + 0.044715 * up * square))
        low = (0.5 * up * (1.0 + bent)).astype(bf16)
        active_ref[i : i + step, :] = low
        slope = 0.5 * (1.0 + bent) + 0.5 * up * (1.0 - bent * bent) * root * (
            1.0 + 3.0 * 0.044715 * square
        )
        back = h_ref[i : i + step, :]
        gup = (chosen * back * slope).astype(bf16)
        gup_ref[i : i + step, :] = gup
        grad_chosen = jnp.sum(low.astype(f32) * back, axis=1, keepdims=True)
        grad_logits = gates * (jnp.where(mine, 1.0, 0.0) - chosen) * grad_chosen
        grad_logits = grad_logits.astype(bf16)
        router = router + mm_at(slots, grad_logits)
        grad = mm_bt(gup, wup_ref[...]) + mm_bt(grad_logits, wr_ref[...])
        if i < rows:
            keep_ref[at : at + step, :] = grad
        else:
            send_ref[at : at + step, :] = grad.astype(bf16)
    router_ref[...] = router


def expert_rest_kernel(own_ref, other_ref, cots_ref, active_ref, gup_ref, chosen_ref, wdown_ref, *refs):
    keep_ref, send_ref, gwup_ref, gwdown_ref = refs
    rows = own_ref.shape[0]
    result = mm_bt(active_ref[...], wdown_ref[...]) * chosen_ref[...]
    keep_ref[...] = result[:rows, :]
    send_ref[...] = result[rows:, :].astype(bf16)
    gwup_ref[...] = mm_at(own_ref[...], gup_ref[:rows, :]) + mm_at(other_ref[...], gup_ref[rows:, :])
    grads = (chosen_ref[...] * cots_ref[...].astype(f32)).astype(bf16)
    gwdown_ref[...] = mm_at(grads, active_ref[...])


def join_kernel(keep_ref, got_ref, *blocks):
    total = keep_ref[...] + got_ref[...].astype(f32)
    rows = blocks[0].shape[0]
    for i, block in enumerate(blocks):
        block[...] = total[i * rows : (i + 1) * rows, :].astype(bf16)


def gather_kernel(back_table_ref, *refs):
    blocks = refs[:-1]
    slots = jnp.concatenate([b[...].astype(f32) for b in blocks], axis=0).astype(bf16)
    refs[-1][...] = mm(back_table_ref[...], slots).astype(bf16)


def hidden_back_kernel(hidden_ref, own_ref, got_ref, cot_ref, gain_ref, grad_ref, low_ref, dgain_ref):
    hidden = hidden_ref[...]
    grad_normed = own_ref[...].astype(f32) + got_ref[...].astype(f32)
    scale = lax.rsqrt(jnp.mean(hidden * hidden, axis=1, keepdims=True) + norm_eps)
    dgain_ref[...] = jnp.sum(grad_normed * hidden * scale, axis=0, keepdims=True)
    pulled = gain_ref[...] * grad_normed
    inner = jnp.mean(pulled * hidden, axis=1, keepdims=True)
    grad = cot_ref[...].astype(f32) + scale * pulled - hidden * (scale * scale * scale) * inner
    grad_ref[...] = grad
    low_ref[...] = grad.astype(bf16)


def attend_back_kernel(heads, parts, ids, own_ref, other_ref, wo_ref, qkv_ref, probs_ref, seq_ref, mixed_ref, *refs):
    dqkv_ref, gwo_ref, diag_ref = refs[:3]
    blocks = refs[3 : 3 + parts]
    ga_ref, gm_ref, ds_ref, gw_ref = refs[3 + parts :]
    core = ids[0]
    me = ids[1]
    half = own_ref.shape[0]
    seq = qkv_ref.shape[0]
    width = heads * HD
    span = seq + TILE
    ga_ref[pl.ds(pl.multiple_of(core * half, half), half), :] = own_ref[...]
    ga_ref[pl.ds(pl.multiple_of((1 - core) * half, half), half), :] = other_ref[...]
    gm_ref[...] = mm(ga_ref[...], wo_ref[...]).astype(bf16)
    gwo_ref[...] = mm_at(ga_ref[...], mixed_ref[...]).astype(bf16)
    flip = (
        lax.broadcasted_iota(jnp.int32, (TILE, TILE), 0)
        + lax.broadcasted_iota(jnp.int32, (TILE, TILE), 1)
        == TILE - 1
    ).astype(bf16)
    diag_ref[...] = jnp.zeros_like(diag_ref)
    for h in range(heads):
        at = h * HD
        key = qkv_ref[:, width + at : width + at + HD]
        value = qkv_ref[:, 2 * width + at : 2 * width + at + HD]
        for i in range(0, seq, TILE):
            probs = probs_ref[h, i : i + TILE, :]
            grad_probs = mm_bt(gm_ref[i : i + TILE, at : at + HD], value)
            inner = jnp.sum(probs * grad_probs, axis=1, keepdims=True)
            grad_scores = (probs * (grad_probs - inner)).astype(bf16)
            ds_ref[i : i + TILE, :] = grad_scores
            dqkv_ref[i : i + TILE, at : at + HD] = (mm(grad_scores, key) * HD**-0.5).astype(bf16)
            flipped = mm(flip, grad_scores)
            padded = jnp.concatenate([flipped, jnp.zeros((TILE, TILE), f32)], axis=1)
            skewed = pltpu.roll(padded, 0, 1, stride=1, stride_axis=0)
            base = seq - TILE - i
            diag_ref[h : h + 1, base : base + span] += jnp.sum(skewed, axis=0, keepdims=True)
        dqkv_ref[:, width + at : width + at + HD] = (
            mm_at(ds_ref[...], qkv_ref[:, at : at + HD]) * HD**-0.5
        ).astype(bf16)
        dqkv_ref[:, 2 * width + at : 2 * width + at + HD] = mm_at(
            probs_ref[h].astype(bf16), gm_ref[:, at : at + HD]
        ).astype(bf16)
    gw_ref[...] = mm_at(seq_ref[...], dqkv_ref[...])
    rows = blocks[0].shape[0]
    for i, block in enumerate(blocks):
        start = 0 if parts == 1 else pl.multiple_of((me ^ i) * rows, rows)
        block[...] = gw_ref[pl.ds(start, rows), :].astype(bf16)


def normed_back_kernel(ids, dqkv_ref, wqkv_ref, keep_ref, send_ref):
    core = ids[0]
    half = keep_ref.shape[0]
    mine = dqkv_ref[pl.ds(pl.multiple_of(core * half, half), half), :]
    keep_ref[...] = mm_bt(mine, wqkv_ref[...])
    theirs = dqkv_ref[pl.ds(pl.multiple_of((1 - core) * half, half), half), :]
    send_ref[...] = mm_bt(theirs, wqkv_ref[...]).astype(bf16)


def rms_scale(values, gain):
    return values * lax.rsqrt(jnp.mean(values * values, axis=-1, keepdims=True) + norm_eps) * gain


def in_order(first, mine, other):
    return jnp.where(first, jnp.concatenate([mine, other]), jnp.concatenate([other, mine]))


def per_device(
    tokens,
    gain_one,
    w_query,
    w_key,
    w_value,
    w_out,
    bias_table,
    gain_two,
    w_router,
    w_up,
    w_down,
    routes,
    doc_lengths,
    buckets,
    cotangent,
):
    own_rows, width = tokens.shape
    block_rows = routes.shape[0]
    seq = block_rows * GROUP
    cols = w_query.shape[1] // GROUP
    heads = cols // HD
    experts = w_router.shape[1]
    capacity = max(2, (5 * block_rows + 4 * experts - 1) // (4 * experts))
    slots = experts * capacity
    nodes = lax.axis_size("node")
    core = lax.axis_index("core")
    side = lax.axis_index("tensor")
    me = lax.axis_index("node")
    direct = nodes == DIRECT
    parts = nodes if direct else 1
    ids = jnp.stack([core, me]).astype(jnp.int32)
    node_rows = width // nodes

    def trade(blocks):
        if direct:
            return [blocks[0]] + [across(blocks[i], "node", i) for i in range(1, nodes)]
        stacked = blocks[0].reshape(nodes, -1, blocks[0].shape[1])
        back = lax.all_to_all(stacked, "node", split_axis=0, concat_axis=0, tiled=True)
        return [back.reshape(blocks[0].shape)]

    def trade_natural(rows):
        stacked = rows.reshape(nodes, -1, rows.shape[-1])
        return lax.all_to_all(stacked, "node", split_axis=0, concat_axis=0, tiled=True)

    def reorder(stacked):
        if not direct:
            return stacked
        return jnp.concatenate(
            [lax.dynamic_slice_in_dim(stacked, me ^ i, 1, 0) for i in range(nodes)]
        )

    shares = jnp.stack([w_query, w_key, w_value, w_out]).reshape(4, -1, GROUP, cols)
    shares = jnp.moveaxis(shares, 0, 2).reshape(-1, GROUP, 4 * cols)
    share_kept = lax.dynamic_index_in_dim(shares, core, 1, keepdims=False)
    share_sent = lax.dynamic_index_in_dim(shares, 1 - core, 1, keepdims=False)
    piece = in_order(core == 0, share_kept, across(share_sent, "core", 1))
    if direct:
        pieces = {0: piece}
        for i in (2, 4, 6):
            pieces[i] = across(piece, "node", i)
        for i in (0, 2, 4, 6):
            pieces[i + 1] = across(pieces[i], "node", 1)
        pieces = [pieces[i] for i in range(nodes)]
    else:
        pieces = [lax.all_gather(piece, "node", axis=0, tiled=True)]

    x_rows = in_order(side == 0, tokens, across(tokens, "tensor", 1))
    gain_first = gain_one.astype(f32)
    gain_second = gain_two.astype(f32)[None, :]
    normed = rms_scale(x_rows.astype(f32), gain_first).astype(bf16)
    normed_other = across(normed, "core", 1)

    expert_ids = routes[:, 0]
    picks = (expert_ids[:, None] == jnp.arange(experts, dtype=jnp.int32)[None, :]).astype(jnp.int32)
    slot_index = jnp.sum((jnp.cumsum(picks, axis=0) - 1) * picks, axis=1)
    target = expert_ids * capacity + slot_index
    codes = jnp.arange(slots, dtype=jnp.int32)
    turned = ((codes // capacity) ^ me) * capacity + codes % capacity if direct else codes
    table = (turned[:, None] == target[None, :]).astype(bf16)
    back_table = (target[:, None] == turned[None, :]).astype(bf16)
    plain_table = (codes[:, None] == target[None, :]).astype(bf16)

    cot_slots = mm(plain_table, cotangent).astype(bf16)
    cots_own = reorder(trade_natural(cot_slots)).reshape(slots, width)
    cots = jnp.concatenate([cots_own, across(cots_own, "core", 1)])
    back_active = mm(cots, w_down)

    lengths_row = lax.dynamic_slice_in_dim(doc_lengths, me, 1, 0)[0]
    ends = jnp.cumsum(lengths_row)
    places = jnp.arange(seq, dtype=jnp.int32)
    docs = jnp.sum((ends[None, :] <= places[:, None]).astype(jnp.int32), axis=1)
    bucket_count = bias_table.shape[0]
    bucket_hot = (
        jnp.pad(buckets, (0, 1))[:, None] == jnp.arange(bucket_count, dtype=jnp.int32)[None, :]
    ).astype(f32)
    head_start = (side * GROUP + core) * heads
    bias_here = lax.dynamic_slice_in_dim(bias_table, head_start, heads, 1)
    bias_vectors = lax.dot_general(
        bias_here, bucket_hot, (((0,), (1,)), ((), ())), precision=exact, preferred_element_type=f32
    )

    wqkv, wo, normed_seq, qkv = call(
        functools.partial(project_kernel, parts),
        "project",
        [
            out((width, 3 * cols), bf16),
            out((width, cols), bf16),
            out((seq, width), bf16),
            out((seq, 3 * cols), bf16),
        ],
        [ids, normed, normed_other, *pieces],
        smem=1,
        flops=2 * seq * width * 3 * cols,
    )
    wo_other = across(wo, "core", 1)
    probs, mixed, mixed_kept, mixed_sent = call(
        functools.partial(attend_kernel, heads),
        "attend",
        [
            out((heads, seq, seq), f32),
            out((seq, cols), bf16),
            out((block_rows, cols), bf16),
            out((block_rows, cols), bf16),
        ],
        [ids, qkv, bias_vectors, docs[:, None], docs[None, :]],
        smem=1,
        flops=8 * heads * seq * seq * 256,
    )
    mixed_got = across(mixed_sent, "core", 1)
    attended = call(
        attended_kernel,
        "attended",
        [out((block_rows, width), bf16)],
        [mixed_kept, mixed_got, wo, wo_other],
        flops=4 * block_rows * width * cols,
    )[0]
    attended_got = across(attended, "tensor", 1)

    block_shapes = [out((slots // parts, width), bf16)] * parts
    hidden, *blocks = call(
        dispatch_kernel,
        "dispatch",
        [out((block_rows, width), f32), *block_shapes],
        [x_rows, attended, attended_got, gain_second, table],
        flops=2 * slots * block_rows * width,
    )
    received = trade(blocks)
    slots_own = jnp.concatenate(received)
    slots_other = across(slots_own, "core", 1)
    active, grad_upward, chosen, grad_kept, grad_sent, router_part = call(
        expert_kernel,
        "expert",
        [
            out((2 * slots, w_up.shape[1]), bf16),
            out((2 * slots, w_up.shape[1]), bf16),
            out((2 * slots, 1), f32),
            out((slots, width), f32),
            out((slots, width), bf16),
            out(w_router.shape, f32),
        ],
        [ids, slots_own, slots_other, back_active, w_up, w_router],
        smem=1,
        flops=8 * slots * width * w_up.shape[1],
    )
    grad_blocks = call(
        join_kernel, "join_grad", block_shapes, [grad_kept, across(grad_sent, "core", 1)]
    )
    grad_back = trade(grad_blocks)
    grad_normed_two = call(
        gather_kernel,
        "gather_grad",
        [out((block_rows, width), bf16)],
        [back_table, *grad_back],
        flops=2 * slots * block_rows * width,
    )[0]
    grad_normed_two_got = across(grad_normed_two, "tensor", 1)

    out_kept, out_sent, grad_w_up_here, grad_w_down_here = call(
        expert_rest_kernel,
        "expert_rest",
        [
            out((slots, width), f32),
            out((slots, width), bf16),
            out(w_up.shape, f32),
            out(w_down.shape, f32),
        ],
        [slots_own, slots_other, cots, active, grad_upward, chosen, w_down],
        flops=12 * slots * width * w_up.shape[1],
    )
    out_slots = (out_kept + across(out_sent, "core", 1).astype(f32)).astype(bf16)
    out_slots = reorder(out_slots.reshape(nodes, -1, width))
    out_back = trade_natural(out_slots).reshape(slots, width)
    returned = lax.dot_general(
        plain_table, out_back, (((0,), (0,)), ((), ())), preferred_element_type=f32
    ).astype(bf16)

    def half_of(rows, index):
        return lax.dynamic_slice_in_dim(rows, index * own_rows, own_rows, 0)

    returned_got = across(half_of(returned, 1 - side), "tensor", 1)
    activations = (
        half_of(hidden, side) + (half_of(returned, side).astype(f32) + returned_got.astype(f32))
    ).astype(bf16)

    grad_hidden, grad_attended, gain_two_part = call(
        hidden_back_kernel,
        "hidden_back",
        [out((block_rows, width), f32), out((block_rows, width), bf16), out((1, width), f32)],
        [hidden, grad_normed_two, grad_normed_two_got, cotangent, gain_second],
    )
    grad_attended_other = across(grad_attended, "core", 1)
    dqkv, gwo, diagonals, *grad_weights = call(
        functools.partial(attend_back_kernel, heads, parts),
        "attend_back",
        [
            out((seq, 3 * cols), bf16),
            out((width, cols), bf16),
            out((heads, 2 * seq), f32),
            *([out((width // parts, 3 * cols), bf16)] * parts),
        ],
        [ids, grad_attended, grad_attended_other, wo, qkv, probs, normed_seq, mixed],
        smem=1,
        scratch=[
            pltpu.VMEM((seq, width), bf16),
            pltpu.VMEM((seq, cols), bf16),
            pltpu.VMEM((seq, seq), bf16),
            pltpu.VMEM((width, 3 * cols), f32),
        ],
        flops=16 * heads * seq * seq * 256,
    )
    received_weights = trade(grad_weights)
    summed_weights = sum(r.reshape(-1, node_rows, 3 * cols).astype(f32).sum(0) for r in received_weights)
    summed_out = jnp.sum(trade_natural(gwo).astype(f32), axis=0)
    node_sums = jnp.concatenate([summed_weights, summed_out], axis=1)
    shard_rows = w_query.shape[0]
    sums_kept = lax.dynamic_slice_in_dim(node_sums, core * shard_rows, shard_rows, 0)
    sums_sent = lax.dynamic_slice_in_dim(node_sums, (1 - core) * shard_rows, shard_rows, 0)
    sums_got = across(sums_sent, "core", 1)

    def columns(index):
        mine = sums_kept[:, index * cols : (index + 1) * cols]
        theirs = sums_got[:, index * cols : (index + 1) * cols]
        return jnp.where(
            core == 0,
            jnp.concatenate([mine, theirs], axis=1),
            jnp.concatenate([theirs, mine], axis=1),
        )

    grad_kept, grad_sent = call(
        normed_back_kernel,
        "normed_back",
        [out((block_rows, width), f32), out((block_rows, width), bf16)],
        [ids, dqkv, wqkv],
        smem=1,
        flops=2 * seq * width * 3 * cols,
    )
    grad_normed = grad_kept + across(grad_sent, "core", 1).astype(f32)
    x_wide = x_rows.astype(f32)
    scale = lax.rsqrt(jnp.mean(x_wide * x_wide, axis=1, keepdims=True) + norm_eps)
    gain_one_part = jnp.sum(grad_normed * x_wide * scale, axis=0)
    grad_normed_got = across(half_of(grad_normed, 1 - side).astype(bf16), "tensor", 1)
    grad_normed_own = half_of(grad_normed, side) + grad_normed_got.astype(f32)
    x_own = tokens.astype(f32)
    norm_first, norm_pull_one = jax.vjp(lambda v: rms_scale(v, gain_first), x_own)
    input_grad = half_of(grad_hidden, side) + norm_pull_one(grad_normed_own)[0]

    bias_part = lax.dot_general(
        bucket_hot, diagonals, (((0,), (1,)), ((), ())), precision=exact, preferred_element_type=f32
    )
    bias_full = lax.dynamic_update_slice(
        jnp.zeros(bias_table.shape, f32), bias_part, (jnp.int32(0), head_start)
    )
    gain_two_part = jnp.where(side == 0, gain_two_part[0], 0.0)
    small = jnp.concatenate(
        [gain_one_part, gain_two_part, bias_full.reshape(-1), router_part.reshape(-1)]
    ).reshape(-1, 128)
    small = small + across(small, "core", 1)
    small = small + across(small, "tensor", 1)
    if direct:
        for bits in (1, 2, 4):
            small = small + across(small, "node", bits)
    else:
        small = lax.psum(small, "node")
    small = small.reshape(-1)
    bias_size = bias_table.size
    return (
        activations,
        input_grad,
        small[:width],
        columns(0),
        columns(1),
        columns(2),
        columns(3),
        small[2 * width : 2 * width + bias_size].reshape(bias_table.shape),
        small[width : 2 * width],
        small[2 * width + bias_size :].reshape(w_router.shape),
        grad_w_up_here,
        grad_w_down_here,
    )


def solution(mesh):
    dp, tensor = mesh.shape["dp"], mesh.shape["tensor"]
    grid = Mesh(mesh.devices.reshape(dp // GROUP, GROUP, tensor), ("node", "core", "tensor"))
    dp = ("node", "core")
    every = ("node", "core", "tensor")
    in_specs = (
        P(every, None),
        P(),
        P(dp, "tensor"),
        P(dp, "tensor"),
        P(dp, "tensor"),
        P(dp, "tensor"),
        P(),
        P(),
        P(),
        P(None, every),
        P(None, every),
        P(dp, None),
        P(),
        P(),
        P(dp, None),
    )
    out_specs = (
        P(every, None),
        P(every, None),
        P(),
        P(dp, "tensor"),
        P(dp, "tensor"),
        P(dp, "tensor"),
        P(dp, "tensor"),
        P(),
        P(),
        P(),
        P(None, every),
        P(None, every),
    )
    return jax.shard_map(
        per_device, mesh=grid, in_specs=in_specs, out_specs=out_specs, check_vma=False
    )
```

time: 582 us -> 219 us (0.38)
  blocking collectives: 148 us -> 0 us
  waiting for transfers between devices: 196 us -> 51.4 us
  matrix products: 97.6 us -> 6.8 us
  starting transfers between devices: 30.9 us -> 83.2 us
  local copies, waits for them, and re-layouts: 68.3 us -> 30.8 us
  Pallas kernels: 0 us -> 31.3 us
  between operations: 14.7 us -> 1.53 us
  other arithmetic: 21.8 us -> 13.1 us
    all_to_all x4 -> x3, waiting for transfers between devices: 113 us -> 0.01 us  [trade_natural(): lax.all_to_all(stacked, 'node', split_axis=0, concat_axis=0, tiled=True)]
    all_gather x7 -> x0, blocking collectives: 107 us -> none  [the longest x1 23.9 us: fetch_attention(): lax.all_gather(w_key, 'dp', axis=0, tiled=True)]
    dot_general x67 -> x5, matrix products: 97.6 us -> 6.8 us  [the longest x2 4.27 us: mm(): return jnp.dot(a, b, preferred_element_type=f32)]
    reduce_scatter x4 -> x0, waiting for transfers between devices: 82.6 us -> none  [the longest x1 36.9 us: per_device(): lax.psum_scatter(jnp.stack(pieces, axis=1), 'dp', scatter_dimension=0, ti...]
    ppermute x3 -> x49, starting transfers between devices: 0.9 us -> 66.9 us  [across(): lax.ppermute(shard, axis, [(i, i ^ bits) for i in range(lax.axis_size(axi...]
    ppermute x3 -> x49, waiting for transfers between devices: 0.29 us -> 51.4 us  [across(): lax.ppermute(shard, axis, [(i, i ^ bits) for i in range(lax.axis_size(axi...]
    psum x1 -> x0, blocking collectives: 40.5 us -> none  [per_device(): lax.psum((grad_gain_first, grad_gain_second, grad_router_part, bias_full)...]
    pallas_call x0 -> x11, Pallas kernels: none -> 31.3 us  [call(): pl.pallas_call(body, name=name, out_shape=outs, in_specs=[SMEM] * smem +...]
  transfers between devices with their start and end apart: 11 -> 52, of which waited for: 9 -> 16; matrix products, arithmetic and copies ran while one was open for 5% -> 16% of each run, Pallas kernels for 0% -> 11%
where the time goes in v1:
time: 219 us; the launch traced here: 218 us
  starting transfers between devices  83.2 us (38%)
  waiting for transfers between devices  51.4 us (23%)
  Pallas kernels  31.3 us (14%)
  local copies, waits for them, and re-layouts  30.8 us (14%)
  other arithmetic  13.1 us (6%)
  matrix products  6.8 us (3%)
    ppermute x49, starting transfers between devices, across(): lax.ppermute(shard, axis, [(i, i ^ bits) for i in range(lax.axis_size(axi...  66.9 us
    ppermute x49, waiting for transfers between devices, across(): lax.ppermute(shard, axis, [(i, i ^ bits) for i in range(lax.axis_size(axi...  51.4 us
    pallas_call x11, Pallas kernels, call(): pl.pallas_call(body, name=name, out_shape=outs, in_specs=[SMEM] * smem +...  31.3 us
    unnamed x102, local copies, waits for them, and re-layouts  24.6 us
    all_to_all x3, starting transfers between devices, trade_natural(): lax.all_to_all(stacked, 'node', split_axis=0, concat_axis=0, tiled=True)  16.3 us
  transfers between devices with their start and end apart: 52, of which 16 were waited for; matrix products, arithmetic and copies ran while one was open for 16% of the time, Pallas kernels for 11%

profile of v1, /device:TPU:0, one launch (start us, length us, event | category | flops | bytes accessed | tf_op | source)
XLA Modules:
  0.0 218.1 jit_solution(9150138372993894802)
XLA Ops:
  3.8 2.1 convolution_convert_fusion
  5.8 7.3 %all-to-all-start = ((bf16[8,40,768]{2,1,0:T(8,128)(2,1)}), bf16[8,40,768]{2,1,0:T(8,128)(2,1)}, u32[]{:S(2)}, u32[]{:S(2)}) async-start(bf16[8,40,768]{2,1,0:T(8,128)(2,1)} %bitcast.13), calls=%async_computation | async-start | bytes 983040 | tf_op jit(solution)/shard_map/all_to_all | solution.py:306
  14.4 1.6 collective-permute-start
  17.1 2.1 collective-permute-start.4
  19.2 2.4 %collective-permute-start.6 = (bf16[96,768]{1,0:T(8,128)(2,1)S(1)}, bf16[96,768]{1,0:T(8,128)(2,1)S(1)}, u32[]{:S(2)}, u32[]{:S(2)}) collective-permute-start(bf16[96,768]{1,0:T(8,128)(2,1)S(1)} %maximum_select_fusion.1.refs_0_), channel_id=1, source_target_pairs={{0,16},{4,20},{8,24},{12,28},{16,0},{20,4},{24,8},{28,12},{1,17},{... | collective-permute-start | bytes 442376 | tf_op jit(solution)/shard_map/ppermute | solution.py:26
  22.6 2.1 collective-permute-start.3
  24.7 1.9 collective-permute-done.4.refs_2_
  26.6 2.1 collective-permute-start.5
  28.7 9.1 %collective-permute-done.6.refs_4_ = bf16[96,768]{1,0:T(8,128)(2,1)S(1)} collective-permute-done((bf16[96,768]{1,0:T(8,128)(2,1)S(1)}, bf16[96,768]{1,0:T(8,128)(2,1)S(1)}, u32[]{:S(2)}, u32[]{:S(2)}) %collective-permute-start.6) | collective-permute-done | bytes 147488 | tf_op jit(solution)/shard_map/ppermute | solution.py:26
  40.2 2.7 %collective-permute-done.7.refs_5_ = bf16[96,768]{1,0:T(8,128)(2,1)S(1)} collective-permute-done((bf16[96,768]{1,0:T(8,128)(2,1)S(1)}, bf16[96,768]{1,0:T(8,128)(2,1)S(1)}, u32[]{:S(2)}, u32[]{:S(2)}) %collective-permute-start.7) | collective-permute-done | bytes 147488 | tf_op jit(solution)/shard_map/ppermute | solution.py:26
  43.0 1.6 collective-permute-done.9.refs_7_
  44.6 1.4 project.1
  47.9 5.2 %attend.1 = (f32[3,512,512]{2,1,0:T(8,128)S(1)}, bf16[512,192]{1,0:T(8,128)(2,1)S(1)}, bf16[256,192]{1,0:T(8,128)(2,1)S(1)}, bf16[256,192]{1,0:T(8,128)(2,1)S(1)}) custom-call(s32[2]{0:T(128)S(1)} %pad_add_fusion.ids, bf16[512,576]{1,0:T(8,128)(2,1)S(1)} %get-tuple-element.63.qkv_ref, f32[3,1024]{1,0:T(4,128)S(1)} %fusion.6.vec_ref, ...), custom_call_target="tpu_custom_call" | custom-call | flops 1610612736 | bytes 4145160 | tf_op jit(solution)/shard_map/attend/pallas_call | solution.py:33
  53.1 1.6 copy-done.14
  56.0 1.5 dynamic-slice_dynamic-update-slice_fusion.15
  57.5 1.5 dynamic-slice_dynamic-update-slice_fusion.14
  58.9 1.5 dynamic-slice_dynamic-update-slice_fusion.13
  60.4 1.5 dynamic-slice_dynamic-update-slice_fusion.12
  62.3 1.6 collective-permute-start.12
  63.9 1.5 dynamic-slice_dynamic-update-slice_fusion.11
  65.3 1.5 dynamic-slice_dynamic-update-slice_fusion.10
  66.8 1.5 dynamic-slice_dynamic-update-slice_fusion.9
  68.2 1.5 dynamic-slice_dynamic-update-slice_fusion.8
  69.7 3.7 %collective-permute-done.12.got_ref = bf16[256,768]{1,0:T(8,128)(2,1)S(1)} collective-permute-done((bf16[256,768]{1,0:T(8,128)(2,1)S(1)}, bf16[256,768]{1,0:T(8,128)(2,1)S(1)}, u32[]{:S(2)}, u32[]{:S(2)}) %collective-permute-start.12) | collective-permute-done | bytes 393248 | tf_op jit(solution)/shard_map/ppermute | solution.py:26
  73.9 1.3 collective-permute-start.13
  76.1 1.3 collective-permute-start.15
  78.6 2.5 %collective-permute-start.17 = (bf16[40,768]{1,0:T(8,128)(2,1)S(1)}, bf16[40,768]{1,0:T(8,128)(2,1)S(1)}, u32[]{:S(2)}, u32[]{:S(2)}) collective-permute-start(bf16[40,768]{1,0:T(8,128)(2,1)S(1)} %get-tuple-element.73), channel_id=1, source_target_pairs={{0,20},{4,16},{8,28},{12,24},{16,4},{20,0},{24,12},{28,8},{1,21},{... | collective-permute-start | bytes 184328 | tf_op jit(solution)/shard_map/ppermute | solution.py:26
  81.2 2.5 %collective-permute-start.18 = (bf16[40,768]{1,0:T(8,128)(2,1)S(1)}, bf16[40,768]{1,0:T(8,128)(2,1)S(1)}, u32[]{:S(2)}, u32[]{:S(2)}) collective-permute-start(bf16[40,768]{1,0:T(8,128)(2,1)S(1)} %get-tuple-element.74), channel_id=1, source_target_pairs={{0,24},{4,28},{8,16},{12,20},{16,8},{20,12},{24,0},{28,4},{1,25},{... | collective-permute-start | bytes 184328 | tf_op jit(solution)/shard_map/ppermute | solution.py:26
  83.6 1.7 collective-permute-start.19
  85.4 3.4 %collective-permute-done.17 = bf16[40,768]{1,0:T(8,128)(2,1)S(1)} collective-permute-done((bf16[40,768]{1,0:T(8,128)(2,1)S(1)}, bf16[40,768]{1,0:T(8,128)(2,1)S(1)}, u32[]{:S(2)}, u32[]{:S(2)}) %collective-permute-start.17) | collective-permute-done | bytes 61472 | tf_op jit(solution)/shard_map/ppermute | solution.py:26
  88.8 1.9 collective-permute-done.19
  92.2 2.2 %fusion.33.h_ref = f32[640,768]{1,0:T(8,128)S(1)} fusion(bf16[768,768]{1,0:T(8,128)(2,1)S(1)} %copy-done.3, bf16[320,768]{1,0:T(8,128)(2,1)} %collective-permute-done.21, bf16[320,768]{1,0:T(8,128)(2,1)} %bitcast.14), kind=kOutput, calls=%fused_computation.113 | convolution fusion | flops 756940800 | bytes 4128768 | tf_op jit(solution)/shard_map/dot_general | solution.py:50
  94.4 6.3 %expert.1 = (bf16[640,768]{1,0:T(8,128)(2,1)S(1)}, bf16[640,768]{1,0:T(8,128)(2,1)S(1)}, f32[640,1]{1,0:T(8,128)S(1)}, f32[320,768]{1,0:T(8,128)S(1)}, bf16[320,...) custom-call(s32[2]{0:T(128)S(1)} %pad_add_fusion.ids, bf16[320,768]{1,0:T(8,128)(2,1)S(1)} %constant_dynamic-update-slice_fusion.own_ref, ...), custom_call_target="tpu_custom_call" | custom-call | flops 1509949440 | bytes 7608840 | tf_op jit(solution)/shard_map/expert/pallas_call | solution.py:33
  101.3 6.1 %expert_rest.1 = (f32[320,768]{1,0:T(8,128)S(1)}, bf16[320,768]{1,0:T(8,128)(2,1)S(1)}, f32[768,768]{1,0:T(8,128)}, f32[768,768]{1,0:T(8,128)}) custom-call(bf16[320,768]{1,0:T(8,128)(2,1)S(1)} %constant_dynamic-update-slice_fusion.own_ref, bf16[320,768]{1,0:T(8,128)(2,1)} %collective-permute-done.20.other_ref, ...), custom_call_target="tpu_custom_call" | custom-call | flops 2264924160 | bytes 11307520 | tf_op jit(solution)/shard_map/expert_rest/pallas_call | solution.py:33
  108.0 1.5 collective-permute-start.26
  109.5 1.7 collective-permute-start.27
  111.2 1.3 collective-permute-start.28
  112.4 1.4 collective-permute-start.29
  115.2 1.9 collective-permute-start.30
  117.1 3.1 %collective-permute-start.31 = (bf16[40,768]{1,0:T(8,128)(2,1)S(1)}, bf16[40,768]{1,0:T(8,128)(2,1)S(1)}, u32[]{:S(2)}, u32[]{:S(2)}) collective-permute-start(bf16[40,768]{1,0:T(8,128)(2,1)S(1)} %get-tuple-element.90), channel_id=1, source_target_pairs={{0,28},{4,24},{8,20},{12,16},{16,12},{20,8},{24,4},{28,0},{1,29},{... | collective-permute-start | bytes 184328 | tf_op jit(solution)/shard_map/ppermute | solution.py:26
  121.7 2.5 %collective-permute-done.31.refs_7_ = bf16[40,768]{1,0:T(8,128)(2,1)S(1)} collective-permute-done((bf16[40,768]{1,0:T(8,128)(2,1)S(1)}, bf16[40,768]{1,0:T(8,128)(2,1)S(1)}, u32[]{:S(2)}, u32[]{:S(2)}) %collective-permute-start.31) | collective-permute-done | bytes 61472 | tf_op jit(solution)/shard_map/ppermute | solution.py:26
  124.5 1.6 collective-permute-start.32
  128.6 4.9 %collective-permute-done.32.got_ref = bf16[256,768]{1,0:T(8,128)(2,1)S(1)} collective-permute-done((bf16[256,768]{1,0:T(8,128)(2,1)S(1)}, bf16[256,768]{1,0:T(8,128)(2,1)S(1)}, u32[]{:S(2)}, u32[]{:S(2)}) %collective-permute-start.32) | collective-permute-done | bytes 393248 | tf_op jit(solution)/shard_map/ppermute | solution.py:26
  135.3 5.0 %all-to-all-start.1 = ((bf16[8,40,768]{2,1,0:T(8,128)(2,1)}), bf16[8,40,768]{2,1,0:T(8,128)(2,1)}, u32[]{:S(2)}, u32[]{:S(2)}) async-start(bf16[8,40,768]{2,1,0:T(8,128)(2,1)} %dynamic-slice_dynamic-update-slice_fusion), calls=%async_computation.1 | async-start | bytes 983040 | tf_op jit(solution)/shard_map/all_to_all | solution.py:306
  142.9 1.9 copy-done.15
  145.7 8.4 %attend_back.1 = (bf16[512,576]{1,0:T(8,128)(2,1)S(1)}, bf16[768,192]{1,0:T(8,128)(2,1)}, f32[3,1024]{1,0:T(4,128)S(1)}, bf16[96,576]{1,0:T(8,128)(2,1)S(1)}, bf...) custom-call(s32[2]{0:T(128)S(1)} %pad_add_fusion.ids, ...), custom_call_target="tpu_custom_call" | custom-call | flops 3221225472 | bytes 7581704 | tf_op jit(solution)/shard_map/attend_back/pallas_call | solution.py:33
  154.1 2.1 collective-permute-start.41
  156.1 1.5 collective-permute-start.42
  158.4 2.2 %collective-permute-start.44 = (bf16[96,576]{1,0:T(8,128)(2,1)}, bf16[96,576]{1,0:T(8,128)(2,1)}, u32[]{:S(2)}, u32[]{:S(2)}) collective-permute-start(bf16[96,576]{1,0:T(8,128)(2,1)} %get-tuple-element.107), channel_id=1, source_target_pairs={{0,16},{4,20},{8,24},{12,28},{16,0},{20,4},{24,8},{28,12},{1,17},{... | collective-permute-start | bytes 331784 | tf_op jit(solution)/shard_map/ppermute | solution.py:26
  160.6 1.4 normed_back.1
  163.0 4.1 %all-to-all-start.2 = ((bf16[8,96,192]{2,1,0:T(8,128)(2,1)}), bf16[8,96,192]{2,1,0:T(8,128)(2,1)}, u32[]{:S(2)}, u32[]{:S(2)}) async-start(bf16[8,96,192]{2,1,0:T(8,128)(2,1)} %bitcast.21), calls=%async_computation.2 | async-start | bytes 786432 | tf_op jit(solution)/shard_map/all_to_all | solution.py:306
  167.2 1.5 convolution_convert_fusion.1
  168.7 3.7 %collective-permute-start.45 = (bf16[96,576]{1,0:T(8,128)(2,1)}, bf16[96,576]{1,0:T(8,128)(2,1)S(1)}, u32[]{:S(2)}, u32[]{:S(2)}) collective-permute-start(bf16[96,576]{1,0:T(8,128)(2,1)} %copy-done.13), channel_id=1, source_target_pairs={{0,20},{4,16},{8,28},{12,24},{16,4},{20,0},{24,12},{28,8},{1,21},{... | collective-permute-start | bytes 331784 | tf_op jit(solution)/shard_map/ppermute | solution.py:26
  173.7 1.5 collective-permute-start.46
  175.2 2.4 %collective-permute-start.47 = (bf16[96,576]{1,0:T(8,128)(2,1)S(1)}, bf16[96,576]{1,0:T(8,128)(2,1)S(1)}, u32[]{:S(2)}, u32[]{:S(2)}) collective-permute-start(bf16[96,576]{1,0:T(8,128)(2,1)S(1)} %get-tuple-element.110), channel_id=1, source_target_pairs={{0,28},{4,24},{8,20},{12,16},{16,12},{20,8},{24,4},{28,0},{1,29},{... | collective-permute-start | bytes 331784 | tf_op jit(solution)/shard_map/ppermute | solution.py:26
  177.6 1.7 collective-permute-start.23
  179.3 12.2 %collective-permute-done.45 = bf16[96,576]{1,0:T(8,128)(2,1)S(1)} collective-permute-done((bf16[96,576]{1,0:T(8,128)(2,1)}, bf16[96,576]{1,0:T(8,128)(2,1)S(1)}, u32[]{:S(2)}, u32[]{:S(2)}) %collective-permute-start.45) | collective-permute-done | bytes 110624 | tf_op jit(solution)/shard_map/ppermute | solution.py:26
  192.7 1.7 collective-permute-start.37
  195.2 1.5 collective-permute-done.37
  197.4 1.7 collective-permute-start.35
  199.1 1.6 collective-permute-done.38
  200.7 5.5 %collective-permute-start.39 = (f32[63,128]{1,0:T(8,128)S(1)}, f32[63,128]{1,0:T(8,128)S(1)}, u32[]{:S(2)}, u32[]{:S(2)}) collective-permute-start(f32[63,128]{1,0:T(8,128)S(1)} %add.218), channel_id=1, source_target_pairs={{0,8},{4,12},{8,0},{12,4},{16,24},{20,28},{24,16},{28,20},{1,9},{5... | collective-permute-start | bytes 96776 | tf_op jit(solution)/shard_map/ppermute | solution.py:26
  208.1 2.0 collective-permute-start.40
  210.2 2.7 %collective-permute-done.40 = f32[63,128]{1,0:T(8,128)S(1)} collective-permute-done((f32[63,128]{1,0:T(8,128)S(1)}, f32[63,128]{1,0:T(8,128)S(1)}, u32[]{:S(2)}, u32[]{:S(2)}) %collective-permute-start.40) | collective-permute-done | bytes 32288 | tf_op jit(solution)/shard_map/ppermute | solution.py:26
  (224 shorter events, 41.2 us)
Async XLA Ops:
  0.6 21.5 %copy-start = (f32[32,12]{0,1:T(8,128)S(1)}, f32[32,12]{0,1:T(8,128)}, u32[]{:S(2)}) copy-start(f32[32,12]{0,1:T(8,128)} %param.21) | copy-start | bytes 4612
  0.7 15.3 %copy-start.34 = (s32[1023]{0:T(1024)S(1)}, s32[1023]{0:T(1024)}, u32[]{:S(2)}) copy-start(s32[1023]{0:T(1024)} %param.28) | copy-start | bytes 12280
  5.8 50.2 %all-to-all-start = ((bf16[8,40,768]{2,1,0:T(8,128)(2,1)}), bf16[8,40,768]{2,1,0:T(8,128)(2,1)}, u32[]{:S(2)}, u32[]{:S(2)}) async-start(bf16[8,40,768]{2,1,0:T(8,128)(2,1)} %bitcast.13), calls=%async_computation | async-start | bytes 983040 | tf_op jit(solution)/shard_map/all_to_all | solution.py:306
  13.5 26.6 %copy-start.38 = (bf16[768]{0:T(1024)(128)(2,1)S(1)}, bf16[768]{0:T(1024)(128)(2,1)}, u32[]{:S(2)}) copy-start(bf16[768]{0:T(1024)(128)(2,1)} %param.22) | copy-start | bytes 4612
  14.3 2.7 %collective-permute-start.2 = (bf16[48,768]{1,0:T(8,128)(2,1)S(1)}, bf16[48,768]{1,0:T(8,128)(2,1)S(1)}, u32[]{:S(2)}, u32[]{:S(2)}) collective-permute-start(bf16[48,768]{1,0:T(8,128)(2,1)S(1)} %get-tuple-element.155), channel_id=1, source_target_pairs={{0,2},{2,0},{1,3},{3,1},{4,6},{6,4},{5,7},{7,5},{8,10},{10,8},{9,1... | collective-permute-start | bytes 221192 | tf_op jit(solution)/shard_map/ppermute | solution.py:26
  14.4 7.3 %collective-permute-start = (bf16[128,768]{1,0:T(8,128)(2,1)S(1)}, bf16[128,768]{1,0:T(8,128)(2,1)S(1)}, u32[]{:S(2)}, u32[]{:S(2)}) collective-permute-start(bf16[128,768]{1,0:T(8,128)(2,1)S(1)} %copy-done.20), channel_id=1, source_target_pairs={{0,1},{1,0},{2,3},{3,2},{4,5},{5,4},{6,7},{7,6},{8,9},{9,8},{10,11... | collective-permute-start | bytes 589832 | tf_op jit(solution)/shard_map/ppermute | solution.py:26
  16.0 30.0 %copy-start.35 = (s32[1024]{0:T(1024)}, s32[1024]{0:T(1024)S(1)}, u32[]{:S(2)}) copy-start(s32[1024]{0:T(1024)S(1)} %pad.4) | copy-start | bytes 12292
  17.1 9.5 %collective-permute-start.4 = (bf16[96,768]{1,0:T(8,128)(2,1)S(1)}, bf16[96,768]{1,0:T(8,128)(2,1)S(1)}, u32[]{:S(2)}, u32[]{:S(2)}) collective-permute-start(bf16[96,768]{1,0:T(8,128)(2,1)S(1)} %maximum_select_fusion.1.refs_0_), channel_id=1, source_target_pairs={{0,8},{4,12},{8,0},{12,4},{16,24},{20,28},{24,16},{28,20},{1,9},{5... | collective-permute-start | bytes 442376 | tf_op jit(solution)/shard_map/ppermute | solution.py:26
  19.2 18.6 %collective-permute-start.6 = (bf16[96,768]{1,0:T(8,128)(2,1)S(1)}, bf16[96,768]{1,0:T(8,128)(2,1)S(1)}, u32[]{:S(2)}, u32[]{:S(2)}) collective-permute-start(bf16[96,768]{1,0:T(8,128)(2,1)S(1)} %maximum_select_fusion.1.refs_0_), channel_id=1, source_target_pairs={{0,16},{4,20},{8,24},{12,28},{16,0},{20,4},{24,8},{28,12},{1,17},{... | collective-permute-start | bytes 442376 | tf_op jit(solution)/shard_map/ppermute | solution.py:26
  21.6 17.3 %collective-permute-start.8 = (bf16[96,768]{1,0:T(8,128)(2,1)S(1)}, bf16[96,768]{1,0:T(8,128)(2,1)S(1)}, u32[]{:S(2)}, u32[]{:S(2)}) collective-permute-start(bf16[96,768]{1,0:T(8,128)(2,1)S(1)} %maximum_select_fusion.1.refs_0_), channel_id=1, source_target_pairs={{0,24},{4,28},{8,16},{12,20},{16,8},{20,12},{24,0},{28,4},{1,25},{... | collective-permute-start | bytes 442376 | tf_op jit(solution)/shard_map/ppermute | solution.py:26
  21.9 31.2 %copy-start.32 = (f32[256]{0:T(256)}, f32[256]{0:T(256)S(1)}, u32[]{:S(2)}) copy-start(f32[256]{0:T(256)S(1)} %add_rsqrt_fusion) | copy-start | bytes 3076
  22.1 22.5 %collective-permute-start.1 = (bf16[256,768]{1,0:T(8,128)(2,1)S(1)}, bf16[256,768]{1,0:T(8,128)(2,1)S(1)}, u32[]{:S(2)}, u32[]{:S(2)}) collective-permute-start(bf16[256,768]{1,0:T(8,128)(2,1)S(1)} %fusion.2.own_ref), channel_id=1, source_target_pairs={{0,2},{2,0},{1,3},{3,1},{4,6},{6,4},{5,7},{7,5},{8,10},{10,8},{9,1... | collective-permute-start | bytes 1179656 | tf_op jit(solution)/shard_map/ppermute | solution.py:26
  22.6 17.6 %collective-permute-start.3 = (bf16[96,768]{1,0:T(8,128)(2,1)S(1)}, bf16[96,768]{1,0:T(8,128)(2,1)S(1)}, u32[]{:S(2)}, u32[]{:S(2)}) collective-permute-start(bf16[96,768]{1,0:T(8,128)(2,1)S(1)} %maximum_select_fusion.1.refs_0_), channel_id=1, source_target_pairs={{0,4},{4,0},{8,12},{12,8},{16,20},{20,16},{24,28},{28,24},{1,5},{5... | collective-permute-start | bytes 442376 | tf_op jit(solution)/shard_map/ppermute | solution.py:26
  26.6 13.6 %collective-permute-start.5 = (bf16[96,768]{1,0:T(8,128)(2,1)S(1)}, bf16[96,768]{1,0:T(8,128)(2,1)S(1)}, u32[]{:S(2)}, u32[]{:S(2)}) collective-permute-start(bf16[96,768]{1,0:T(8,128)(2,1)S(1)} %collective-permute-done.4.refs_2_), channel_id=1, source_target_pairs={{0,4},{4,0},{8,12},{12,8},{16,20},{20,16},{24,28},{28,24},{1,5},{5... | collective-permute-start | bytes 442376 | tf_op jit(solution)/shard_map/ppermute | solution.py:26
  37.8 5.1 %collective-permute-start.7 = (bf16[96,768]{1,0:T(8,128)(2,1)S(1)}, bf16[96,768]{1,0:T(8,128)(2,1)S(1)}, u32[]{:S(2)}, u32[]{:S(2)}) collective-permute-start(bf16[96,768]{1,0:T(8,128)(2,1)S(1)} %collective-permute-done.6.refs_4_), channel_id=1, source_target_pairs={{0,4},{4,0},{8,12},{12,8},{16,20},{20,16},{24,28},{28,24},{1,5},{5... | collective-permute-start | bytes 442376 | tf_op jit(solution)/shard_map/ppermute | solution.py:26
  38.9 5.7 %collective-permute-start.9 = (bf16[96,768]{1,0:T(8,128)(2,1)S(1)}, bf16[96,768]{1,0:T(8,128)(2,1)S(1)}, u32[]{:S(2)}, u32[]{:S(2)}) collective-permute-start(bf16[96,768]{1,0:T(8,128)(2,1)S(1)} %collective-permute-done.8.refs_6_), channel_id=1, source_target_pairs={{0,4},{4,0},{8,12},{12,8},{16,20},{20,16},{24,28},{28,24},{1,5},{5... | collective-permute-start | bytes 442376 | tf_op jit(solution)/shard_map/ppermute | solution.py:26
  55.5 6.3 %collective-permute-start.10 = (bf16[256,192]{1,0:T(8,128)(2,1)S(1)}, bf16[256,192]{1,0:T(8,128)(2,1)S(1)}, u32[]{:S(2)}, u32[]{:S(2)}) collective-permute-start(bf16[256,192]{1,0:T(8,128)(2,1)S(1)} %get-tuple-element.65), channel_id=1, source_target_pairs={{0,2},{2,0},{1,3},{3,1},{4,6},{6,4},{5,7},{7,5},{8,10},{10,8},{9,1... | collective-permute-start | bytes 294920 | tf_op jit(solution)/shard_map/ppermute | solution.py:26
  55.5 6.3 %collective-permute-start.11 = (bf16[768,192]{1,0:T(8,128)(2,1)S(1)}, bf16[768,192]{1,0:T(8,128)(2,1)S(1)}, u32[]{:S(2)}, u32[]{:S(2)}) collective-permute-start(bf16[768,192]{1,0:T(8,128)(2,1)S(1)} %get-tuple-element.66.wo_ref), channel_id=1, source_target_pairs={{0,2},{2,0},{1,3},{3,1},{4,6},{6,4},{5,7},{7,5},{8,10},{10,8},{9,1... | collective-permute-start | bytes 884744 | tf_op jit(solution)/shard_map/ppermute | solution.py:26
  61.9 28.9 %copy-start.31 = (bf16[768,8]{0,1:T(8,128)(2,1)S(1)}, bf16[768,8]{0,1:T(8,128)(2,1)}, u32[]{:S(2)}) copy-start(bf16[768,8]{0,1:T(8,128)(2,1)} %param.23) | copy-start | bytes 36868
  62.3 11.1 %collective-permute-start.12 = (bf16[256,768]{1,0:T(8,128)(2,1)S(1)}, bf16[256,768]{1,0:T(8,128)(2,1)S(1)}, u32[]{:S(2)}, u32[]{:S(2)}) collective-permute-start(bf16[256,768]{1,0:T(8,128)(2,1)S(1)} %attended.1.own_ref), channel_id=1, source_target_pairs={{0,1},{1,0},{2,3},{3,2},{4,5},{5,4},{6,7},{7,6},{8,9},{9,8},{10,11... | collective-permute-start | bytes 1179656 | tf_op jit(solution)/shard_map/ppermute | solution.py:26
  69.7 22.5 %copy-start.3 = (bf16[768,768]{1,0:T(8,128)(2,1)S(1)}, bf16[768,768]{1,0:T(8,128)(2,1)}, u32[]{:S(2)}) copy-start(bf16[768,768]{1,0:T(8,128)(2,1)} %wdown_ref.1) | copy-start | bytes 3538948
  69.7 21.2 %collective-permute-start.21 = (bf16[320,768]{1,0:T(8,128)(2,1)}, bf16[320,768]{1,0:T(8,128)(2,1)}, u32[]{:S(2)}, u32[]{:S(2)}) collective-permute-start(bf16[320,768]{1,0:T(8,128)(2,1)} %bitcast.14), channel_id=1, source_target_pairs={{0,2},{2,0},{1,3},{3,1},{4,6},{6,4},{5,7},{7,5},{8,10},{10,8},{9,1... | collective-permute-start | bytes 1474568 | tf_op jit(solution)/shard_map/ppermute | solution.py:26
  73.9 4.7 %collective-permute-start.13 = (bf16[40,768]{1,0:T(8,128)(2,1)S(1)}, bf16[40,768]{1,0:T(8,128)(2,1)S(1)}, u32[]{:S(2)}, u32[]{:S(2)}) collective-permute-start(bf16[40,768]{1,0:T(8,128)(2,1)S(1)} %get-tuple-element.69), channel_id=1, source_target_pairs={{0,4},{4,0},{8,12},{12,8},{16,20},{20,16},{24,28},{28,24},{1,5},{5... | collective-permute-start | bytes 184328 | tf_op jit(solution)/shard_map/ppermute | solution.py:26
  75.2 5.9 %collective-permute-start.14 = (bf16[40,768]{1,0:T(8,128)(2,1)S(1)}, bf16[40,768]{1,0:T(8,128)(2,1)S(1)}, u32[]{:S(2)}, u32[]{:S(2)}) collective-permute-start(bf16[40,768]{1,0:T(8,128)(2,1)S(1)} %get-tuple-element.70), channel_id=1, source_target_pairs={{0,8},{4,12},{8,0},{12,4},{16,24},{20,28},{24,16},{28,20},{1,9},{5... | collective-permute-start | bytes 184328 | tf_op jit(solution)/shard_map/ppermute | solution.py:26
  76.1 7.5 %collective-permute-start.15 = (bf16[40,768]{1,0:T(8,128)(2,1)S(1)}, bf16[40,768]{1,0:T(8,128)(2,1)S(1)}, u32[]{:S(2)}, u32[]{:S(2)}) collective-permute-start(bf16[40,768]{1,0:T(8,128)(2,1)S(1)} %get-tuple-element.71), channel_id=1, source_target_pairs={{0,12},{4,8},{8,4},{12,0},{16,28},{20,24},{24,20},{28,16},{1,13},{... | collective-permute-start | bytes 184328 | tf_op jit(solution)/shard_map/ppermute | solution.py:26
  77.5 7.9 %collective-permute-start.16 = (bf16[40,768]{1,0:T(8,128)(2,1)S(1)}, bf16[40,768]{1,0:T(8,128)(2,1)S(1)}, u32[]{:S(2)}, u32[]{:S(2)}) collective-permute-start(bf16[40,768]{1,0:T(8,128)(2,1)S(1)} %get-tuple-element.72), channel_id=1, source_target_pairs={{0,16},{4,20},{8,24},{12,28},{16,0},{20,4},{24,8},{28,12},{1,17},{... | collective-permute-start | bytes 184328 | tf_op jit(solution)/shard_map/ppermute | solution.py:26
  78.6 10.2 %collective-permute-start.17 = (bf16[40,768]{1,0:T(8,128)(2,1)S(1)}, bf16[40,768]{1,0:T(8,128)(2,1)S(1)}, u32[]{:S(2)}, u32[]{:S(2)}) collective-permute-start(bf16[40,768]{1,0:T(8,128)(2,1)S(1)} %get-tuple-element.73), channel_id=1, source_target_pairs={{0,20},{4,16},{8,28},{12,24},{16,4},{20,0},{24,12},{28,8},{1,21},{... | collective-permute-start | bytes 184328 | tf_op jit(solution)/shard_map/ppermute | solution.py:26
  81.2 7.6 %collective-permute-start.18 = (bf16[40,768]{1,0:T(8,128)(2,1)S(1)}, bf16[40,768]{1,0:T(8,128)(2,1)S(1)}, u32[]{:S(2)}, u32[]{:S(2)}) collective-permute-start(bf16[40,768]{1,0:T(8,128)(2,1)S(1)} %get-tuple-element.74), channel_id=1, source_target_pairs={{0,24},{4,28},{8,16},{12,20},{16,8},{20,12},{24,0},{28,4},{1,25},{... | collective-permute-start | bytes 184328 | tf_op jit(solution)/shard_map/ppermute | solution.py:26
  83.6 7.1 %collective-permute-start.19 = (bf16[40,768]{1,0:T(8,128)(2,1)S(1)}, bf16[40,768]{1,0:T(8,128)(2,1)S(1)}, u32[]{:S(2)}, u32[]{:S(2)}) collective-permute-start(bf16[40,768]{1,0:T(8,128)(2,1)S(1)} %get-tuple-element.75), channel_id=1, source_target_pairs={{0,28},{4,24},{8,20},{12,16},{16,12},{20,8},{24,4},{28,0},{1,29},{... | collective-permute-start | bytes 184328 | tf_op jit(solution)/shard_map/ppermute | solution.py:26
  90.7 3.7 %collective-permute-start.20 = (bf16[320,768]{1,0:T(8,128)(2,1)S(1)}, bf16[320,768]{1,0:T(8,128)(2,1)}, u32[]{:S(2)}, u32[]{:S(2)}) collective-permute-start(bf16[320,768]{1,0:T(8,128)(2,1)S(1)} %constant_dynamic-update-slice_fusion.own_ref), channel_id=1, source_target_pairs={{0,2},{2,0},{1,3},{3,1},{4,6},{6,4},{5,7},{7,5},{8,10},{10,8},{9,1... | collective-permute-start | bytes 1474568 | tf_op jit(solution)/shard_map/ppermute | solution.py:26
  100.7 6.8 %collective-permute-start.24 = (bf16[320,768]{1,0:T(8,128)(2,1)S(1)}, bf16[320,768]{1,0:T(8,128)(2,1)S(1)}, u32[]{:S(2)}, u32[]{:S(2)}) collective-permute-start(bf16[320,768]{1,0:T(8,128)(2,1)S(1)} %get-tuple-element.82), channel_id=1, source_target_pairs={{0,2},{2,0},{1,3},{3,1},{4,6},{6,4},{5,7},{7,5},{8,10},{10,8},{9,1... | collective-permute-start | bytes 1474568 | tf_op jit(solution)/shard_map/ppermute | solution.py:26
  107.4 5.1 %collective-permute-start.22 = (bf16[320,768]{1,0:T(8,128)(2,1)S(1)}, bf16[320,768]{1,0:T(8,128)(2,1)S(1)}, u32[]{:S(2)}, u32[]{:S(2)}) collective-permute-start(bf16[320,768]{1,0:T(8,128)(2,1)S(1)} %get-tuple-element.80), channel_id=1, source_target_pairs={{0,2},{2,0},{1,3},{3,1},{4,6},{6,4},{5,7},{7,5},{8,10},{10,8},{9,1... | collective-permute-start | bytes 1474568 | tf_op jit(solution)/shard_map/ppermute | solution.py:26
  107.6 25.9 %copy-start.1 = (bf16[256,768]{1,0:T(8,128)(2,1)S(1)}, bf16[256,768]{1,0:T(8,128)(2,1)}, u32[]{:S(2)}) copy-start(bf16[256,768]{1,0:T(8,128)(2,1)} %cot_ref.1) | copy-start | bytes 1179652
  107.6 7.6 %collective-permute-start.25 = (bf16[40,768]{1,0:T(8,128)(2,1)S(1)}, bf16[40,768]{1,0:T(8,128)(2,1)S(1)}, u32[]{:S(2)}, u32[]{:S(2)}) collective-permute-start(bf16[40,768]{1,0:T(8,128)(2,1)S(1)} %get-tuple-element.84), channel_id=1, source_target_pairs={{0,4},{4,0},{8,12},{12,8},{16,20},{20,16},{24,28},{28,24},{1,5},{5... | collective-permute-start | bytes 184328 | tf_op jit(solution)/shard_map/ppermute | solution.py:26
  108.0 9.2 %collective-permute-start.26 = (bf16[40,768]{1,0:T(8,128)(2,1)S(1)}, bf16[40,768]{1,0:T(8,128)(2,1)S(1)}, u32[]{:S(2)}, u32[]{:S(2)}) collective-permute-start(bf16[40,768]{1,0:T(8,128)(2,1)S(1)} %get-tuple-element.85), channel_id=1, source_target_pairs={{0,8},{4,12},{8,0},{12,4},{16,24},{20,28},{24,16},{28,20},{1,9},{5... | collective-permute-start | bytes 184328 | tf_op jit(solution)/shard_map/ppermute | solution.py:26
  109.5 11.4 %collective-permute-start.27 = (bf16[40,768]{1,0:T(8,128)(2,1)S(1)}, bf16[40,768]{1,0:T(8,128)(2,1)S(1)}, u32[]{:S(2)}, u32[]{:S(2)}) collective-permute-start(bf16[40,768]{1,0:T(8,128)(2,1)S(1)} %get-tuple-element.86), channel_id=1, source_target_pairs={{0,12},{4,8},{8,4},{12,0},{16,28},{20,24},{24,20},{28,16},{1,13},{... | collective-permute-start | bytes 184328 | tf_op jit(solution)/shard_map/ppermute | solution.py:26
  111.2 9.7 %collective-permute-start.28 = (bf16[40,768]{1,0:T(8,128)(2,1)S(1)}, bf16[40,768]{1,0:T(8,128)(2,1)S(1)}, u32[]{:S(2)}, u32[]{:S(2)}) collective-permute-start(bf16[40,768]{1,0:T(8,128)(2,1)S(1)} %get-tuple-element.87), channel_id=1, source_target_pairs={{0,16},{4,20},{8,24},{12,28},{16,0},{20,4},{24,8},{28,12},{1,17},{... | collective-permute-start | bytes 184328 | tf_op jit(solution)/shard_map/ppermute | solution.py:26
  112.4 8.4 %collective-permute-start.29 = (bf16[40,768]{1,0:T(8,128)(2,1)S(1)}, bf16[40,768]{1,0:T(8,128)(2,1)S(1)}, u32[]{:S(2)}, u32[]{:S(2)}) collective-permute-start(bf16[40,768]{1,0:T(8,128)(2,1)S(1)} %get-tuple-element.88), channel_id=1, source_target_pairs={{0,20},{4,16},{8,28},{12,24},{16,4},{20,0},{24,12},{28,8},{1,21},{... | collective-permute-start | bytes 184328 | tf_op jit(solution)/shard_map/ppermute | solution.py:26
  115.2 6.4 %collective-permute-start.30 = (bf16[40,768]{1,0:T(8,128)(2,1)S(1)}, bf16[40,768]{1,0:T(8,128)(2,1)S(1)}, u32[]{:S(2)}, u32[]{:S(2)}) collective-permute-start(bf16[40,768]{1,0:T(8,128)(2,1)S(1)} %get-tuple-element.89), channel_id=1, source_target_pairs={{0,24},{4,28},{8,16},{12,20},{16,8},{20,12},{24,0},{28,4},{1,25},{... | collective-permute-start | bytes 184328 | tf_op jit(solution)/shard_map/ppermute | solution.py:26
  117.1 7.0 %collective-permute-start.31 = (bf16[40,768]{1,0:T(8,128)(2,1)S(1)}, bf16[40,768]{1,0:T(8,128)(2,1)S(1)}, u32[]{:S(2)}, u32[]{:S(2)}) collective-permute-start(bf16[40,768]{1,0:T(8,128)(2,1)S(1)} %get-tuple-element.90), channel_id=1, source_target_pairs={{0,28},{4,24},{8,20},{12,16},{16,12},{20,8},{24,4},{28,0},{1,29},{... | collective-permute-start | bytes 184328 | tf_op jit(solution)/shard_map/ppermute | solution.py:26
  124.5 8.9 %collective-permute-start.32 = (bf16[256,768]{1,0:T(8,128)(2,1)S(1)}, bf16[256,768]{1,0:T(8,128)(2,1)S(1)}, u32[]{:S(2)}, u32[]{:S(2)}) collective-permute-start(bf16[256,768]{1,0:T(8,128)(2,1)S(1)} %gather_grad.1.own_ref), channel_id=1, source_target_pairs={{0,1},{1,0},{2,3},{3,2},{4,5},{5,4},{6,7},{7,6},{8,9},{9,8},{10,11... | collective-permute-start | bytes 1179656 | tf_op jit(solution)/shard_map/ppermute | solution.py:26
  134.7 7.0 %collective-permute-start.33 = (bf16[256,768]{1,0:T(8,128)(2,1)}, bf16[256,768]{1,0:T(8,128)(2,1)}, u32[]{:S(2)}, u32[]{:S(2)}) collective-permute-start(bf16[256,768]{1,0:T(8,128)(2,1)} %get-tuple-element.92.own_ref), channel_id=1, source_target_pairs={{0,2},{2,0},{1,3},{3,1},{4,6},{6,4},{5,7},{7,5},{8,10},{10,8},{9,1... | collective-permute-start | bytes 1179656 | tf_op jit(solution)/shard_map/ppermute | solution.py:26
  135.3 27.7 %all-to-all-start.1 = ((bf16[8,40,768]{2,1,0:T(8,128)(2,1)}), bf16[8,40,768]{2,1,0:T(8,128)(2,1)}, u32[]{:S(2)}, u32[]{:S(2)}) async-start(bf16[8,40,768]{2,1,0:T(8,128)(2,1)} %dynamic-slice_dynamic-update-slice_fusion), calls=%async_computation.1 | async-start | bytes 983040 | tf_op jit(solution)/shard_map/all_to_all | solution.py:306
  145.7 16.4 %copy-start.36 = (s32[1024]{0:T(1024)S(1)}, s32[1024]{0:T(1024)}, u32[]{:S(2)}) copy-start(s32[1024]{0:T(1024)} %copy-done.35) | copy-start | bytes 12292
  154.1 19.6 %collective-permute-start.41 = (bf16[96,576]{1,0:T(8,128)(2,1)}, bf16[96,576]{1,0:T(8,128)(2,1)}, u32[]{:S(2)}, u32[]{:S(2)}) collective-permute-start(bf16[96,576]{1,0:T(8,128)(2,1)} %get-tuple-element.104), channel_id=1, source_target_pairs={{0,4},{4,0},{8,12},{12,8},{16,20},{20,16},{24,28},{28,24},{1,5},{5... | collective-permute-start | bytes 331784 | tf_op jit(solution)/shard_map/ppermute | solution.py:26
  156.1 19.1 %collective-permute-start.42 = (bf16[96,576]{1,0:T(8,128)(2,1)}, bf16[96,576]{1,0:T(8,128)(2,1)}, u32[]{:S(2)}, u32[]{:S(2)}) collective-permute-start(bf16[96,576]{1,0:T(8,128)(2,1)} %get-tuple-element.105), channel_id=1, source_target_pairs={{0,8},{4,12},{8,0},{12,4},{16,24},{20,28},{24,16},{28,20},{1,9},{5... | collective-permute-start | bytes 331784 | tf_op jit(solution)/shard_map/ppermute | solution.py:26
  157.6 20.0 %collective-permute-start.43 = (bf16[96,576]{1,0:T(8,128)(2,1)}, bf16[96,576]{1,0:T(8,128)(2,1)}, u32[]{:S(2)}, u32[]{:S(2)}) collective-permute-start(bf16[96,576]{1,0:T(8,128)(2,1)} %get-tuple-element.106), channel_id=1, source_target_pairs={{0,12},{4,8},{8,4},{12,0},{16,28},{20,24},{24,20},{28,16},{1,13},{... | collective-permute-start | bytes 331784 | tf_op jit(solution)/shard_map/ppermute | solution.py:26
  158.4 21.0 %collective-permute-start.44 = (bf16[96,576]{1,0:T(8,128)(2,1)}, bf16[96,576]{1,0:T(8,128)(2,1)}, u32[]{:S(2)}, u32[]{:S(2)}) collective-permute-start(bf16[96,576]{1,0:T(8,128)(2,1)} %get-tuple-element.107), channel_id=1, source_target_pairs={{0,16},{4,20},{8,24},{12,28},{16,0},{20,4},{24,8},{28,12},{1,17},{... | collective-permute-start | bytes 331784 | tf_op jit(solution)/shard_map/ppermute | solution.py:26
  162.0 6.8 %collective-permute-start.34 = (bf16[256,768]{1,0:T(8,128)(2,1)S(1)}, bf16[256,768]{1,0:T(8,128)(2,1)}, u32[]{:S(2)}, u32[]{:S(2)}) collective-permute-start(bf16[256,768]{1,0:T(8,128)(2,1)S(1)} %get-tuple-element.99), channel_id=1, source_target_pairs={{0,2},{2,0},{1,3},{3,1},{4,6},{6,4},{5,7},{7,5},{8,10},{10,8},{9,1... | collective-permute-start | bytes 1179656 | tf_op jit(solution)/shard_map/ppermute | solution.py:26
  163.0 43.2 %all-to-all-start.2 = ((bf16[8,96,192]{2,1,0:T(8,128)(2,1)}), bf16[8,96,192]{2,1,0:T(8,128)(2,1)}, u32[]{:S(2)}, u32[]{:S(2)}) async-start(bf16[8,96,192]{2,1,0:T(8,128)(2,1)} %bitcast.21), calls=%async_computation.2 | async-start | bytes 786432 | tf_op jit(solution)/shard_map/all_to_all | solution.py:306
  168.7 22.7 %collective-permute-start.45 = (bf16[96,576]{1,0:T(8,128)(2,1)}, bf16[96,576]{1,0:T(8,128)(2,1)S(1)}, u32[]{:S(2)}, u32[]{:S(2)}) collective-permute-start(bf16[96,576]{1,0:T(8,128)(2,1)} %copy-done.13), channel_id=1, source_target_pairs={{0,20},{4,16},{8,28},{12,24},{16,4},{20,0},{24,12},{28,8},{1,21},{... | collective-permute-start | bytes 331784 | tf_op jit(solution)/shard_map/ppermute | solution.py:26
  173.7 23.7 %copy-start.18 = (f32[256,768]{1,0:T(8,128)}, f32[256,768]{1,0:T(8,128)S(1)}, u32[]{:S(2)}) copy-start(f32[256,768]{1,0:T(8,128)S(1)} %get-tuple-element.141) | copy-start | bytes 2359300
  173.7 17.8 %collective-permute-start.46 = (bf16[96,576]{1,0:T(8,128)(2,1)S(1)}, bf16[96,576]{1,0:T(8,128)(2,1)S(1)}, u32[]{:S(2)}, u32[]{:S(2)}) collective-permute-start(bf16[96,576]{1,0:T(8,128)(2,1)S(1)} %copy-done.12), channel_id=1, source_target_pairs={{0,24},{4,28},{8,16},{12,20},{16,8},{20,12},{24,0},{28,4},{1,25},{... | collective-permute-start | bytes 331784 | tf_op jit(solution)/shard_map/ppermute | solution.py:26
  175.2 16.3 %collective-permute-start.47 = (bf16[96,576]{1,0:T(8,128)(2,1)S(1)}, bf16[96,576]{1,0:T(8,128)(2,1)S(1)}, u32[]{:S(2)}, u32[]{:S(2)}) collective-permute-start(bf16[96,576]{1,0:T(8,128)(2,1)S(1)} %get-tuple-element.110), channel_id=1, source_target_pairs={{0,28},{4,24},{8,20},{12,16},{16,12},{20,8},{24,4},{28,0},{1,29},{... | collective-permute-start | bytes 331784 | tf_op jit(solution)/shard_map/ppermute | solution.py:26
  177.6 16.8 %collective-permute-start.23 = (bf16[128,768]{1,0:T(8,128)(2,1)S(1)}, bf16[128,768]{1,0:T(8,128)(2,1)S(1)}, u32[]{:S(2)}, u32[]{:S(2)}) collective-permute-start(bf16[128,768]{1,0:T(8,128)(2,1)S(1)} %constant_dynamic-slice_fusion), channel_id=1, source_target_pairs={{0,1},{1,0},{2,3},{3,2},{4,5},{5,4},{6,7},{7,6},{8,9},{9,8},{10,11... | collective-permute-start | bytes 589832 | tf_op jit(solution)/shard_map/ppermute | solution.py:26
  179.3 13.4 %collective-permute-start.36 = (f32[63,128]{1,0:T(8,128)S(1)}, f32[63,128]{1,0:T(8,128)S(1)}, u32[]{:S(2)}, u32[]{:S(2)}) collective-permute-start(f32[63,128]{1,0:T(8,128)S(1)} %maximum_bitcast_fusion.1), channel_id=1, source_target_pairs={{0,2},{2,0},{1,3},{3,1},{4,6},{6,4},{5,7},{7,5},{8,10},{10,8},{9,1... | collective-permute-start | bytes 96776 | tf_op jit(solution)/shard_map/ppermute | solution.py:26
  192.7 22.6 %copy-start.21 = (bf16[128,768]{1,0:T(8,128)(2,1)S(1)}, bf16[128,768]{1,0:T(8,128)(2,1)}, u32[]{:S(2)}) copy-start(bf16[128,768]{1,0:T(8,128)(2,1)} %param.15) | copy-start | bytes 589828
  192.7 4.0 %collective-permute-start.37 = (f32[63,128]{1,0:T(8,128)S(1)}, f32[63,128]{1,0:T(8,128)S(1)}, u32[]{:S(2)}, u32[]{:S(2)}) collective-permute-start(f32[63,128]{1,0:T(8,128)S(1)} %fusion.40), channel_id=1, source_target_pairs={{0,1},{1,0},{2,3},{3,2},{4,5},{5,4},{6,7},{7,6},{8,9},{9,8},{10,11... | collective-permute-start | bytes 96776 | tf_op jit(solution)/shard_map/ppermute | solution.py:26
  196.7 4.0 %collective-permute-start.38 = (f32[63,128]{1,0:T(8,128)S(1)}, f32[63,128]{1,0:T(8,128)S(1)}, u32[]{:S(2)}, u32[]{:S(2)}) collective-permute-start(f32[63,128]{1,0:T(8,128)S(1)} %fusion.41), channel_id=1, source_target_pairs={{0,4},{4,0},{8,12},{12,8},{16,20},{20,16},{24,28},{28,24},{1,5},{5... | collective-permute-start | bytes 96776 | tf_op jit(solution)/shard_map/ppermute | solution.py:26
  197.4 18.0 %copy-start.19 = (f32[256,768]{1,0:T(8,128)S(1)}, f32[256,768]{1,0:T(8,128)}, u32[]{:S(2)}) copy-start(f32[256,768]{1,0:T(8,128)} %copy-done.18) | copy-start | bytes 2359300
  197.4 17.9 %collective-permute-start.35 = (bf16[128,768]{1,0:T(8,128)(2,1)S(1)}, bf16[128,768]{1,0:T(8,128)(2,1)S(1)}, u32[]{:S(2)}, u32[]{:S(2)}) collective-permute-start(bf16[128,768]{1,0:T(8,128)(2,1)S(1)} %dynamic-slice_convert_fusion), channel_id=1, source_target_pairs={{0,1},{1,0},{2,3},{3,2},{4,5},{5,4},{6,7},{7,6},{8,9},{9,8},{10,11... | collective-permute-start | bytes 589832 | tf_op jit(solution)/shard_map/ppermute | solution.py:26
  200.7 7.4 %collective-permute-start.39 = (f32[63,128]{1,0:T(8,128)S(1)}, f32[63,128]{1,0:T(8,128)S(1)}, u32[]{:S(2)}, u32[]{:S(2)}) collective-permute-start(f32[63,128]{1,0:T(8,128)S(1)} %add.218), channel_id=1, source_target_pairs={{0,8},{4,12},{8,0},{12,4},{16,24},{20,28},{24,16},{28,20},{1,9},{5... | collective-permute-start | bytes 96776 | tf_op jit(solution)/shard_map/ppermute | solution.py:26
  207.4 9.0 %collective-permute-start.48 = (f32[48,768]{1,0:T(8,128)S(1)}, f32[48,768]{1,0:T(8,128)S(1)}, u32[]{:S(2)}, u32[]{:S(2)}) collective-permute-start(f32[48,768]{1,0:T(8,128)S(1)} %get-tuple-element.145), channel_id=1, source_target_pairs={{0,2},{2,0},{1,3},{3,1},{4,6},{6,4},{5,7},{7,5},{8,10},{10,8},{9,1... | collective-permute-start | bytes 442376 | tf_op jit(solution)/shard_map/ppermute | solution.py:26
  208.1 4.8 %collective-permute-start.40 = (f32[63,128]{1,0:T(8,128)S(1)}, f32[63,128]{1,0:T(8,128)S(1)}, u32[]{:S(2)}, u32[]{:S(2)}) collective-permute-start(f32[63,128]{1,0:T(8,128)S(1)} %add.219), channel_id=1, source_target_pairs={{0,16},{4,20},{8,24},{12,28},{16,0},{20,4},{24,8},{28,12},{1,17},{... | collective-permute-start | bytes 96776 | tf_op jit(solution)/shard_map/ppermute | solution.py:26
  (27 other events, 219.7 us)

commit v2 on v1

--- a/solution.py
+++ b/solution.py
@@ -20,26 +20,40 @@
 
 VMEM = pl.BlockSpec(memory_space=pltpu.VMEM)
 SMEM = pl.BlockSpec(memory_space=pltpu.SMEM)
+ANY = pl.BlockSpec(memory_space=pl.ANY)
 
 
 def across(shard, axis, bits):
     return lax.ppermute(shard, axis, [(i, i ^ bits) for i in range(lax.axis_size(axis))])
 
 
-def call(body, name, outs, args, smem=0, scratch=(), flops=0, limit=40):
-    moved = sum(a.size * a.dtype.itemsize for a in args) + sum(
-        o.size * jnp.dtype(o.dtype).itemsize for o in outs
-    )
+def call(body, name, outs, args, smem=0, scratch=(), flops=0, after=()):
+    held = [a for a in args] + list(outs)
+    moved = sum(a.size * jnp.dtype(a.dtype).itemsize for a in held)
+    kept = sum(padded_bytes(a) for a in held) + sum(padded_bytes(a) for a in scratch)
+    count = len(args)
+
+    def kernel(*refs):
+        body(*refs[:count], *refs[count + len(after) :])
+
     return pl.pallas_call(
-        body,
+        kernel,
         name=name,
         out_shape=outs,
-        in_specs=[SMEM] * smem + [VMEM] * (len(args) - smem),
+        in_specs=[SMEM] * smem + [VMEM] * (count - smem) + [ANY] * len(after),
         out_specs=[VMEM] * len(outs),
         scratch_shapes=scratch,
-        compiler_params=pltpu.CompilerParams(vmem_limit_bytes=limit * 1024 * 1024),
+        compiler_params=pltpu.CompilerParams(vmem_limit_bytes=kept + 12 * 1024 * 1024),
         cost_estimate=pl.CostEstimate(flops=flops, bytes_accessed=moved, transcendentals=0),
-    )(*args)
+    )(*args, *after)
+
+
+def padded_bytes(array):
+    *lead, rows, cols = (1, 1, *array.shape)
+    size = jnp.dtype(array.dtype).itemsize
+    for extent in lead:
+        size *= extent
+    return size * (-(-rows // 16) * 16) * (-(-cols // 128) * 128)
 
 
 def out(shape, dtype):
@@ -58,16 +72,21 @@
     return lax.dot_general(a, b, (((0,), (0,)), ((), ())), preferred_element_type=f32)
 
 
-def project_kernel(parts, ids, own_ref, other_ref, *refs):
+def project_kernel(parts, ids, own_ref, other_ref, gain_ref, *refs):
     pieces = refs[:parts]
-    wqkv_ref, wo_ref, seq_ref, qkv_ref = refs[parts:]
+    wqkv_ref, wo_ref, x_ref, seq_ref, qkv_ref = refs[parts:]
     core = ids[0]
     me = ids[1]
     rows = pieces[0].shape[0]
     cols = wqkv_ref.shape[1]
     half = own_ref.shape[0]
-    seq_ref[pl.ds(pl.multiple_of(core * half, half), half), :] = own_ref[...]
-    seq_ref[pl.ds(pl.multiple_of((1 - core) * half, half), half), :] = other_ref[...]
+    for place, source in ((core, own_ref), (1 - core, other_ref)):
+        at = pl.ds(pl.multiple_of(place * half, half), half)
+        x = source[...]
+        x_ref[at, :] = x
+        wide = x.astype(f32)
+        scale = lax.rsqrt(jnp.mean(wide * wide, axis=1, keepdims=True) + norm_eps)
+        seq_ref[at, :] = (wide * scale * gain_ref[...]).astype(bf16)
     for i, piece in enumerate(pieces):
         start = 0 if parts == 1 else pl.multiple_of((me ^ i) * rows, rows)
         wqkv_ref[pl.ds(start, rows), :] = piece[:, :cols]
@@ -76,8 +95,26 @@
         qkv_ref[i : i + 256, :] = mm(seq_ref[i : i + 256, :], wqkv_ref[...]).astype(bf16)
 
 
+def slots_kernel(table_ref, rows_ref, out_ref):
+    out_ref[...] = mm(table_ref[...], rows_ref[...]).astype(bf16)
+
+
+def cots_kernel(parts, ids, own_ref, other_ref, wdown_ref, cots_ref, back_ref, *scratch):
+    slots = cots_ref.shape[0] // 2
+    me = ids[1]
+    for at, source in ((0, own_ref), (slots, other_ref)):
+        if parts == 1:
+            cots_ref[at : at + slots, :] = source[...]
+        else:
+            rows = slots // parts
+            for i in range(parts):
+                scratch[0][i * rows : (i + 1) * rows, :] = source[me ^ i].astype(f32)
+            cots_ref[at : at + slots, :] = scratch[0][...].astype(bf16)
+        back_ref[at : at + slots, :] = mm(cots_ref[at : at + slots, :], wdown_ref[...])
+
+
 def attend_kernel(heads, ids, qkv_ref, vec_ref, row_docs, col_docs, *refs):
-    probs_ref, mixed_ref, keep_ref, send_ref = refs
+    mixed_ref, keep_ref, send_ref, *probs_refs = refs
     core = ids[0]
     seq = qkv_ref.shape[0]
     width = heads * HD
@@ -96,7 +133,7 @@
             peak = jnp.max(scores, axis=1, keepdims=True)
             exp_scores = jnp.exp(scores - peak)
             probs = exp_scores / jnp.sum(exp_scores, axis=1, keepdims=True)
-            probs_ref[h, i : i + TILE, :] = probs
+            probs_refs[h][i : i + TILE, :] = probs
             mixed_ref[i : i + TILE, at : at + HD] = mm(probs.astype(bf16), value).astype(bf16)
     keep_ref[...] = mixed_ref[pl.ds(pl.multiple_of(core * half, half), half), :]
     send_ref[...] = mixed_ref[pl.ds(pl.multiple_of((1 - core) * half, half), half), :]
@@ -149,7 +186,7 @@
         grad_chosen = jnp.sum(low.astype(f32) * back, axis=1, keepdims=True)
         grad_logits = gates * (jnp.where(mine, 1.0, 0.0) - chosen) * grad_chosen
         grad_logits = grad_logits.astype(bf16)
-        router = router + mm_at(slots, grad_logits)
+        router = router + mm_at(grad_logits, slots)
         grad = mm_bt(gup, wup_ref[...]) + mm_bt(grad_logits, wr_ref[...])
         if i < rows:
             keep_ref[at : at + step, :] = grad
@@ -174,6 +211,16 @@
     rows = blocks[0].shape[0]
     for i, block in enumerate(blocks):
         block[...] = total[i * rows : (i + 1) * rows, :].astype(bf16)
+
+
+def join_natural_kernel(parts, ids, keep_ref, got_ref, out_ref):
+    total = keep_ref[...] + got_ref[...].astype(f32)
+    if parts == 1:
+        out_ref[...] = total.astype(bf16)
+        return
+    rows = out_ref.shape[1]
+    for i in range(parts):
+        out_ref[ids[1] ^ i] = total[i * rows : (i + 1) * rows, :].astype(bf16)
 
 
 def gather_kernel(back_table_ref, *refs):
@@ -194,66 +241,176 @@
     low_ref[...] = grad.astype(bf16)
 
 
-def attend_back_kernel(heads, parts, ids, own_ref, other_ref, wo_ref, qkv_ref, probs_ref, seq_ref, mixed_ref, *refs):
-    dqkv_ref, gwo_ref, diag_ref = refs[:3]
-    blocks = refs[3 : 3 + parts]
-    ga_ref, gm_ref, ds_ref, gw_ref = refs[3 + parts :]
-    core = ids[0]
-    me = ids[1]
-    half = own_ref.shape[0]
+def heads_back(heads, first, qkv_ref, gm_ref, probs, dqkv_ref, diag_ref, ds_ref):
     seq = qkv_ref.shape[0]
     width = heads * HD
+    here = len(probs) * HD
     span = seq + TILE
-    ga_ref[pl.ds(pl.multiple_of(core * half, half), half), :] = own_ref[...]
-    ga_ref[pl.ds(pl.multiple_of((1 - core) * half, half), half), :] = other_ref[...]
-    gm_ref[...] = mm(ga_ref[...], wo_ref[...]).astype(bf16)
-    gwo_ref[...] = mm_at(ga_ref[...], mixed_ref[...]).astype(bf16)
     flip = (
         lax.broadcasted_iota(jnp.int32, (TILE, TILE), 0)
         + lax.broadcasted_iota(jnp.int32, (TILE, TILE), 1)
         == TILE - 1
     ).astype(bf16)
-    diag_ref[...] = jnp.zeros_like(diag_ref)
-    for h in range(heads):
-        at = h * HD
+    for h, probs_ref in enumerate(probs):
+        at = (first + h) * HD
+        to = h * HD
         key = qkv_ref[:, width + at : width + at + HD]
         value = qkv_ref[:, 2 * width + at : 2 * width + at + HD]
         for i in range(0, seq, TILE):
-            probs = probs_ref[h, i : i + TILE, :]
+            probs_rows = probs_ref[i : i + TILE, :]
             grad_probs = mm_bt(gm_ref[i : i + TILE, at : at + HD], value)
-            inner = jnp.sum(probs * grad_probs, axis=1, keepdims=True)
-            grad_scores = (probs * (grad_probs - inner)).astype(bf16)
+            inner = jnp.sum(probs_rows * grad_probs, axis=1, keepdims=True)
+            grad_scores = (probs_rows * (grad_probs - inner)).astype(bf16)
             ds_ref[i : i + TILE, :] = grad_scores
-            dqkv_ref[i : i + TILE, at : at + HD] = (mm(grad_scores, key) * HD**-0.5).astype(bf16)
+            dqkv_ref[i : i + TILE, to : to + HD] = (mm(grad_scores, key) * HD**-0.5).astype(bf16)
             flipped = mm(flip, grad_scores)
             padded = jnp.concatenate([flipped, jnp.zeros((TILE, TILE), f32)], axis=1)
             skewed = pltpu.roll(padded, 0, 1, stride=1, stride_axis=0)
             base = seq - TILE - i
-            diag_ref[h : h + 1, base : base + span] += jnp.sum(skewed, axis=0, keepdims=True)
-        dqkv_ref[:, width + at : width + at + HD] = (
+            row = first + h
+            diag_ref[row : row + 1, base : base + span] += jnp.sum(skewed, axis=0, keepdims=True)
+        dqkv_ref[:, here + to : here + to + HD] = (
             mm_at(ds_ref[...], qkv_ref[:, at : at + HD]) * HD**-0.5
         ).astype(bf16)
-        dqkv_ref[:, 2 * width + at : 2 * width + at + HD] = mm_at(
-            probs_ref[h].astype(bf16), gm_ref[:, at : at + HD]
+        dqkv_ref[:, 2 * here + to : 2 * here + to + HD] = mm_at(
+            probs_ref[...].astype(bf16), gm_ref[:, at : at + HD]
         ).astype(bf16)
+
+
+def send_rows(parts, me, gw_ref, outs):
+    if parts == 1:
+        outs[0][...] = gw_ref[...].astype(bf16)
+        return
+    rows = gw_ref.shape[0] // parts
+    for i in range(parts // 2):
+        at = slice(i * rows, (i + 1) * rows)
+        outs[0][at, :] = gw_ref[pl.ds(pl.multiple_of((me ^ 2 * i) * rows, rows), rows), :]
+        there = pl.ds(pl.multiple_of((me ^ 2 * i ^ 1) * rows, rows), rows)
+        outs[1][at, :] = gw_ref[there, :].astype(bf16)
+
+
+def first_back_kernel(heads, parts, ids, own_ref, other_ref, wo_ref, qkv_ref, probs_ref, seq_ref, mixed_ref, *refs):
+    gm_ref, dqkv_ref, diag_ref, *outs = refs[:-3]
+    ga_ref, ds_ref, gw_ref = refs[-3:]
+    core = ids[0]
+    half = own_ref.shape[0]
+    ga_ref[pl.ds(pl.multiple_of(core * half, half), half), :] = own_ref[...]
+    ga_ref[pl.ds(pl.multiple_of((1 - core) * half, half), half), :] = other_ref[...]
+    gm_ref[...] = mm(ga_ref[...], wo_ref[...]).astype(bf16)
+    diag_ref[...] = jnp.zeros_like(diag_ref)
+    heads_back(heads, 0, qkv_ref, gm_ref, [probs_ref], dqkv_ref, diag_ref, ds_ref)
+    cut = dqkv_ref.shape[1]
+    gw_ref[:, :cut] = mm_at(seq_ref[...], dqkv_ref[...])
+    gw_ref[:, cut:] = mm_at(ga_ref[...], mixed_ref[...])
+    send_rows(parts, ids[1], gw_ref, outs)
+
+
+def second_back_kernel(
+    heads, parts, ids, gm_ref, qkv_ref, first_ref, diag_in_ref, hot_ref, x_ref, seq_ref, wqkv_ref, gain_ref, router_ref, *refs
+):
+    probs = refs[: heads - 1]
+    keep_ref, send_ref, small_ref, *outs = refs[heads - 1 : -5]
+    diag_ref, dqkv_ref, all_ref, ds_ref, gw_ref = refs[-5:]
+    core, me, side = ids[0], ids[1], ids[2]
+    half = keep_ref.shape[0]
+    diag_ref[...] = diag_in_ref[...]
+    heads_back(heads, 1, qkv_ref, gm_ref, probs, dqkv_ref, diag_ref, ds_ref)
     gw_ref[...] = mm_at(seq_ref[...], dqkv_ref[...])
-    rows = blocks[0].shape[0]
-    for i, block in enumerate(blocks):
-        start = 0 if parts == 1 else pl.multiple_of((me ^ i) * rows, rows)
-        block[...] = gw_ref[pl.ds(start, rows), :].astype(bf16)
-
-
-def normed_back_kernel(ids, dqkv_ref, wqkv_ref, keep_ref, send_ref):
+    send_rows(parts, me, gw_ref, outs)
+    rest = (heads - 1) * HD
+    for i in range(3):
+        at = i * heads * HD
+        all_ref[:, at : at + HD] = first_ref[:, i * HD : (i + 1) * HD]
+        all_ref[:, at + HD : at + heads * HD] = dqkv_ref[:, i * rest : (i + 1) * rest]
+    gain = jnp.zeros((1, x_ref.shape[1]), f32)
+    for place, mine in ((core, True), (1 - core, False)):
+        rows = pl.ds(pl.multiple_of(place * half, half), half)
+        grad = mm_bt(all_ref[rows, :], wqkv_ref[...])
+        wide = x_ref[rows, :].astype(f32)
+        scale = lax.rsqrt(jnp.mean(wide * wide, axis=1, keepdims=True) + norm_eps)
+        gain = gain + jnp.sum(grad * wide * scale, axis=0, keepdims=True)
+        if mine:
+            keep_ref[...] = grad
+        else:
+            send_ref[...] = grad.astype(bf16)
+    small_ref[...] = jnp.zeros_like(small_ref)
+    small_ref[0:1, :] = gain
+    small_ref[1:2, :] = jnp.where(side == 0, gain_ref[...], 0.0)
+    experts = router_ref.shape[0]
+    small_ref[2 : 2 + experts, :] = router_ref[...]
+    bias = jnp.dot(diag_ref[...], hot_ref[...], precision=exact, preferred_element_type=f32)
+    lanes = bias.shape[1]
+    for i in range(2 * GROUP):
+        small_ref[2 + experts : 2 + experts + heads, i * lanes : (i + 1) * lanes] = jnp.where(
+            side * GROUP + core == i, bias[:heads, :], 0.0
+        )
+
+
+def fold_kernel(keep_ref, got_ref, own_ref, *sends):
+    total = keep_ref[...] + got_ref[...].astype(f32)
+    rows = own_ref.shape[0]
+    own_ref[...] = total[:rows, :]
+    for i, send in enumerate(sends):
+        send[...] = total[(i + 1) * rows : (i + 2) * rows, :].astype(bf16)
+
+
+def fold_small_kernel(keep_ref, got_ref, small_ref, small_got_ref, own_ref, *sends):
+    total = keep_ref[...] + got_ref[...].astype(f32)
+    rows = keep_ref.shape[0] // (len(sends) + 1)
+    cols = own_ref.shape[1]
+    small = small_ref[...] + small_got_ref[...]
+    high = small.shape[0]
+    for i, block in enumerate((own_ref, *sends)):
+        block[:rows, :] = total[i * rows : (i + 1) * rows, :].astype(block.dtype)
+        block[rows : rows + high, :] = small[:, :cols].astype(bf16).astype(block.dtype)
+        block[rows + high :, :] = small[:, cols:].astype(bf16).astype(block.dtype)
+
+
+def sum_nodes_kernel(ids, *refs):
+    first, second = refs[:4], refs[4:8]
+    keep_ref, send_ref, small_ref = refs[8:]
     core = ids[0]
-    half = keep_ref.shape[0]
-    mine = dqkv_ref[pl.ds(pl.multiple_of(core * half, half), half), :]
-    keep_ref[...] = mm_bt(mine, wqkv_ref[...])
-    theirs = dqkv_ref[pl.ds(pl.multiple_of((1 - core) * half, half), half), :]
-    send_ref[...] = mm_bt(theirs, wqkv_ref[...]).astype(bf16)
-
-
-def rms_scale(values, gain):
-    return values * lax.rsqrt(jnp.mean(values * values, axis=-1, keepdims=True) + norm_eps) * gain
+    rows = keep_ref.shape[0]
+    cols = keep_ref.shape[1] // 2
+
+    def part(group, at):
+        a, b, c, d = (r[at, :].astype(f32) for r in group)
+        return (a + b) + (c + d)
+
+    mine = pl.ds(pl.multiple_of(core * rows, rows), rows)
+    theirs = pl.ds(pl.multiple_of((1 - core) * rows, rows), rows)
+    keep_ref[:, :cols] = part(first, mine)
+    keep_ref[:, cols:] = part(second, mine)
+    send_ref[:, :cols] = part(first, theirs)
+    send_ref[:, cols:] = part(second, theirs)
+    high = small_ref.shape[0]
+    small_ref[:, :cols] = part(second, slice(2 * rows, 2 * rows + high))
+    small_ref[:, cols:] = part(second, slice(2 * rows + high, 2 * rows + 2 * high))
+
+
+def columns_kernel(heads, ids, keep_ref, got_ref, *outs):
+    core = ids[0]
+    cols = heads * HD
+    rest = cols - HD
+    zero = core == 0
+    pair = (jnp.where(zero, keep_ref[...], got_ref[...]), jnp.where(zero, got_ref[...], keep_ref[...]))
+    middle = keep_ref.shape[1] // 2
+    for c, part in enumerate(pair):
+        at = c * cols
+        for i in range(3):
+            outs[i][:, at : at + HD] = part[:, i * HD : (i + 1) * HD]
+            start = middle + i * rest
+            outs[i][:, at + HD : at + cols] = part[:, start : start + rest]
+        outs[3][:, at : at + cols] = part[:, 3 * HD : 3 * HD + cols]
+
+
+def input_kernel(keep_ref, got_ref, grad_ref, x_ref, gain_ref, out_ref):
+    grad_normed = keep_ref[...] + got_ref[...].astype(f32)
+    wide = x_ref[...].astype(f32)
+    scale = lax.rsqrt(jnp.mean(wide * wide, axis=1, keepdims=True) + norm_eps)
+    pulled = gain_ref[...] * grad_normed
+    inner = jnp.mean(pulled * wide, axis=1, keepdims=True)
+    out_ref[...] = grad_ref[...] + scale * pulled - wide * (scale * scale * scale) * inner
 
 
 def in_order(first, mine, other):
@@ -291,7 +448,7 @@
     me = lax.axis_index("node")
     direct = nodes == DIRECT
     parts = nodes if direct else 1
-    ids = jnp.stack([core, me]).astype(jnp.int32)
+    ids = jnp.stack([core, me, side]).astype(jnp.int32)
     node_rows = width // nodes
 
     def trade(blocks):
@@ -304,13 +461,6 @@
     def trade_natural(rows):
         stacked = rows.reshape(nodes, -1, rows.shape[-1])
         return lax.all_to_all(stacked, "node", split_axis=0, concat_axis=0, tiled=True)
-
-    def reorder(stacked):
-        if not direct:
-            return stacked
-        return jnp.concatenate(
-            [lax.dynamic_slice_in_dim(stacked, me ^ i, 1, 0) for i in range(nodes)]
-        )
 
     shares = jnp.stack([w_query, w_key, w_value, w_out]).reshape(4, -1, GROUP, cols)
     shares = jnp.moveaxis(shares, 0, 2).reshape(-1, GROUP, 4 * cols)
@@ -328,10 +478,9 @@
         pieces = [lax.all_gather(piece, "node", axis=0, tiled=True)]
 
     x_rows = in_order(side == 0, tokens, across(tokens, "tensor", 1))
-    gain_first = gain_one.astype(f32)
+    x_other = across(x_rows, "core", 1)
+    gain_first = gain_one.astype(f32)[None, :]
     gain_second = gain_two.astype(f32)[None, :]
-    normed = rms_scale(x_rows.astype(f32), gain_first).astype(bf16)
-    normed_other = across(normed, "core", 1)
 
     expert_ids = routes[:, 0]
     picks = (expert_ids[:, None] == jnp.arange(experts, dtype=jnp.int32)[None, :]).astype(jnp.int32)
@@ -343,10 +492,25 @@
     back_table = (target[:, None] == turned[None, :]).astype(bf16)
     plain_table = (codes[:, None] == target[None, :]).astype(bf16)
 
-    cot_slots = mm(plain_table, cotangent).astype(bf16)
-    cots_own = reorder(trade_natural(cot_slots)).reshape(slots, width)
-    cots = jnp.concatenate([cots_own, across(cots_own, "core", 1)])
-    back_active = mm(cots, w_down)
+    natural = (nodes, slots // nodes, width) if direct else (slots, width)
+    cot_slots = call(
+        slots_kernel,
+        "cot_slots",
+        [out((slots, width), bf16)],
+        [plain_table, cotangent],
+        flops=2 * slots * block_rows * width,
+        after=[pieces[min(2, parts - 1)]],
+    )[0]
+    cots_own = trade_natural(cot_slots).reshape(natural)
+    cots, back_active = call(
+        functools.partial(cots_kernel, parts),
+        "cots",
+        [out((2 * slots, width), bf16), out((2 * slots, w_down.shape[1]), f32)],
+        [ids, cots_own, across(cots_own, "core", 1), w_down],
+        smem=1,
+        scratch=[pltpu.VMEM((slots, width), f32)] if direct else [],
+        flops=4 * slots * width * w_down.shape[1],
+    )
 
     lengths_row = lax.dynamic_slice_in_dim(doc_lengths, me, 1, 0)[0]
     ends = jnp.cumsum(lengths_row)
@@ -354,36 +518,38 @@
     docs = jnp.sum((ends[None, :] <= places[:, None]).astype(jnp.int32), axis=1)
     bucket_count = bias_table.shape[0]
     bucket_hot = (
-        jnp.pad(buckets, (0, 1))[:, None] == jnp.arange(bucket_count, dtype=jnp.int32)[None, :]
+        jnp.pad(buckets, (0, 1))[:, None] == jnp.arange(128, dtype=jnp.int32)[None, :]
     ).astype(f32)
     head_start = (side * GROUP + core) * heads
     bias_here = lax.dynamic_slice_in_dim(bias_table, head_start, heads, 1)
+    bias_here = jnp.pad(bias_here, ((0, 128 - bucket_count), (0, 0)))
     bias_vectors = lax.dot_general(
         bias_here, bucket_hot, (((0,), (1,)), ((), ())), precision=exact, preferred_element_type=f32
     )
 
-    wqkv, wo, normed_seq, qkv = call(
+    wqkv, wo, x_seq, normed_seq, qkv = call(
         functools.partial(project_kernel, parts),
         "project",
         [
             out((width, 3 * cols), bf16),
             out((width, cols), bf16),
             out((seq, width), bf16),
+            out((seq, width), bf16),
             out((seq, 3 * cols), bf16),
         ],
-        [ids, normed, normed_other, *pieces],
+        [ids, x_rows, x_other, gain_first, *pieces],
         smem=1,
         flops=2 * seq * width * 3 * cols,
     )
     wo_other = across(wo, "core", 1)
-    probs, mixed, mixed_kept, mixed_sent = call(
+    mixed, mixed_kept, mixed_sent, *probs = call(
         functools.partial(attend_kernel, heads),
         "attend",
         [
-            out((heads, seq, seq), f32),
             out((seq, cols), bf16),
             out((block_rows, cols), bf16),
             out((block_rows, cols), bf16),
+            *([out((seq, seq), f32)] * heads),
         ],
         [ids, qkv, bias_vectors, docs[:, None], docs[None, :]],
         smem=1,
@@ -419,7 +585,7 @@
             out((2 * slots, 1), f32),
             out((slots, width), f32),
             out((slots, width), bf16),
-            out(w_router.shape, f32),
+            out(w_router.shape[::-1], f32),
         ],
         [ids, slots_own, slots_other, back_active, w_up, w_router],
         smem=1,
@@ -449,10 +615,17 @@
         ],
         [slots_own, slots_other, cots, active, grad_upward, chosen, w_down],
         flops=12 * slots * width * w_up.shape[1],
-    )
-    out_slots = (out_kept + across(out_sent, "core", 1).astype(f32)).astype(bf16)
-    out_slots = reorder(out_slots.reshape(nodes, -1, width))
-    out_back = trade_natural(out_slots).reshape(slots, width)
+        after=grad_blocks[-1:],
+    )
+    out_slots = call(
+        functools.partial(join_natural_kernel, parts),
+        "join_out",
+        [out(natural, bf16)],
+        [ids, out_kept, across(out_sent, "core", 1)],
+        smem=1,
+        after=[grad_normed_two],
+    )[0]
+    out_back = trade_natural(out_slots.reshape(slots, width)).reshape(slots, width)
     returned = lax.dot_general(
         plain_table, out_back, (((0,), (0,)), ((), ())), preferred_element_type=f32
     ).astype(bf16)
@@ -472,91 +645,139 @@
         [hidden, grad_normed_two, grad_normed_two_got, cotangent, gain_second],
     )
     grad_attended_other = across(grad_attended, "core", 1)
-    dqkv, gwo, diagonals, *grad_weights = call(
-        functools.partial(attend_back_kernel, heads, parts),
-        "attend_back",
+    chunk = 3 * HD + cols
+    other_chunk = 3 * (cols - HD)
+    if direct:
+        half_width = width // 2
+        chunk_shapes = [[out((half_width, c), f32), out((half_width, c), bf16)] for c in (chunk, other_chunk)]
+    else:
+        chunk_shapes = [[out((width, c), bf16)] for c in (chunk, other_chunk)]
+    grad_mixed, first_dqkv, diagonals, *first_chunk = call(
+        functools.partial(first_back_kernel, heads, parts),
+        "first_back",
         [
-            out((seq, 3 * cols), bf16),
-            out((width, cols), bf16),
-            out((heads, 2 * seq), f32),
-            *([out((width // parts, 3 * cols), bf16)] * parts),
-        ],
-        [ids, grad_attended, grad_attended_other, wo, qkv, probs, normed_seq, mixed],
+            out((seq, cols), bf16),
+            out((seq, 3 * HD), bf16),
+            out((8, 2 * seq), f32),
+            *chunk_shapes[0],
+        ],
+        [ids, grad_attended, grad_attended_other, wo, qkv, probs[0], normed_seq, mixed],
         smem=1,
         scratch=[
             pltpu.VMEM((seq, width), bf16),
-            pltpu.VMEM((seq, cols), bf16),
             pltpu.VMEM((seq, seq), bf16),
-            pltpu.VMEM((width, 3 * cols), f32),
-        ],
-        flops=16 * heads * seq * seq * 256,
-    )
-    received_weights = trade(grad_weights)
-    summed_weights = sum(r.reshape(-1, node_rows, 3 * cols).astype(f32).sum(0) for r in received_weights)
-    summed_out = jnp.sum(trade_natural(gwo).astype(f32), axis=0)
-    node_sums = jnp.concatenate([summed_weights, summed_out], axis=1)
+            pltpu.VMEM((width, chunk), f32),
+        ],
+        flops=16 * seq * seq * 256,
+    )
+    small_rows = -(-(2 + experts + heads) // 16) * 16
+    grad_kept, grad_sent, small, *second_chunk = call(
+        functools.partial(second_back_kernel, heads, parts),
+        "second_back",
+        [
+            out((block_rows, width), f32),
+            out((block_rows, width), bf16),
+            out((small_rows, width), f32),
+            *chunk_shapes[1],
+        ],
+        [
+            ids,
+            grad_mixed,
+            qkv,
+            first_dqkv,
+            diagonals,
+            bucket_hot,
+            x_seq,
+            normed_seq,
+            wqkv,
+            gain_two_part,
+            router_part,
+            *probs[1:],
+        ],
+        smem=1,
+        scratch=[
+            pltpu.VMEM((8, 2 * seq), f32),
+            pltpu.VMEM((seq, other_chunk), bf16),
+            pltpu.VMEM((seq, 3 * cols), bf16),
+            pltpu.VMEM((seq, seq), bf16),
+            pltpu.VMEM((width, other_chunk), f32),
+        ],
+        flops=16 * (heads - 1) * seq * seq * 256,
+    )
+
     shard_rows = w_query.shape[0]
-    sums_kept = lax.dynamic_slice_in_dim(node_sums, core * shard_rows, shard_rows, 0)
-    sums_sent = lax.dynamic_slice_in_dim(node_sums, (1 - core) * shard_rows, shard_rows, 0)
-    sums_got = across(sums_sent, "core", 1)
-
-    def columns(index):
-        mine = sums_kept[:, index * cols : (index + 1) * cols]
-        theirs = sums_got[:, index * cols : (index + 1) * cols]
-        return jnp.where(
-            core == 0,
-            jnp.concatenate([mine, theirs], axis=1),
-            jnp.concatenate([theirs, mine], axis=1),
+    if direct:
+        own_one, *send_one = call(
+            fold_kernel,
+            "fold_first",
+            [out((node_rows, chunk), f32), *([out((node_rows, chunk), bf16)] * 3)],
+            [first_chunk[0], across(first_chunk[1], "node", 1)],
         )
-
-    grad_kept, grad_sent = call(
-        normed_back_kernel,
-        "normed_back",
-        [out((block_rows, width), f32), out((block_rows, width), bf16)],
-        [ids, dqkv, wqkv],
+        got_one = [across(b, "node", 2 * i + 2) for i, b in enumerate(send_one)]
+        small = small + across(small, "tensor", 1)
+        small = small + across(small, "core", 1)
+        tall = node_rows + 2 * small_rows
+        own_two, *send_two = call(
+            fold_small_kernel,
+            "fold_second",
+            [out((tall, other_chunk), f32), *([out((tall, other_chunk), bf16)] * 3)],
+            [second_chunk[0], across(second_chunk[1], "node", 1), small, across(small, "node", 1)],
+        )
+        got_two = [across(b, "node", 2 * i + 2) for i, b in enumerate(send_two)]
+        sums_kept, sums_sent, small = call(
+            sum_nodes_kernel,
+            "sum_nodes",
+            [
+                out((shard_rows, 2 * chunk), f32),
+                out((shard_rows, 2 * chunk), f32),
+                out((small_rows, width), f32),
+            ],
+            [ids, own_one, *got_one, own_two, *got_two],
+            smem=1,
+        )
+    else:
+        sums = jnp.concatenate(
+            [
+                jnp.sum(trade_natural(c[0]).astype(f32), axis=0)
+                for c in (first_chunk, second_chunk)
+            ],
+            axis=1,
+        )
+        sums_kept = lax.dynamic_slice_in_dim(sums, core * shard_rows, shard_rows, 0)
+        sums_sent = lax.dynamic_slice_in_dim(sums, (1 - core) * shard_rows, shard_rows, 0)
+        small = lax.psum(small, ("node", "core", "tensor"))
+    weight_grads = call(
+        functools.partial(columns_kernel, heads),
+        "columns",
+        [out(w_query.shape, f32)] * 4,
+        [ids, sums_kept, across(sums_sent, "core", 1)],
         smem=1,
-        flops=2 * seq * width * 3 * cols,
-    )
+    )
+
     grad_normed = grad_kept + across(grad_sent, "core", 1).astype(f32)
-    x_wide = x_rows.astype(f32)
-    scale = lax.rsqrt(jnp.mean(x_wide * x_wide, axis=1, keepdims=True) + norm_eps)
-    gain_one_part = jnp.sum(grad_normed * x_wide * scale, axis=0)
     grad_normed_got = across(half_of(grad_normed, 1 - side).astype(bf16), "tensor", 1)
-    grad_normed_own = half_of(grad_normed, side) + grad_normed_got.astype(f32)
-    x_own = tokens.astype(f32)
-    norm_first, norm_pull_one = jax.vjp(lambda v: rms_scale(v, gain_first), x_own)
-    input_grad = half_of(grad_hidden, side) + norm_pull_one(grad_normed_own)[0]
-
-    bias_part = lax.dot_general(
-        bucket_hot, diagonals, (((0,), (1,)), ((), ())), precision=exact, preferred_element_type=f32
-    )
-    bias_full = lax.dynamic_update_slice(
-        jnp.zeros(bias_table.shape, f32), bias_part, (jnp.int32(0), head_start)
-    )
-    gain_two_part = jnp.where(side == 0, gain_two_part[0], 0.0)
-    small = jnp.concatenate(
-        [gain_one_part, gain_two_part, bias_full.reshape(-1), router_part.reshape(-1)]
-    ).reshape(-1, 128)
-    small = small + across(small, "core", 1)
-    small = small + across(small, "tensor", 1)
-    if direct:
-        for bits in (1, 2, 4):
-            small = small + across(small, "node", bits)
-    else:
-        small = lax.psum(small, "node")
-    small = small.reshape(-1)
-    bias_size = bias_table.size
+    input_grad = call(
+        input_kernel,
+        "input_grad",
+        [out((own_rows, width), f32)],
+        [
+            half_of(grad_normed, side),
+            grad_normed_got,
+            half_of(grad_hidden, side),
+            tokens,
+            gain_first,
+        ],
+    )[0]
+    bias_rows = small[2 + experts : 2 + experts + heads, : 4 * 128].reshape(heads, 4, 128)
+    grad_bias = bias_rows[:, :, :bucket_count].transpose(2, 1, 0).reshape(bias_table.shape)
     return (
         activations,
         input_grad,
-        small[:width],
-        columns(0),
-        columns(1),
-        columns(2),
-        columns(3),
-        small[2 * width : 2 * width + bias_size].reshape(bias_table.shape),
-        small[width : 2 * width],
-        small[2 * width + bias_size :].reshape(w_router.shape),
+        small[0],
+        *weight_grads,
+        grad_bias,
+        small[1],
+        small[2 : 2 + experts].T,
         grad_w_up_here,
         grad_w_down_here,
     )

time: 219 us -> 199 us (0.909)
  starting transfers between devices: 83.2 us -> 63.4 us
  Pallas kernels: 31.3 us -> 42.2 us
  other arithmetic: 13.1 us -> 6.74 us
  matrix products: 6.8 us -> 1.54 us
  local copies, waits for them, and re-layouts: 30.8 us -> 33.1 us
  waiting for transfers between devices: 51.4 us -> 49.2 us
    ppermute x49 -> x48, starting transfers between devices: 66.9 us -> 55.1 us  [across(): lax.ppermute(shard, axis, [(i, i ^ bits) for i in range(lax.axis_size(axi...]
    pallas_call x11 -> x19, Pallas kernels: 31.3 us -> 42.2 us  [call(): pl.pallas_call(kernel, name=name, out_shape=outs, in_specs=[SMEM] * smem...]
    all_to_all x3 -> x2, starting transfers between devices: 16.3 us -> 8.29 us  [trade_natural(): lax.all_to_all(stacked, 'node', split_axis=0, concat_axis=0, tiled=True)]
    dot_general x3 -> x0, matrix products: 4.86 us -> none  [the longest x2 4.27 us: mm(): return jnp.dot(a, b, preferred_element_type=f32)]
    ppermute x49 -> x48, waiting for transfers between devices: 51.4 us -> 46.7 us  [across(): lax.ppermute(shard, axis, [(i, i ^ bits) for i in range(lax.axis_size(axi...]
    another operation x4, local copies, waits for them, and re-layouts: 0.39 us -> 3.51 us  [per_device(): jnp.stack([w_query, w_key, w_value, w_out]).reshape(4, -1, GROUP, cols)]
    reduce_sum x4 -> x0, other arithmetic: 2.64 us -> none  [the longest x1 1.19 us: per_device(): gain_one_part = jnp.sum(grad_normed * x_wide * scale, axis=0)]
    all_to_all x3 -> x2, waiting for transfers between devices: 0.01 us -> 2.52 us  [trade_natural(): lax.all_to_all(stacked, 'node', split_axis=0, concat_axis=0, tiled=True)]
  transfers between devices with their start and end apart: 52 -> 50, of which waited for: 16 -> 14; matrix products, arithmetic and copies ran while one was open for 16% -> 7% of each run, Pallas kernels for 11% -> 18%
where the time goes in v2:
time: 199 us; the launch traced here: 198 us
  starting transfers between devices  63.4 us (32%)
  waiting for transfers between devices  49.2 us (25%)
  Pallas kernels  42.2 us (21%)
  local copies, waits for them, and re-layouts  33.1 us (17%)
  other arithmetic  6.74 us (3%)
    ppermute x48, starting transfers between devices, across(): lax.ppermute(shard, axis, [(i, i ^ bits) for i in range(lax.axis_size(axi...  55.1 us
    ppermute x48, waiting for transfers between devices, across(): lax.ppermute(shard, axis, [(i, i ^ bits) for i in range(lax.axis_size(axi...  46.7 us
    pallas_call x19, Pallas kernels, call(): pl.pallas_call(kernel, name=name, out_shape=outs, in_specs=[SMEM] * smem...  42.2 us
    unnamed x110, local copies, waits for them, and re-layouts  22.5 us
    all_to_all x2, starting transfers between devices, trade_natural(): lax.all_to_all(stacked, 'node', split_axis=0, concat_axis=0, tiled=True)  8.29 us
  transfers between devices with their start and end apart: 50, of which 14 were waited for; matrix products, arithmetic and copies ran while one was open for 7% of the time, Pallas kernels for 18%

profile of v2, /device:TPU:0, one launch (start us, length us, event | category | flops | bytes accessed | tf_op | source)
XLA Modules:
  0.0 197.6 jit_solution(15753642729239441501)
XLA Ops:
  5.5 2.6 %collective-permute-start = (bf16[128,768]{1,0:T(8,128)(2,1)}, bf16[128,768]{1,0:T(8,128)(2,1)S(1)}, u32[]{:S(2)}, u32[]{:S(2)}) collective-permute-start(bf16[128,768]{1,0:T(8,128)(2,1)} %refs_3_.5), channel_id=1, source_target_pairs={{0,1},{1,0},{2,3},{3,2},{4,5},{5,4},{6,7},{7,6},{8,9},{9,8},{10,11... | collective-permute-start | bytes 589832 | tf_op jit(solution)/shard_map/ppermute | solution.py:27
  12.0 1.6 collective-permute-start.4
  13.6 2.6 %collective-permute-start.6 = (bf16[96,768]{1,0:T(8,128)(2,1)S(1)}, bf16[96,768]{1,0:T(8,128)(2,1)S(1)}, u32[]{:S(2)}, u32[]{:S(2)}) collective-permute-start(bf16[96,768]{1,0:T(8,128)(2,1)S(1)} %maximum_select_fusion.1.refs_4_), channel_id=1, source_target_pairs={{0,16},{4,20},{8,24},{12,28},{16,0},{20,4},{24,8},{28,12},{1,17},{... | collective-permute-start | bytes 442376 | tf_op jit(solution)/shard_map/ppermute | solution.py:27
  17.1 1.5 collective-permute-start.3
  18.6 1.8 collective-permute-done.4.refs_6_.refs_2_
  20.4 1.5 collective-permute-start.5
  21.9 5.7 %collective-permute-done.6.refs_8_ = bf16[96,768]{1,0:T(8,128)(2,1)S(1)} collective-permute-done((bf16[96,768]{1,0:T(8,128)(2,1)S(1)}, bf16[96,768]{1,0:T(8,128)(2,1)S(1)}, u32[]{:S(2)}, u32[]{:S(2)}) %collective-permute-start.6) | collective-permute-done | bytes 147488 | tf_op jit(solution)/shard_map/ppermute | solution.py:27
  27.6 1.5 collective-permute-start.7
  30.3 1.1 cot_slots.1
  31.4 4.7 %all-to-all-start = ((bf16[8,40,768]{2,1,0:T(8,128)(2,1)}), bf16[8,40,768]{2,1,0:T(8,128)(2,1)S(1)}, u32[]{:S(2)}, u32[]{:S(2)}) async-start(bf16[8,40,768]{2,1,0:T(8,128)(2,1)} %bitcast.14), calls=%async_computation | async-start | bytes 983040 | tf_op jit(solution)/shard_map/all_to_all | solution.py:463
  39.5 2.2 %project.1 = (bf16[768,576]{1,0:T(8,128)(2,1)S(1)}, bf16[768,192]{1,0:T(8,128)(2,1)S(1)}, bf16[512,768]{1,0:T(8,128)(2,1)S(1)}, bf16[512,768]{1,0:T(8,128)(2,1)S(1)}, bf16[512,576]{1,0:T(8,128)(2,1)S(1)}) custom-call(s32[3]{0:T(128)S(1)} %pad_add_fusion.refs_0_, bf16[256,768]{1,0:T(8,128)(2,1)S(1)} %maximum_select_fusion.refs_1_.refs_0_, ...), custom_call_target="tpu_custom_call" | custom-call | flops 452984832 | bytes 5311500 | tf_op jit(solution)/shard_map/project/pallas_call | solution.py:39
  41.7 1.0 copy-done.25
  45.6 1.1 copy-done.32
  46.7 5.2 %attend.1 = (bf16[512,192]{1,0:T(8,128)(2,1)S(1)}, bf16[256,192]{1,0:T(8,128)(2,1)S(1)}, bf16[256,192]{1,0:T(8,128)(2,1)S(1)}, f32[512,512]{1,0:T(8,128)S(1)}, f...) custom-call(s32[3]{0:T(128)S(1)} %pad_add_fusion.refs_0_, bf16[512,576]{1,0:T(8,128)(2,1)S(1)} %copy-done.32, ...), custom_call_target="tpu_custom_call" | custom-call | flops 1610612736 | bytes 4145164 | tf_op jit(solution)/shard_map/attend/pallas_call | solution.py:39
  52.0 1.0 copy-done.39
  53.0 1.0 copy-done.41
  54.5 1.0 collective-permute-done.10.refs_1_
  56.6 10.7 %collective-permute-done.12.refs_2_ = bf16[256,768]{1,0:T(8,128)(2,1)S(1)} collective-permute-done((bf16[256,768]{1,0:T(8,128)(2,1)S(1)}, bf16[256,768]{1,0:T(8,128)(2,1)S(1)}, u32[]{:S(2)}, u32[]{:S(2)}) %collective-permute-start.12) | collective-permute-done | bytes 393248 | tf_op jit(solution)/shard_map/ppermute | solution.py:27
  68.1 1.0 copy-done.6
  69.6 2.1 %collective-permute-start.13 = (bf16[40,768]{1,0:T(8,128)(2,1)S(1)}, bf16[40,768]{1,0:T(8,128)(2,1)S(1)}, u32[]{:S(2)}, u32[]{:S(2)}) collective-permute-start(bf16[40,768]{1,0:T(8,128)(2,1)S(1)} %get-tuple-element.86), channel_id=1, source_target_pairs={{0,4},{4,0},{8,12},{12,8},{16,20},{20,16},{24,28},{28,24},{1,5},{5... | collective-permute-start | bytes 184328 | tf_op jit(solution)/shard_map/ppermute | solution.py:27
  71.7 1.5 collective-permute-start.14
  73.2 2.8 %collective-permute-start.16 = (bf16[40,768]{1,0:T(8,128)(2,1)S(1)}, bf16[40,768]{1,0:T(8,128)(2,1)S(1)}, u32[]{:S(2)}, u32[]{:S(2)}) collective-permute-start(bf16[40,768]{1,0:T(8,128)(2,1)S(1)} %get-tuple-element.89), channel_id=1, source_target_pairs={{0,16},{4,20},{8,24},{12,28},{16,0},{20,4},{24,8},{28,12},{1,17},{... | collective-permute-start | bytes 184328 | tf_op jit(solution)/shard_map/ppermute | solution.py:27
  76.1 1.6 collective-permute-start.17
  77.7 3.2 %collective-permute-start.18 = (bf16[40,768]{1,0:T(8,128)(2,1)S(1)}, bf16[40,768]{1,0:T(8,128)(2,1)S(1)}, u32[]{:S(2)}, u32[]{:S(2)}) collective-permute-start(bf16[40,768]{1,0:T(8,128)(2,1)S(1)} %get-tuple-element.91), channel_id=1, source_target_pairs={{0,24},{4,28},{8,16},{12,20},{16,8},{20,12},{24,0},{28,4},{1,25},{... | collective-permute-start | bytes 184328 | tf_op jit(solution)/shard_map/ppermute | solution.py:27
  81.7 3.9 %collective-permute-done.17 = bf16[40,768]{1,0:T(8,128)(2,1)S(1)} collective-permute-done((bf16[40,768]{1,0:T(8,128)(2,1)S(1)}, bf16[40,768]{1,0:T(8,128)(2,1)S(1)}, u32[]{:S(2)}, u32[]{:S(2)}) %collective-permute-start.17) | collective-permute-done | bytes 61472 | tf_op jit(solution)/shard_map/ppermute | solution.py:27
  85.7 2.4 %collective-permute-done.19 = bf16[40,768]{1,0:T(8,128)(2,1)S(1)} collective-permute-done((bf16[40,768]{1,0:T(8,128)(2,1)S(1)}, bf16[40,768]{1,0:T(8,128)(2,1)S(1)}, u32[]{:S(2)}, u32[]{:S(2)}) %collective-permute-start.19) | collective-permute-done | bytes 61472 | tf_op jit(solution)/shard_map/ppermute | solution.py:27
  89.1 1.4 copy-done.23
  90.4 2.0 %cots.1 = (bf16[640,768]{1,0:T(8,128)(2,1)S(1)}, f32[640,768]{1,0:T(8,128)S(1)}) custom-call(s32[3]{0:T(128)S(1)} %pad_add_fusion.refs_0_, bf16[8,40,768]{2,1,0:T(8,128)(2,1)S(1)} %all-to-all-done.refs_1_, bf16[8,40,768]{2,1,0:T(8,128)(2,1)} %collective-permute-done.21.refs_2_, bf16[768,768]{1,0:T(8,128)(2,1)S(1)} %copy-done.23), custom_call_target="tpu_custom_call" | custom-call | flops 754974720 | bytes 5111820 | tf_op jit(solution)/shard_map/cots/pallas_call | solution.py:39
  92.5 5.9 %expert.1 = (bf16[640,768]{1,0:T(8,128)(2,1)S(1)}, bf16[640,768]{1,0:T(8,128)(2,1)S(1)}, f32[640,1]{1,0:T(8,128)S(1)}, f32[320,768]{1,0:T(8,128)S(1)}, bf16[320,...) custom-call(s32[3]{0:T(128)S(1)} %pad_add_fusion.refs_0_, ...), custom_call_target="tpu_custom_call" | custom-call | flops 1509949440 | bytes 7608844 | tf_op jit(solution)/shard_map/expert/pallas_call | solution.py:39
  98.9 1.5 collective-permute-done.22.refs_1_
  101.2 1.0 collective-permute-start.25
  102.2 2.0 %collective-permute-start.26 = (bf16[40,768]{1,0:T(8,128)(2,1)S(1)}, bf16[40,768]{1,0:T(8,128)(2,1)S(1)}, u32[]{:S(2)}, u32[]{:S(2)}) collective-permute-start(bf16[40,768]{1,0:T(8,128)(2,1)S(1)} %get-tuple-element.106), channel_id=1, source_target_pairs={{0,12},{4,8},{8,4},{12,0},{16,28},{20,24},{24,20},{28,16},{1,13},{... | collective-permute-start | bytes 184328 | tf_op jit(solution)/shard_map/ppermute | solution.py:27
  104.2 1.7 collective-permute-start.27
  105.9 1.3 collective-permute-start.28
  107.2 1.4 collective-permute-start.29
  108.6 3.3 %collective-permute-start.30 = (bf16[40,768]{1,0:T(8,128)(2,1)S(1)}, bf16[40,768]{1,0:T(8,128)(2,1)S(1)}, u32[]{:S(2)}, u32[]{:S(2)}) collective-permute-start(bf16[40,768]{1,0:T(8,128)(2,1)S(1)} %get-tuple-element.100.refs_7_), channel_id=1, source_target_pairs={{0,28},{4,24},{8,20},{12,16},{16,12},{20,8},{24,4},{28,0},{1,29},{... | collective-permute-start | bytes 184328 | tf_op jit(solution)/shard_map/ppermute | solution.py:27
  112.6 3.0 %collective-permute-done.28.refs_6_ = bf16[40,768]{1,0:T(8,128)(2,1)S(1)} collective-permute-done((bf16[40,768]{1,0:T(8,128)(2,1)S(1)}, bf16[40,768]{1,0:T(8,128)(2,1)S(1)}, u32[]{:S(2)}, u32[]{:S(2)}) %collective-permute-start.28) | collective-permute-done | bytes 61472 | tf_op jit(solution)/shard_map/ppermute | solution.py:27
  116.6 9.5 %collective-permute-done.32.refs_2_ = bf16[256,768]{1,0:T(8,128)(2,1)S(1)} collective-permute-done((bf16[256,768]{1,0:T(8,128)(2,1)S(1)}, bf16[256,768]{1,0:T(8,128)(2,1)S(1)}, u32[]{:S(2)}, u32[]{:S(2)}) %collective-permute-start.32) | collective-permute-done | bytes 393248 | tf_op jit(solution)/shard_map/ppermute | solution.py:27
  127.5 6.2 %expert_rest.1 = (f32[320,768]{1,0:T(8,128)S(1)}, bf16[320,768]{1,0:T(8,128)(2,1)}, f32[768,768]{1,0:T(8,128)}, f32[768,768]{1,0:T(8,128)}) custom-call(bf16[320,768]{1,0:T(8,128)(2,1)S(1)} %copy-done.21, bf16[320,768]{1,0:T(8,128)(2,1)} %collective-permute-done.20.refs_2_.refs_1_, bf16[640,768]{1,0:T(8,128)(2,1)S(1)} %get-tuple-element.93.refs_2_, ...), custom_call_target="tpu_custom_call" | custom-call | flops 2264924160 | bytes 11307520 | tf_op jit(solution)/shard_map/expert_rest/pallas_call | solution.py:39
  133.8 3.6 %first_back.1 = (bf16[512,192]{1,0:T(8,128)(2,1)S(1)}, bf16[512,192]{1,0:T(8,128)(2,1)S(1)}, f32[8,1024]{1,0:T(8,128)S(1)}, f32[384,384]{1,0:T(8,128)S(1)}, bf16[384,384]{1,0:T(8,128)(2,1)S(1)}) custom-call(s32[3]{0:T(128)S(1)} %pad_add_fusion.refs_0_, bf16[256,768]{1,0:T(8,128)(2,1)S(1)} %get-tuple-element.110.refs_1_, ...), custom_call_target="tpu_custom_call" | custom-call | flops 1073741824 | bytes 5013516 | tf_op jit(solution)/shard_map/first_back/pallas_call | solution.py:39
  138.0 6.4 %second_back.1 = (f32[256,768]{1,0:T(8,128)S(1)}, bf16[256,768]{1,0:T(8,128)(2,1)}, f32[16,768]{1,0:T(8,128)S(1)}, f32[384,384]{1,0:T(8,128)S(1)}, bf16[384,384]{1,0:T(8,128)(2,1)}) custom-call(s32[3]{0:T(128)S(1)} %pad_add_fusion.refs_0_, bf16[512,192]{1,0:T(8,128)(2,1)S(1)} %get-tuple-element.114.refs_1_, bf16[512,576]{1,0:T(8,128)(2,1)S(1)} %copy-done.33, ...), custom_call_target="tpu_custom_call" | custom-call | flops 2147483648 | bytes 8236044 | tf_op jit(solution)/shard_map/second_back/pallas_call | solution.py:39
  144.4 1.5 collective-permute-start.40
  146.4 3.6 %collective-permute-done.41 = f32[16,768]{1,0:T(8,128)S(1)} collective-permute-done((f32[16,768]{1,0:T(8,128)S(1)}, f32[16,768]{1,0:T(8,128)S(1)}, u32[]{:S(2)}, u32[]{:S(2)}) %collective-permute-start.41) | collective-permute-done | bytes 49184 | tf_op jit(solution)/shard_map/ppermute | solution.py:27
  150.1 1.2 collective-permute-done.42
  154.0 3.8 %collective-permute-start.37 = (bf16[96,384]{1,0:T(8,128)(2,1)}, bf16[96,384]{1,0:T(8,128)(2,1)S(1)}, u32[]{:S(2)}, u32[]{:S(2)}) collective-permute-start(bf16[96,384]{1,0:T(8,128)(2,1)} %get-tuple-element.129), channel_id=1, source_target_pairs={{0,8},{4,12},{8,0},{12,4},{16,24},{20,28},{24,16},{28,20},{1,9},{5... | collective-permute-start | bytes 221192 | tf_op jit(solution)/shard_map/ppermute | solution.py:27
  157.8 1.8 collective-permute-start.38
  159.6 1.1 copy-done.4
  160.7 1.7 fold_second.1
  163.1 1.1 collective-permute-start.44
  164.2 1.6 collective-permute-start.45
  166.4 1.7 collective-permute-start.46
  168.7 2.1 %collective-permute-start.39 = (bf16[96,384]{1,0:T(8,128)(2,1)}, bf16[96,384]{1,0:T(8,128)(2,1)}, u32[]{:S(2)}, u32[]{:S(2)}) collective-permute-start(bf16[96,384]{1,0:T(8,128)(2,1)} %copy-done.34), channel_id=1, source_target_pairs={{0,24},{4,28},{8,16},{12,20},{16,8},{20,12},{24,0},{28,4},{1,25},{... | collective-permute-start | bytes 221192 | tf_op jit(solution)/shard_map/ppermute | solution.py:27
  170.8 1.0 constant_dynamic-slice_fusion.refs_2_
  171.8 1.9 join_out.1
  173.8 3.6 %all-to-all-start.1 = ((bf16[8,40,768]{2,1,0:T(8,128)(2,1)}), bf16[8,40,768]{2,1,0:T(8,128)(2,1)S(1)}, u32[]{:S(2)}, u32[]{:S(2)}) async-start(bf16[8,40,768]{2,1,0:T(8,128)(2,1)} %join_out.1), calls=%async_computation.1 | async-start | bytes 983040 | tf_op jit(solution)/shard_map/all_to_all | solution.py:463
  181.0 1.1 sum_nodes.1
  182.2 2.0 %convert_add_fusion = f32[256,768]{1,0:T(8,128)} fusion(f32[256,768]{1,0:T(8,128)S(1)} %get-tuple-element.123, bf16[256,768]{1,0:T(8,128)(2,1)} %collective-permute-done.34), kind=kLoop, calls=%fused_computation.1 | loop fusion | flops 393216 | bytes 1966080 | tf_op jit(solution)/shard_map/add | solution.py:757
  184.2 1.0 dynamic-slice_convert_fusion
  186.5 2.5 %all-to-all-done.1 = bf16[8,40,768]{2,1,0:T(8,128)(2,1)S(1)} async-done(((bf16[8,40,768]{2,1,0:T(8,128)(2,1)}), bf16[8,40,768]{2,1,0:T(8,128)(2,1)S(1)}, u32[]{:S(2)}, u32[]{:S(2)}) %all-to-all-start.1) | async-done | bytes 491552 | tf_op jit(solution)/shard_map/all_to_all | solution.py:463
  189.0 1.1 convolution_convert_fusion
  191.9 1.0 constant_dynamic-slice_fusion.1.refs_0_
  192.9 1.3 columns.1
  194.3 1.0 input_grad.1
  195.2 1.6 collective-permute-done.31
  (212 shorter events, 39.4 us)
Async XLA Ops:
  0.6 11.3 %copy-start = (f32[32,12]{0,1:T(8,128)S(1)}, f32[32,12]{0,1:T(8,128)}, u32[]{:S(2)}) copy-start(f32[32,12]{0,1:T(8,128)} %param.21) | copy-start | bytes 4612
  0.7 15.8 %copy-start.2 = (bf16[128,768]{1,0:T(8,128)(2,1)S(1)}, bf16[128,768]{1,0:T(8,128)(2,1)}, u32[]{:S(2)}) copy-start(bf16[128,768]{1,0:T(8,128)(2,1)} %refs_3_.5) | copy-start | bytes 589828
  0.7 29.7 %copy-start.1 = (bf16[256,768]{1,0:T(8,128)(2,1)S(1)}, bf16[256,768]{1,0:T(8,128)(2,1)}, u32[]{:S(2)}) copy-start(bf16[256,768]{1,0:T(8,128)(2,1)} %refs_3_.4) | copy-start | bytes 1179652
  5.0 31.2 %copy-start.49 = (bf16[768]{0:T(1024)(128)(2,1)S(1)}, bf16[768]{0:T(1024)(128)(2,1)}, u32[]{:S(2)}) copy-start(bf16[768]{0:T(1024)(128)(2,1)} %param.16) | copy-start | bytes 4612
  5.0 7.0 %collective-permute-start.2 = (bf16[48,768]{1,0:T(8,128)(2,1)S(1)}, bf16[48,768]{1,0:T(8,128)(2,1)S(1)}, u32[]{:S(2)}, u32[]{:S(2)}) collective-permute-start(bf16[48,768]{1,0:T(8,128)(2,1)S(1)} %get-tuple-element.151), channel_id=1, source_target_pairs={{0,2},{2,0},{1,3},{3,1},{4,6},{6,4},{5,7},{7,5},{8,10},{10,8},{9,1... | collective-permute-start | bytes 221192 | tf_op jit(solution)/shard_map/ppermute | solution.py:27
  5.5 10.9 %collective-permute-start = (bf16[128,768]{1,0:T(8,128)(2,1)}, bf16[128,768]{1,0:T(8,128)(2,1)S(1)}, u32[]{:S(2)}, u32[]{:S(2)}) collective-permute-start(bf16[128,768]{1,0:T(8,128)(2,1)} %refs_3_.5), channel_id=1, source_target_pairs={{0,1},{1,0},{2,3},{3,2},{4,5},{5,4},{6,7},{7,6},{8,9},{9,8},{10,11... | collective-permute-start | bytes 589832 | tf_op jit(solution)/shard_map/ppermute | solution.py:27
  8.8 32.9 %copy-start.43 = (s32[1024]{0:T(1024)}, s32[1024]{0:T(1024)S(1)}, u32[]{:S(2)}) copy-start(s32[1024]{0:T(1024)S(1)} %pad.9) | copy-start | bytes 12292
  11.8 40.2 %copy-start.48 = (s32[256]{0:T(256)}, s32[256]{0:T(256)S(1)}, u32[]{:S(2)}) copy-start(s32[256]{0:T(256)S(1)} %multiply_add_fusion.1) | copy-start | bytes 3076
  12.0 8.4 %collective-permute-start.4 = (bf16[96,768]{1,0:T(8,128)(2,1)S(1)}, bf16[96,768]{1,0:T(8,128)(2,1)S(1)}, u32[]{:S(2)}, u32[]{:S(2)}) collective-permute-start(bf16[96,768]{1,0:T(8,128)(2,1)S(1)} %maximum_select_fusion.1.refs_4_), channel_id=1, source_target_pairs={{0,8},{4,12},{8,0},{12,4},{16,24},{20,28},{24,16},{28,20},{1,9},{5... | collective-permute-start | bytes 442376 | tf_op jit(solution)/shard_map/ppermute | solution.py:27
  13.6 14.0 %collective-permute-start.6 = (bf16[96,768]{1,0:T(8,128)(2,1)S(1)}, bf16[96,768]{1,0:T(8,128)(2,1)S(1)}, u32[]{:S(2)}, u32[]{:S(2)}) collective-permute-start(bf16[96,768]{1,0:T(8,128)(2,1)S(1)} %maximum_select_fusion.1.refs_4_), channel_id=1, source_target_pairs={{0,16},{4,20},{8,24},{12,28},{16,0},{20,4},{24,8},{28,12},{1,17},{... | collective-permute-start | bytes 442376 | tf_op jit(solution)/shard_map/ppermute | solution.py:27
  16.2 12.9 %collective-permute-start.8 = (bf16[96,768]{1,0:T(8,128)(2,1)S(1)}, bf16[96,768]{1,0:T(8,128)(2,1)S(1)}, u32[]{:S(2)}, u32[]{:S(2)}) collective-permute-start(bf16[96,768]{1,0:T(8,128)(2,1)S(1)} %maximum_select_fusion.1.refs_4_), channel_id=1, source_target_pairs={{0,24},{4,28},{8,16},{12,20},{16,8},{20,12},{24,0},{28,4},{1,25},{... | collective-permute-start | bytes 442376 | tf_op jit(solution)/shard_map/ppermute | solution.py:27
  16.6 21.1 %collective-permute-start.1 = (bf16[256,768]{1,0:T(8,128)(2,1)S(1)}, bf16[256,768]{1,0:T(8,128)(2,1)S(1)}, u32[]{:S(2)}, u32[]{:S(2)}) collective-permute-start(bf16[256,768]{1,0:T(8,128)(2,1)S(1)} %maximum_select_fusion.refs_1_.refs_0_), channel_id=1, source_target_pairs={{0,2},{2,0},{1,3},{3,1},{4,6},{6,4},{5,7},{7,5},{8,10},{10,8},{9,1... | collective-permute-start | bytes 1179656 | tf_op jit(solution)/shard_map/ppermute | solution.py:27
  17.1 19.3 %collective-permute-start.3 = (bf16[96,768]{1,0:T(8,128)(2,1)S(1)}, bf16[96,768]{1,0:T(8,128)(2,1)S(1)}, u32[]{:S(2)}, u32[]{:S(2)}) collective-permute-start(bf16[96,768]{1,0:T(8,128)(2,1)S(1)} %maximum_select_fusion.1.refs_4_), channel_id=1, source_target_pairs={{0,4},{4,0},{8,12},{12,8},{16,20},{20,16},{24,28},{28,24},{1,5},{5... | collective-permute-start | bytes 442376 | tf_op jit(solution)/shard_map/ppermute | solution.py:27
  20.4 15.9 %collective-permute-start.5 = (bf16[96,768]{1,0:T(8,128)(2,1)S(1)}, bf16[96,768]{1,0:T(8,128)(2,1)S(1)}, u32[]{:S(2)}, u32[]{:S(2)}) collective-permute-start(bf16[96,768]{1,0:T(8,128)(2,1)S(1)} %collective-permute-done.4.refs_6_.refs_2_), channel_id=1, source_target_pairs={{0,4},{4,0},{8,12},{12,8},{16,20},{20,16},{24,28},{28,24},{1,5},{5... | collective-permute-start | bytes 442376 | tf_op jit(solution)/shard_map/ppermute | solution.py:27
  27.6 9.4 %collective-permute-start.7 = (bf16[96,768]{1,0:T(8,128)(2,1)S(1)}, bf16[96,768]{1,0:T(8,128)(2,1)S(1)}, u32[]{:S(2)}, u32[]{:S(2)}) collective-permute-start(bf16[96,768]{1,0:T(8,128)(2,1)S(1)} %collective-permute-done.6.refs_8_), channel_id=1, source_target_pairs={{0,4},{4,0},{8,12},{12,8},{16,20},{20,16},{24,28},{28,24},{1,5},{5... | collective-permute-start | bytes 442376 | tf_op jit(solution)/shard_map/ppermute | solution.py:27
  29.1 8.6 %collective-permute-start.9 = (bf16[96,768]{1,0:T(8,128)(2,1)S(1)}, bf16[96,768]{1,0:T(8,128)(2,1)}, u32[]{:S(2)}, u32[]{:S(2)}) collective-permute-start(bf16[96,768]{1,0:T(8,128)(2,1)S(1)} %collective-permute-done.8.refs_10_), channel_id=1, source_target_pairs={{0,4},{4,0},{8,12},{12,8},{16,20},{20,16},{24,28},{28,24},{1,5},{5... | collective-permute-start | bytes 442376 | tf_op jit(solution)/shard_map/ppermute | solution.py:27
  31.4 25.1 %all-to-all-start = ((bf16[8,40,768]{2,1,0:T(8,128)(2,1)}), bf16[8,40,768]{2,1,0:T(8,128)(2,1)S(1)}, u32[]{:S(2)}, u32[]{:S(2)}) async-start(bf16[8,40,768]{2,1,0:T(8,128)(2,1)} %bitcast.14), calls=%async_computation | async-start | bytes 983040 | tf_op jit(solution)/shard_map/all_to_all | solution.py:463
  45.4 10.1 %collective-permute-start.11 = (bf16[768,192]{1,0:T(8,128)(2,1)S(1)}, bf16[768,192]{1,0:T(8,128)(2,1)S(1)}, u32[]{:S(2)}, u32[]{:S(2)}) collective-permute-start(bf16[768,192]{1,0:T(8,128)(2,1)S(1)} %get-tuple-element.83.refs_2_.refs_3_), channel_id=1, source_target_pairs={{0,2},{2,0},{1,3},{3,1},{4,6},{6,4},{5,7},{7,5},{8,10},{10,8},{9,1... | collective-permute-start | bytes 884744 | tf_op jit(solution)/shard_map/ppermute | solution.py:27
  46.7 9.7 %copy-start.50 = (bf16[768]{0:T(1024)(128)(2,1)S(1)}, bf16[768]{0:T(1024)(128)(2,1)}, u32[]{:S(2)}) copy-start(bf16[768]{0:T(1024)(128)(2,1)} %param.22) | copy-start | bytes 4612
  54.0 13.4 %copy-start.37 = (bf16[512,192]{1,0:T(8,128)(2,1)}, bf16[512,192]{1,0:T(8,128)(2,1)S(1)}, u32[]{:S(2)}) copy-start(bf16[512,192]{1,0:T(8,128)(2,1)S(1)} %get-tuple-element.113.refs_7_) | copy-start | bytes 589828
  54.0 1.5 collective-permute-start.10
  55.9 11.4 %collective-permute-start.12 = (bf16[256,768]{1,0:T(8,128)(2,1)S(1)}, bf16[256,768]{1,0:T(8,128)(2,1)S(1)}, u32[]{:S(2)}, u32[]{:S(2)}) collective-permute-start(bf16[256,768]{1,0:T(8,128)(2,1)S(1)} %attended.1.refs_1_), channel_id=1, source_target_pairs={{0,1},{1,0},{2,3},{3,2},{4,5},{5,4},{6,7},{7,6},{8,9},{9,8},{10,11... | collective-permute-start | bytes 1179656 | tf_op jit(solution)/shard_map/ppermute | solution.py:27
  56.5 32.6 %collective-permute-start.21 = (bf16[8,40,768]{2,1,0:T(8,128)(2,1)S(1)}, bf16[8,40,768]{2,1,0:T(8,128)(2,1)}, u32[]{:S(2)}, u32[]{:S(2)}) collective-permute-start(bf16[8,40,768]{2,1,0:T(8,128)(2,1)S(1)} %all-to-all-done.refs_1_), channel_id=1, source_target_pairs={{0,2},{2,0},{1,3},{3,1},{4,6},{6,4},{5,7},{7,5},{8,10},{10,8},{9,1... | collective-permute-start | bytes 1474568 | tf_op jit(solution)/shard_map/ppermute | solution.py:27
  69.6 6.5 %collective-permute-start.13 = (bf16[40,768]{1,0:T(8,128)(2,1)S(1)}, bf16[40,768]{1,0:T(8,128)(2,1)S(1)}, u32[]{:S(2)}, u32[]{:S(2)}) collective-permute-start(bf16[40,768]{1,0:T(8,128)(2,1)S(1)} %get-tuple-element.86), channel_id=1, source_target_pairs={{0,4},{4,0},{8,12},{12,8},{16,20},{20,16},{24,28},{28,24},{1,5},{5... | collective-permute-start | bytes 184328 | tf_op jit(solution)/shard_map/ppermute | solution.py:27
  71.7 6.0 %collective-permute-start.14 = (bf16[40,768]{1,0:T(8,128)(2,1)S(1)}, bf16[40,768]{1,0:T(8,128)(2,1)S(1)}, u32[]{:S(2)}, u32[]{:S(2)}) collective-permute-start(bf16[40,768]{1,0:T(8,128)(2,1)S(1)} %get-tuple-element.87), channel_id=1, source_target_pairs={{0,8},{4,12},{8,0},{12,4},{16,24},{20,28},{24,16},{28,20},{1,9},{5... | collective-permute-start | bytes 184328 | tf_op jit(solution)/shard_map/ppermute | solution.py:27
  73.1 7.8 %collective-permute-start.15 = (bf16[40,768]{1,0:T(8,128)(2,1)S(1)}, bf16[40,768]{1,0:T(8,128)(2,1)S(1)}, u32[]{:S(2)}, u32[]{:S(2)}) collective-permute-start(bf16[40,768]{1,0:T(8,128)(2,1)S(1)} %get-tuple-element.88), channel_id=1, source_target_pairs={{0,12},{4,8},{8,4},{12,0},{16,28},{20,24},{24,20},{28,16},{1,13},{... | collective-permute-start | bytes 184328 | tf_op jit(solution)/shard_map/ppermute | solution.py:27
  73.2 8.5 %collective-permute-start.16 = (bf16[40,768]{1,0:T(8,128)(2,1)S(1)}, bf16[40,768]{1,0:T(8,128)(2,1)S(1)}, u32[]{:S(2)}, u32[]{:S(2)}) collective-permute-start(bf16[40,768]{1,0:T(8,128)(2,1)S(1)} %get-tuple-element.89), channel_id=1, source_target_pairs={{0,16},{4,20},{8,24},{12,28},{16,0},{20,4},{24,8},{28,12},{1,17},{... | collective-permute-start | bytes 184328 | tf_op jit(solution)/shard_map/ppermute | solution.py:27
  76.1 9.6 %collective-permute-start.17 = (bf16[40,768]{1,0:T(8,128)(2,1)S(1)}, bf16[40,768]{1,0:T(8,128)(2,1)S(1)}, u32[]{:S(2)}, u32[]{:S(2)}) collective-permute-start(bf16[40,768]{1,0:T(8,128)(2,1)S(1)} %get-tuple-element.90), channel_id=1, source_target_pairs={{0,20},{4,16},{8,28},{12,24},{16,4},{20,0},{24,12},{28,8},{1,21},{... | collective-permute-start | bytes 184328 | tf_op jit(solution)/shard_map/ppermute | solution.py:27
  77.7 7.9 %collective-permute-start.18 = (bf16[40,768]{1,0:T(8,128)(2,1)S(1)}, bf16[40,768]{1,0:T(8,128)(2,1)S(1)}, u32[]{:S(2)}, u32[]{:S(2)}) collective-permute-start(bf16[40,768]{1,0:T(8,128)(2,1)S(1)} %get-tuple-element.91), channel_id=1, source_target_pairs={{0,24},{4,28},{8,16},{12,20},{16,8},{20,12},{24,0},{28,4},{1,25},{... | collective-permute-start | bytes 184328 | tf_op jit(solution)/shard_map/ppermute | solution.py:27
  81.0 7.1 %collective-permute-start.19 = (bf16[40,768]{1,0:T(8,128)(2,1)S(1)}, bf16[40,768]{1,0:T(8,128)(2,1)S(1)}, u32[]{:S(2)}, u32[]{:S(2)}) collective-permute-start(bf16[40,768]{1,0:T(8,128)(2,1)S(1)} %get-tuple-element.92), channel_id=1, source_target_pairs={{0,28},{4,24},{8,20},{12,16},{16,12},{20,8},{24,4},{28,0},{1,29},{... | collective-permute-start | bytes 184328 | tf_op jit(solution)/shard_map/ppermute | solution.py:27
  88.0 10.4 %copy-start.20 = (bf16[320,768]{1,0:T(8,128)(2,1)}, bf16[320,768]{1,0:T(8,128)(2,1)S(1)}, u32[]{:S(2)}) copy-start(bf16[320,768]{1,0:T(8,128)(2,1)S(1)} %constant_dynamic-update-slice_fusion.refs_1_.refs_0_) | copy-start | bytes 1474564
  88.1 4.4 %collective-permute-start.20 = (bf16[320,768]{1,0:T(8,128)(2,1)S(1)}, bf16[320,768]{1,0:T(8,128)(2,1)}, u32[]{:S(2)}, u32[]{:S(2)}) collective-permute-start(bf16[320,768]{1,0:T(8,128)(2,1)S(1)} %constant_dynamic-update-slice_fusion.refs_1_.refs_0_), channel_id=1, source_target_pairs={{0,2},{2,0},{1,3},{3,1},{4,6},{6,4},{5,7},{7,5},{8,10},{10,8},{9,1... | collective-permute-start | bytes 1474568 | tf_op jit(solution)/shard_map/ppermute | solution.py:27
  92.5 9.7 %copy-start.45 = (s32[256,1]{0,1:T(1,128)S(1)}, s32[256,1]{0,1:T(1,128)}, u32[]{:S(2)}) copy-start(s32[256,1]{0,1:T(1,128)} %param.26) | copy-start | bytes 3076
  92.5 9.7 %copy-start.47 = (s32[256]{0:T(256)S(1)}, s32[256]{0:T(256)}, u32[]{:S(2)}) copy-start(s32[256]{0:T(256)} %copy-done.46) | copy-start | bytes 3076
  98.4 2.0 %collective-permute-start.22 = (bf16[320,768]{1,0:T(8,128)(2,1)S(1)}, bf16[320,768]{1,0:T(8,128)(2,1)S(1)}, u32[]{:S(2)}, u32[]{:S(2)}) collective-permute-start(bf16[320,768]{1,0:T(8,128)(2,1)S(1)} %get-tuple-element.99), channel_id=1, source_target_pairs={{0,2},{2,0},{1,3},{3,1},{4,6},{6,4},{5,7},{7,5},{8,10},{10,8},{9,1... | collective-permute-start | bytes 1474568 | tf_op jit(solution)/shard_map/ppermute | solution.py:27
  100.6 26.1 %copy-start.44 = (s32[1024]{0:T(1024)S(1)}, s32[1024]{0:T(1024)}, u32[]{:S(2)}) copy-start(s32[1024]{0:T(1024)} %copy-done.43) | copy-start | bytes 12292
  100.6 26.9 %copy-start.21 = (bf16[320,768]{1,0:T(8,128)(2,1)S(1)}, bf16[320,768]{1,0:T(8,128)(2,1)}, u32[]{:S(2)}) copy-start(bf16[320,768]{1,0:T(8,128)(2,1)} %copy-done.20) | copy-start | bytes 1474564
  100.6 26.9 %copy-start.24 = (bf16[768,768]{1,0:T(8,128)(2,1)S(1)}, bf16[768,768]{1,0:T(8,128)(2,1)}, u32[]{:S(2)}) copy-start(bf16[768,768]{1,0:T(8,128)(2,1)} %refs_6_.1) | copy-start | bytes 3538948
  100.6 6.6 %collective-permute-start.24 = (bf16[40,768]{1,0:T(8,128)(2,1)S(1)}, bf16[40,768]{1,0:T(8,128)(2,1)S(1)}, u32[]{:S(2)}, u32[]{:S(2)}) collective-permute-start(bf16[40,768]{1,0:T(8,128)(2,1)S(1)} %get-tuple-element.104), channel_id=1, source_target_pairs={{0,4},{4,0},{8,12},{12,8},{16,20},{20,16},{24,28},{28,24},{1,5},{5... | collective-permute-start | bytes 184328 | tf_op jit(solution)/shard_map/ppermute | solution.py:27
  101.2 7.3 %collective-permute-start.25 = (bf16[40,768]{1,0:T(8,128)(2,1)S(1)}, bf16[40,768]{1,0:T(8,128)(2,1)S(1)}, u32[]{:S(2)}, u32[]{:S(2)}) collective-permute-start(bf16[40,768]{1,0:T(8,128)(2,1)S(1)} %get-tuple-element.105), channel_id=1, source_target_pairs={{0,8},{4,12},{8,0},{12,4},{16,24},{20,28},{24,16},{28,20},{1,9},{5... | collective-permute-start | bytes 184328 | tf_op jit(solution)/shard_map/ppermute | solution.py:27
  102.2 9.8 %collective-permute-start.26 = (bf16[40,768]{1,0:T(8,128)(2,1)S(1)}, bf16[40,768]{1,0:T(8,128)(2,1)S(1)}, u32[]{:S(2)}, u32[]{:S(2)}) collective-permute-start(bf16[40,768]{1,0:T(8,128)(2,1)S(1)} %get-tuple-element.106), channel_id=1, source_target_pairs={{0,12},{4,8},{8,4},{12,0},{16,28},{20,24},{24,20},{28,16},{1,13},{... | collective-permute-start | bytes 184328 | tf_op jit(solution)/shard_map/ppermute | solution.py:27
  104.2 8.4 %collective-permute-start.27 = (bf16[40,768]{1,0:T(8,128)(2,1)S(1)}, bf16[40,768]{1,0:T(8,128)(2,1)S(1)}, u32[]{:S(2)}, u32[]{:S(2)}) collective-permute-start(bf16[40,768]{1,0:T(8,128)(2,1)S(1)} %get-tuple-element.107), channel_id=1, source_target_pairs={{0,16},{4,20},{8,24},{12,28},{16,0},{20,4},{24,8},{28,12},{1,17},{... | collective-permute-start | bytes 184328 | tf_op jit(solution)/shard_map/ppermute | solution.py:27
  105.9 9.8 %collective-permute-start.28 = (bf16[40,768]{1,0:T(8,128)(2,1)S(1)}, bf16[40,768]{1,0:T(8,128)(2,1)S(1)}, u32[]{:S(2)}, u32[]{:S(2)}) collective-permute-start(bf16[40,768]{1,0:T(8,128)(2,1)S(1)} %get-tuple-element.108), channel_id=1, source_target_pairs={{0,20},{4,16},{8,28},{12,24},{16,4},{20,0},{24,12},{28,8},{1,21},{... | collective-permute-start | bytes 184328 | tf_op jit(solution)/shard_map/ppermute | solution.py:27
  107.2 8.5 %collective-permute-start.29 = (bf16[40,768]{1,0:T(8,128)(2,1)S(1)}, bf16[40,768]{1,0:T(8,128)(2,1)S(1)}, u32[]{:S(2)}, u32[]{:S(2)}) collective-permute-start(bf16[40,768]{1,0:T(8,128)(2,1)S(1)} %get-tuple-element.109), channel_id=1, source_target_pairs={{0,24},{4,28},{8,16},{12,20},{16,8},{20,12},{24,0},{28,4},{1,25},{... | collective-permute-start | bytes 184328 | tf_op jit(solution)/shard_map/ppermute | solution.py:27
  108.6 7.1 %collective-permute-start.30 = (bf16[40,768]{1,0:T(8,128)(2,1)S(1)}, bf16[40,768]{1,0:T(8,128)(2,1)S(1)}, u32[]{:S(2)}, u32[]{:S(2)}) collective-permute-start(bf16[40,768]{1,0:T(8,128)(2,1)S(1)} %get-tuple-element.100.refs_7_), channel_id=1, source_target_pairs={{0,28},{4,24},{8,20},{12,16},{16,12},{20,8},{24,4},{28,0},{1,29},{... | collective-permute-start | bytes 184328 | tf_op jit(solution)/shard_map/ppermute | solution.py:27
  116.0 10.1 %collective-permute-start.32 = (bf16[256,768]{1,0:T(8,128)(2,1)S(1)}, bf16[256,768]{1,0:T(8,128)(2,1)S(1)}, u32[]{:S(2)}, u32[]{:S(2)}) collective-permute-start(bf16[256,768]{1,0:T(8,128)(2,1)S(1)} %gather_grad.1.refs_3_.refs_1_), channel_id=1, source_target_pairs={{0,1},{1,0},{2,3},{3,2},{4,5},{5,4},{6,7},{7,6},{8,9},{9,8},{10,11... | collective-permute-start | bytes 1179656 | tf_op jit(solution)/shard_map/ppermute | solution.py:27
  126.6 7.1 %collective-permute-start.33 = (bf16[256,768]{1,0:T(8,128)(2,1)S(1)}, bf16[256,768]{1,0:T(8,128)(2,1)S(1)}, u32[]{:S(2)}, u32[]{:S(2)}) collective-permute-start(bf16[256,768]{1,0:T(8,128)(2,1)S(1)} %get-tuple-element.110.refs_1_), channel_id=1, source_target_pairs={{0,2},{2,0},{1,3},{3,1},{4,6},{6,4},{5,7},{7,5},{8,10},{10,8},{9,1... | collective-permute-start | bytes 1179656 | tf_op jit(solution)/shard_map/ppermute | solution.py:27
  133.7 30.5 %collective-permute-start.23 = (bf16[320,768]{1,0:T(8,128)(2,1)}, bf16[320,768]{1,0:T(8,128)(2,1)}, u32[]{:S(2)}, u32[]{:S(2)}) collective-permute-start(bf16[320,768]{1,0:T(8,128)(2,1)} %get-tuple-element.102), channel_id=1, source_target_pairs={{0,2},{2,0},{1,3},{3,1},{4,6},{6,4},{5,7},{7,5},{8,10},{10,8},{9,1... | collective-permute-start | bytes 1474568 | tf_op jit(solution)/shard_map/ppermute | solution.py:27
  137.4 14.6 %collective-permute-start.36 = (bf16[384,384]{1,0:T(8,128)(2,1)S(1)}, bf16[384,384]{1,0:T(8,128)(2,1)S(1)}, u32[]{:S(2)}, u32[]{:S(2)}) collective-permute-start(bf16[384,384]{1,0:T(8,128)(2,1)S(1)} %get-tuple-element.127), channel_id=1, source_target_pairs={{0,4},{4,0},{8,12},{12,8},{16,20},{20,16},{24,28},{28,24},{1,5},{5... | collective-permute-start | bytes 884744 | tf_op jit(solution)/shard_map/ppermute | solution.py:27
  144.4 15.2 %collective-permute-start.40 = (bf16[384,384]{1,0:T(8,128)(2,1)}, bf16[384,384]{1,0:T(8,128)(2,1)}, u32[]{:S(2)}, u32[]{:S(2)}) collective-permute-start(bf16[384,384]{1,0:T(8,128)(2,1)} %get-tuple-element.133), channel_id=1, source_target_pairs={{0,4},{4,0},{8,12},{12,8},{16,20},{20,16},{24,28},{28,24},{1,5},{5... | collective-permute-start | bytes 884744 | tf_op jit(solution)/shard_map/ppermute | solution.py:27
  145.9 36.3 %collective-permute-start.34 = (bf16[256,768]{1,0:T(8,128)(2,1)}, bf16[256,768]{1,0:T(8,128)(2,1)}, u32[]{:S(2)}, u32[]{:S(2)}) collective-permute-start(bf16[256,768]{1,0:T(8,128)(2,1)} %get-tuple-element.124), channel_id=1, source_target_pairs={{0,2},{2,0},{1,3},{3,1},{4,6},{6,4},{5,7},{7,5},{8,10},{10,8},{9,1... | collective-permute-start | bytes 1179656 | tf_op jit(solution)/shard_map/ppermute | solution.py:27
  145.9 4.2 %collective-permute-start.41 = (f32[16,768]{1,0:T(8,128)S(1)}, f32[16,768]{1,0:T(8,128)S(1)}, u32[]{:S(2)}, u32[]{:S(2)}) collective-permute-start(f32[16,768]{1,0:T(8,128)S(1)} %get-tuple-element.134), channel_id=1, source_target_pairs={{0,1},{1,0},{2,3},{3,2},{4,5},{5,4},{6,7},{7,6},{8,9},{9,8},{10,11... | collective-permute-start | bytes 147464 | tf_op jit(solution)/shard_map/ppermute | solution.py:27
  150.1 1.3 collective-permute-start.42
  151.4 6.4 %collective-permute-start.43 = (f32[16,768]{1,0:T(8,128)S(1)}, f32[16,768]{1,0:T(8,128)S(1)}, u32[]{:S(2)}, u32[]{:S(2)}) collective-permute-start(f32[16,768]{1,0:T(8,128)S(1)} %add.108.refs_2_), channel_id=1, source_target_pairs={{0,4},{4,0},{8,12},{12,8},{16,20},{20,16},{24,28},{28,24},{1,5},{5... | collective-permute-start | bytes 147464 | tf_op jit(solution)/shard_map/ppermute | solution.py:27
  154.0 11.8 %collective-permute-start.37 = (bf16[96,384]{1,0:T(8,128)(2,1)}, bf16[96,384]{1,0:T(8,128)(2,1)S(1)}, u32[]{:S(2)}, u32[]{:S(2)}) collective-permute-start(bf16[96,384]{1,0:T(8,128)(2,1)} %get-tuple-element.129), channel_id=1, source_target_pairs={{0,8},{4,12},{8,0},{12,4},{16,24},{20,28},{24,16},{28,20},{1,9},{5... | collective-permute-start | bytes 221192 | tf_op jit(solution)/shard_map/ppermute | solution.py:27
  157.8 10.3 %collective-permute-start.38 = (bf16[96,384]{1,0:T(8,128)(2,1)}, bf16[96,384]{1,0:T(8,128)(2,1)S(1)}, u32[]{:S(2)}, u32[]{:S(2)}) collective-permute-start(bf16[96,384]{1,0:T(8,128)(2,1)} %get-tuple-element.130), channel_id=1, source_target_pairs={{0,16},{4,20},{8,24},{12,28},{16,0},{20,4},{24,8},{28,12},{1,17},{... | collective-permute-start | bytes 221192 | tf_op jit(solution)/shard_map/ppermute | solution.py:27
  163.1 14.3 %collective-permute-start.44 = (bf16[128,384]{1,0:T(8,128)(2,1)}, bf16[128,384]{1,0:T(8,128)(2,1)}, u32[]{:S(2)}, u32[]{:S(2)}) collective-permute-start(bf16[128,384]{1,0:T(8,128)(2,1)} %get-tuple-element.136), channel_id=1, source_target_pairs={{0,8},{4,12},{8,0},{12,4},{16,24},{20,28},{24,16},{28,20},{1,9},{5... | collective-permute-start | bytes 294920 | tf_op jit(solution)/shard_map/ppermute | solution.py:27
  164.2 13.2 %collective-permute-start.45 = (bf16[128,384]{1,0:T(8,128)(2,1)}, bf16[128,384]{1,0:T(8,128)(2,1)}, u32[]{:S(2)}, u32[]{:S(2)}) collective-permute-start(bf16[128,384]{1,0:T(8,128)(2,1)} %get-tuple-element.137), channel_id=1, source_target_pairs={{0,16},{4,20},{8,24},{12,28},{16,0},{20,4},{24,8},{28,12},{1,17},{... | collective-permute-start | bytes 294920 | tf_op jit(solution)/shard_map/ppermute | solution.py:27
  166.4 11.1 %collective-permute-start.46 = (bf16[128,384]{1,0:T(8,128)(2,1)}, bf16[128,384]{1,0:T(8,128)(2,1)}, u32[]{:S(2)}, u32[]{:S(2)}) collective-permute-start(bf16[128,384]{1,0:T(8,128)(2,1)} %get-tuple-element.138), channel_id=1, source_target_pairs={{0,24},{4,28},{8,16},{12,20},{16,8},{20,12},{24,0},{28,4},{1,25},{... | collective-permute-start | bytes 294920 | tf_op jit(solution)/shard_map/ppermute | solution.py:27
  168.7 8.7 %collective-permute-start.39 = (bf16[96,384]{1,0:T(8,128)(2,1)}, bf16[96,384]{1,0:T(8,128)(2,1)}, u32[]{:S(2)}, u32[]{:S(2)}) collective-permute-start(bf16[96,384]{1,0:T(8,128)(2,1)} %copy-done.34), channel_id=1, source_target_pairs={{0,24},{4,28},{8,16},{12,20},{16,8},{20,12},{24,0},{28,4},{1,25},{... | collective-permute-start | bytes 221192 | tf_op jit(solution)/shard_map/ppermute | solution.py:27
  173.8 15.2 %all-to-all-start.1 = ((bf16[8,40,768]{2,1,0:T(8,128)(2,1)}), bf16[8,40,768]{2,1,0:T(8,128)(2,1)S(1)}, u32[]{:S(2)}, u32[]{:S(2)}) async-start(bf16[8,40,768]{2,1,0:T(8,128)(2,1)} %join_out.1), calls=%async_computation.1 | async-start | bytes 983040 | tf_op jit(solution)/shard_map/all_to_all | solution.py:463
  182.2 10.8 %collective-permute-start.47 = (f32[48,768]{1,0:T(8,128)S(1)}, f32[48,768]{1,0:T(8,128)S(1)}, u32[]{:S(2)}, u32[]{:S(2)}) collective-permute-start(f32[48,768]{1,0:T(8,128)S(1)} %get-tuple-element.141), channel_id=1, source_target_pairs={{0,2},{2,0},{1,3},{3,1},{4,6},{6,4},{5,7},{7,5},{8,10},{10,8},{9,1... | collective-permute-start | bytes 442376 | tf_op jit(solution)/shard_map/ppermute | solution.py:27
  185.3 9.0 %collective-permute-start.35 = (bf16[128,768]{1,0:T(8,128)(2,1)S(1)}, bf16[128,768]{1,0:T(8,128)(2,1)S(1)}, u32[]{:S(2)}, u32[]{:S(2)}) collective-permute-start(bf16[128,768]{1,0:T(8,128)(2,1)S(1)} %dynamic-slice_convert_fusion), channel_id=1, source_target_pairs={{0,1},{1,0},{2,3},{3,2},{4,5},{5,4},{6,7},{7,6},{8,9},{9,8},{10,11... | collective-permute-start | bytes 589832 | tf_op jit(solution)/shard_map/ppermute | solution.py:27
  190.1 6.7 %collective-permute-start.31 = (bf16[128,768]{1,0:T(8,128)(2,1)S(1)}, bf16[128,768]{1,0:T(8,128)(2,1)S(1)}, u32[]{:S(2)}, u32[]{:S(2)}) collective-permute-start(bf16[128,768]{1,0:T(8,128)(2,1)S(1)} %constant_dynamic-slice_fusion.2), channel_id=1, source_target_pairs={{0,1},{1,0},{2,3},{3,2},{4,5},{5,4},{6,7},{7,6},{8,9},{9,8},{10,11... | collective-permute-start | bytes 589832 | tf_op jit(solution)/shard_map/ppermute | solution.py:27
  (37 other events, 78.5 us)

commit v3 on v2

v3 whole, which is shorter than its diff:
```python
import functools

import jax
import jax.numpy as jnp
from jax import lax
from jax.experimental import pallas as pl
from jax.experimental.pallas import tpu as pltpu
from jax.sharding import Mesh, PartitionSpec as P

HD = 64
GROUP = 2
FLOPS1 = 0
FLOPS2 = 0
DIRECT = 8
TILE = 128

norm_eps = 1e-06
masked_value = -1e30
exact = lax.Precision.HIGHEST
bf16 = jnp.bfloat16
f32 = jnp.float32

VMEM = pl.BlockSpec(memory_space=pltpu.VMEM)
SMEM = pl.BlockSpec(memory_space=pltpu.SMEM)
ANY = pl.BlockSpec(memory_space=pl.ANY)


def across(shard, axis, bits):
    return lax.ppermute(shard, axis, [(i, i ^ bits) for i in range(lax.axis_size(axis))])


class Near:
    def __init__(self, array):
        self.array = array


class Raw(Near):
    pass


class Far(Raw):
    pass


def call(body, name, outs, args, smem=0, scratch=(), flops=0):
    arrays = [a.array if isinstance(a, Near) else a for a in args]
    results = [o.array if isinstance(o, Near) else o for o in outs]
    kept = sum(padded_bytes(a) for a in [*arrays, *results, *scratch] if is_plain(a))
    space = {Near: pltpu.VMEM, Far: pltpu.HBM}
    given = [
        pltpu.with_memory_space_constraint(x, space[type(a)]) if type(a) in space else x
        for a, x in zip(args, arrays)
    ]
    return pl.pallas_call(
        body,
        name=name,
        out_shape=[
            space[type(o)](x.shape, x.dtype) if type(o) in space else x
            for o, x in zip(outs, results)
        ],
        in_specs=[SMEM] * smem + [ANY if isinstance(a, Raw) else VMEM for a in args[smem:]],
        out_specs=[ANY if isinstance(o, Raw) else VMEM for o in outs],
        scratch_shapes=scratch,
        compiler_params=pltpu.CompilerParams(vmem_limit_bytes=kept + 10 * 1024 * 1024),
        cost_estimate=pl.CostEstimate(flops=flops, bytes_accessed=0, transcendentals=0),
    )(*given)


def is_plain(array):
    return array.dtype in (bf16, f32, jnp.int32)


def padded_bytes(array):
    *lead, rows, cols = (1, 1, *array.shape)
    size = jnp.dtype(array.dtype).itemsize
    for extent in lead:
        size *= extent
    return size * (-(-rows // 16) * 16) * (-(-cols // 128) * 128)


def out(shape, dtype):
    return jax.ShapeDtypeStruct(shape, dtype)


def mm(a, b):
    return jnp.dot(a, b, preferred_element_type=f32)


def mm_bt(a, b):
    return lax.dot_general(a, b, (((1,), (1,)), ((), ())), preferred_element_type=f32)


def mm_at(a, b):
    return lax.dot_general(a, b, (((0,), (0,)), ((), ())), preferred_element_type=f32)


def shares_kernel(ids, *refs):
    weights, (keep_ref, send_ref, near_ref, sems) = refs[:4], refs[4:]
    copies = [
        pltpu.make_async_copy(w, near_ref.at[i], sems.at[i]) for i, w in enumerate(weights)
    ]
    for copy in copies:
        copy.start()
    for copy in copies:
        copy.wait()
    first = ids[0] == 0
    cols = keep_ref.shape[1] // 4
    for i in range(4):
        low, high = near_ref[i, :, :cols], near_ref[i, :, cols:]
        keep_ref[:, i * cols : (i + 1) * cols] = jnp.where(first, low, high)
        send_ref[:, i * cols : (i + 1) * cols] = jnp.where(first, high, low)


def rows_kernel(ids, own_ref, got_ref, held_ref, out_ref):
    rows = own_ref.shape[0]
    out_ref[pl.ds(pl.multiple_of(ids[2] * rows, rows), rows), :] = own_ref[...]
    out_ref[pl.ds(pl.multiple_of((1 - ids[2]) * rows, rows), rows), :] = got_ref[...]


def move_kernel(count, *refs):
    sources, targets, sems = refs[:count], refs[-count - 1 : -1], refs[-1]
    copies = [
        pltpu.make_async_copy(a, b, sems.at[i]) for i, (a, b) in enumerate(zip(sources, targets))
    ]
    for copy in copies:
        copy.start()
    for copy in copies:
        copy.wait()


def unit_rows(x):
    wide = x.astype(f32)
    return wide * lax.rsqrt(jnp.mean(wide * wide, axis=1, keepdims=True) + norm_eps)


def slots_kernel(table_ref, rows_ref, held_ref, out_ref):
    out_ref[...] = mm(table_ref[...], rows_ref[...]).astype(bf16)


def cots_kernel(parts, ids, own_ref, other_ref, wdown_ref, held_ref, cots_ref, back_ref, *scratch):
    slots = cots_ref.shape[0] // 2
    me = ids[1]
    for at, source in ((0, own_ref), (slots, other_ref)):
        if parts == 1:
            cots_ref[at : at + slots, :] = source[...]
        else:
            rows = slots // parts
            for i in range(parts):
                scratch[0][i * rows : (i + 1) * rows, :] = source[me ^ i].astype(f32)
            cots_ref[at : at + slots, :] = scratch[0][...].astype(bf16)
        back_ref[at : at + slots, :] = mm(cots_ref[at : at + slots, :], wdown_ref[...])


def attend_kernel(heads, parts, ids, own_ref, other_ref, gain_ref, vec_ref, row_docs, col_docs, *refs):
    pieces = refs[:parts]
    w_ref, wo_ref, x_ref, qkv_ref, mixed_ref, keep_ref, send_ref, *probs_refs = refs[parts:-1]
    seq_ref = refs[-1]
    core = ids[0]
    me = ids[1]
    seq = x_ref.shape[0]
    width = heads * HD
    half = seq // GROUP
    span = seq + TILE
    rows = pieces[0].shape[0]
    for i, piece in enumerate(pieces):
        start = 0 if parts == 1 else pl.multiple_of((me ^ i) * rows, rows)
        w_ref[pl.ds(start, rows), :] = piece[...]
    for place, source in ((core, own_ref), (1 - core, other_ref)):
        at = pl.ds(pl.multiple_of(place * half, half), half)
        x = source[...]
        x_ref[at, :] = x
        seq_ref[at, :] = (unit_rows(x) * gain_ref[...]).astype(bf16)
    wo_ref[...] = w_ref[:, 3 * width :]
    for i in range(0, seq, 256):
        qkv_ref[i : i + 256, :] = mm(seq_ref[i : i + 256, :], w_ref[:, : 3 * width]).astype(bf16)
    for h in range(heads):
        at = h * HD
        key = qkv_ref[:, width + at : width + at + HD]
        value = qkv_ref[:, 2 * width + at : 2 * width + at + HD]
        for i in range(0, seq, TILE):
            base = seq - TILE - i
            seg = jnp.broadcast_to(vec_ref[h : h + 1, base : base + span], (TILE, span))
            bias = pltpu.roll(seg, span - TILE + 1, 1, stride=1, stride_axis=0)[:, :seq]
            scores = mm_bt(qkv_ref[i : i + TILE, at : at + HD], key) * HD**-0.5 + bias
            scores = jnp.where(row_docs[i : i + TILE, :] == col_docs[...], scores, masked_value)
            peak = jnp.max(scores, axis=1, keepdims=True)
            exp_scores = jnp.exp(scores - peak)
            probs = exp_scores / jnp.sum(exp_scores, axis=1, keepdims=True)
            probs_refs[h][i : i + TILE, :] = probs.astype(bf16)
            mixed_ref[i : i + TILE, at : at + HD] = mm(probs.astype(bf16), value).astype(bf16)
    keep_ref[...] = mixed_ref[pl.ds(pl.multiple_of(core * half, half), half), :]
    send_ref[...] = mixed_ref[pl.ds(pl.multiple_of((1 - core) * half, half), half), :]


def attended_kernel(keep_ref, got_ref, wo_ref, wo_other_ref, held_ref, out_ref):
    total = mm_bt(keep_ref[...], wo_ref[...]) + mm_bt(got_ref[...], wo_other_ref[...])
    out_ref[...] = total.astype(bf16)


def dispatch_kernel(x_ref, own_ref, got_ref, gain_ref, table_ref, hidden_ref, *blocks):
    hidden = x_ref[...].astype(f32) + (own_ref[...].astype(f32) + got_ref[...].astype(f32))
    hidden_ref[...] = hidden
    scale = lax.rsqrt(jnp.mean(hidden * hidden, axis=1, keepdims=True) + norm_eps)
    normed = (hidden * scale * gain_ref[...]).astype(bf16)
    slots = mm(table_ref[...], normed)
    rows = blocks[0].shape[0]
    for i, block in enumerate(blocks):
        block[...] = slots[i * rows : (i + 1) * rows, :].astype(bf16)


def expert_kernel(ids, own_ref, other_ref, h_ref, wup_ref, wr_ref, *refs):
    active_ref, gup_ref, chosen_ref, keep_ref, send_ref, router_ref, all_ref = refs
    rows = own_ref.shape[0]
    step = rows // 2
    router = jnp.zeros(router_ref.shape, f32)
    root = 0.7978845608028654
    for i in range(0, 2 * rows, step):
        src = own_ref if i < rows else other_ref
        at = i % rows
        slots = src[at : at + step, :]
        all_ref[i : i + step, :] = slots
        logits = mm_bt(slots, wr_ref[...])
        peak = jnp.max(logits, axis=1, keepdims=True)
        exp_logits = jnp.exp(logits - peak)
        gates = exp_logits / jnp.sum(exp_logits, axis=1, keepdims=True)
        mine = lax.broadcasted_iota(jnp.int32, gates.shape, 1) == ids[1]
        chosen = jnp.sum(jnp.where(mine, gates, 0.0), axis=1, keepdims=True)
        chosen_ref[i : i + step, :] = chosen
        up = mm(slots, wup_ref[...])
        square = up * up
        bent = jnp.tanh(root * (up + 0.044715 * up * square))
        low = (0.5 * up * (1.0 + bent)).astype(bf16)
        active_ref[i : i + step, :] = low
        slope = 0.5 * (1.0 + bent) + 0.5 * up * (1.0 - bent * bent) * root * (
            1.0 + 3.0 * 0.044715 * square
        )
        back = h_ref[i : i + step, :]
        gup = (chosen * back * slope).astype(bf16)
        gup_ref[i : i + step, :] = gup
        grad_chosen = jnp.sum(low.astype(f32) * back, axis=1, keepdims=True)
        grad_logits = gates * (jnp.where(mine, 1.0, 0.0) - chosen) * grad_chosen
        grad_logits = grad_logits.astype(bf16)
        router = router + mm_at(grad_logits, slots)
        grad = mm_bt(gup, wup_ref[...]) + mm(grad_logits, wr_ref[...])
        if i < rows:
            keep_ref[at : at + step, :] = grad
        else:
            send_ref[at : at + step, :] = grad.astype(bf16)
    router_ref[...] = router


def expert_out_kernel(active_ref, chosen_ref, wdown_ref, held_ref, keep_ref, send_ref):
    rows = keep_ref.shape[0]
    result = mm_bt(active_ref[...], wdown_ref[...]) * chosen_ref[...]
    keep_ref[...] = result[:rows, :]
    send_ref[...] = result[rows:, :].astype(bf16)


def expert_grads_kernel(slots_ref, cots_ref, active_ref, gup_ref, chosen_ref, held_ref, gwup_ref, gwdown_ref):
    gwup_ref[...] = mm_at(slots_ref[...], gup_ref[...])
    grads = (chosen_ref[...] * cots_ref[...].astype(f32)).astype(bf16)
    gwdown_ref[...] = mm_at(grads, active_ref[...])


def join_kernel(keep_ref, got_ref, *blocks):
    total = keep_ref[...] + got_ref[...].astype(f32)
    rows = blocks[0].shape[0]
    for i, block in enumerate(blocks):
        block[...] = total[i * rows : (i + 1) * rows, :].astype(bf16)


def join_natural_kernel(parts, ids, keep_ref, got_ref, out_ref):
    total = keep_ref[...] + got_ref[...].astype(f32)
    if parts == 1:
        out_ref[...] = total.astype(bf16)
        return
    rows = out_ref.shape[1]
    for i in range(parts):
        out_ref[ids[1] ^ i] = total[i * rows : (i + 1) * rows, :].astype(bf16)


def gather_kernel(back_table_ref, *refs):
    blocks = refs[:-1]
    slots = jnp.concatenate([b[...].astype(f32) for b in blocks], axis=0).astype(bf16)
    refs[-1][...] = mm(back_table_ref[...], slots).astype(bf16)


def hidden_back_kernel(ids, hidden_ref, own_ref, got_ref, cot_ref, gain_ref, held_ref, grad_ref, low_ref, dgain_ref, all_ref):
    hidden = hidden_ref[...]
    grad_normed = own_ref[...].astype(f32) + got_ref[...].astype(f32)
    scale = lax.rsqrt(jnp.mean(hidden * hidden, axis=1, keepdims=True) + norm_eps)
    dgain_ref[...] = jnp.sum(grad_normed * hidden * scale, axis=0, keepdims=True)
    pulled = gain_ref[...] * grad_normed
    inner = jnp.mean(pulled * hidden, axis=1, keepdims=True)
    grad = cot_ref[...].astype(f32) + scale * pulled - hidden * (scale * scale * scale) * inner
    low_ref[...] = grad.astype(bf16)
    all_ref[...] = grad
    rows = grad_ref.shape[0]
    grad_ref[...] = all_ref[pl.ds(pl.multiple_of(ids[2] * rows, rows), rows), :]


def returned_kernel(ids, table_ref, slots_ref, held_ref, keep_ref, send_ref):
    rows = keep_ref.shape[0]
    mine = table_ref[pl.ds(pl.multiple_of(ids[2] * rows, rows), rows), :]
    keep_ref[...] = mm(mine, slots_ref[...]).astype(bf16)
    theirs = table_ref[pl.ds(pl.multiple_of((1 - ids[2]) * rows, rows), rows), :]
    send_ref[...] = mm(theirs, slots_ref[...]).astype(bf16)


def activations_kernel(ids, hidden_ref, own_ref, got_ref, out_ref):
    rows = out_ref.shape[0]
    hidden = hidden_ref[pl.ds(pl.multiple_of(ids[2] * rows, rows), rows), :]
    out_ref[...] = (hidden + (own_ref[...].astype(f32) + got_ref[...].astype(f32))).astype(bf16)


def normed_sum_kernel(ids, keep_ref, got_ref, held_ref, own_ref, send_ref, all_ref):
    all_ref[...] = keep_ref[...] + got_ref[...].astype(f32)
    rows = own_ref.shape[0]
    own_ref[...] = all_ref[pl.ds(pl.multiple_of(ids[2] * rows, rows), rows), :]
    theirs = pl.ds(pl.multiple_of((1 - ids[2]) * rows, rows), rows)
    send_ref[...] = all_ref[theirs, :].astype(bf16)


def heads_back(heads, first, qkv_ref, gm_ref, probs, dqkv_ref, diag_ref, ds_ref):
    seq = qkv_ref.shape[0]
    width = heads * HD
    here = len(probs) * HD
    span = seq + TILE
    flip = (
        lax.broadcasted_iota(jnp.int32, (TILE, TILE), 0)
        + lax.broadcasted_iota(jnp.int32, (TILE, TILE), 1)
        == TILE - 1
    ).astype(bf16)
    for h, probs_ref in enumerate(probs):
        at = (first + h) * HD
        to = h * HD
        key = qkv_ref[:, width + at : width + at + HD]
        value = qkv_ref[:, 2 * width + at : 2 * width + at + HD]
        for i in range(0, seq, TILE):
            probs_rows = probs_ref[i : i + TILE, :].astype(f32)
            grad_probs = mm_bt(gm_ref[i : i + TILE, at : at + HD], value)
            inner = jnp.sum(probs_rows * grad_probs, axis=1, keepdims=True)
            grad_scores = (probs_rows * (grad_probs - inner)).astype(bf16)
            ds_ref[i : i + TILE, :] = grad_scores
            dqkv_ref[i : i + TILE, to : to + HD] = (mm(grad_scores, key) * HD**-0.5).astype(bf16)
            flipped = mm(flip, grad_scores)
            padded = jnp.concatenate([flipped, jnp.zeros((TILE, TILE), f32)], axis=1)
            skewed = pltpu.roll(padded, 0, 1, stride=1, stride_axis=0)
            base = seq - TILE - i
            row = first + h
            diag_ref[row : row + 1, base : base + span] += jnp.sum(skewed, axis=0, keepdims=True)
        dqkv_ref[:, here + to : here + to + HD] = (
            mm_at(ds_ref[...], qkv_ref[:, at : at + HD]) * HD**-0.5
        ).astype(bf16)
        dqkv_ref[:, 2 * here + to : 2 * here + to + HD] = mm_at(
            probs_ref[...], gm_ref[:, at : at + HD]
        ).astype(bf16)


def send_rows(parts, me, gw_ref, outs):
    if parts == 1:
        outs[0][...] = gw_ref[...].astype(bf16)
        return
    rows = gw_ref.shape[0] // parts
    for i in range(parts // 2):
        at = slice(i * rows, (i + 1) * rows)
        outs[0][at, :] = gw_ref[pl.ds(pl.multiple_of((me ^ 2 * i) * rows, rows), rows), :]
        there = pl.ds(pl.multiple_of((me ^ 2 * i ^ 1) * rows, rows), rows)
        outs[1][at, :] = gw_ref[there, :].astype(bf16)


def fetch(sources, targets, sems):
    copies = [
        pltpu.make_async_copy(a, b, sems.at[i]) for i, (a, b) in enumerate(zip(sources, targets))
    ]
    for copy in copies:
        copy.start()
    return copies


def first_back_kernel(heads, parts, ids, own_ref, other_ref, gain_ref, *refs):
    far = refs[:5]
    gm_ref, dqkv_ref, diag_ref, seq_ref, *outs = refs[5:-9]
    ga_ref, ds_ref, gw_ref = refs[-9:-6]
    wo_ref, qkv_ref, probs_ref, x_ref, mixed_ref = refs[-6:-1]
    copies = fetch(far, refs[-6:-1], refs[-1])
    core = ids[0]
    half = own_ref.shape[0]
    ga_ref[pl.ds(pl.multiple_of(core * half, half), half), :] = own_ref[...]
    ga_ref[pl.ds(pl.multiple_of((1 - core) * half, half), half), :] = other_ref[...]
    copies[0].wait()
    gm_ref[...] = mm(ga_ref[...], wo_ref[...]).astype(bf16)
    diag_ref[...] = jnp.zeros_like(diag_ref)
    copies[1].wait()
    copies[2].wait()
    heads_back(heads, 0, qkv_ref, gm_ref, [probs_ref], dqkv_ref, diag_ref, ds_ref)
    cut = dqkv_ref.shape[1]
    copies[3].wait()
    copies[4].wait()
    seq_ref[...] = (unit_rows(x_ref[...]) * gain_ref[...]).astype(bf16)
    gw_ref[:, :cut] = mm_at(seq_ref[...], dqkv_ref[...])
    gw_ref[:, cut:] = mm_at(ga_ref[...], mixed_ref[...])
    send_rows(parts, ids[1], gw_ref, outs)


def second_back_kernel(
    heads, parts, ids, gm_ref, first_ref, diag_in_ref, hot_ref, seq_ref, gain_ref, router_ref, *refs
):
    count = heads + 2
    far, near = refs[:count], refs[-count - 1 : -1]
    qkv_ref, *probs, x_ref, w_ref = near
    copies = fetch(far, near, refs[-1])
    refs = refs[count : -count - 1]
    keep_ref, send_ref, *outs = refs[:-6]
    diag_ref, dqkv_ref, all_ref, ds_ref, gw_ref, small_ref = refs[-6:]
    core, me, side = ids[0], ids[1], ids[2]
    half = keep_ref.shape[0]
    diag_ref[...] = diag_in_ref[...]
    for copy in copies[:heads]:
        copy.wait()
    heads_back(heads, 1, qkv_ref, gm_ref, probs, dqkv_ref, diag_ref, ds_ref)
    gw_ref[...] = mm_at(seq_ref[...], dqkv_ref[...])
    send_rows(parts, me, gw_ref, outs)
    rest = (heads - 1) * HD
    for i in range(3):
        at = i * heads * HD
        all_ref[:, at : at + HD] = first_ref[:, i * HD : (i + 1) * HD]
        all_ref[:, at + HD : at + heads * HD] = dqkv_ref[:, i * rest : (i + 1) * rest]
    for copy in copies[heads:]:
        copy.wait()
    gain = jnp.zeros((1, x_ref.shape[1]), f32)
    for place, mine in ((core, True), (1 - core, False)):
        rows = pl.ds(pl.multiple_of(place * half, half), half)
        grad = mm_bt(all_ref[rows, :], w_ref[:, : all_ref.shape[1]])
        gain = gain + jnp.sum(grad * unit_rows(x_ref[rows, :]), axis=0, keepdims=True)
        if mine:
            keep_ref[...] = grad
        else:
            send_ref[...] = grad.astype(bf16)
    small_ref[...] = jnp.zeros_like(small_ref)
    small_ref[0:1, :] = gain
    small_ref[1:2, :] = jnp.where(side == 0, gain_ref[...], 0.0)
    experts = router_ref.shape[0]
    small_ref[2 : 2 + experts, :] = router_ref[...]
    bias = jnp.dot(diag_ref[...], hot_ref[...], precision=exact, preferred_element_type=f32)
    lanes = bias.shape[1]
    for i in range(2 * GROUP):
        small_ref[2 + experts : 2 + experts + heads, i * lanes : (i + 1) * lanes] = jnp.where(
            side * GROUP + core == i, bias[:heads, :], 0.0
        )
    if parts == 1:
        outs[1][...] = small_ref[...]
        return
    high = small_ref.shape[0]
    end = outs[0].shape[0] - 2 * high
    cols = outs[0].shape[1]
    for i in range(2):
        low = small_ref[:, i * cols : (i + 1) * cols].astype(bf16)
        outs[0][end + i * high : end + (i + 1) * high, :] = low.astype(f32)
        outs[1][end + i * high : end + (i + 1) * high, :] = low


def fold_kernel(parts, keep_ref, got_ref, *refs):
    count = (len(refs) - parts // 2) // 2
    passed, (own_ref, *sends) = refs[:count], refs[2 * count :]
    for source, target in zip(passed, refs[count:]):
        target[...] = source[...]
    total = keep_ref[...] + got_ref[...].astype(f32)
    rows = own_ref.shape[0]
    own_ref[...] = total[:rows, :]
    for i, send in enumerate(sends):
        send[...] = total[(i + 1) * rows : (i + 2) * rows, :].astype(bf16)


def quarters(refs, at):
    a, b, c, d = (r[at, :].astype(f32) for r in refs)
    return (a + b) + (c + d)


def split_cores(core, refs, keep_ref, send_ref):
    rows = keep_ref.shape[0]
    keep_ref[...] = quarters(refs, pl.ds(pl.multiple_of(core * rows, rows), rows))
    send_ref[:rows, :] = quarters(refs, pl.ds(pl.multiple_of((1 - core) * rows, rows), rows))


def fold_second_kernel(small_rows, ids, keep_ref, got_ref, *refs):
    first = refs[:4]
    refs[5][...] = refs[4][...]
    keep_one_ref, send_one_ref, own_ref, *sends = refs[6:]
    total = keep_ref[...] + got_ref[...].astype(f32)
    rows = keep_one_ref.shape[0] * 2
    end = total.shape[0] - small_rows
    small = total[end:, :].astype(bf16)
    for i, block in enumerate((own_ref, *sends)):
        block[:rows, :] = total[i * rows : (i + 1) * rows, :].astype(block.dtype)
        block[rows:, :] = small.astype(block.dtype)
    split_cores(ids[0], first, keep_one_ref, send_one_ref)


def sum_nodes_kernel(ids, *refs):
    second = refs[:4]
    keep_ref, send_ref = refs[-2:]
    split_cores(ids[0], second, keep_ref, send_ref)
    rows = keep_ref.shape[0]
    send_ref[rows:, :] = quarters(second, slice(2 * rows, second[0].shape[0]))


def columns_kernel(heads, ids, keep_one, got_one, keep_two, got_two, *outs):
    core = ids[0]
    rows = keep_one.shape[0]
    cols = heads * HD
    rest = cols - HD
    for c in range(2):
        at = c * cols
        mine = core == c
        one = jnp.where(mine, keep_one[...], got_one[...])
        two = jnp.where(mine, keep_two[...], got_two[:rows, :])
        for i in range(3):
            outs[i][:, at : at + HD] = one[:, i * HD : (i + 1) * HD]
            outs[i][:, at + HD : at + cols] = two[:, i * rest : (i + 1) * rest]
        outs[3][:, at : at + cols] = one[:, 3 * HD : 3 * HD + cols]


def input_kernel(keep_ref, got_ref, grad_ref, x_ref, gain_ref, out_ref):
    grad_normed = keep_ref[...] + got_ref[...].astype(f32)
    wide = x_ref[...].astype(f32)
    scale = lax.rsqrt(jnp.mean(wide * wide, axis=1, keepdims=True) + norm_eps)
    pulled = gain_ref[...] * grad_normed
    inner = jnp.mean(pulled * wide, axis=1, keepdims=True)
    out_ref[...] = grad_ref[...] + scale * pulled - wide * (scale * scale * scale) * inner


def in_order(first, mine, other):
    return jnp.where(first, jnp.concatenate([mine, other]), jnp.concatenate([other, mine]))


def per_device(
    tokens,
    gain_one,
    w_query,
    w_key,
    w_value,
    w_out,
    bias_table,
    gain_two,
    w_router,
    w_up,
    w_down,
    routes,
    doc_lengths,
    buckets,
    cotangent,
):
    own_rows, width = tokens.shape
    block_rows = routes.shape[0]
    seq = block_rows * GROUP
    cols = w_query.shape[1] // GROUP
    heads = cols // HD
    experts = w_router.shape[1]
    capacity = max(2, (5 * block_rows + 4 * experts - 1) // (4 * experts))
    slots = experts * capacity
    nodes = lax.axis_size("node")
    core = lax.axis_index("core")
    side = lax.axis_index("tensor")
    me = lax.axis_index("node")
    direct = nodes == DIRECT
    parts = nodes if direct else 1
    ids = jnp.stack([core, me, side]).astype(jnp.int32)
    node_rows = width // nodes

    def trade(blocks):
        if direct:
            return [blocks[0]] + [across(blocks[i], "node", i) for i in range(1, nodes)]
        stacked = blocks[0].reshape(nodes, -1, blocks[0].shape[1])
        back = lax.all_to_all(stacked, "node", split_axis=0, concat_axis=0, tiled=True)
        return [back.reshape(blocks[0].shape)]

    def trade_natural(rows):
        stacked = rows.reshape(nodes, -1, rows.shape[-1])
        return lax.all_to_all(stacked, "node", split_axis=0, concat_axis=0, tiled=True)

    share = out((w_query.shape[0], 4 * cols), bf16)
    share_kept, share_sent = call(
        shares_kernel,
        "shares",
        [share, share],
        [ids, *(Far(w) for w in (w_query, w_key, w_value, w_out))],
        smem=1,
        scratch=[pltpu.VMEM((4, *w_query.shape), bf16), pltpu.SemaphoreType.DMA((4,))],
    )
    piece = in_order(core == 0, share_kept, across(share_sent, "core", 1))
    if direct:
        pieces = {0: piece}
        for i in (2, 4, 6):
            pieces[i] = across(piece, "node", i)
        for i in (0, 2, 4, 6):
            pieces[i + 1] = across(pieces[i], "node", 1)
        pieces = [pieces[i] for i in range(nodes)]
    else:
        pieces = [lax.all_gather(piece, "node", axis=0, tiled=True)]

    x_rows = call(
        rows_kernel,
        "rows",
        [out((block_rows, width), bf16)],
        [ids, tokens, across(tokens, "tensor", 1), Raw(pieces[min(1, parts - 1)])],
        smem=1,
    )[0]
    x_other = across(x_rows, "core", 1)
    gain_first = gain_one.astype(f32)[None, :]
    gain_second = gain_two.astype(f32)[None, :]

    expert_ids = routes[:, 0]
    picks = (expert_ids[:, None] == jnp.arange(experts, dtype=jnp.int32)[None, :]).astype(jnp.int32)
    slot_index = jnp.sum((jnp.cumsum(picks, axis=0) - 1) * picks, axis=1)
    target = expert_ids * capacity + slot_index
    codes = jnp.arange(slots, dtype=jnp.int32)
    turned = ((codes // capacity) ^ me) * capacity + codes % capacity if direct else codes
    table = (turned[:, None] == target[None, :]).astype(bf16)
    back_table = (target[:, None] == turned[None, :]).astype(bf16)
    plain_table = (codes[:, None] == target[None, :]).astype(bf16)
    plain_back_table = (target[:, None] == codes[None, :]).astype(bf16)

    lengths_row = lax.dynamic_slice_in_dim(doc_lengths, me, 1, 0)[0]
    ends = jnp.cumsum(lengths_row)
    places = jnp.arange(seq, dtype=jnp.int32)
    docs = jnp.sum((ends[None, :] <= places[:, None]).astype(jnp.int32), axis=1)
    bucket_count = bias_table.shape[0]
    bucket_hot = (
        jnp.pad(buckets, (0, 1))[:, None] == jnp.arange(128, dtype=jnp.int32)[None, :]
    ).astype(f32)
    head_start = (side * GROUP + core) * heads
    bias_here = lax.dynamic_slice_in_dim(bias_table, head_start, heads, 1)
    bias_here = jnp.pad(bias_here, ((0, 128 - bucket_count), (0, 0)))
    bias_vectors = lax.dot_general(
        bias_here, bucket_hot, (((0,), (1,)), ((), ())), precision=exact, preferred_element_type=f32
    )

    weights, wo, x_seq, qkv, mixed, mixed_kept, mixed_sent, *probs = call(
        functools.partial(attend_kernel, heads, parts),
        "attend",
        [
            out((width, 4 * cols), bf16),
            out((width, cols), bf16),
            out((seq, width), bf16),
            out((seq, 3 * cols), bf16),
            out((seq, cols), bf16),
            out((block_rows, cols), bf16),
            out((block_rows, cols), bf16),
            *([out((seq, seq), bf16)] * heads),
        ],
        [
            ids,
            x_rows,
            Near(x_other),
            gain_first,
            bias_vectors,
            docs[:, None],
            docs[None, :],
            *(Near(p) for p in pieces),
        ],
        smem=1,
        scratch=[pltpu.VMEM((seq, width), bf16)],
    )
    kept = [weights, wo, x_seq, qkv, mixed, *probs]
    weights, wo_far, x_seq, qkv, mixed, *probs = call(
        functools.partial(move_kernel, len(kept)),
        "park",
        [Far(out(a.shape, a.dtype)) for a in kept],
        [*(Near(a) for a in kept)],
        scratch=[pltpu.SemaphoreType.DMA((len(kept),))],
    )

    natural = (nodes, slots // nodes, width) if direct else (slots, width)
    cot_slots = call(
        slots_kernel,
        "cot_slots",
        [out((slots, width), bf16)],
        [plain_table, cotangent, Raw(mixed_sent)],
    )[0]
    cots_own = trade_natural(cot_slots).reshape(natural)
    cots_other = across(cots_own, "core", 1)

    mixed_got = across(mixed_sent, "core", 1)
    attended = call(
        attended_kernel,
        "attended",
        [out((block_rows, width), bf16)],
        [mixed_kept, mixed_got, wo, across(wo, "core", 1), Far(mixed)],
    )[0]
    attended_got = across(attended, "tensor", 1)
    block_shapes = [out((slots // parts, width), bf16)] * parts
    hidden, *blocks = call(
        dispatch_kernel,
        "dispatch",
        [Near(out((block_rows, width), f32)), *block_shapes],
        [Near(x_rows), attended, Near(attended_got), gain_second, Near(table)],
    )
    received = trade(blocks)
    cots, back_active = call(
        functools.partial(cots_kernel, parts),
        "cots",
        [Near(out((2 * slots, width), bf16)), Near(out((2 * slots, w_down.shape[1]), f32))],
        [ids, Near(cots_own), Near(cots_other), w_down, Raw(blocks[0])],
        smem=1,
        scratch=[pltpu.VMEM((slots, width), f32)] if direct else [],
    )
    slots_own = jnp.concatenate(received)
    slots_other = across(slots_own, "core", 1)
    active, grad_upward, chosen, grad_kept, grad_sent, router_part, slots_all = call(
        expert_kernel,
        "expert",
        [
            Near(out((2 * slots, w_up.shape[1]), bf16)),
            Near(out((2 * slots, w_up.shape[1]), bf16)),
            Near(out((2 * slots, 1), f32)),
            out((slots, width), f32),
            out((slots, width), bf16),
            Near(out(w_router.shape[::-1], f32)),
            Near(out((2 * slots, width), bf16)),
        ],
        [ids, slots_own, Near(slots_other), Near(back_active), w_up, w_router.T],
        smem=1,
    )
    grad_blocks = call(
        join_kernel, "join_grad", block_shapes, [grad_kept, Near(across(grad_sent, "core", 1))]
    )
    grad_back = trade(grad_blocks)
    grad_normed_two = call(
        gather_kernel,
        "gather_grad",
        [out((block_rows, width), bf16)],
        [Near(back_table), *grad_back],
    )[0]
    grad_normed_two_got = across(grad_normed_two, "tensor", 1)

    out_kept, out_sent = call(
        expert_out_kernel,
        "expert_out",
        [out((slots, width), f32), out((slots, width), bf16)],
        [Near(active), Near(chosen), w_down, Raw(grad_blocks[-1])],
    )
    out_slots = call(
        functools.partial(join_natural_kernel, parts),
        "join_out",
        [out(natural, bf16)],
        [ids, out_kept, Near(across(out_sent, "core", 1))],
        smem=1,
    )[0]
    out_back = trade_natural(out_slots.reshape(slots, width)).reshape(slots, width)
    half_block = (own_rows, width)

    grad_hidden, grad_attended, gain_two_part = call(
        hidden_back_kernel,
        "hidden_back",
        [Near(out(half_block, f32)), out((block_rows, width), bf16), Near(out((1, width), f32))],
        [
            ids,
            Near(hidden),
            grad_normed_two,
            Near(grad_normed_two_got),
            cotangent,
            gain_second,
            Raw(out_slots),
        ],
        smem=1,
        scratch=[pltpu.VMEM((block_rows, width), f32)],
    )
    grad_attended_other = across(grad_attended, "core", 1)
    chunk = 3 * HD + cols
    other_chunk = 3 * (cols - HD)
    small_rows = -(-(2 + experts + heads) // 16) * 16
    if direct:
        tall = width // 2 + 2 * small_rows
        first_shapes = [out((width // 2, chunk), t) for t in (f32, bf16)]
        second_shapes = [out((tall, other_chunk), t) for t in (f32, bf16)]
    else:
        first_shapes = [out((width, chunk), bf16)]
        second_shapes = [out((width, other_chunk), bf16), out((small_rows, width), f32)]
    grad_mixed, first_dqkv, diagonals, normed_seq, *first_chunk = call(
        functools.partial(first_back_kernel, heads, parts),
        "first_back",
        [
            out((seq, cols), bf16),
            out((seq, 3 * HD), bf16),
            out((8, 2 * seq), f32),
            out((seq, width), bf16),
            *first_shapes,
        ],
        [
            ids,
            grad_attended,
            Near(grad_attended_other),
            gain_first,
            *(Far(a) for a in (wo_far, qkv, probs[0], x_seq, mixed)),
        ],
        smem=1,
        flops=FLOPS1,
        scratch=[
            pltpu.VMEM((seq, width), bf16),
            pltpu.VMEM((seq, seq), bf16),
            pltpu.VMEM((width, chunk), f32),
            *(pltpu.VMEM(a.shape, bf16) for a in (wo_far, qkv, probs[0], x_seq, mixed)),
            pltpu.SemaphoreType.DMA((5,)),
        ],
    )
    grad_kept, grad_sent, *second_chunk = call(
        functools.partial(second_back_kernel, heads, parts),
        "second_back",
        [
            out((block_rows, width), f32),
            out((block_rows, width), bf16),
            *second_shapes,
        ],
        [
            ids,
            grad_mixed,
            first_dqkv,
            diagonals,
            bucket_hot,
            normed_seq,
            Near(gain_two_part),
            Near(router_part),
            *(Far(a) for a in (qkv, *probs[1:], x_seq, weights)),
        ],
        smem=1,
        flops=FLOPS2,
        scratch=[
            pltpu.VMEM((8, 2 * seq), f32),
            pltpu.VMEM((seq, other_chunk), bf16),
            pltpu.VMEM((seq, 3 * cols), bf16),
            pltpu.VMEM((seq, seq), bf16),
            pltpu.VMEM((width, other_chunk), f32),
            pltpu.VMEM((small_rows, width), f32),
            *(pltpu.VMEM(a.shape, bf16) for a in (qkv, *probs[1:], x_seq, weights)),
            pltpu.SemaphoreType.DMA((heads + 2,)),
        ],
    )

    shard_rows = w_query.shape[0]
    returned, returned_sent = call(
        returned_kernel,
        "returned",
        [out(half_block, bf16), out(half_block, bf16)],
        [ids, Near(plain_back_table), Near(out_back), Raw(grad_kept)],
        smem=1,
    )
    part = out((shard_rows, chunk), f32)
    if direct:
        passed = [second_chunk[1], grad_sent, returned_sent]
        second_sent, grad_sent, returned_sent, own_one, *send_one = call(
            functools.partial(fold_kernel, parts),
            "fold_first",
            [
                *(out(a.shape, a.dtype) for a in passed),
                out((node_rows, chunk), f32),
                *([out((node_rows, chunk), bf16)] * 3),
            ],
            [first_chunk[0], across(first_chunk[1], "node", 1), *passed],
        )
        got_one = [across(b, "node", 2 * i + 2) for i, b in enumerate(send_one)]
        first_done = send_one[0]
    else:
        sums = [jnp.sum(trade_natural(c[0]).astype(f32), axis=0) for c in (first_chunk, second_chunk)]
        kept_one, kept_two = (
            lax.dynamic_slice_in_dim(s, core * shard_rows, shard_rows, 0) for s in sums
        )
        sent_one, sent_two = (
            lax.dynamic_slice_in_dim(s, (1 - core) * shard_rows, shard_rows, 0) for s in sums
        )
        first_done, second_done = kept_one, kept_two
    grad_normed, grad_normed_sent = call(
        normed_sum_kernel,
        "normed_sum",
        [Near(out(half_block, f32)), out(half_block, bf16)],
        [ids, grad_kept, Near(across(grad_sent, "core", 1)), Raw(first_done)],
        smem=1,
        scratch=[pltpu.VMEM((block_rows, width), f32)],
    )
    if direct:
        high = node_rows + 2 * small_rows
        grad_normed_sent, kept_one, sent_one, own_two, *send_two = call(
            functools.partial(fold_second_kernel, 2 * small_rows),
            "fold_second",
            [out(half_block, bf16), part, part, out((high, chunk), f32), *([out((high, chunk), bf16)] * 3)],
            [
                ids,
                second_chunk[0],
                across(second_sent, "node", 1),
                own_one,
                *got_one,
                grad_normed_sent,
            ],
            smem=1,
        )
        got_two = [across(b, "node", 2 * i + 2) for i, b in enumerate(send_two)]
        second_done = send_two[0]
    grad_w_up_here, grad_w_down_here = call(
        expert_grads_kernel,
        "expert_grads",
        [out(w_up.shape, f32), out(w_down.shape, f32)],
        [
            *(Near(a) for a in (slots_all, cots, active, grad_upward, chosen)),
            Raw(second_done),
        ],
    )
    input_grad = call(
        input_kernel,
        "input_grad",
        [out(half_block, f32)],
        [
            Near(grad_normed),
            Near(across(grad_normed_sent, "tensor", 1)),
            Near(grad_hidden),
            tokens,
            gain_first,
        ],
    )[0]
    activations = call(
        activations_kernel,
        "activations",
        [out(half_block, bf16)],
        [ids, Near(hidden), Near(returned), Near(across(returned_sent, "tensor", 1))],
        smem=1,
    )[0]
    if direct:
        kept_two, sent_two = call(
            sum_nodes_kernel,
            "sum_nodes",
            [part, out((shard_rows + 2 * small_rows, chunk), f32)],
            [
                ids,
                own_two,
                *got_two,
                *(Far(a) for a in (grad_w_up_here, activations, input_grad)),
            ],
            smem=1,
        )
    got_one = across(sent_one, "core", 1)
    got_two = across(sent_two, "core", 1)
    if direct:
        small = sent_two[shard_rows:, :] + got_two[shard_rows:, :]
        small = small + across(small, "tensor", 1)
        small = jnp.concatenate([small[:small_rows], small[small_rows:]], axis=1)
    else:
        small = lax.psum(second_chunk[1], ("node", "core", "tensor"))
    weight_grads = call(
        functools.partial(columns_kernel, heads),
        "columns",
        [out(w_query.shape, f32)] * 4,
        [ids, kept_one, got_one, kept_two, got_two],
        smem=1,
    )

    bias_rows = small[2 + experts : 2 + experts + heads, : 4 * 128].reshape(heads, 4, 128)
    grad_bias = bias_rows[:, :, :bucket_count].transpose(2, 1, 0).reshape(bias_table.shape)
    return (
        activations,
        input_grad,
        small[0],
        *weight_grads,
        grad_bias,
        small[1],
        small[2 : 2 + experts].T,
        grad_w_up_here,
        grad_w_down_here,
    )


def solution(mesh):
    dp, tensor = mesh.shape["dp"], mesh.shape["tensor"]
    grid = Mesh(mesh.devices.reshape(dp // GROUP, GROUP, tensor), ("node", "core", "tensor"))
    dp = ("node", "core")
    every = ("node", "core", "tensor")
    in_specs = (
        P(every, None),
        P(),
        P(dp, "tensor"),
        P(dp, "tensor"),
        P(dp, "tensor"),
        P(dp, "tensor"),
        P(),
        P(),
        P(),
        P(None, every),
        P(None, every),
        P(dp, None),
        P(),
        P(),
        P(dp, None),
    )
    out_specs = (
        P(every, None),
        P(every, None),
        P(),
        P(dp, "tensor"),
        P(dp, "tensor"),
        P(dp, "tensor"),
        P(dp, "tensor"),
        P(),
        P(),
        P(),
        P(None, every),
        P(None, every),
    )
    return jax.shard_map(
        per_device, mesh=grid, in_specs=in_specs, out_specs=out_specs, check_vma=False
    )
```

time: 199 us -> 169 us (0.85)
  local copies, waits for them, and re-layouts: 33.1 us -> 9.69 us
  Pallas kernels: 42.2 us -> 49 us
  waiting for transfers between devices: 49.2 us -> 44.2 us
  starting transfers between devices: 63.4 us -> 60.1 us
  other arithmetic: 6.74 us -> 3.45 us
    unnamed x110 -> x71, local copies, waits for them, and re-layouts: 22.5 us -> 8 us
    pallas_call x19 -> x25, Pallas kernels: 42.2 us -> 49 us  [call(): pl.pallas_call(body, name=name, out_shape=[space[type(o)](x.shape, x.dtyp...]
    another operation x6 -> x2, local copies, waits for them, and re-layouts: 4.21 us -> 0.7 us  [the longest x4 3.51 us: per_device(): jnp.stack([w_query, w_key, w_value, w_out]).reshape(4, -1, GROUP, cols)]
    ppermute x48 -> x47, starting transfers between devices: 55.1 us -> 52.3 us  [across(): lax.ppermute(shard, axis, [(i, i ^ bits) for i in range(lax.axis_size(axi...]
    all_to_all x2, waiting for transfers between devices: 2.52 us -> 0.01 us  [trade_natural(): lax.all_to_all(stacked, 'node', split_axis=0, concat_axis=0, tiled=True)]
    ppermute x48 -> x47, waiting for transfers between devices: 46.7 us -> 44.2 us  [across(): lax.ppermute(shard, axis, [(i, i ^ bits) for i in range(lax.axis_size(axi...]
    dynamic_slice x3 -> x0, local copies, waits for them, and re-layouts: 2.07 us -> none  [half_of(): return lax.dynamic_slice_in_dim(rows, index * own_rows, own_rows, 0)]
  transfers between devices with their start and end apart: 50 -> 49, of which waited for: 14 -> 18; matrix products, arithmetic and copies ran while one was open for 7% -> 2% of each run, Pallas kernels for 18% -> 20%
where the time goes in v3:
time: 169 us; the launch traced here: 168 us
  starting transfers between devices  60.1 us (36%)
  Pallas kernels  49 us (29%)
  waiting for transfers between devices  44.2 us (26%)
  local copies, waits for them, and re-layouts  9.69 us (6%)
  other arithmetic  3.45 us (2%)
    ppermute x47, starting transfers between devices, across(): lax.ppermute(shard, axis, [(i, i ^ bits) for i in range(lax.axis_size(axi...  52.3 us
    pallas_call x25, Pallas kernels, call(): pl.pallas_call(body, name=name, out_shape=[space[type(o)](x.shape, x.dtyp...  49 us
    ppermute x47, waiting for transfers between devices, across(): lax.ppermute(shard, axis, [(i, i ^ bits) for i in range(lax.axis_size(axi...  44.2 us
    unnamed x71, local copies, waits for them, and re-layouts  8 us
    all_to_all x2, starting transfers between devices, trade_natural(): lax.all_to_all(stacked, 'node', split_axis=0, concat_axis=0, tiled=True)  7.8 us
  transfers between devices with their start and end apart: 49, of which 18 were waited for; matrix products, arithmetic and copies ran while one was open for 2% of the time, Pallas kernels for 20%

profile of v3, /device:TPU:0, one launch (start us, length us, event | category | flops | bytes accessed | tf_op | source)
XLA Modules:
  0.0 168.2 jit_solution(10191776590404133629)
XLA Ops:
  0.8 1.6 shares.1
  2.9 2.6 %collective-permute-start = (bf16[128,768]{1,0:T(8,128)(2,1)}, bf16[128,768]{1,0:T(8,128)(2,1)S(1)}, u32[]{:S(2)}, u32[]{:S(2)}) collective-permute-start(bf16[128,768]{1,0:T(8,128)(2,1)} %x_ref.1), channel_id=1, source_target_pairs={{0,1},{1,0},{2,3},{3,2},{4,5},{5,4},{6,7},{7,6},{8,9},{9,8},{10,11... | collective-permute-start | bytes 589832 | tf_op jit(solution)/shard_map/ppermute | solution.py:29
  6.2 1.6 collective-permute-start.2
  9.2 1.6 collective-permute-start.4
  10.8 2.6 %collective-permute-start.6 = (bf16[96,768]{1,0:T(8,128)(2,1)S(1)}, bf16[96,768]{1,0:T(8,128)(2,1)S(1)}, u32[]{:S(2)}, u32[]{:S(2)}) collective-permute-start(bf16[96,768]{1,0:T(8,128)(2,1)S(1)} %maximum_select_fusion.refs_0_), channel_id=1, source_target_pairs={{0,16},{4,20},{8,24},{12,28},{16,0},{20,4},{24,8},{28,12},{1,17},{... | collective-permute-start | bytes 442376 | tf_op jit(solution)/shard_map/ppermute | solution.py:29
  13.6 0.9 copy-done.13
  15.7 1.3 collective-permute-done.4.refs_2_
  17.5 7.3 %collective-permute-done.6.refs_4_ = bf16[96,768]{1,0:T(8,128)(2,1)S(1)} collective-permute-done((bf16[96,768]{1,0:T(8,128)(2,1)S(1)}, bf16[96,768]{1,0:T(8,128)(2,1)S(1)}, u32[]{:S(2)}, u32[]{:S(2)}) %collective-permute-start.6) | collective-permute-done | bytes 147488 | tf_op jit(solution)/shard_map/ppermute | solution.py:29
  25.4 1.5 collective-permute-start.9
  27.3 2.7 %collective-permute-done.7.refs_5_ = bf16[96,768]{1,0:T(8,128)(2,1)S(1)} collective-permute-done((bf16[96,768]{1,0:T(8,128)(2,1)S(1)}, bf16[96,768]{1,0:T(8,128)(2,1)S(1)}, u32[]{:S(2)}, u32[]{:S(2)}) %collective-permute-start.7) | collective-permute-done | bytes 147488 | tf_op jit(solution)/shard_map/ppermute | solution.py:29
  30.0 1.6 collective-permute-done.9.refs_7_
  31.5 6.4 %attend.1 = (bf16[768,768]{1,0:T(8,128)(2,1)S(1)}, bf16[768,192]{1,0:T(8,128)(2,1)S(1)}, bf16[512,768]{1,0:T(8,128)(2,1)S(1)}, bf16[512,576]{1,0:T(8,128)(2,1)S(...) custom-call(s32[3]{0:T(128)S(1)} %pad_add_fusion.ids, ...), custom_call_target="tpu_custom_call" | custom-call | tf_op jit(solution)/shard_map/attend/pallas_call | solution.py:54
  38.7 2.3 %park.1 = (bf16[768,768]{1,0:T(8,128)(2,1)}, bf16[768,192]{1,0:T(8,128)(2,1)}, bf16[512,768]{1,0:T(8,128)(2,1)}, bf16[512,576]{1,0:T(8,128)(2,1)}, bf16[512,192]...) custom-call(bf16[768,768]{1,0:T(8,128)(2,1)S(1)} %get-tuple-element.104.refs_0_, ...), custom_call_target="tpu_custom_call" | custom-call | tf_op jit(solution)/shard_map/park/pallas_call | solution.py:54
  42.2 1.1 cot_slots.1
  43.2 3.7 %all-to-all-start = ((bf16[8,40,768]{2,1,0:T(8,128)(2,1)}), bf16[8,40,768]{2,1,0:T(8,128)(2,1)S(1)}, u32[]{:S(2)}, u32[]{:S(2)}) async-start(bf16[8,40,768]{2,1,0:T(8,128)(2,1)} %bitcast.13), calls=%async_computation | async-start | bytes 983040 | tf_op jit(solution)/shard_map/all_to_all | solution.py:580
  46.9 5.6 %collective-permute-done.12.got_ref = bf16[256,768]{1,0:T(8,128)(2,1)S(1)} collective-permute-done((bf16[256,768]{1,0:T(8,128)(2,1)S(1)}, bf16[256,768]{1,0:T(8,128)(2,1)S(1)}, u32[]{:S(2)}, u32[]{:S(2)}) %collective-permute-start.12) | collective-permute-done | bytes 393248 | tf_op jit(solution)/shard_map/ppermute | solution.py:29
  53.3 1.0 copy-done.24
  54.3 1.2 dispatch.1
  56.0 1.1 collective-permute-start.14
  57.1 1.9 %collective-permute-start.15 = (bf16[40,768]{1,0:T(8,128)(2,1)S(1)}, bf16[40,768]{1,0:T(8,128)(2,1)S(1)}, u32[]{:S(2)}, u32[]{:S(2)}) collective-permute-start(bf16[40,768]{1,0:T(8,128)(2,1)S(1)} %get-tuple-element.116), channel_id=1, source_target_pairs={{0,12},{4,8},{8,4},{12,0},{16,28},{20,24},{24,20},{28,16},{1,13},{... | collective-permute-start | bytes 184328 | tf_op jit(solution)/shard_map/ppermute | solution.py:29
  59.0 1.8 %collective-permute-start.16 = (bf16[40,768]{1,0:T(8,128)(2,1)S(1)}, bf16[40,768]{1,0:T(8,128)(2,1)S(1)}, u32[]{:S(2)}, u32[]{:S(2)}) collective-permute-start(bf16[40,768]{1,0:T(8,128)(2,1)S(1)} %get-tuple-element.117), channel_id=1, source_target_pairs={{0,16},{4,20},{8,24},{12,28},{16,0},{20,4},{24,8},{28,12},{1,17},{... | collective-permute-start | bytes 184328 | tf_op jit(solution)/shard_map/ppermute | solution.py:29
  60.8 1.1 collective-permute-start.17
  61.9 2.4 %collective-permute-start.18 = (bf16[40,768]{1,0:T(8,128)(2,1)S(1)}, bf16[40,768]{1,0:T(8,128)(2,1)S(1)}, u32[]{:S(2)}, u32[]{:S(2)}) collective-permute-start(bf16[40,768]{1,0:T(8,128)(2,1)S(1)} %get-tuple-element.119), channel_id=1, source_target_pairs={{0,24},{4,28},{8,16},{12,20},{16,8},{20,12},{24,0},{28,4},{1,25},{... | collective-permute-start | bytes 184328 | tf_op jit(solution)/shard_map/ppermute | solution.py:29
  64.3 2.5 %collective-permute-start.19 = (bf16[40,768]{1,0:T(8,128)(2,1)}, bf16[40,768]{1,0:T(8,128)(2,1)S(1)}, u32[]{:S(2)}, u32[]{:S(2)}) collective-permute-start(bf16[40,768]{1,0:T(8,128)(2,1)} %get-tuple-element.120), channel_id=1, source_target_pairs={{0,28},{4,24},{8,20},{12,16},{16,12},{20,8},{24,4},{28,0},{1,29},{... | collective-permute-start | bytes 184328 | tf_op jit(solution)/shard_map/ppermute | solution.py:29
  67.1 2.9 %collective-permute-done.17 = bf16[40,768]{1,0:T(8,128)(2,1)S(1)} collective-permute-done((bf16[40,768]{1,0:T(8,128)(2,1)S(1)}, bf16[40,768]{1,0:T(8,128)(2,1)S(1)}, u32[]{:S(2)}, u32[]{:S(2)}) %collective-permute-start.17) | collective-permute-done | bytes 61472 | tf_op jit(solution)/shard_map/ppermute | solution.py:29
  70.1 1.4 collective-permute-done.19
  72.0 1.5 cots.1
  73.5 1.0 copy-done.7
  74.4 5.3 %expert.1 = (bf16[640,768]{1,0:T(8,128)(2,1)S(1)}, bf16[640,768]{1,0:T(8,128)(2,1)S(1)}, f32[640,1]{1,0:T(8,128)S(1)}, f32[320,768]{1,0:T(8,128)S(1)}, bf16[320,...) custom-call(s32[3]{0:T(128)S(1)} %pad_add_fusion.ids, ...), custom_call_target="tpu_custom_call" | custom-call | tf_op jit(solution)/shard_map/expert/pallas_call | solution.py:54
  79.9 1.7 %collective-permute-done.22.got_ref = bf16[320,768]{1,0:T(8,128)(2,1)S(1)} collective-permute-done((bf16[320,768]{1,0:T(8,128)(2,1)S(1)}, bf16[320,768]{1,0:T(8,128)(2,1)S(1)}, u32[]{:S(2)}, u32[]{:S(2)}) %collective-permute-start.22) | collective-permute-done | bytes 491552 | tf_op jit(solution)/shard_map/ppermute | solution.py:29
  81.8 1.3 collective-permute-start.24
  83.1 1.6 collective-permute-start.25
  85.3 1.0 expert_out.1
  86.4 2.7 %collective-permute-start.30 = (bf16[40,768]{1,0:T(8,128)(2,1)S(1)}, bf16[40,768]{1,0:T(8,128)(2,1)S(1)}, u32[]{:S(2)}, u32[]{:S(2)}) collective-permute-start(bf16[40,768]{1,0:T(8,128)(2,1)S(1)} %get-tuple-element.126.held_ref), channel_id=1, source_target_pairs={{0,28},{4,24},{8,20},{12,16},{16,12},{20,8},{24,4},{28,0},{1,29},{... | collective-permute-start | bytes 184328 | tf_op jit(solution)/shard_map/ppermute | solution.py:29
  89.1 1.2 collective-permute-start.27
  90.3 2.1 %collective-permute-start.28 = (bf16[40,768]{1,0:T(8,128)(2,1)S(1)}, bf16[40,768]{1,0:T(8,128)(2,1)S(1)}, u32[]{:S(2)}, u32[]{:S(2)}) collective-permute-start(bf16[40,768]{1,0:T(8,128)(2,1)S(1)} %get-tuple-element.134), channel_id=1, source_target_pairs={{0,20},{4,16},{8,28},{12,24},{16,4},{20,0},{24,12},{28,8},{1,21},{... | collective-permute-start | bytes 184328 | tf_op jit(solution)/shard_map/ppermute | solution.py:29
  92.3 1.8 %collective-permute-start.29 = (bf16[40,768]{1,0:T(8,128)(2,1)S(1)}, bf16[40,768]{1,0:T(8,128)(2,1)S(1)}, u32[]{:S(2)}, u32[]{:S(2)}) collective-permute-start(bf16[40,768]{1,0:T(8,128)(2,1)S(1)} %get-tuple-element.135), channel_id=1, source_target_pairs={{0,24},{4,28},{8,16},{12,20},{16,8},{20,12},{24,0},{28,4},{1,25},{... | collective-permute-start | bytes 184328 | tf_op jit(solution)/shard_map/ppermute | solution.py:29
  94.3 5.3 %collective-permute-done.27.refs_4_ = bf16[40,768]{1,0:T(8,128)(2,1)S(1)} collective-permute-done((bf16[40,768]{1,0:T(8,128)(2,1)S(1)}, bf16[40,768]{1,0:T(8,128)(2,1)S(1)}, u32[]{:S(2)}, u32[]{:S(2)}) %collective-permute-start.27) | collective-permute-done | bytes 61472 | tf_op jit(solution)/shard_map/ppermute | solution.py:29
  100.6 1.4 collective-permute-start.31
  102.0 1.4 join_out.1.held_ref
  103.5 4.1 %all-to-all-start.1 = ((bf16[8,40,768]{2,1,0:T(8,128)(2,1)}), bf16[8,40,768]{2,1,0:T(8,128)(2,1)S(1)}, u32[]{:S(2)}, u32[]{:S(2)}) async-start(bf16[8,40,768]{2,1,0:T(8,128)(2,1)} %join_out.1.held_ref), calls=%async_computation.1 | async-start | bytes 983040 | tf_op jit(solution)/shard_map/all_to_all | solution.py:580
  107.6 4.3 %collective-permute-done.31.got_ref = bf16[256,768]{1,0:T(8,128)(2,1)} collective-permute-done((bf16[256,768]{1,0:T(8,128)(2,1)S(1)}, bf16[256,768]{1,0:T(8,128)(2,1)}, u32[]{:S(2)}, u32[]{:S(2)}) %collective-permute-start.31) | collective-permute-done | bytes 393248 | tf_op jit(solution)/shard_map/ppermute | solution.py:29
  111.9 1.5 hidden_back.1
  114.2 1.7 %collective-permute-done.32.other_ref = bf16[256,768]{1,0:T(8,128)(2,1)S(1)} collective-permute-done((bf16[256,768]{1,0:T(8,128)(2,1)S(1)}, bf16[256,768]{1,0:T(8,128)(2,1)S(1)}, u32[]{:S(2)}, u32[]{:S(2)}) %collective-permute-start.32) | collective-permute-done | bytes 393248 | tf_op jit(solution)/shard_map/ppermute | solution.py:29
  115.9 5.8 %first_back.1 = (bf16[512,192]{1,0:T(8,128)(2,1)S(1)}, bf16[512,192]{1,0:T(8,128)(2,1)S(1)}, f32[8,1024]{1,0:T(8,128)S(1)}, bf16[512,768]{1,0:T(8,128)(2,1)S(1)}...) custom-call(s32[3]{0:T(128)S(1)} %pad_add_fusion.ids, bf16[256,768]{1,0:T(8,128)(2,1)S(1)} %get-tuple-element.136.own_ref, ...), custom_call_target="tpu_custom_call" | custom-call | tf_op jit(solution)/shard_map/first_back/pallas_call | solution.py:54
  122.5 1.3 collective-permute-start.33
  124.0 7.4 %second_back.1 = (f32[256,768]{1,0:T(8,128)S(1)}, bf16[256,768]{1,0:T(8,128)(2,1)S(1)}, f32[416,384]{1,0:T(8,128)S(1)}, bf16[416,384]{1,0:T(8,128)(2,1)S(1)}) custom-call(s32[3]{0:T(128)S(1)} %pad_add_fusion.ids, bf16[512,192]{1,0:T(8,128)(2,1)S(1)} %get-tuple-element.141.gm_ref, bf16[512,192]{1,0:T(8,128)(2,1)S(1)} %get-tuple-element.142.first_ref, ...), custom_call_target="tpu_custom_call" | custom-call | tf_op jit(solution)/shard_map/second_back/pallas_call | solution.py:54
  133.7 0.9 returned.1
  135.0 1.1 fold_first.1
  136.2 0.8 collective-permute-start.36
  137.0 1.7 collective-permute-start.37
  139.4 2.0 %collective-permute-start.39 = (bf16[96,384]{1,0:T(8,128)(2,1)S(1)}, bf16[96,384]{1,0:T(8,128)(2,1)S(1)}, u32[]{:S(2)}, u32[]{:S(2)}) collective-permute-start(bf16[96,384]{1,0:T(8,128)(2,1)S(1)} %get-tuple-element.165), channel_id=1, source_target_pairs={{0,24},{4,28},{8,16},{12,20},{16,8},{20,12},{24,0},{28,4},{1,25},{... | collective-permute-start | bytes 221192 | tf_op jit(solution)/shard_map/ppermute | solution.py:29
  141.4 1.2 collective-permute-start.34
  143.3 4.1 %collective-permute-done.38.refs_2_ = bf16[96,384]{1,0:T(8,128)(2,1)S(1)} collective-permute-done((bf16[96,384]{1,0:T(8,128)(2,1)S(1)}, bf16[96,384]{1,0:T(8,128)(2,1)S(1)}, u32[]{:S(2)}, u32[]{:S(2)}) %collective-permute-start.38) | collective-permute-done | bytes 73760 | tf_op jit(solution)/shard_map/ppermute | solution.py:29
  148.1 1.2 collective-permute-start.40
  149.2 1.6 collective-permute-start.41
  151.5 2.1 %collective-permute-start.43 = (bf16[128,384]{1,0:T(8,128)(2,1)S(1)}, bf16[128,384]{1,0:T(8,128)(2,1)S(1)}, u32[]{:S(2)}, u32[]{:S(2)}) collective-permute-start(bf16[128,384]{1,0:T(8,128)(2,1)S(1)} %get-tuple-element.172), channel_id=1, source_target_pairs={{0,24},{4,28},{8,16},{12,20},{16,8},{20,12},{24,0},{28,4},{1,25},{... | collective-permute-start | bytes 294920 | tf_op jit(solution)/shard_map/ppermute | solution.py:29
  153.6 1.3 activations.1.refs_5_
  155.0 3.7 %expert_grads.1 = (f32[768,768]{1,0:T(8,128)}, f32[768,768]{1,0:T(8,128)}) custom-call(bf16[640,768]{1,0:T(8,128)(2,1)S(1)} %copy-done.12, bf16[640,768]{1,0:T(8,128)(2,1)S(1)} %copy-done.8, bf16[640,768]{1,0:T(8,128)(2,1)S(1)} %get-tuple-element.122.active_ref, bf16[640,768]{1,0:T(8,128)(2,1)S(1)} %copy-done.10, f32[640,1]{1,0:T(8,128)S(1)} %copy-done.5, ...), custom_call_target="tpu_custom_call" | custom-call | tf_op jit(solution)/shard_map/expert_grads/pallas_call | solution.py:54
  158.7 0.9 input_grad.1.refs_6_
  161.4 0.8 collective-permute-done.44.got_two
  162.2 1.2 collective-permute-start.45
  163.4 1.3 columns.1
  164.8 1.6 collective-permute-done.45
  (162 shorter events, 22.5 us)
Async XLA Ops:
  0.6 15.0 %copy-start = (f32[32,12]{0,1:T(8,128)S(1)}, f32[32,12]{0,1:T(8,128)}, u32[]{:S(2)}) copy-start(f32[32,12]{0,1:T(8,128)} %param.21) | copy-start | bytes 4612
  0.7 14.8 %copy-start.29 = (s32[1023]{0:T(1024)S(1)}, s32[1023]{0:T(1024)}, u32[]{:S(2)}) copy-start(s32[1023]{0:T(1024)} %param.28) | copy-start | bytes 12280
  0.7 15.0 %copy-start.30 = (bf16[768]{0:T(1024)(128)(2,1)S(1)}, bf16[768]{0:T(1024)(128)(2,1)}, u32[]{:S(2)}) copy-start(bf16[768]{0:T(1024)(128)(2,1)} %param.16) | copy-start | bytes 4612
  2.3 3.8 %collective-permute-start.1 = (bf16[48,768]{1,0:T(8,128)(2,1)S(1)}, bf16[48,768]{1,0:T(8,128)(2,1)S(1)}, u32[]{:S(2)}, u32[]{:S(2)}) collective-permute-start(bf16[48,768]{1,0:T(8,128)(2,1)S(1)} %get-tuple-element.100), channel_id=1, source_target_pairs={{0,2},{2,0},{1,3},{3,1},{4,6},{6,4},{5,7},{7,5},{8,10},{10,8},{9,1... | collective-permute-start | bytes 221192 | tf_op jit(solution)/shard_map/ppermute | solution.py:29
  2.9 10.8 %collective-permute-start = (bf16[128,768]{1,0:T(8,128)(2,1)}, bf16[128,768]{1,0:T(8,128)(2,1)S(1)}, u32[]{:S(2)}, u32[]{:S(2)}) collective-permute-start(bf16[128,768]{1,0:T(8,128)(2,1)} %x_ref.1), channel_id=1, source_target_pairs={{0,1},{1,0},{2,3},{3,2},{4,5},{5,4},{6,7},{7,6},{8,9},{9,8},{10,11... | collective-permute-start | bytes 589832 | tf_op jit(solution)/shard_map/ppermute | solution.py:29
  6.2 7.5 %collective-permute-start.2 = (bf16[96,768]{1,0:T(8,128)(2,1)S(1)}, bf16[96,768]{1,0:T(8,128)(2,1)S(1)}, u32[]{:S(2)}, u32[]{:S(2)}) collective-permute-start(bf16[96,768]{1,0:T(8,128)(2,1)S(1)} %maximum_select_fusion.refs_0_), channel_id=1, source_target_pairs={{0,4},{4,0},{8,12},{12,8},{16,20},{20,16},{24,28},{28,24},{1,5},{5... | collective-permute-start | bytes 442376 | tf_op jit(solution)/shard_map/ppermute | solution.py:29
  9.2 7.8 %collective-permute-start.4 = (bf16[96,768]{1,0:T(8,128)(2,1)S(1)}, bf16[96,768]{1,0:T(8,128)(2,1)S(1)}, u32[]{:S(2)}, u32[]{:S(2)}) collective-permute-start(bf16[96,768]{1,0:T(8,128)(2,1)S(1)} %maximum_select_fusion.refs_0_), channel_id=1, source_target_pairs={{0,8},{4,12},{8,0},{12,4},{16,24},{20,28},{24,16},{28,20},{1,9},{5... | collective-permute-start | bytes 442376 | tf_op jit(solution)/shard_map/ppermute | solution.py:29
  10.8 14.0 %collective-permute-start.6 = (bf16[96,768]{1,0:T(8,128)(2,1)S(1)}, bf16[96,768]{1,0:T(8,128)(2,1)S(1)}, u32[]{:S(2)}, u32[]{:S(2)}) collective-permute-start(bf16[96,768]{1,0:T(8,128)(2,1)S(1)} %maximum_select_fusion.refs_0_), channel_id=1, source_target_pairs={{0,16},{4,20},{8,24},{12,28},{16,0},{20,4},{24,8},{28,12},{1,17},{... | collective-permute-start | bytes 442376 | tf_op jit(solution)/shard_map/ppermute | solution.py:29
  13.4 11.9 %collective-permute-start.8 = (bf16[96,768]{1,0:T(8,128)(2,1)S(1)}, bf16[96,768]{1,0:T(8,128)(2,1)S(1)}, u32[]{:S(2)}, u32[]{:S(2)}) collective-permute-start(bf16[96,768]{1,0:T(8,128)(2,1)S(1)} %maximum_select_fusion.refs_0_), channel_id=1, source_target_pairs={{0,24},{4,28},{8,16},{12,20},{16,8},{20,12},{24,0},{28,4},{1,25},{... | collective-permute-start | bytes 442376 | tf_op jit(solution)/shard_map/ppermute | solution.py:29
  15.2 16.4 %collective-permute-start.3 = (bf16[256,768]{1,0:T(8,128)(2,1)S(1)}, bf16[256,768]{1,0:T(8,128)(2,1)S(1)}, u32[]{:S(2)}, u32[]{:S(2)}) collective-permute-start(bf16[256,768]{1,0:T(8,128)(2,1)S(1)} %rows.1.own_ref.x_ref), channel_id=1, source_target_pairs={{0,2},{2,0},{1,3},{3,1},{4,6},{6,4},{5,7},{7,5},{8,10},{10,8},{9,1... | collective-permute-start | bytes 1179656 | tf_op jit(solution)/shard_map/ppermute | solution.py:29
  15.7 22.4 %copy-start.28 = (s32[256,1]{0,1:T(1,128)S(1)}, s32[256,1]{0,1:T(1,128)}, u32[]{:S(2)}) copy-start(s32[256,1]{0,1:T(1,128)} %param.26) | copy-start | bytes 3076
  17.0 10.3 %collective-permute-start.5 = (bf16[96,768]{1,0:T(8,128)(2,1)S(1)}, bf16[96,768]{1,0:T(8,128)(2,1)S(1)}, u32[]{:S(2)}, u32[]{:S(2)}) collective-permute-start(bf16[96,768]{1,0:T(8,128)(2,1)S(1)} %collective-permute-done.4.refs_2_), channel_id=1, source_target_pairs={{0,4},{4,0},{8,12},{12,8},{16,20},{20,16},{24,28},{28,24},{1,5},{5... | collective-permute-start | bytes 442376 | tf_op jit(solution)/shard_map/ppermute | solution.py:29
  24.8 5.1 %collective-permute-start.7 = (bf16[96,768]{1,0:T(8,128)(2,1)S(1)}, bf16[96,768]{1,0:T(8,128)(2,1)S(1)}, u32[]{:S(2)}, u32[]{:S(2)}) collective-permute-start(bf16[96,768]{1,0:T(8,128)(2,1)S(1)} %collective-permute-done.6.refs_4_), channel_id=1, source_target_pairs={{0,4},{4,0},{8,12},{12,8},{16,20},{20,16},{24,28},{28,24},{1,5},{5... | collective-permute-start | bytes 442376 | tf_op jit(solution)/shard_map/ppermute | solution.py:29
  25.4 6.2 %collective-permute-start.9 = (bf16[96,768]{1,0:T(8,128)(2,1)S(1)}, bf16[96,768]{1,0:T(8,128)(2,1)S(1)}, u32[]{:S(2)}, u32[]{:S(2)}) collective-permute-start(bf16[96,768]{1,0:T(8,128)(2,1)S(1)} %collective-permute-done.8.refs_6_), channel_id=1, source_target_pairs={{0,4},{4,0},{8,12},{12,8},{16,20},{20,16},{24,28},{28,24},{1,5},{5... | collective-permute-start | bytes 442376 | tf_op jit(solution)/shard_map/ppermute | solution.py:29
  38.0 3.0 %collective-permute-start.11 = (bf16[768,192]{1,0:T(8,128)(2,1)S(1)}, bf16[768,192]{1,0:T(8,128)(2,1)S(1)}, u32[]{:S(2)}, u32[]{:S(2)}) collective-permute-start(bf16[768,192]{1,0:T(8,128)(2,1)S(1)} %get-tuple-element.103.refs_1_.wo_ref), channel_id=1, source_target_pairs={{0,2},{2,0},{1,3},{3,1},{4,6},{6,4},{5,7},{7,5},{8,10},{10,8},{9,1... | collective-permute-start | bytes 884744 | tf_op jit(solution)/shard_map/ppermute | solution.py:29
  38.2 2.8 %collective-permute-start.10 = (bf16[256,192]{1,0:T(8,128)(2,1)S(1)}, bf16[256,192]{1,0:T(8,128)(2,1)S(1)}, u32[]{:S(2)}, u32[]{:S(2)}) collective-permute-start(bf16[256,192]{1,0:T(8,128)(2,1)S(1)} %get-tuple-element.102.held_ref), channel_id=1, source_target_pairs={{0,2},{2,0},{1,3},{3,1},{4,6},{6,4},{5,7},{7,5},{8,10},{10,8},{9,1... | collective-permute-start | bytes 294920 | tf_op jit(solution)/shard_map/ppermute | solution.py:29
  41.4 11.1 %collective-permute-start.12 = (bf16[256,768]{1,0:T(8,128)(2,1)S(1)}, bf16[256,768]{1,0:T(8,128)(2,1)S(1)}, u32[]{:S(2)}, u32[]{:S(2)}) collective-permute-start(bf16[256,768]{1,0:T(8,128)(2,1)S(1)} %attended.1.own_ref), channel_id=1, source_target_pairs={{0,1},{1,0},{2,3},{3,2},{4,5},{5,4},{6,7},{7,6},{8,9},{9,8},{10,11... | collective-permute-start | bytes 1179656 | tf_op jit(solution)/shard_map/ppermute | solution.py:29
  42.0 4.9 %copy-start.31 = (bf16[768]{0:T(1024)(128)(2,1)S(1)}, bf16[768]{0:T(1024)(128)(2,1)}, u32[]{:S(2)}) copy-start(bf16[768]{0:T(1024)(128)(2,1)} %param.22) | copy-start | bytes 4612
  43.2 26.8 %all-to-all-start = ((bf16[8,40,768]{2,1,0:T(8,128)(2,1)}), bf16[8,40,768]{2,1,0:T(8,128)(2,1)S(1)}, u32[]{:S(2)}, u32[]{:S(2)}) async-start(bf16[8,40,768]{2,1,0:T(8,128)(2,1)} %bitcast.13), calls=%async_computation | async-start | bytes 983040 | tf_op jit(solution)/shard_map/all_to_all | solution.py:580
  46.9 25.0 %copy-start.1 = (bf16[768,768]{1,0:T(8,128)(2,1)S(1)}, bf16[768,768]{1,0:T(8,128)(2,1)}, u32[]{:S(2)}) copy-start(bf16[768,768]{1,0:T(8,128)(2,1)} %wdown_ref.3) | copy-start | bytes 3538948
  55.5 6.4 %collective-permute-start.13 = (bf16[40,768]{1,0:T(8,128)(2,1)S(1)}, bf16[40,768]{1,0:T(8,128)(2,1)S(1)}, u32[]{:S(2)}, u32[]{:S(2)}) collective-permute-start(bf16[40,768]{1,0:T(8,128)(2,1)S(1)} %get-tuple-element.114), channel_id=1, source_target_pairs={{0,4},{4,0},{8,12},{12,8},{16,20},{20,16},{24,28},{28,24},{1,5},{5... | collective-permute-start | bytes 184328 | tf_op jit(solution)/shard_map/ppermute | solution.py:29
  56.0 8.3 %collective-permute-start.14 = (bf16[40,768]{1,0:T(8,128)(2,1)S(1)}, bf16[40,768]{1,0:T(8,128)(2,1)S(1)}, u32[]{:S(2)}, u32[]{:S(2)}) collective-permute-start(bf16[40,768]{1,0:T(8,128)(2,1)S(1)} %get-tuple-element.115), channel_id=1, source_target_pairs={{0,8},{4,12},{8,0},{12,4},{16,24},{20,28},{24,16},{28,20},{1,9},{5... | collective-permute-start | bytes 184328 | tf_op jit(solution)/shard_map/ppermute | solution.py:29
  57.1 9.7 %collective-permute-start.15 = (bf16[40,768]{1,0:T(8,128)(2,1)S(1)}, bf16[40,768]{1,0:T(8,128)(2,1)S(1)}, u32[]{:S(2)}, u32[]{:S(2)}) collective-permute-start(bf16[40,768]{1,0:T(8,128)(2,1)S(1)} %get-tuple-element.116), channel_id=1, source_target_pairs={{0,12},{4,8},{8,4},{12,0},{16,28},{20,24},{24,20},{28,16},{1,13},{... | collective-permute-start | bytes 184328 | tf_op jit(solution)/shard_map/ppermute | solution.py:29
  59.0 8.1 %collective-permute-start.16 = (bf16[40,768]{1,0:T(8,128)(2,1)S(1)}, bf16[40,768]{1,0:T(8,128)(2,1)S(1)}, u32[]{:S(2)}, u32[]{:S(2)}) collective-permute-start(bf16[40,768]{1,0:T(8,128)(2,1)S(1)} %get-tuple-element.117), channel_id=1, source_target_pairs={{0,16},{4,20},{8,24},{12,28},{16,0},{20,4},{24,8},{28,12},{1,17},{... | collective-permute-start | bytes 184328 | tf_op jit(solution)/shard_map/ppermute | solution.py:29
  60.8 9.2 %collective-permute-start.17 = (bf16[40,768]{1,0:T(8,128)(2,1)S(1)}, bf16[40,768]{1,0:T(8,128)(2,1)S(1)}, u32[]{:S(2)}, u32[]{:S(2)}) collective-permute-start(bf16[40,768]{1,0:T(8,128)(2,1)S(1)} %get-tuple-element.118), channel_id=1, source_target_pairs={{0,20},{4,16},{8,28},{12,24},{16,4},{20,0},{24,12},{28,8},{1,21},{... | collective-permute-start | bytes 184328 | tf_op jit(solution)/shard_map/ppermute | solution.py:29
  61.9 8.1 %collective-permute-start.18 = (bf16[40,768]{1,0:T(8,128)(2,1)S(1)}, bf16[40,768]{1,0:T(8,128)(2,1)S(1)}, u32[]{:S(2)}, u32[]{:S(2)}) collective-permute-start(bf16[40,768]{1,0:T(8,128)(2,1)S(1)} %get-tuple-element.119), channel_id=1, source_target_pairs={{0,24},{4,28},{8,16},{12,20},{16,8},{20,12},{24,0},{28,4},{1,25},{... | collective-permute-start | bytes 184328 | tf_op jit(solution)/shard_map/ppermute | solution.py:29
  64.3 7.3 %collective-permute-start.19 = (bf16[40,768]{1,0:T(8,128)(2,1)}, bf16[40,768]{1,0:T(8,128)(2,1)S(1)}, u32[]{:S(2)}, u32[]{:S(2)}) collective-permute-start(bf16[40,768]{1,0:T(8,128)(2,1)} %get-tuple-element.120), channel_id=1, source_target_pairs={{0,28},{4,24},{8,20},{12,16},{16,12},{20,8},{24,4},{28,0},{1,29},{... | collective-permute-start | bytes 184328 | tf_op jit(solution)/shard_map/ppermute | solution.py:29
  70.0 1.9 %collective-permute-start.21 = (bf16[8,40,768]{2,1,0:T(8,128)(2,1)S(1)}, bf16[8,40,768]{2,1,0:T(8,128)(2,1)S(1)}, u32[]{:S(2)}, u32[]{:S(2)}) collective-permute-start(bf16[8,40,768]{2,1,0:T(8,128)(2,1)S(1)} %all-to-all-done.own_ref), channel_id=1, source_target_pairs={{0,2},{2,0},{1,3},{3,1},{4,6},{6,4},{5,7},{7,5},{8,10},{10,8},{9,1... | collective-permute-start | bytes 1474568 | tf_op jit(solution)/shard_map/ppermute | solution.py:29
  71.6 2.9 %collective-permute-start.20 = (bf16[320,768]{1,0:T(8,128)(2,1)S(1)}, bf16[320,768]{1,0:T(8,128)(2,1)S(1)}, u32[]{:S(2)}, u32[]{:S(2)}) collective-permute-start(bf16[320,768]{1,0:T(8,128)(2,1)S(1)} %constant_dynamic-update-slice_fusion.own_ref), channel_id=1, source_target_pairs={{0,2},{2,0},{1,3},{3,1},{4,6},{6,4},{5,7},{7,5},{8,10},{10,8},{9,1... | collective-permute-start | bytes 1474568 | tf_op jit(solution)/shard_map/ppermute | solution.py:29
  79.7 6.6 %copy-start.4 = (f32[640,1]{1,0:T(8,128)}, f32[640,1]{1,0:T(8,128)S(1)}, u32[]{:S(2)}) copy-start(f32[640,1]{1,0:T(8,128)S(1)} %get-tuple-element.123.chosen_ref) | copy-start | bytes 7684
  79.7 6.6 %copy-start.9 = (bf16[640,768]{1,0:T(8,128)(2,1)}, bf16[640,768]{1,0:T(8,128)(2,1)S(1)}, u32[]{:S(2)}) copy-start(bf16[640,768]{1,0:T(8,128)(2,1)S(1)} %get-tuple-element.175.gup_ref) | copy-start | bytes 2949124
  79.7 6.6 %copy-start.11 = (bf16[640,768]{1,0:T(8,128)(2,1)}, bf16[640,768]{1,0:T(8,128)(2,1)S(1)}, u32[]{:S(2)}) copy-start(bf16[640,768]{1,0:T(8,128)(2,1)S(1)} %get-tuple-element.173.slots_ref) | copy-start | bytes 2949124
  79.7 1.9 %collective-permute-start.22 = (bf16[320,768]{1,0:T(8,128)(2,1)S(1)}, bf16[320,768]{1,0:T(8,128)(2,1)S(1)}, u32[]{:S(2)}, u32[]{:S(2)}) collective-permute-start(bf16[320,768]{1,0:T(8,128)(2,1)S(1)} %get-tuple-element.125), channel_id=1, source_target_pairs={{0,2},{2,0},{1,3},{3,1},{4,6},{6,4},{5,7},{7,5},{8,10},{10,8},{9,1... | collective-permute-start | bytes 1474568 | tf_op jit(solution)/shard_map/ppermute | solution.py:29
  81.8 7.3 %collective-permute-start.24 = (bf16[40,768]{1,0:T(8,128)(2,1)S(1)}, bf16[40,768]{1,0:T(8,128)(2,1)S(1)}, u32[]{:S(2)}, u32[]{:S(2)}) collective-permute-start(bf16[40,768]{1,0:T(8,128)(2,1)S(1)} %get-tuple-element.130), channel_id=1, source_target_pairs={{0,4},{4,0},{8,12},{12,8},{16,20},{20,16},{24,28},{28,24},{1,5},{5... | collective-permute-start | bytes 184328 | tf_op jit(solution)/shard_map/ppermute | solution.py:29
  83.1 7.2 %collective-permute-start.25 = (bf16[40,768]{1,0:T(8,128)(2,1)S(1)}, bf16[40,768]{1,0:T(8,128)(2,1)S(1)}, u32[]{:S(2)}, u32[]{:S(2)}) collective-permute-start(bf16[40,768]{1,0:T(8,128)(2,1)S(1)} %get-tuple-element.131), channel_id=1, source_target_pairs={{0,8},{4,12},{8,0},{12,4},{16,24},{20,28},{24,16},{28,20},{1,9},{5... | collective-permute-start | bytes 184328 | tf_op jit(solution)/shard_map/ppermute | solution.py:29
  84.7 7.6 %collective-permute-start.26 = (bf16[40,768]{1,0:T(8,128)(2,1)S(1)}, bf16[40,768]{1,0:T(8,128)(2,1)S(1)}, u32[]{:S(2)}, u32[]{:S(2)}) collective-permute-start(bf16[40,768]{1,0:T(8,128)(2,1)S(1)} %get-tuple-element.132), channel_id=1, source_target_pairs={{0,12},{4,8},{8,4},{12,0},{16,28},{20,24},{24,20},{28,16},{1,13},{... | collective-permute-start | bytes 184328 | tf_op jit(solution)/shard_map/ppermute | solution.py:29
  86.3 15.7 %collective-permute-start.23 = (bf16[320,768]{1,0:T(8,128)(2,1)S(1)}, bf16[320,768]{1,0:T(8,128)(2,1)S(1)}, u32[]{:S(2)}, u32[]{:S(2)}) collective-permute-start(bf16[320,768]{1,0:T(8,128)(2,1)S(1)} %get-tuple-element.128), channel_id=1, source_target_pairs={{0,2},{2,0},{1,3},{3,1},{4,6},{6,4},{5,7},{7,5},{8,10},{10,8},{9,1... | collective-permute-start | bytes 1474568 | tf_op jit(solution)/shard_map/ppermute | solution.py:29
  86.4 13.8 %collective-permute-start.30 = (bf16[40,768]{1,0:T(8,128)(2,1)S(1)}, bf16[40,768]{1,0:T(8,128)(2,1)S(1)}, u32[]{:S(2)}, u32[]{:S(2)}) collective-permute-start(bf16[40,768]{1,0:T(8,128)(2,1)S(1)} %get-tuple-element.126.held_ref), channel_id=1, source_target_pairs={{0,28},{4,24},{8,20},{12,16},{16,12},{20,8},{24,4},{28,0},{1,29},{... | collective-permute-start | bytes 184328 | tf_op jit(solution)/shard_map/ppermute | solution.py:29
  89.1 10.6 %collective-permute-start.27 = (bf16[40,768]{1,0:T(8,128)(2,1)S(1)}, bf16[40,768]{1,0:T(8,128)(2,1)S(1)}, u32[]{:S(2)}, u32[]{:S(2)}) collective-permute-start(bf16[40,768]{1,0:T(8,128)(2,1)S(1)} %get-tuple-element.133), channel_id=1, source_target_pairs={{0,16},{4,20},{8,24},{12,28},{16,0},{20,4},{24,8},{28,12},{1,17},{... | collective-permute-start | bytes 184328 | tf_op jit(solution)/shard_map/ppermute | solution.py:29
  90.3 9.9 %collective-permute-start.28 = (bf16[40,768]{1,0:T(8,128)(2,1)S(1)}, bf16[40,768]{1,0:T(8,128)(2,1)S(1)}, u32[]{:S(2)}, u32[]{:S(2)}) collective-permute-start(bf16[40,768]{1,0:T(8,128)(2,1)S(1)} %get-tuple-element.134), channel_id=1, source_target_pairs={{0,20},{4,16},{8,28},{12,24},{16,4},{20,0},{24,12},{28,8},{1,21},{... | collective-permute-start | bytes 184328 | tf_op jit(solution)/shard_map/ppermute | solution.py:29
  92.3 7.9 %collective-permute-start.29 = (bf16[40,768]{1,0:T(8,128)(2,1)S(1)}, bf16[40,768]{1,0:T(8,128)(2,1)S(1)}, u32[]{:S(2)}, u32[]{:S(2)}) collective-permute-start(bf16[40,768]{1,0:T(8,128)(2,1)S(1)} %get-tuple-element.135), channel_id=1, source_target_pairs={{0,24},{4,28},{8,16},{12,20},{16,8},{20,12},{24,0},{28,4},{1,25},{... | collective-permute-start | bytes 184328 | tf_op jit(solution)/shard_map/ppermute | solution.py:29
  100.6 11.3 %collective-permute-start.31 = (bf16[256,768]{1,0:T(8,128)(2,1)S(1)}, bf16[256,768]{1,0:T(8,128)(2,1)}, u32[]{:S(2)}, u32[]{:S(2)}) collective-permute-start(bf16[256,768]{1,0:T(8,128)(2,1)S(1)} %gather_grad.1.own_ref), channel_id=1, source_target_pairs={{0,1},{1,0},{2,3},{3,2},{4,5},{5,4},{6,7},{7,6},{8,9},{9,8},{10,11... | collective-permute-start | bytes 1179656 | tf_op jit(solution)/shard_map/ppermute | solution.py:29
  102.0 9.9 %copy-start.3 = (bf16[256,768]{1,0:T(8,128)(2,1)S(1)}, bf16[256,768]{1,0:T(8,128)(2,1)}, u32[]{:S(2)}) copy-start(bf16[256,768]{1,0:T(8,128)(2,1)} %cot_ref.1) | copy-start | bytes 1179652
  103.5 30.2 %all-to-all-start.1 = ((bf16[8,40,768]{2,1,0:T(8,128)(2,1)}), bf16[8,40,768]{2,1,0:T(8,128)(2,1)S(1)}, u32[]{:S(2)}, u32[]{:S(2)}) async-start(bf16[8,40,768]{2,1,0:T(8,128)(2,1)} %join_out.1.held_ref), calls=%async_computation.1 | async-start | bytes 983040 | tf_op jit(solution)/shard_map/all_to_all | solution.py:580
  114.2 1.7 %collective-permute-start.32 = (bf16[256,768]{1,0:T(8,128)(2,1)S(1)}, bf16[256,768]{1,0:T(8,128)(2,1)S(1)}, u32[]{:S(2)}, u32[]{:S(2)}) collective-permute-start(bf16[256,768]{1,0:T(8,128)(2,1)S(1)} %get-tuple-element.136.own_ref), channel_id=1, source_target_pairs={{0,2},{2,0},{1,3},{3,1},{4,6},{6,4},{5,7},{7,5},{8,10},{10,8},{9,1... | collective-permute-start | bytes 1179656 | tf_op jit(solution)/shard_map/ppermute | solution.py:29
  122.5 12.1 %collective-permute-start.33 = (bf16[384,384]{1,0:T(8,128)(2,1)}, bf16[384,384]{1,0:T(8,128)(2,1)}, u32[]{:S(2)}, u32[]{:S(2)}) collective-permute-start(bf16[384,384]{1,0:T(8,128)(2,1)} %get-tuple-element.153), channel_id=1, source_target_pairs={{0,4},{4,0},{8,12},{12,8},{16,20},{20,16},{24,28},{28,24},{1,5},{5... | collective-permute-start | bytes 884744 | tf_op jit(solution)/shard_map/ppermute | solution.py:29
  135.0 12.4 %copy-start.16 = (f32[416,384]{1,0:T(8,128)S(1)}, f32[416,384]{1,0:T(8,128)}, u32[]{:S(2)}) copy-start(f32[416,384]{1,0:T(8,128)} %copy-done.15) | copy-start | bytes 1916932
  136.1 5.3 %collective-permute-start.35 = (bf16[256,768]{1,0:T(8,128)(2,1)S(1)}, bf16[256,768]{1,0:T(8,128)(2,1)S(1)}, u32[]{:S(2)}, u32[]{:S(2)}) collective-permute-start(bf16[256,768]{1,0:T(8,128)(2,1)S(1)} %get-tuple-element.158), channel_id=1, source_target_pairs={{0,2},{2,0},{1,3},{3,1},{4,6},{6,4},{5,7},{7,5},{8,10},{10,8},{9,1... | collective-permute-start | bytes 1179656 | tf_op jit(solution)/shard_map/ppermute | solution.py:29
  136.2 11.2 %collective-permute-start.36 = (bf16[416,384]{1,0:T(8,128)(2,1)S(1)}, bf16[416,384]{1,0:T(8,128)(2,1)S(1)}, u32[]{:S(2)}, u32[]{:S(2)}) collective-permute-start(bf16[416,384]{1,0:T(8,128)(2,1)S(1)} %get-tuple-element.162), channel_id=1, source_target_pairs={{0,4},{4,0},{8,12},{12,8},{16,20},{20,16},{24,28},{28,24},{1,5},{5... | collective-permute-start | bytes 958472 | tf_op jit(solution)/shard_map/ppermute | solution.py:29
  137.0 6.3 %collective-permute-start.37 = (bf16[96,384]{1,0:T(8,128)(2,1)S(1)}, bf16[96,384]{1,0:T(8,128)(2,1)S(1)}, u32[]{:S(2)}, u32[]{:S(2)}) collective-permute-start(bf16[96,384]{1,0:T(8,128)(2,1)S(1)} %get-tuple-element.159.held_ref), channel_id=1, source_target_pairs={{0,8},{4,12},{8,0},{12,4},{16,24},{20,28},{24,16},{28,20},{1,9},{5... | collective-permute-start | bytes 221192 | tf_op jit(solution)/shard_map/ppermute | solution.py:29
  138.7 8.7 %collective-permute-start.38 = (bf16[96,384]{1,0:T(8,128)(2,1)S(1)}, bf16[96,384]{1,0:T(8,128)(2,1)S(1)}, u32[]{:S(2)}, u32[]{:S(2)}) collective-permute-start(bf16[96,384]{1,0:T(8,128)(2,1)S(1)} %get-tuple-element.164), channel_id=1, source_target_pairs={{0,16},{4,20},{8,24},{12,28},{16,0},{20,4},{24,8},{28,12},{1,17},{... | collective-permute-start | bytes 221192 | tf_op jit(solution)/shard_map/ppermute | solution.py:29
  139.4 8.0 %collective-permute-start.39 = (bf16[96,384]{1,0:T(8,128)(2,1)S(1)}, bf16[96,384]{1,0:T(8,128)(2,1)S(1)}, u32[]{:S(2)}, u32[]{:S(2)}) collective-permute-start(bf16[96,384]{1,0:T(8,128)(2,1)S(1)} %get-tuple-element.165), channel_id=1, source_target_pairs={{0,24},{4,28},{8,16},{12,20},{16,8},{20,12},{24,0},{28,4},{1,25},{... | collective-permute-start | bytes 221192 | tf_op jit(solution)/shard_map/ppermute | solution.py:29
  141.4 12.2 %collective-permute-start.34 = (bf16[128,768]{1,0:T(8,128)(2,1)S(1)}, bf16[128,768]{1,0:T(8,128)(2,1)S(1)}, u32[]{:S(2)}, u32[]{:S(2)}) collective-permute-start(bf16[128,768]{1,0:T(8,128)(2,1)S(1)} %get-tuple-element.157), channel_id=1, source_target_pairs={{0,1},{1,0},{2,3},{3,2},{4,5},{5,4},{6,7},{7,6},{8,9},{9,8},{10,11... | collective-permute-start | bytes 589832 | tf_op jit(solution)/shard_map/ppermute | solution.py:29
  142.6 12.3 %copy-start.12 = (bf16[640,768]{1,0:T(8,128)(2,1)S(1)}, bf16[640,768]{1,0:T(8,128)(2,1)}, u32[]{:S(2)}) copy-start(bf16[640,768]{1,0:T(8,128)(2,1)} %copy-done.11) | copy-start | bytes 2949124
  147.4 7.5 %copy-start.5 = (f32[640,1]{1,0:T(8,128)S(1)}, f32[640,1]{1,0:T(8,128)}, u32[]{:S(2)}) copy-start(f32[640,1]{1,0:T(8,128)} %copy-done.4) | copy-start | bytes 7684
  147.4 7.5 %copy-start.8 = (bf16[640,768]{1,0:T(8,128)(2,1)S(1)}, bf16[640,768]{1,0:T(8,128)(2,1)}, u32[]{:S(2)}) copy-start(bf16[640,768]{1,0:T(8,128)(2,1)} %copy-done.7) | copy-start | bytes 2949124
  147.4 7.5 %copy-start.10 = (bf16[640,768]{1,0:T(8,128)(2,1)S(1)}, bf16[640,768]{1,0:T(8,128)(2,1)}, u32[]{:S(2)}) copy-start(bf16[640,768]{1,0:T(8,128)(2,1)} %copy-done.9) | copy-start | bytes 2949124
  148.1 10.6 %collective-permute-start.40 = (bf16[128,768]{1,0:T(8,128)(2,1)S(1)}, bf16[128,768]{1,0:T(8,128)(2,1)S(1)}, u32[]{:S(2)}, u32[]{:S(2)}) collective-permute-start(bf16[128,768]{1,0:T(8,128)(2,1)S(1)} %get-tuple-element.167), channel_id=1, source_target_pairs={{0,1},{1,0},{2,3},{3,2},{4,5},{5,4},{6,7},{7,6},{8,9},{9,8},{10,11... | collective-permute-start | bytes 589832 | tf_op jit(solution)/shard_map/ppermute | solution.py:29
  149.2 10.4 %collective-permute-start.41 = (bf16[128,384]{1,0:T(8,128)(2,1)S(1)}, bf16[128,384]{1,0:T(8,128)(2,1)S(1)}, u32[]{:S(2)}, u32[]{:S(2)}) collective-permute-start(bf16[128,384]{1,0:T(8,128)(2,1)S(1)} %get-tuple-element.170.held_ref), channel_id=1, source_target_pairs={{0,8},{4,12},{8,0},{12,4},{16,24},{20,28},{24,16},{28,20},{1,9},{5... | collective-permute-start | bytes 294920 | tf_op jit(solution)/shard_map/ppermute | solution.py:29
  150.8 9.4 %collective-permute-start.42 = (bf16[128,384]{1,0:T(8,128)(2,1)S(1)}, bf16[128,384]{1,0:T(8,128)(2,1)S(1)}, u32[]{:S(2)}, u32[]{:S(2)}) collective-permute-start(bf16[128,384]{1,0:T(8,128)(2,1)S(1)} %get-tuple-element.171), channel_id=1, source_target_pairs={{0,16},{4,20},{8,24},{12,28},{16,0},{20,4},{24,8},{28,12},{1,17},{... | collective-permute-start | bytes 294920 | tf_op jit(solution)/shard_map/ppermute | solution.py:29
  151.5 8.7 %collective-permute-start.43 = (bf16[128,384]{1,0:T(8,128)(2,1)S(1)}, bf16[128,384]{1,0:T(8,128)(2,1)S(1)}, u32[]{:S(2)}, u32[]{:S(2)}) collective-permute-start(bf16[128,384]{1,0:T(8,128)(2,1)S(1)} %get-tuple-element.172), channel_id=1, source_target_pairs={{0,24},{4,28},{8,16},{12,20},{16,8},{20,12},{24,0},{28,4},{1,25},{... | collective-permute-start | bytes 294920 | tf_op jit(solution)/shard_map/ppermute | solution.py:29
  160.8 1.4 collective-permute-start.44
  160.9 2.6 %collective-permute-start.46 = (f32[48,384]{1,0:T(8,128)S(1)}, f32[48,384]{1,0:T(8,128)S(1)}, u32[]{:S(2)}, u32[]{:S(2)}) collective-permute-start(f32[48,384]{1,0:T(8,128)S(1)} %get-tuple-element.179), channel_id=1, source_target_pairs={{0,2},{2,0},{1,3},{3,1},{4,6},{6,4},{5,7},{7,5},{8,10},{10,8},{9,1... | collective-permute-start | bytes 221192 | tf_op jit(solution)/shard_map/ppermute | solution.py:29
  162.2 4.2 %collective-permute-start.45 = (f32[32,384]{1,0:T(8,128)S(1)}, f32[32,384]{1,0:T(8,128)S(1)}, u32[]{:S(2)}, u32[]{:S(2)}) collective-permute-start(f32[32,384]{1,0:T(8,128)S(1)} %slice_add_fusion), channel_id=1, source_target_pairs={{0,1},{1,0},{2,3},{3,2},{4,5},{5,4},{6,7},{7,6},{8,9},{9,8},{10,11... | collective-permute-start | bytes 147464 | tf_op jit(solution)/shard_map/ppermute | solution.py:29
  (17 other events, 28.6 us)

commit v4 on v3

--- a/solution.py
+++ b/solution.py
@@ -12,7 +12,8 @@
 FLOPS1 = 0
 FLOPS2 = 0
 DIRECT = 8
-TILE = 128
+FORWARD_TILE = 256
+BACK_TILE = 512
 
 norm_eps = 1e-06
 masked_value = -1e30
@@ -160,7 +161,7 @@
     seq = x_ref.shape[0]
     width = heads * HD
     half = seq // GROUP
-    span = seq + TILE
+    span = seq + FORWARD_TILE
     rows = pieces[0].shape[0]
     for i, piece in enumerate(pieces):
         start = 0 if parts == 1 else pl.multiple_of((me ^ i) * rows, rows)
@@ -177,17 +178,17 @@
         at = h * HD
         key = qkv_ref[:, width + at : width + at + HD]
         value = qkv_ref[:, 2 * width + at : 2 * width + at + HD]
-        for i in range(0, seq, TILE):
-            base = seq - TILE - i
-            seg = jnp.broadcast_to(vec_ref[h : h + 1, base : base + span], (TILE, span))
-            bias = pltpu.roll(seg, span - TILE + 1, 1, stride=1, stride_axis=0)[:, :seq]
-            scores = mm_bt(qkv_ref[i : i + TILE, at : at + HD], key) * HD**-0.5 + bias
-            scores = jnp.where(row_docs[i : i + TILE, :] == col_docs[...], scores, masked_value)
+        for i in range(0, seq, FORWARD_TILE):
+            base = seq - FORWARD_TILE - i
+            seg = jnp.broadcast_to(vec_ref[h : h + 1, base : base + span], (FORWARD_TILE, span))
+            bias = pltpu.roll(seg, span - FORWARD_TILE + 1, 1, stride=1, stride_axis=0)[:, :seq]
+            scores = mm_bt(qkv_ref[i : i + FORWARD_TILE, at : at + HD], key) * HD**-0.5 + bias
+            scores = jnp.where(row_docs[i : i + FORWARD_TILE, :] == col_docs[...], scores, masked_value)
             peak = jnp.max(scores, axis=1, keepdims=True)
             exp_scores = jnp.exp(scores - peak)
             probs = exp_scores / jnp.sum(exp_scores, axis=1, keepdims=True)
-            probs_refs[h][i : i + TILE, :] = probs.astype(bf16)
-            mixed_ref[i : i + TILE, at : at + HD] = mm(probs.astype(bf16), value).astype(bf16)
+            probs_refs[h][i : i + FORWARD_TILE, :] = probs.astype(bf16)
+            mixed_ref[i : i + FORWARD_TILE, at : at + HD] = mm(probs.astype(bf16), value).astype(bf16)
     keep_ref[...] = mixed_ref[pl.ds(pl.multiple_of(core * half, half), half), :]
     send_ref[...] = mixed_ref[pl.ds(pl.multiple_of((1 - core) * half, half), half), :]
 
@@ -325,28 +326,28 @@
     seq = qkv_ref.shape[0]
     width = heads * HD
     here = len(probs) * HD
-    span = seq + TILE
+    span = seq + BACK_TILE
     flip = (
-        lax.broadcasted_iota(jnp.int32, (TILE, TILE), 0)
-        + lax.broadcasted_iota(jnp.int32, (TILE, TILE), 1)
-        == TILE - 1
+        lax.broadcasted_iota(jnp.int32, (BACK_TILE, BACK_TILE), 0)
+        + lax.broadcasted_iota(jnp.int32, (BACK_TILE, BACK_TILE), 1)
+        == BACK_TILE - 1
     ).astype(bf16)
     for h, probs_ref in enumerate(probs):
         at = (first + h) * HD
         to = h * HD
         key = qkv_ref[:, width + at : width + at + HD]
         value = qkv_ref[:, 2 * width + at : 2 * width + at + HD]
-        for i in range(0, seq, TILE):
-            probs_rows = probs_ref[i : i + TILE, :].astype(f32)
-            grad_probs = mm_bt(gm_ref[i : i + TILE, at : at + HD], value)
+        for i in range(0, seq, BACK_TILE):
+            probs_rows = probs_ref[i : i + BACK_TILE, :].astype(f32)
+            grad_probs = mm_bt(gm_ref[i : i + BACK_TILE, at : at + HD], value)
             inner = jnp.sum(probs_rows * grad_probs, axis=1, keepdims=True)
             grad_scores = (probs_rows * (grad_probs - inner)).astype(bf16)
-            ds_ref[i : i + TILE, :] = grad_scores
-            dqkv_ref[i : i + TILE, to : to + HD] = (mm(grad_scores, key) * HD**-0.5).astype(bf16)
+            ds_ref[i : i + BACK_TILE, :] = grad_scores
+            dqkv_ref[i : i + BACK_TILE, to : to + HD] = (mm(grad_scores, key) * HD**-0.5).astype(bf16)
             flipped = mm(flip, grad_scores)
-            padded = jnp.concatenate([flipped, jnp.zeros((TILE, TILE), f32)], axis=1)
+            padded = jnp.concatenate([flipped, jnp.zeros((BACK_TILE, BACK_TILE), f32)], axis=1)
             skewed = pltpu.roll(padded, 0, 1, stride=1, stride_axis=0)
-            base = seq - TILE - i
+            base = seq - BACK_TILE - i
             row = first + h
             diag_ref[row : row + 1, base : base + span] += jnp.sum(skewed, axis=0, keepdims=True)
         dqkv_ref[:, here + to : here + to + HD] = (
@@ -369,34 +370,18 @@
         outs[1][at, :] = gw_ref[there, :].astype(bf16)
 
 
-def fetch(sources, targets, sems):
-    copies = [
-        pltpu.make_async_copy(a, b, sems.at[i]) for i, (a, b) in enumerate(zip(sources, targets))
-    ]
-    for copy in copies:
-        copy.start()
-    return copies
-
-
 def first_back_kernel(heads, parts, ids, own_ref, other_ref, gain_ref, *refs):
-    far = refs[:5]
-    gm_ref, dqkv_ref, diag_ref, seq_ref, *outs = refs[5:-9]
-    ga_ref, ds_ref, gw_ref = refs[-9:-6]
-    wo_ref, qkv_ref, probs_ref, x_ref, mixed_ref = refs[-6:-1]
-    copies = fetch(far, refs[-6:-1], refs[-1])
+    wo_ref, qkv_ref, probs_ref, x_ref, mixed_ref = refs[:5]
+    gm_ref, dqkv_ref, diag_ref, seq_ref, *outs = refs[5:-3]
+    ga_ref, ds_ref, gw_ref = refs[-3:]
     core = ids[0]
     half = own_ref.shape[0]
     ga_ref[pl.ds(pl.multiple_of(core * half, half), half), :] = own_ref[...]
     ga_ref[pl.ds(pl.multiple_of((1 - core) * half, half), half), :] = other_ref[...]
-    copies[0].wait()
     gm_ref[...] = mm(ga_ref[...], wo_ref[...]).astype(bf16)
     diag_ref[...] = jnp.zeros_like(diag_ref)
-    copies[1].wait()
-    copies[2].wait()
     heads_back(heads, 0, qkv_ref, gm_ref, [probs_ref], dqkv_ref, diag_ref, ds_ref)
     cut = dqkv_ref.shape[1]
-    copies[3].wait()
-    copies[4].wait()
     seq_ref[...] = (unit_rows(x_ref[...]) * gain_ref[...]).astype(bf16)
     gw_ref[:, :cut] = mm_at(seq_ref[...], dqkv_ref[...])
     gw_ref[:, cut:] = mm_at(ga_ref[...], mixed_ref[...])
@@ -407,17 +392,13 @@
     heads, parts, ids, gm_ref, first_ref, diag_in_ref, hot_ref, seq_ref, gain_ref, router_ref, *refs
 ):
     count = heads + 2
-    far, near = refs[:count], refs[-count - 1 : -1]
-    qkv_ref, *probs, x_ref, w_ref = near
-    copies = fetch(far, near, refs[-1])
-    refs = refs[count : -count - 1]
-    keep_ref, send_ref, *outs = refs[:-6]
-    diag_ref, dqkv_ref, all_ref, ds_ref, gw_ref, small_ref = refs[-6:]
+    qkv_ref, *probs, x_ref, w_ref = refs[:count]
+    refs = refs[count:]
+    keep_ref, send_ref, small_ref, *outs = refs[:-5]
+    diag_ref, dqkv_ref, all_ref, ds_ref, gw_ref = refs[-5:]
     core, me, side = ids[0], ids[1], ids[2]
     half = keep_ref.shape[0]
     diag_ref[...] = diag_in_ref[...]
-    for copy in copies[:heads]:
-        copy.wait()
     heads_back(heads, 1, qkv_ref, gm_ref, probs, dqkv_ref, diag_ref, ds_ref)
     gw_ref[...] = mm_at(seq_ref[...], dqkv_ref[...])
     send_rows(parts, me, gw_ref, outs)
@@ -426,8 +407,6 @@
         at = i * heads * HD
         all_ref[:, at : at + HD] = first_ref[:, i * HD : (i + 1) * HD]
         all_ref[:, at + HD : at + heads * HD] = dqkv_ref[:, i * rest : (i + 1) * rest]
-    for copy in copies[heads:]:
-        copy.wait()
     gain = jnp.zeros((1, x_ref.shape[1]), f32)
     for place, mine in ((core, True), (1 - core, False)):
         rows = pl.ds(pl.multiple_of(place * half, half), half)
@@ -448,23 +427,22 @@
         small_ref[2 + experts : 2 + experts + heads, i * lanes : (i + 1) * lanes] = jnp.where(
             side * GROUP + core == i, bias[:heads, :], 0.0
         )
-    if parts == 1:
-        outs[1][...] = small_ref[...]
-        return
+
+
+def fold_kernel(
+    keep_ref, got_ref, small_ref, small_got_ref, second_ref, grad_ref, returned_ref,
+    second_out, grad_out, returned_out, small_out, own_ref, *sends
+):
+    grad_out[...] = grad_ref[...]
+    returned_out[...] = returned_ref[...]
+    end, cols = second_ref.shape
     high = small_ref.shape[0]
-    end = outs[0].shape[0] - 2 * high
-    cols = outs[0].shape[1]
+    second_out[:end, :] = second_ref[...]
     for i in range(2):
-        low = small_ref[:, i * cols : (i + 1) * cols].astype(bf16)
-        outs[0][end + i * high : end + (i + 1) * high, :] = low.astype(f32)
-        outs[1][end + i * high : end + (i + 1) * high, :] = low
-
-
-def fold_kernel(parts, keep_ref, got_ref, *refs):
-    count = (len(refs) - parts // 2) // 2
-    passed, (own_ref, *sends) = refs[:count], refs[2 * count :]
-    for source, target in zip(passed, refs[count:]):
-        target[...] = source[...]
+        at = slice(i * cols, (i + 1) * cols)
+        low = (small_ref[:, at] + small_got_ref[:, at]).astype(bf16)
+        second_out[end + i * high : end + (i + 1) * high, :] = low
+        small_out[i * high : (i + 1) * high, :] = low.astype(f32)
     total = keep_ref[...] + got_ref[...].astype(f32)
     rows = own_ref.shape[0]
     own_ref[...] = total[:rows, :]
@@ -483,14 +461,14 @@
     send_ref[:rows, :] = quarters(refs, pl.ds(pl.multiple_of((1 - core) * rows, rows), rows))
 
 
-def fold_second_kernel(small_rows, ids, keep_ref, got_ref, *refs):
+def fold_second_kernel(ids, keep_ref, got_ref, small_ref, grad_ref, *refs):
     first = refs[:4]
-    refs[5][...] = refs[4][...]
-    keep_one_ref, send_one_ref, own_ref, *sends = refs[6:]
-    total = keep_ref[...] + got_ref[...].astype(f32)
+    grad_out, keep_one_ref, send_one_ref, own_ref, *sends = refs[4:]
+    grad_out[...] = grad_ref[...]
+    end = keep_ref.shape[0]
+    total = keep_ref[...] + got_ref[:end, :].astype(f32)
+    small = (small_ref[...] + got_ref[end:, :].astype(f32)).astype(bf16)
     rows = keep_one_ref.shape[0] * 2
-    end = total.shape[0] - small_rows
-    small = total[end:, :].astype(bf16)
     for i, block in enumerate((own_ref, *sends)):
         block[:rows, :] = total[i * rows : (i + 1) * rows, :].astype(block.dtype)
         block[rows:, :] = small.astype(block.dtype)
@@ -505,7 +483,8 @@
     send_ref[rows:, :] = quarters(second, slice(2 * rows, second[0].shape[0]))
 
 
-def columns_kernel(heads, ids, keep_one, got_one, keep_two, got_two, *outs):
+def columns_kernel(heads, ids, keep_one, got_one, keep_two, got_two, *refs):
+    outs = refs[:4] if len(refs) == 4 else refs[1:5]
     core = ids[0]
     rows = keep_one.shape[0]
     cols = heads * HD
@@ -519,6 +498,22 @@
             outs[i][:, at : at + HD] = one[:, i * HD : (i + 1) * HD]
             outs[i][:, at + HD : at + cols] = two[:, i * rest : (i + 1) * rest]
         outs[3][:, at : at + cols] = one[:, 3 * HD : 3 * HD + cols]
+    if len(refs) == 4:
+        return
+    gain_one_ref, gain_two_ref, router_ref, bias_ref = refs[5:]
+    small = refs[0][rows:, :] + got_two[rows:, :]
+    high = small.shape[0] // 2
+    wide = jnp.concatenate([small[:high, :], small[high:, :]], axis=1)
+    experts = router_ref.shape[0]
+    gain_one_ref[...] = wide[0:1, :]
+    gain_two_ref[...] = wide[1:2, :]
+    router_ref[...] = wide[2 : 2 + experts, :]
+    for i in range(2 * GROUP):
+        for h in range(heads):
+            row = 2 + experts + h
+            bias_ref[i * heads + h : i * heads + h + 1, :] = wide[
+                row : row + 1, i * 128 : i * 128 + bias_ref.shape[1]
+            ]
 
 
 def input_kernel(keep_ref, got_ref, grad_ref, x_ref, gain_ref, out_ref):
@@ -591,7 +586,7 @@
     piece = in_order(core == 0, share_kept, across(share_sent, "core", 1))
     if direct:
         pieces = {0: piece}
-        for i in (2, 4, 6):
+        for i in (4, 6, 2):
             pieces[i] = across(piece, "node", i)
         for i in (0, 2, 4, 6):
             pieces[i + 1] = across(pieces[i], "node", 1)
@@ -750,6 +745,14 @@
     out_back = trade_natural(out_slots.reshape(slots, width)).reshape(slots, width)
     half_block = (own_rows, width)
 
+    kept = [weights, wo_far, x_seq, qkv, mixed, *probs]
+    weights, wo, x_seq, qkv, mixed, *probs = call(
+        functools.partial(move_kernel, len(kept)),
+        "unpark",
+        [out(a.shape, a.dtype) for a in kept],
+        [*(Far(a) for a in kept), Raw(out_slots)],
+        scratch=[pltpu.SemaphoreType.DMA((len(kept),))],
+    )
     grad_hidden, grad_attended, gain_two_part = call(
         hidden_back_kernel,
         "hidden_back",
@@ -761,7 +764,7 @@
             Near(grad_normed_two_got),
             cotangent,
             gain_second,
-            Raw(out_slots),
+            Raw(mixed),
         ],
         smem=1,
         scratch=[pltpu.VMEM((block_rows, width), f32)],
@@ -771,12 +774,11 @@
     other_chunk = 3 * (cols - HD)
     small_rows = -(-(2 + experts + heads) // 16) * 16
     if direct:
-        tall = width // 2 + 2 * small_rows
         first_shapes = [out((width // 2, chunk), t) for t in (f32, bf16)]
-        second_shapes = [out((tall, other_chunk), t) for t in (f32, bf16)]
+        second_shapes = [out((width // 2, other_chunk), t) for t in (f32, bf16)]
     else:
         first_shapes = [out((width, chunk), bf16)]
-        second_shapes = [out((width, other_chunk), bf16), out((small_rows, width), f32)]
+        second_shapes = [out((width, other_chunk), bf16)]
     grad_mixed, first_dqkv, diagonals, normed_seq, *first_chunk = call(
         functools.partial(first_back_kernel, heads, parts),
         "first_back",
@@ -792,7 +794,7 @@
             grad_attended,
             Near(grad_attended_other),
             gain_first,
-            *(Far(a) for a in (wo_far, qkv, probs[0], x_seq, mixed)),
+            *(wo, qkv, probs[0], x_seq, mixed),
         ],
         smem=1,
         flops=FLOPS1,
@@ -800,16 +802,15 @@
             pltpu.VMEM((seq, width), bf16),
             pltpu.VMEM((seq, seq), bf16),
             pltpu.VMEM((width, chunk), f32),
-            *(pltpu.VMEM(a.shape, bf16) for a in (wo_far, qkv, probs[0], x_seq, mixed)),
-            pltpu.SemaphoreType.DMA((5,)),
-        ],
-    )
-    grad_kept, grad_sent, *second_chunk = call(
+        ],
+    )
+    grad_kept, grad_sent, small, *second_chunk = call(
         functools.partial(second_back_kernel, heads, parts),
         "second_back",
         [
             out((block_rows, width), f32),
             out((block_rows, width), bf16),
+            out((small_rows, width), f32),
             *second_shapes,
         ],
         [
@@ -821,7 +822,7 @@
             normed_seq,
             Near(gain_two_part),
             Near(router_part),
-            *(Far(a) for a in (qkv, *probs[1:], x_seq, weights)),
+            *(qkv, *probs[1:], x_seq, weights),
         ],
         smem=1,
         flops=FLOPS2,
@@ -831,9 +832,6 @@
             pltpu.VMEM((seq, 3 * cols), bf16),
             pltpu.VMEM((seq, seq), bf16),
             pltpu.VMEM((width, other_chunk), f32),
-            pltpu.VMEM((small_rows, width), f32),
-            *(pltpu.VMEM(a.shape, bf16) for a in (qkv, *probs[1:], x_seq, weights)),
-            pltpu.SemaphoreType.DMA((heads + 2,)),
         ],
     )
 
@@ -847,16 +845,27 @@
     )
     part = out((shard_rows, chunk), f32)
     if direct:
-        passed = [second_chunk[1], grad_sent, returned_sent]
-        second_sent, grad_sent, returned_sent, own_one, *send_one = call(
-            functools.partial(fold_kernel, parts),
+        tall = width // 2 + 2 * small_rows
+        second_sent, grad_sent, returned_sent, small, own_one, *send_one = call(
+            fold_kernel,
             "fold_first",
             [
-                *(out(a.shape, a.dtype) for a in passed),
+                out((tall, chunk), bf16),
+                out(grad_sent.shape, bf16),
+                out(returned_sent.shape, bf16),
+                out((2 * small_rows, chunk), f32),
                 out((node_rows, chunk), f32),
                 *([out((node_rows, chunk), bf16)] * 3),
             ],
-            [first_chunk[0], across(first_chunk[1], "node", 1), *passed],
+            [
+                first_chunk[0],
+                across(first_chunk[1], "node", 1),
+                small,
+                across(small, "tensor", 1),
+                second_chunk[1],
+                grad_sent,
+                returned_sent,
+            ],
         )
         got_one = [across(b, "node", 2 * i + 2) for i, b in enumerate(send_one)]
         first_done = send_one[0]
@@ -880,16 +889,17 @@
     if direct:
         high = node_rows + 2 * small_rows
         grad_normed_sent, kept_one, sent_one, own_two, *send_two = call(
-            functools.partial(fold_second_kernel, 2 * small_rows),
+            fold_second_kernel,
             "fold_second",
             [out(half_block, bf16), part, part, out((high, chunk), f32), *([out((high, chunk), bf16)] * 3)],
             [
                 ids,
                 second_chunk[0],
                 across(second_sent, "node", 1),
+                small,
+                grad_normed_sent,
                 own_one,
                 *got_one,
-                grad_normed_sent,
             ],
             smem=1,
         )
@@ -938,30 +948,36 @@
         )
     got_one = across(sent_one, "core", 1)
     got_two = across(sent_two, "core", 1)
+    small_outs = []
     if direct:
-        small = sent_two[shard_rows:, :] + got_two[shard_rows:, :]
-        small = small + across(small, "tensor", 1)
-        small = jnp.concatenate([small[:small_rows], small[small_rows:]], axis=1)
-    else:
-        small = lax.psum(second_chunk[1], ("node", "core", "tensor"))
+        small_outs = [
+            out((1, width), f32),
+            out((1, width), f32),
+            out((experts, width), f32),
+            out(bias_table.shape[::-1], f32),
+        ]
     weight_grads = call(
         functools.partial(columns_kernel, heads),
         "columns",
-        [out(w_query.shape, f32)] * 4,
-        [ids, kept_one, got_one, kept_two, got_two],
-        smem=1,
-    )
-
-    bias_rows = small[2 + experts : 2 + experts + heads, : 4 * 128].reshape(heads, 4, 128)
-    grad_bias = bias_rows[:, :, :bucket_count].transpose(2, 1, 0).reshape(bias_table.shape)
+        [out(w_query.shape, f32)] * 4 + small_outs,
+        [ids, kept_one, got_one, kept_two, got_two] + ([sent_two] if direct else []),
+        smem=1,
+    )
+    if direct:
+        sum_one, sum_two, sum_router, sum_bias = weight_grads[4:]
+    else:
+        small = lax.psum(small, ("node", "core", "tensor"))
+        sum_one, sum_two, sum_router = small[:1], small[1:2], small[2 : 2 + experts]
+        sum_bias = small[2 + experts : 2 + experts + heads, : 4 * 128].reshape(heads, 4, 128)
+        sum_bias = sum_bias[:, :, :bucket_count].transpose(1, 0, 2).reshape(bias_table.shape[::-1])
     return (
         activations,
         input_grad,
-        small[0],
-        *weight_grads,
-        grad_bias,
-        small[1],
-        small[2 : 2 + experts].T,
+        sum_one[0],
+        *weight_grads[:4],
+        sum_bias.T,
+        sum_two[0],
+        sum_router.T,
         grad_w_up_here,
         grad_w_down_here,
     )

time: 169 us -> 161 us (0.953)
  Pallas kernels: 49 us -> 45.6 us
  waiting for transfers between devices: 44.2 us -> 41.9 us
    pallas_call x25 -> x26, Pallas kernels: 49 us -> 45.6 us  [call(): pl.pallas_call(body, name=name, out_shape=[space[type(o)](x.shape, x.dtyp...]
    ppermute x47, waiting for transfers between devices: 44.2 us -> 41.9 us  [across(): lax.ppermute(shard, axis, [(i, i ^ bits) for i in range(lax.axis_size(axi...]
    unnamed x71 -> x81, local copies, waits for them, and re-layouts: 8 us -> 7.67 us
  transfers between devices with their start and end apart: 49 -> 49, of which waited for: 18 -> 18; matrix products, arithmetic and copies ran while one was open for 2% -> 2% of each run, Pallas kernels for 20% -> 18%
where the time goes in v4:
time: 161 us
  starting transfers between devices  59.4 us (37%)
  Pallas kernels  45.6 us (28%)
  waiting for transfers between devices  41.9 us (26%)
  local copies, waits for them, and re-layouts  8.74 us (5%)
  other arithmetic  3.42 us (2%)
    ppermute x47, starting transfers between devices, across(): lax.ppermute(shard, axis, [(i, i ^ bits) for i in range(lax.axis_size(axi...  52.1 us
    pallas_call x26, Pallas kernels, call(): pl.pallas_call(body, name=name, out_shape=[space[type(o)](x.shape, x.dtyp...  45.6 us
    ppermute x47, waiting for transfers between devices, across(): lax.ppermute(shard, axis, [(i, i ^ bits) for i in range(lax.axis_size(axi...  41.9 us
    unnamed x81, local copies, waits for them, and re-layouts  7.67 us
    all_to_all x2, starting transfers between devices, trade_natural(): lax.all_to_all(stacked, 'node', split_axis=0, concat_axis=0, tiled=True)  7.37 us
  transfers between devices with their start and end apart: 49, of which 18 were waited for; matrix products, arithmetic and copies ran while one was open for 2% of the time, Pallas kernels for 18%

profile of v4, /device:TPU:0, one launch (start us, length us, event | category | flops | bytes accessed | tf_op | source)
XLA Modules:
  0.0 160.9 jit_solution(17716047429368335476)
XLA Ops:
  0.8 1.6 shares.1
  2.9 2.6 %collective-permute-start = (bf16[128,768]{1,0:T(8,128)(2,1)}, bf16[128,768]{1,0:T(8,128)(2,1)S(1)}, u32[]{:S(2)}, u32[]{:S(2)}) collective-permute-start(bf16[128,768]{1,0:T(8,128)(2,1)} %x_ref.1), channel_id=1, source_target_pairs={{0,1},{1,0},{2,3},{3,2},{4,5},{5,4},{6,7},{7,6},{8,9},{9,8},{10,11... | collective-permute-start | bytes 589832 | tf_op jit(solution)/shard_map/ppermute | solution.py:30
  6.2 1.6 collective-permute-start.2
  9.3 1.6 collective-permute-start.4
  10.8 2.6 %collective-permute-start.6 = (bf16[96,768]{1,0:T(8,128)(2,1)S(1)}, bf16[96,768]{1,0:T(8,128)(2,1)S(1)}, u32[]{:S(2)}, u32[]{:S(2)}) collective-permute-start(bf16[96,768]{1,0:T(8,128)(2,1)S(1)} %maximum_select_fusion.refs_0_), channel_id=1, source_target_pairs={{0,16},{4,20},{8,24},{12,28},{16,0},{20,4},{24,8},{28,12},{1,17},{... | collective-permute-start | bytes 442376 | tf_op jit(solution)/shard_map/ppermute | solution.py:30
  15.7 1.3 collective-permute-done.4.refs_2_
  17.5 7.3 %collective-permute-done.6.refs_4_ = bf16[96,768]{1,0:T(8,128)(2,1)S(1)} collective-permute-done((bf16[96,768]{1,0:T(8,128)(2,1)S(1)}, bf16[96,768]{1,0:T(8,128)(2,1)S(1)}, u32[]{:S(2)}, u32[]{:S(2)}) %collective-permute-start.6) | collective-permute-done | bytes 147488 | tf_op jit(solution)/shard_map/ppermute | solution.py:30
  25.4 1.5 collective-permute-start.9
  27.3 2.7 %collective-permute-done.7.refs_5_ = bf16[96,768]{1,0:T(8,128)(2,1)S(1)} collective-permute-done((bf16[96,768]{1,0:T(8,128)(2,1)S(1)}, bf16[96,768]{1,0:T(8,128)(2,1)S(1)}, u32[]{:S(2)}, u32[]{:S(2)}) %collective-permute-start.7) | collective-permute-done | bytes 147488 | tf_op jit(solution)/shard_map/ppermute | solution.py:30
  30.0 1.6 collective-permute-done.9.refs_7_
  31.5 5.2 %attend.1 = (bf16[768,768]{1,0:T(8,128)(2,1)S(1)}, bf16[768,192]{1,0:T(8,128)(2,1)S(1)}, bf16[512,768]{1,0:T(8,128)(2,1)S(1)}, bf16[512,576]{1,0:T(8,128)(2,1)S(...) custom-call(s32[3]{0:T(128)S(1)} %pad_add_fusion.ids, ...), custom_call_target="tpu_custom_call" | custom-call | tf_op jit(solution)/shard_map/attend/pallas_call | solution.py:55
  37.5 2.3 %park.1 = (bf16[768,768]{1,0:T(8,128)(2,1)}, bf16[768,192]{1,0:T(8,128)(2,1)}, bf16[512,768]{1,0:T(8,128)(2,1)}, bf16[512,576]{1,0:T(8,128)(2,1)}, bf16[512,192]...) custom-call(bf16[768,768]{1,0:T(8,128)(2,1)S(1)} %get-tuple-element.118.refs_0_, ...), custom_call_target="tpu_custom_call" | custom-call | tf_op jit(solution)/shard_map/park/pallas_call | solution.py:55
  41.0 1.1 cot_slots.1
  42.1 3.7 %all-to-all-start = ((bf16[8,40,768]{2,1,0:T(8,128)(2,1)}), bf16[8,40,768]{2,1,0:T(8,128)(2,1)S(1)}, u32[]{:S(2)}, u32[]{:S(2)}) async-start(bf16[8,40,768]{2,1,0:T(8,128)(2,1)} %bitcast.13), calls=%async_computation | async-start | bytes 983040 | tf_op jit(solution)/shard_map/all_to_all | solution.py:575
  45.8 5.6 %collective-permute-done.12.got_ref = bf16[256,768]{1,0:T(8,128)(2,1)S(1)} collective-permute-done((bf16[256,768]{1,0:T(8,128)(2,1)S(1)}, bf16[256,768]{1,0:T(8,128)(2,1)S(1)}, u32[]{:S(2)}, u32[]{:S(2)}) %collective-permute-start.12) | collective-permute-done | bytes 393248 | tf_op jit(solution)/shard_map/ppermute | solution.py:30
  52.1 1.0 copy-done.24
  53.1 1.2 dispatch.1
  54.8 1.1 collective-permute-start.14
  55.9 1.9 %collective-permute-start.15 = (bf16[40,768]{1,0:T(8,128)(2,1)S(1)}, bf16[40,768]{1,0:T(8,128)(2,1)S(1)}, u32[]{:S(2)}, u32[]{:S(2)}) collective-permute-start(bf16[40,768]{1,0:T(8,128)(2,1)S(1)} %get-tuple-element.130), channel_id=1, source_target_pairs={{0,12},{4,8},{8,4},{12,0},{16,28},{20,24},{24,20},{28,16},{1,13},{... | collective-permute-start | bytes 184328 | tf_op jit(solution)/shard_map/ppermute | solution.py:30
  57.8 1.8 %collective-permute-start.16 = (bf16[40,768]{1,0:T(8,128)(2,1)S(1)}, bf16[40,768]{1,0:T(8,128)(2,1)S(1)}, u32[]{:S(2)}, u32[]{:S(2)}) collective-permute-start(bf16[40,768]{1,0:T(8,128)(2,1)S(1)} %get-tuple-element.131), channel_id=1, source_target_pairs={{0,16},{4,20},{8,24},{12,28},{16,0},{20,4},{24,8},{28,12},{1,17},{... | collective-permute-start | bytes 184328 | tf_op jit(solution)/shard_map/ppermute | solution.py:30
  59.5 1.1 collective-permute-start.17
  60.7 2.4 %collective-permute-start.18 = (bf16[40,768]{1,0:T(8,128)(2,1)S(1)}, bf16[40,768]{1,0:T(8,128)(2,1)S(1)}, u32[]{:S(2)}, u32[]{:S(2)}) collective-permute-start(bf16[40,768]{1,0:T(8,128)(2,1)S(1)} %get-tuple-element.133), channel_id=1, source_target_pairs={{0,24},{4,28},{8,16},{12,20},{16,8},{20,12},{24,0},{28,4},{1,25},{... | collective-permute-start | bytes 184328 | tf_op jit(solution)/shard_map/ppermute | solution.py:30
  63.0 2.5 %collective-permute-start.19 = (bf16[40,768]{1,0:T(8,128)(2,1)}, bf16[40,768]{1,0:T(8,128)(2,1)S(1)}, u32[]{:S(2)}, u32[]{:S(2)}) collective-permute-start(bf16[40,768]{1,0:T(8,128)(2,1)} %get-tuple-element.134), channel_id=1, source_target_pairs={{0,28},{4,24},{8,20},{12,16},{16,12},{20,8},{24,4},{28,0},{1,29},{... | collective-permute-start | bytes 184328 | tf_op jit(solution)/shard_map/ppermute | solution.py:30
  65.9 2.9 %collective-permute-done.17 = bf16[40,768]{1,0:T(8,128)(2,1)S(1)} collective-permute-done((bf16[40,768]{1,0:T(8,128)(2,1)S(1)}, bf16[40,768]{1,0:T(8,128)(2,1)S(1)}, u32[]{:S(2)}, u32[]{:S(2)}) %collective-permute-start.17) | collective-permute-done | bytes 61472 | tf_op jit(solution)/shard_map/ppermute | solution.py:30
  68.9 1.4 collective-permute-done.19
  70.8 1.5 cots.1
  72.3 1.0 copy-done.7
  73.3 5.3 %expert.1 = (bf16[640,768]{1,0:T(8,128)(2,1)S(1)}, bf16[640,768]{1,0:T(8,128)(2,1)S(1)}, f32[640,1]{1,0:T(8,128)S(1)}, f32[320,768]{1,0:T(8,128)S(1)}, bf16[320,...) custom-call(s32[3]{0:T(128)S(1)} %pad_add_fusion.ids, ...), custom_call_target="tpu_custom_call" | custom-call | tf_op jit(solution)/shard_map/expert/pallas_call | solution.py:55
  78.8 1.7 %collective-permute-done.22.got_ref = bf16[320,768]{1,0:T(8,128)(2,1)S(1)} collective-permute-done((bf16[320,768]{1,0:T(8,128)(2,1)S(1)}, bf16[320,768]{1,0:T(8,128)(2,1)S(1)}, u32[]{:S(2)}, u32[]{:S(2)}) %collective-permute-start.22) | collective-permute-done | bytes 491552 | tf_op jit(solution)/shard_map/ppermute | solution.py:30
  80.6 1.0 expert_out.1
  81.8 1.5 collective-permute-start.24
  83.3 1.4 collective-permute-start.25
  85.3 2.7 %collective-permute-start.30 = (bf16[40,768]{1,0:T(8,128)(2,1)S(1)}, bf16[40,768]{1,0:T(8,128)(2,1)S(1)}, u32[]{:S(2)}, u32[]{:S(2)}) collective-permute-start(bf16[40,768]{1,0:T(8,128)(2,1)S(1)} %get-tuple-element.140.held_ref), channel_id=1, source_target_pairs={{0,28},{4,24},{8,20},{12,16},{16,12},{20,8},{24,4},{28,0},{1,29},{... | collective-permute-start | bytes 184328 | tf_op jit(solution)/shard_map/ppermute | solution.py:30
  88.0 1.2 collective-permute-start.27
  89.2 2.1 %collective-permute-start.28 = (bf16[40,768]{1,0:T(8,128)(2,1)S(1)}, bf16[40,768]{1,0:T(8,128)(2,1)S(1)}, u32[]{:S(2)}, u32[]{:S(2)}) collective-permute-start(bf16[40,768]{1,0:T(8,128)(2,1)S(1)} %get-tuple-element.148), channel_id=1, source_target_pairs={{0,20},{4,16},{8,28},{12,24},{16,4},{20,0},{24,12},{28,8},{1,21},{... | collective-permute-start | bytes 184328 | tf_op jit(solution)/shard_map/ppermute | solution.py:30
  91.3 1.8 %collective-permute-start.29 = (bf16[40,768]{1,0:T(8,128)(2,1)S(1)}, bf16[40,768]{1,0:T(8,128)(2,1)S(1)}, u32[]{:S(2)}, u32[]{:S(2)}) collective-permute-start(bf16[40,768]{1,0:T(8,128)(2,1)S(1)} %get-tuple-element.149), channel_id=1, source_target_pairs={{0,24},{4,28},{8,16},{12,20},{16,8},{20,12},{24,0},{28,4},{1,25},{... | collective-permute-start | bytes 184328 | tf_op jit(solution)/shard_map/ppermute | solution.py:30
  93.2 4.7 %collective-permute-done.27.refs_4_ = bf16[40,768]{1,0:T(8,128)(2,1)S(1)} collective-permute-done((bf16[40,768]{1,0:T(8,128)(2,1)S(1)}, bf16[40,768]{1,0:T(8,128)(2,1)S(1)}, u32[]{:S(2)}, u32[]{:S(2)}) %collective-permute-start.27) | collective-permute-done | bytes 61472 | tf_op jit(solution)/shard_map/ppermute | solution.py:30
  97.9 1.5 collective-permute-done.28.refs_5_
  99.7 1.5 collective-permute-start.31
  101.3 1.4 join_out.1.refs_8_
  102.7 3.7 %all-to-all-start.1 = ((bf16[8,40,768]{2,1,0:T(8,128)(2,1)}), bf16[8,40,768]{2,1,0:T(8,128)(2,1)S(1)}, u32[]{:S(2)}, u32[]{:S(2)}) async-start(bf16[8,40,768]{2,1,0:T(8,128)(2,1)} %join_out.1.refs_8_), calls=%async_computation.1 | async-start | bytes 983040 | tf_op jit(solution)/shard_map/all_to_all | solution.py:575
  106.4 2.5 %unpark.1 = (bf16[768,768]{1,0:T(8,128)(2,1)S(1)}, bf16[768,192]{1,0:T(8,128)(2,1)S(1)}, bf16[512,768]{1,0:T(8,128)(2,1)S(1)}, bf16[512,576]{1,0:T(8,128)(2,1)S(...) custom-call(bf16[768,768]{1,0:T(8,128)(2,1)} %get-tuple-element.150., ...), custom_call_target="tpu_custom_call" | custom-call | tf_op jit(solution)/shard_map/unpark/pallas_call | solution.py:55
  109.8 1.5 hidden_back.1
  112.1 1.7 %collective-permute-done.32.other_ref = bf16[256,768]{1,0:T(8,128)(2,1)S(1)} collective-permute-done((bf16[256,768]{1,0:T(8,128)(2,1)S(1)}, bf16[256,768]{1,0:T(8,128)(2,1)S(1)}, u32[]{:S(2)}, u32[]{:S(2)}) %collective-permute-start.32) | collective-permute-done | bytes 393248 | tf_op jit(solution)/shard_map/ppermute | solution.py:30
  113.8 3.8 %first_back.1 = (bf16[512,192]{1,0:T(8,128)(2,1)S(1)}, bf16[512,192]{1,0:T(8,128)(2,1)S(1)}, f32[8,1024]{1,0:T(8,128)S(1)}, bf16[512,768]{1,0:T(8,128)(2,1)S(1)}...) custom-call(s32[3]{0:T(128)S(1)} %pad_add_fusion.ids, bf16[256,768]{1,0:T(8,128)(2,1)S(1)} %get-tuple-element.158.own_ref, ...), custom_call_target="tpu_custom_call" | custom-call | tf_op jit(solution)/shard_map/first_back/pallas_call | solution.py:55
  119.6 4.6 %second_back.1 = (f32[256,768]{1,0:T(8,128)S(1)}, bf16[256,768]{1,0:T(8,128)(2,1)S(1)}, f32[16,768]{1,0:T(8,128)S(1)}, f32[384,384]{1,0:T(8,128)S(1)}, bf16[384,384]{1,0:T(8,128)(2,1)S(1)}) custom-call(s32[3]{0:T(128)S(1)} %pad_add_fusion.ids, bf16[512,192]{1,0:T(8,128)(2,1)S(1)} %get-tuple-element.163.gm_ref, ...), custom_call_target="tpu_custom_call" | custom-call | tf_op jit(solution)/shard_map/second_back/pallas_call | solution.py:55
  126.5 1.1 collective-permute-start.34
  128.5 2.2 %collective-permute-done.34.small_got_ref = f32[16,768]{1,0:T(8,128)} collective-permute-done((f32[16,768]{1,0:T(8,128)S(1)}, f32[16,768]{1,0:T(8,128)}, u32[]{:S(2)}, u32[]{:S(2)}) %collective-permute-start.34) | collective-permute-done | bytes 49184 | tf_op jit(solution)/shard_map/ppermute | solution.py:30
  130.7 1.2 fold_first.1
  131.9 1.2 collective-permute-start.37
  133.1 1.3 collective-permute-start.38
  134.4 1.8 %collective-permute-start.39 = (bf16[96,384]{1,0:T(8,128)(2,1)S(1)}, bf16[96,384]{1,0:T(8,128)(2,1)S(1)}, u32[]{:S(2)}, u32[]{:S(2)}) collective-permute-start(bf16[96,384]{1,0:T(8,128)(2,1)S(1)} %get-tuple-element.189), channel_id=1, source_target_pairs={{0,16},{4,20},{8,24},{12,28},{16,0},{20,4},{24,8},{28,12},{1,17},{... | collective-permute-start | bytes 221192 | tf_op jit(solution)/shard_map/ppermute | solution.py:30
  136.3 1.2 collective-permute-start.40
  137.5 1.0 collective-permute-start.35
  139.3 4.1 %collective-permute-done.39.refs_2_ = bf16[96,384]{1,0:T(8,128)(2,1)S(1)} collective-permute-done((bf16[96,384]{1,0:T(8,128)(2,1)S(1)}, bf16[96,384]{1,0:T(8,128)(2,1)S(1)}, u32[]{:S(2)}, u32[]{:S(2)}) %collective-permute-start.39) | collective-permute-done | bytes 73760 | tf_op jit(solution)/shard_map/ppermute | solution.py:30
  144.0 1.1 collective-permute-start.41
  145.1 1.4 collective-permute-start.43
  146.5 1.2 collective-permute-start.44
  147.8 1.8 %collective-permute-start.45 = (bf16[128,384]{1,0:T(8,128)(2,1)S(1)}, bf16[128,384]{1,0:T(8,128)(2,1)S(1)}, u32[]{:S(2)}, u32[]{:S(2)}) collective-permute-start(bf16[128,384]{1,0:T(8,128)(2,1)S(1)} %get-tuple-element.198), channel_id=1, source_target_pairs={{0,24},{4,28},{8,16},{12,20},{16,8},{20,12},{24,0},{28,4},{1,25},{... | collective-permute-start | bytes 294920 | tf_op jit(solution)/shard_map/ppermute | solution.py:30
  149.5 1.3 activations.1.refs_5_
  150.9 3.7 %expert_grads.1 = (f32[768,768]{1,0:T(8,128)}, f32[768,768]{1,0:T(8,128)}) custom-call(bf16[640,768]{1,0:T(8,128)(2,1)S(1)} %copy-done.12, bf16[640,768]{1,0:T(8,128)(2,1)S(1)} %copy-done.8, bf16[640,768]{1,0:T(8,128)(2,1)S(1)} %get-tuple-element.136.active_ref, bf16[640,768]{1,0:T(8,128)(2,1)S(1)} %copy-done.10, f32[640,1]{1,0:T(8,128)S(1)} %copy-done.5, ...), custom_call_target="tpu_custom_call" | custom-call | tf_op jit(solution)/shard_map/expert_grads/pallas_call | solution.py:55
  154.6 0.9 input_grad.1.refs_6_
  157.4 0.9 collective-permute-done.42.got_one
  158.4 1.4 columns.1
  (167 shorter events, 23.5 us)
Async XLA Ops:
  0.6 15.1 %copy-start = (f32[32,12]{0,1:T(8,128)S(1)}, f32[32,12]{0,1:T(8,128)}, u32[]{:S(2)}) copy-start(f32[32,12]{0,1:T(8,128)} %param.21) | copy-start | bytes 4612
  0.7 14.8 %copy-start.34 = (s32[1023]{0:T(1024)S(1)}, s32[1023]{0:T(1024)}, u32[]{:S(2)}) copy-start(s32[1023]{0:T(1024)} %param.28) | copy-start | bytes 12280
  0.7 15.0 %copy-start.35 = (bf16[768]{0:T(1024)(128)(2,1)S(1)}, bf16[768]{0:T(1024)(128)(2,1)}, u32[]{:S(2)}) copy-start(bf16[768]{0:T(1024)(128)(2,1)} %param.16) | copy-start | bytes 4612
  2.3 3.8 %collective-permute-start.1 = (bf16[48,768]{1,0:T(8,128)(2,1)S(1)}, bf16[48,768]{1,0:T(8,128)(2,1)S(1)}, u32[]{:S(2)}, u32[]{:S(2)}) collective-permute-start(bf16[48,768]{1,0:T(8,128)(2,1)S(1)} %get-tuple-element.114), channel_id=1, source_target_pairs={{0,2},{2,0},{1,3},{3,1},{4,6},{6,4},{5,7},{7,5},{8,10},{10,8},{9,1... | collective-permute-start | bytes 221192 | tf_op jit(solution)/shard_map/ppermute | solution.py:30
  2.9 10.8 %collective-permute-start = (bf16[128,768]{1,0:T(8,128)(2,1)}, bf16[128,768]{1,0:T(8,128)(2,1)S(1)}, u32[]{:S(2)}, u32[]{:S(2)}) collective-permute-start(bf16[128,768]{1,0:T(8,128)(2,1)} %x_ref.1), channel_id=1, source_target_pairs={{0,1},{1,0},{2,3},{3,2},{4,5},{5,4},{6,7},{7,6},{8,9},{9,8},{10,11... | collective-permute-start | bytes 589832 | tf_op jit(solution)/shard_map/ppermute | solution.py:30
  6.2 7.5 %collective-permute-start.2 = (bf16[96,768]{1,0:T(8,128)(2,1)S(1)}, bf16[96,768]{1,0:T(8,128)(2,1)S(1)}, u32[]{:S(2)}, u32[]{:S(2)}) collective-permute-start(bf16[96,768]{1,0:T(8,128)(2,1)S(1)} %maximum_select_fusion.refs_0_), channel_id=1, source_target_pairs={{0,4},{4,0},{8,12},{12,8},{16,20},{20,16},{24,28},{28,24},{1,5},{5... | collective-permute-start | bytes 442376 | tf_op jit(solution)/shard_map/ppermute | solution.py:30
  9.3 7.8 %collective-permute-start.4 = (bf16[96,768]{1,0:T(8,128)(2,1)S(1)}, bf16[96,768]{1,0:T(8,128)(2,1)S(1)}, u32[]{:S(2)}, u32[]{:S(2)}) collective-permute-start(bf16[96,768]{1,0:T(8,128)(2,1)S(1)} %maximum_select_fusion.refs_0_), channel_id=1, source_target_pairs={{0,8},{4,12},{8,0},{12,4},{16,24},{20,28},{24,16},{28,20},{1,9},{5... | collective-permute-start | bytes 442376 | tf_op jit(solution)/shard_map/ppermute | solution.py:30
  10.8 14.0 %collective-permute-start.6 = (bf16[96,768]{1,0:T(8,128)(2,1)S(1)}, bf16[96,768]{1,0:T(8,128)(2,1)S(1)}, u32[]{:S(2)}, u32[]{:S(2)}) collective-permute-start(bf16[96,768]{1,0:T(8,128)(2,1)S(1)} %maximum_select_fusion.refs_0_), channel_id=1, source_target_pairs={{0,16},{4,20},{8,24},{12,28},{16,0},{20,4},{24,8},{28,12},{1,17},{... | collective-permute-start | bytes 442376 | tf_op jit(solution)/shard_map/ppermute | solution.py:30
  13.4 11.9 %collective-permute-start.8 = (bf16[96,768]{1,0:T(8,128)(2,1)S(1)}, bf16[96,768]{1,0:T(8,128)(2,1)S(1)}, u32[]{:S(2)}, u32[]{:S(2)}) collective-permute-start(bf16[96,768]{1,0:T(8,128)(2,1)S(1)} %maximum_select_fusion.refs_0_), channel_id=1, source_target_pairs={{0,24},{4,28},{8,16},{12,20},{16,8},{20,12},{24,0},{28,4},{1,25},{... | collective-permute-start | bytes 442376 | tf_op jit(solution)/shard_map/ppermute | solution.py:30
  15.2 16.4 %collective-permute-start.3 = (bf16[256,768]{1,0:T(8,128)(2,1)S(1)}, bf16[256,768]{1,0:T(8,128)(2,1)S(1)}, u32[]{:S(2)}, u32[]{:S(2)}) collective-permute-start(bf16[256,768]{1,0:T(8,128)(2,1)S(1)} %rows.1.own_ref.x_ref), channel_id=1, source_target_pairs={{0,2},{2,0},{1,3},{3,1},{4,6},{6,4},{5,7},{7,5},{8,10},{10,8},{9,1... | collective-permute-start | bytes 1179656 | tf_op jit(solution)/shard_map/ppermute | solution.py:30
  15.5 21.3 %copy-start.28 = (s32[1024]{0:T(1024)}, s32[1024]{0:T(1024)S(1)}, u32[]{:S(2)}) copy-start(s32[1024]{0:T(1024)S(1)} %pad.9) | copy-start | bytes 12292
  15.7 21.1 %copy-start.30 = (s32[256,1]{0,1:T(1,128)S(1)}, s32[256,1]{0,1:T(1,128)}, u32[]{:S(2)}) copy-start(s32[256,1]{0,1:T(1,128)} %param.26) | copy-start | bytes 3076
  17.0 10.3 %collective-permute-start.5 = (bf16[96,768]{1,0:T(8,128)(2,1)S(1)}, bf16[96,768]{1,0:T(8,128)(2,1)S(1)}, u32[]{:S(2)}, u32[]{:S(2)}) collective-permute-start(bf16[96,768]{1,0:T(8,128)(2,1)S(1)} %collective-permute-done.4.refs_2_), channel_id=1, source_target_pairs={{0,4},{4,0},{8,12},{12,8},{16,20},{20,16},{24,28},{28,24},{1,5},{5... | collective-permute-start | bytes 442376 | tf_op jit(solution)/shard_map/ppermute | solution.py:30
  24.8 5.1 %collective-permute-start.7 = (bf16[96,768]{1,0:T(8,128)(2,1)S(1)}, bf16[96,768]{1,0:T(8,128)(2,1)S(1)}, u32[]{:S(2)}, u32[]{:S(2)}) collective-permute-start(bf16[96,768]{1,0:T(8,128)(2,1)S(1)} %collective-permute-done.6.refs_4_), channel_id=1, source_target_pairs={{0,4},{4,0},{8,12},{12,8},{16,20},{20,16},{24,28},{28,24},{1,5},{5... | collective-permute-start | bytes 442376 | tf_op jit(solution)/shard_map/ppermute | solution.py:30
  25.4 6.2 %collective-permute-start.9 = (bf16[96,768]{1,0:T(8,128)(2,1)S(1)}, bf16[96,768]{1,0:T(8,128)(2,1)S(1)}, u32[]{:S(2)}, u32[]{:S(2)}) collective-permute-start(bf16[96,768]{1,0:T(8,128)(2,1)S(1)} %collective-permute-done.8.refs_6_), channel_id=1, source_target_pairs={{0,4},{4,0},{8,12},{12,8},{16,20},{20,16},{24,28},{28,24},{1,5},{5... | collective-permute-start | bytes 442376 | tf_op jit(solution)/shard_map/ppermute | solution.py:30
  36.8 3.1 %collective-permute-start.11 = (bf16[768,192]{1,0:T(8,128)(2,1)S(1)}, bf16[768,192]{1,0:T(8,128)(2,1)S(1)}, u32[]{:S(2)}, u32[]{:S(2)}) collective-permute-start(bf16[768,192]{1,0:T(8,128)(2,1)S(1)} %get-tuple-element.117.refs_1_.wo_ref), channel_id=1, source_target_pairs={{0,2},{2,0},{1,3},{3,1},{4,6},{6,4},{5,7},{7,5},{8,10},{10,8},{9,1... | collective-permute-start | bytes 884744 | tf_op jit(solution)/shard_map/ppermute | solution.py:30
  37.0 2.9 %collective-permute-start.10 = (bf16[256,192]{1,0:T(8,128)(2,1)S(1)}, bf16[256,192]{1,0:T(8,128)(2,1)S(1)}, u32[]{:S(2)}, u32[]{:S(2)}) collective-permute-start(bf16[256,192]{1,0:T(8,128)(2,1)S(1)} %get-tuple-element.116.held_ref), channel_id=1, source_target_pairs={{0,2},{2,0},{1,3},{3,1},{4,6},{6,4},{5,7},{7,5},{8,10},{10,8},{9,1... | collective-permute-start | bytes 294920 | tf_op jit(solution)/shard_map/ppermute | solution.py:30
  40.3 11.1 %collective-permute-start.12 = (bf16[256,768]{1,0:T(8,128)(2,1)S(1)}, bf16[256,768]{1,0:T(8,128)(2,1)S(1)}, u32[]{:S(2)}, u32[]{:S(2)}) collective-permute-start(bf16[256,768]{1,0:T(8,128)(2,1)S(1)} %attended.1.own_ref), channel_id=1, source_target_pairs={{0,1},{1,0},{2,3},{3,2},{4,5},{5,4},{6,7},{7,6},{8,9},{9,8},{10,11... | collective-permute-start | bytes 1179656 | tf_op jit(solution)/shard_map/ppermute | solution.py:30
  40.8 4.9 %copy-start.36 = (bf16[768]{0:T(1024)(128)(2,1)S(1)}, bf16[768]{0:T(1024)(128)(2,1)}, u32[]{:S(2)}) copy-start(bf16[768]{0:T(1024)(128)(2,1)} %param.22) | copy-start | bytes 4612
  42.1 26.8 %all-to-all-start = ((bf16[8,40,768]{2,1,0:T(8,128)(2,1)}), bf16[8,40,768]{2,1,0:T(8,128)(2,1)S(1)}, u32[]{:S(2)}, u32[]{:S(2)}) async-start(bf16[8,40,768]{2,1,0:T(8,128)(2,1)} %bitcast.13), calls=%async_computation | async-start | bytes 983040 | tf_op jit(solution)/shard_map/all_to_all | solution.py:575
  45.7 25.0 %copy-start.1 = (bf16[768,768]{1,0:T(8,128)(2,1)S(1)}, bf16[768,768]{1,0:T(8,128)(2,1)}, u32[]{:S(2)}) copy-start(bf16[768,768]{1,0:T(8,128)(2,1)} %wdown_ref.3) | copy-start | bytes 3538948
  54.3 6.4 %collective-permute-start.13 = (bf16[40,768]{1,0:T(8,128)(2,1)S(1)}, bf16[40,768]{1,0:T(8,128)(2,1)S(1)}, u32[]{:S(2)}, u32[]{:S(2)}) collective-permute-start(bf16[40,768]{1,0:T(8,128)(2,1)S(1)} %get-tuple-element.128), channel_id=1, source_target_pairs={{0,4},{4,0},{8,12},{12,8},{16,20},{20,16},{24,28},{28,24},{1,5},{5... | collective-permute-start | bytes 184328 | tf_op jit(solution)/shard_map/ppermute | solution.py:30
  54.8 8.2 %collective-permute-start.14 = (bf16[40,768]{1,0:T(8,128)(2,1)S(1)}, bf16[40,768]{1,0:T(8,128)(2,1)S(1)}, u32[]{:S(2)}, u32[]{:S(2)}) collective-permute-start(bf16[40,768]{1,0:T(8,128)(2,1)S(1)} %get-tuple-element.129), channel_id=1, source_target_pairs={{0,8},{4,12},{8,0},{12,4},{16,24},{20,28},{24,16},{28,20},{1,9},{5... | collective-permute-start | bytes 184328 | tf_op jit(solution)/shard_map/ppermute | solution.py:30
  55.9 9.7 %collective-permute-start.15 = (bf16[40,768]{1,0:T(8,128)(2,1)S(1)}, bf16[40,768]{1,0:T(8,128)(2,1)S(1)}, u32[]{:S(2)}, u32[]{:S(2)}) collective-permute-start(bf16[40,768]{1,0:T(8,128)(2,1)S(1)} %get-tuple-element.130), channel_id=1, source_target_pairs={{0,12},{4,8},{8,4},{12,0},{16,28},{20,24},{24,20},{28,16},{1,13},{... | collective-permute-start | bytes 184328 | tf_op jit(solution)/shard_map/ppermute | solution.py:30
  57.8 8.1 %collective-permute-start.16 = (bf16[40,768]{1,0:T(8,128)(2,1)S(1)}, bf16[40,768]{1,0:T(8,128)(2,1)S(1)}, u32[]{:S(2)}, u32[]{:S(2)}) collective-permute-start(bf16[40,768]{1,0:T(8,128)(2,1)S(1)} %get-tuple-element.131), channel_id=1, source_target_pairs={{0,16},{4,20},{8,24},{12,28},{16,0},{20,4},{24,8},{28,12},{1,17},{... | collective-permute-start | bytes 184328 | tf_op jit(solution)/shard_map/ppermute | solution.py:30
  59.5 9.2 %collective-permute-start.17 = (bf16[40,768]{1,0:T(8,128)(2,1)S(1)}, bf16[40,768]{1,0:T(8,128)(2,1)S(1)}, u32[]{:S(2)}, u32[]{:S(2)}) collective-permute-start(bf16[40,768]{1,0:T(8,128)(2,1)S(1)} %get-tuple-element.132), channel_id=1, source_target_pairs={{0,20},{4,16},{8,28},{12,24},{16,4},{20,0},{24,12},{28,8},{1,21},{... | collective-permute-start | bytes 184328 | tf_op jit(solution)/shard_map/ppermute | solution.py:30
  60.7 8.1 %collective-permute-start.18 = (bf16[40,768]{1,0:T(8,128)(2,1)S(1)}, bf16[40,768]{1,0:T(8,128)(2,1)S(1)}, u32[]{:S(2)}, u32[]{:S(2)}) collective-permute-start(bf16[40,768]{1,0:T(8,128)(2,1)S(1)} %get-tuple-element.133), channel_id=1, source_target_pairs={{0,24},{4,28},{8,16},{12,20},{16,8},{20,12},{24,0},{28,4},{1,25},{... | collective-permute-start | bytes 184328 | tf_op jit(solution)/shard_map/ppermute | solution.py:30
  63.0 7.3 %collective-permute-start.19 = (bf16[40,768]{1,0:T(8,128)(2,1)}, bf16[40,768]{1,0:T(8,128)(2,1)S(1)}, u32[]{:S(2)}, u32[]{:S(2)}) collective-permute-start(bf16[40,768]{1,0:T(8,128)(2,1)} %get-tuple-element.134), channel_id=1, source_target_pairs={{0,28},{4,24},{8,20},{12,16},{16,12},{20,8},{24,4},{28,0},{1,29},{... | collective-permute-start | bytes 184328 | tf_op jit(solution)/shard_map/ppermute | solution.py:30
  68.8 1.9 %collective-permute-start.21 = (bf16[8,40,768]{2,1,0:T(8,128)(2,1)S(1)}, bf16[8,40,768]{2,1,0:T(8,128)(2,1)S(1)}, u32[]{:S(2)}, u32[]{:S(2)}) collective-permute-start(bf16[8,40,768]{2,1,0:T(8,128)(2,1)S(1)} %all-to-all-done.own_ref), channel_id=1, source_target_pairs={{0,2},{2,0},{1,3},{3,1},{4,6},{6,4},{5,7},{7,5},{8,10},{10,8},{9,1... | collective-permute-start | bytes 1474568 | tf_op jit(solution)/shard_map/ppermute | solution.py:30
  70.4 2.9 %collective-permute-start.20 = (bf16[320,768]{1,0:T(8,128)(2,1)S(1)}, bf16[320,768]{1,0:T(8,128)(2,1)S(1)}, u32[]{:S(2)}, u32[]{:S(2)}) collective-permute-start(bf16[320,768]{1,0:T(8,128)(2,1)S(1)} %constant_dynamic-update-slice_fusion.own_ref), channel_id=1, source_target_pairs={{0,2},{2,0},{1,3},{3,1},{4,6},{6,4},{5,7},{7,5},{8,10},{10,8},{9,1... | collective-permute-start | bytes 1474568 | tf_op jit(solution)/shard_map/ppermute | solution.py:30
  78.5 1.9 %collective-permute-start.22 = (bf16[320,768]{1,0:T(8,128)(2,1)S(1)}, bf16[320,768]{1,0:T(8,128)(2,1)S(1)}, u32[]{:S(2)}, u32[]{:S(2)}) collective-permute-start(bf16[320,768]{1,0:T(8,128)(2,1)S(1)} %get-tuple-element.139), channel_id=1, source_target_pairs={{0,2},{2,0},{1,3},{3,1},{4,6},{6,4},{5,7},{7,5},{8,10},{10,8},{9,1... | collective-permute-start | bytes 1474568 | tf_op jit(solution)/shard_map/ppermute | solution.py:30
  80.6 4.7 %copy-start.31 = (s32[256,1]{0,1:T(1,128)S(1)}, s32[256,1]{0,1:T(1,128)}, u32[]{:S(2)}) copy-start(s32[256,1]{0,1:T(1,128)} %param.26) | copy-start | bytes 3076
  80.6 4.7 %copy-start.33 = (s32[256]{0:T(256)S(1)}, s32[256]{0:T(256)}, u32[]{:S(2)}) copy-start(s32[256]{0:T(256)} %copy-done.32) | copy-start | bytes 3076
  81.6 19.7 %collective-permute-start.23 = (bf16[320,768]{1,0:T(8,128)(2,1)S(1)}, bf16[320,768]{1,0:T(8,128)(2,1)S(1)}, u32[]{:S(2)}, u32[]{:S(2)}) collective-permute-start(bf16[320,768]{1,0:T(8,128)(2,1)S(1)} %get-tuple-element.142), channel_id=1, source_target_pairs={{0,2},{2,0},{1,3},{3,1},{4,6},{6,4},{5,7},{7,5},{8,10},{10,8},{9,1... | collective-permute-start | bytes 1474568 | tf_op jit(solution)/shard_map/ppermute | solution.py:30
  81.8 6.2 %collective-permute-start.24 = (bf16[40,768]{1,0:T(8,128)(2,1)S(1)}, bf16[40,768]{1,0:T(8,128)(2,1)S(1)}, u32[]{:S(2)}, u32[]{:S(2)}) collective-permute-start(bf16[40,768]{1,0:T(8,128)(2,1)S(1)} %get-tuple-element.144), channel_id=1, source_target_pairs={{0,4},{4,0},{8,12},{12,8},{16,20},{20,16},{24,28},{28,24},{1,5},{5... | collective-permute-start | bytes 184328 | tf_op jit(solution)/shard_map/ppermute | solution.py:30
  83.3 5.9 %collective-permute-start.25 = (bf16[40,768]{1,0:T(8,128)(2,1)S(1)}, bf16[40,768]{1,0:T(8,128)(2,1)S(1)}, u32[]{:S(2)}, u32[]{:S(2)}) collective-permute-start(bf16[40,768]{1,0:T(8,128)(2,1)S(1)} %get-tuple-element.145), channel_id=1, source_target_pairs={{0,8},{4,12},{8,0},{12,4},{16,24},{20,28},{24,16},{28,20},{1,9},{5... | collective-permute-start | bytes 184328 | tf_op jit(solution)/shard_map/ppermute | solution.py:30
  84.7 6.6 %collective-permute-start.26 = (bf16[40,768]{1,0:T(8,128)(2,1)S(1)}, bf16[40,768]{1,0:T(8,128)(2,1)S(1)}, u32[]{:S(2)}, u32[]{:S(2)}) collective-permute-start(bf16[40,768]{1,0:T(8,128)(2,1)S(1)} %get-tuple-element.146), channel_id=1, source_target_pairs={{0,12},{4,8},{8,4},{12,0},{16,28},{20,24},{24,20},{28,16},{1,13},{... | collective-permute-start | bytes 184328 | tf_op jit(solution)/shard_map/ppermute | solution.py:30
  85.3 14.1 %collective-permute-start.30 = (bf16[40,768]{1,0:T(8,128)(2,1)S(1)}, bf16[40,768]{1,0:T(8,128)(2,1)S(1)}, u32[]{:S(2)}, u32[]{:S(2)}) collective-permute-start(bf16[40,768]{1,0:T(8,128)(2,1)S(1)} %get-tuple-element.140.held_ref), channel_id=1, source_target_pairs={{0,28},{4,24},{8,20},{12,16},{16,12},{20,8},{24,4},{28,0},{1,29},{... | collective-permute-start | bytes 184328 | tf_op jit(solution)/shard_map/ppermute | solution.py:30
  88.0 9.9 %collective-permute-start.27 = (bf16[40,768]{1,0:T(8,128)(2,1)S(1)}, bf16[40,768]{1,0:T(8,128)(2,1)S(1)}, u32[]{:S(2)}, u32[]{:S(2)}) collective-permute-start(bf16[40,768]{1,0:T(8,128)(2,1)S(1)} %get-tuple-element.147), channel_id=1, source_target_pairs={{0,16},{4,20},{8,24},{12,28},{16,0},{20,4},{24,8},{28,12},{1,17},{... | collective-permute-start | bytes 184328 | tf_op jit(solution)/shard_map/ppermute | solution.py:30
  89.2 10.2 %collective-permute-start.28 = (bf16[40,768]{1,0:T(8,128)(2,1)S(1)}, bf16[40,768]{1,0:T(8,128)(2,1)S(1)}, u32[]{:S(2)}, u32[]{:S(2)}) collective-permute-start(bf16[40,768]{1,0:T(8,128)(2,1)S(1)} %get-tuple-element.148), channel_id=1, source_target_pairs={{0,20},{4,16},{8,28},{12,24},{16,4},{20,0},{24,12},{28,8},{1,21},{... | collective-permute-start | bytes 184328 | tf_op jit(solution)/shard_map/ppermute | solution.py:30
  91.3 8.1 %collective-permute-start.29 = (bf16[40,768]{1,0:T(8,128)(2,1)S(1)}, bf16[40,768]{1,0:T(8,128)(2,1)S(1)}, u32[]{:S(2)}, u32[]{:S(2)}) collective-permute-start(bf16[40,768]{1,0:T(8,128)(2,1)S(1)} %get-tuple-element.149), channel_id=1, source_target_pairs={{0,24},{4,28},{8,16},{12,20},{16,8},{20,12},{24,0},{28,4},{1,25},{... | collective-permute-start | bytes 184328 | tf_op jit(solution)/shard_map/ppermute | solution.py:30
  99.7 10.1 %collective-permute-start.31 = (bf16[256,768]{1,0:T(8,128)(2,1)S(1)}, bf16[256,768]{1,0:T(8,128)(2,1)}, u32[]{:S(2)}, u32[]{:S(2)}) collective-permute-start(bf16[256,768]{1,0:T(8,128)(2,1)S(1)} %gather_grad.1.own_ref), channel_id=1, source_target_pairs={{0,1},{1,0},{2,3},{3,2},{4,5},{5,4},{6,7},{7,6},{8,9},{9,8},{10,11... | collective-permute-start | bytes 1179656 | tf_op jit(solution)/shard_map/ppermute | solution.py:30
  102.7 24.9 %all-to-all-start.1 = ((bf16[8,40,768]{2,1,0:T(8,128)(2,1)}), bf16[8,40,768]{2,1,0:T(8,128)(2,1)S(1)}, u32[]{:S(2)}, u32[]{:S(2)}) async-start(bf16[8,40,768]{2,1,0:T(8,128)(2,1)} %join_out.1.refs_8_), calls=%async_computation.1 | async-start | bytes 983040 | tf_op jit(solution)/shard_map/all_to_all | solution.py:575
  112.1 1.7 %collective-permute-start.32 = (bf16[256,768]{1,0:T(8,128)(2,1)S(1)}, bf16[256,768]{1,0:T(8,128)(2,1)S(1)}, u32[]{:S(2)}, u32[]{:S(2)}) collective-permute-start(bf16[256,768]{1,0:T(8,128)(2,1)S(1)} %get-tuple-element.158.own_ref), channel_id=1, source_target_pairs={{0,2},{2,0},{1,3},{3,1},{4,6},{6,4},{5,7},{7,5},{8,10},{10,8},{9,1... | collective-permute-start | bytes 1179656 | tf_op jit(solution)/shard_map/ppermute | solution.py:30
  113.8 5.6 %copy-start.29 = (s32[1024]{0:T(1024)S(1)}, s32[1024]{0:T(1024)}, u32[]{:S(2)}) copy-start(s32[1024]{0:T(1024)} %copy-done.28) | copy-start | bytes 12292
  118.5 12.2 %collective-permute-start.33 = (bf16[384,384]{1,0:T(8,128)(2,1)}, bf16[384,384]{1,0:T(8,128)(2,1)}, u32[]{:S(2)}, u32[]{:S(2)}) collective-permute-start(bf16[384,384]{1,0:T(8,128)(2,1)} %get-tuple-element.175), channel_id=1, source_target_pairs={{0,4},{4,0},{8,12},{12,8},{16,20},{20,16},{24,28},{28,24},{1,5},{5... | collective-permute-start | bytes 884744 | tf_op jit(solution)/shard_map/ppermute | solution.py:30
  126.5 4.2 %collective-permute-start.34 = (f32[16,768]{1,0:T(8,128)S(1)}, f32[16,768]{1,0:T(8,128)}, u32[]{:S(2)}, u32[]{:S(2)}) collective-permute-start(f32[16,768]{1,0:T(8,128)S(1)} %get-tuple-element.176.small_ref), channel_id=1, source_target_pairs={{0,1},{1,0},{2,3},{3,2},{4,5},{5,4},{6,7},{7,6},{8,9},{9,8},{10,11... | collective-permute-start | bytes 147464 | tf_op jit(solution)/shard_map/ppermute | solution.py:30
  130.7 12.7 %copy-start.18 = (f32[384,384]{1,0:T(8,128)S(1)}, f32[384,384]{1,0:T(8,128)}, u32[]{:S(2)}) copy-start(f32[384,384]{1,0:T(8,128)} %copy-done.17) | copy-start | bytes 1769476
  131.9 5.7 %collective-permute-start.36 = (bf16[256,768]{1,0:T(8,128)(2,1)S(1)}, bf16[256,768]{1,0:T(8,128)(2,1)S(1)}, u32[]{:S(2)}, u32[]{:S(2)}) collective-permute-start(bf16[256,768]{1,0:T(8,128)(2,1)S(1)} %get-tuple-element.181), channel_id=1, source_target_pairs={{0,2},{2,0},{1,3},{3,1},{4,6},{6,4},{5,7},{7,5},{8,10},{10,8},{9,1... | collective-permute-start | bytes 1179656 | tf_op jit(solution)/shard_map/ppermute | solution.py:30
  131.9 11.4 %collective-permute-start.37 = (bf16[416,384]{1,0:T(8,128)(2,1)S(1)}, bf16[416,384]{1,0:T(8,128)(2,1)S(1)}, u32[]{:S(2)}, u32[]{:S(2)}) collective-permute-start(bf16[416,384]{1,0:T(8,128)(2,1)S(1)} %get-tuple-element.185), channel_id=1, source_target_pairs={{0,4},{4,0},{8,12},{12,8},{16,20},{20,16},{24,28},{28,24},{1,5},{5... | collective-permute-start | bytes 958472 | tf_op jit(solution)/shard_map/ppermute | solution.py:30
  133.1 6.1 %collective-permute-start.38 = (bf16[96,384]{1,0:T(8,128)(2,1)S(1)}, bf16[96,384]{1,0:T(8,128)(2,1)S(1)}, u32[]{:S(2)}, u32[]{:S(2)}) collective-permute-start(bf16[96,384]{1,0:T(8,128)(2,1)S(1)} %get-tuple-element.182.held_ref), channel_id=1, source_target_pairs={{0,8},{4,12},{8,0},{12,4},{16,24},{20,28},{24,16},{28,20},{1,9},{5... | collective-permute-start | bytes 221192 | tf_op jit(solution)/shard_map/ppermute | solution.py:30
  134.4 8.9 %collective-permute-start.39 = (bf16[96,384]{1,0:T(8,128)(2,1)S(1)}, bf16[96,384]{1,0:T(8,128)(2,1)S(1)}, u32[]{:S(2)}, u32[]{:S(2)}) collective-permute-start(bf16[96,384]{1,0:T(8,128)(2,1)S(1)} %get-tuple-element.189), channel_id=1, source_target_pairs={{0,16},{4,20},{8,24},{12,28},{16,0},{20,4},{24,8},{28,12},{1,17},{... | collective-permute-start | bytes 221192 | tf_op jit(solution)/shard_map/ppermute | solution.py:30
  136.3 7.0 %collective-permute-start.40 = (bf16[96,384]{1,0:T(8,128)(2,1)S(1)}, bf16[96,384]{1,0:T(8,128)(2,1)S(1)}, u32[]{:S(2)}, u32[]{:S(2)}) collective-permute-start(bf16[96,384]{1,0:T(8,128)(2,1)S(1)} %get-tuple-element.190), channel_id=1, source_target_pairs={{0,24},{4,28},{8,16},{12,20},{16,8},{20,12},{24,0},{28,4},{1,25},{... | collective-permute-start | bytes 221192 | tf_op jit(solution)/shard_map/ppermute | solution.py:30
  137.5 12.0 %collective-permute-start.35 = (bf16[128,768]{1,0:T(8,128)(2,1)S(1)}, bf16[128,768]{1,0:T(8,128)(2,1)S(1)}, u32[]{:S(2)}, u32[]{:S(2)}) collective-permute-start(bf16[128,768]{1,0:T(8,128)(2,1)S(1)} %get-tuple-element.180), channel_id=1, source_target_pairs={{0,1},{1,0},{2,3},{3,2},{4,5},{5,4},{6,7},{7,6},{8,9},{9,8},{10,11... | collective-permute-start | bytes 589832 | tf_op jit(solution)/shard_map/ppermute | solution.py:30
  138.6 12.3 %copy-start.12 = (bf16[640,768]{1,0:T(8,128)(2,1)S(1)}, bf16[640,768]{1,0:T(8,128)(2,1)}, u32[]{:S(2)}) copy-start(bf16[640,768]{1,0:T(8,128)(2,1)} %copy-done.11) | copy-start | bytes 2949124
  143.3 7.5 %copy-start.5 = (f32[640,1]{1,0:T(8,128)S(1)}, f32[640,1]{1,0:T(8,128)}, u32[]{:S(2)}) copy-start(f32[640,1]{1,0:T(8,128)} %copy-done.4) | copy-start | bytes 7684
  143.4 7.5 %copy-start.8 = (bf16[640,768]{1,0:T(8,128)(2,1)S(1)}, bf16[640,768]{1,0:T(8,128)(2,1)}, u32[]{:S(2)}) copy-start(bf16[640,768]{1,0:T(8,128)(2,1)} %copy-done.7) | copy-start | bytes 2949124
  143.4 7.5 %copy-start.10 = (bf16[640,768]{1,0:T(8,128)(2,1)S(1)}, bf16[640,768]{1,0:T(8,128)(2,1)}, u32[]{:S(2)}) copy-start(bf16[640,768]{1,0:T(8,128)(2,1)} %copy-done.9) | copy-start | bytes 2949124
  144.0 10.6 %collective-permute-start.41 = (bf16[128,768]{1,0:T(8,128)(2,1)S(1)}, bf16[128,768]{1,0:T(8,128)(2,1)S(1)}, u32[]{:S(2)}, u32[]{:S(2)}) collective-permute-start(bf16[128,768]{1,0:T(8,128)(2,1)S(1)} %get-tuple-element.191), channel_id=1, source_target_pairs={{0,1},{1,0},{2,3},{3,2},{4,5},{5,4},{6,7},{7,6},{8,9},{9,8},{10,11... | collective-permute-start | bytes 589832 | tf_op jit(solution)/shard_map/ppermute | solution.py:30
  145.1 10.4 %collective-permute-start.43 = (bf16[128,384]{1,0:T(8,128)(2,1)S(1)}, bf16[128,384]{1,0:T(8,128)(2,1)S(1)}, u32[]{:S(2)}, u32[]{:S(2)}) collective-permute-start(bf16[128,384]{1,0:T(8,128)(2,1)S(1)} %get-tuple-element.196.held_ref), channel_id=1, source_target_pairs={{0,8},{4,12},{8,0},{12,4},{16,24},{20,28},{24,16},{28,20},{1,9},{5... | collective-permute-start | bytes 294920 | tf_op jit(solution)/shard_map/ppermute | solution.py:30
  146.5 9.7 %collective-permute-start.44 = (bf16[128,384]{1,0:T(8,128)(2,1)S(1)}, bf16[128,384]{1,0:T(8,128)(2,1)S(1)}, u32[]{:S(2)}, u32[]{:S(2)}) collective-permute-start(bf16[128,384]{1,0:T(8,128)(2,1)S(1)} %get-tuple-element.197), channel_id=1, source_target_pairs={{0,16},{4,20},{8,24},{12,28},{16,0},{20,4},{24,8},{28,12},{1,17},{... | collective-permute-start | bytes 294920 | tf_op jit(solution)/shard_map/ppermute | solution.py:30
  147.8 8.5 %collective-permute-start.45 = (bf16[128,384]{1,0:T(8,128)(2,1)S(1)}, bf16[128,384]{1,0:T(8,128)(2,1)S(1)}, u32[]{:S(2)}, u32[]{:S(2)}) collective-permute-start(bf16[128,384]{1,0:T(8,128)(2,1)S(1)} %get-tuple-element.198), channel_id=1, source_target_pairs={{0,24},{4,28},{8,16},{12,20},{16,8},{20,12},{24,0},{28,4},{1,25},{... | collective-permute-start | bytes 294920 | tf_op jit(solution)/shard_map/ppermute | solution.py:30
  156.8 1.5 collective-permute-start.46
  156.9 1.4 collective-permute-start.42
  (22 other events, 49.9 us)

commit v5 on v4

--- a/solution.py
+++ b/solution.py
@@ -134,22 +134,49 @@
     return wide * lax.rsqrt(jnp.mean(wide * wide, axis=1, keepdims=True) + norm_eps)
 
 
+def tables_kernel(experts, capacity, direct, ids, routes_ref, turned_ref, plain_ref):
+    rows, slots = plain_ref.shape
+    routes = routes_ref[...]
+    picks = routes == lax.broadcasted_iota(jnp.int32, (rows, experts), 1)
+    upto = lax.broadcasted_iota(jnp.int32, (rows, rows), 0) >= lax.broadcasted_iota(
+        jnp.int32, (rows, rows), 1
+    )
+    counts = mm(upto.astype(f32).astype(bf16), picks.astype(f32).astype(bf16))
+    slot = jnp.sum(jnp.where(picks, counts - 1.0, 0.0), axis=1, keepdims=True).astype(jnp.int32)
+    codes = lax.broadcasted_iota(jnp.int32, (1, slots), 1)
+    expert = jnp.zeros((1, slots), jnp.int32)
+    for i in range(1, experts):
+        expert = expert + jnp.where(codes >= i * capacity, 1, 0)
+    place = codes - expert * capacity
+    plain = (routes == expert) & (slot == place)
+    plain_ref[...] = plain.astype(f32).astype(bf16)
+    turned = (routes == (expert ^ ids[1])) & (slot == place) if direct else plain
+    turned_ref[...] = turned.astype(f32).astype(bf16)
+
+
 def slots_kernel(table_ref, rows_ref, held_ref, out_ref):
-    out_ref[...] = mm(table_ref[...], rows_ref[...]).astype(bf16)
-
-
-def cots_kernel(parts, ids, own_ref, other_ref, wdown_ref, held_ref, cots_ref, back_ref, *scratch):
+    out_ref[...] = mm_at(table_ref[...], rows_ref[...]).astype(bf16)
+
+
+def cots_kernel(parts, ids, own_ref, other_ref, wdown_ref, held_ref, cots_ref, back_ref, near_ref, sems, *scratch):
     slots = cots_ref.shape[0] // 2
+    copies = []
     me = ids[1]
     for at, source in ((0, own_ref), (slots, other_ref)):
         if parts == 1:
-            cots_ref[at : at + slots, :] = source[...]
+            near_ref[at : at + slots, :] = source[...]
         else:
             rows = slots // parts
             for i in range(parts):
                 scratch[0][i * rows : (i + 1) * rows, :] = source[me ^ i].astype(f32)
-            cots_ref[at : at + slots, :] = scratch[0][...].astype(bf16)
-        back_ref[at : at + slots, :] = mm(cots_ref[at : at + slots, :], wdown_ref[...])
+            near_ref[at : at + slots, :] = scratch[0][...].astype(bf16)
+        copies.append(
+            pltpu.make_async_copy(near_ref.at[at : at + slots], cots_ref.at[at : at + slots], sems.at[len(copies)])
+        )
+        copies[-1].start()
+        back_ref[at : at + slots, :] = mm(near_ref[at : at + slots, :], wdown_ref[...])
+    for copy in copies:
+        copy.wait()
 
 
 def attend_kernel(heads, parts, ids, own_ref, other_ref, gain_ref, vec_ref, row_docs, col_docs, *refs):
@@ -198,12 +225,11 @@
     out_ref[...] = total.astype(bf16)
 
 
-def dispatch_kernel(x_ref, own_ref, got_ref, gain_ref, table_ref, hidden_ref, *blocks):
-    hidden = x_ref[...].astype(f32) + (own_ref[...].astype(f32) + got_ref[...].astype(f32))
-    hidden_ref[...] = hidden
+def dispatch_kernel(hidden_ref, gain_ref, table_ref, *blocks):
+    hidden = hidden_ref[...]
     scale = lax.rsqrt(jnp.mean(hidden * hidden, axis=1, keepdims=True) + norm_eps)
     normed = (hidden * scale * gain_ref[...]).astype(bf16)
-    slots = mm(table_ref[...], normed)
+    slots = mm_at(table_ref[...], normed)
     rows = blocks[0].shape[0]
     for i, block in enumerate(blocks):
         block[...] = slots[i * rows : (i + 1) * rows, :].astype(bf16)
@@ -430,10 +456,9 @@
 
 
 def fold_kernel(
-    keep_ref, got_ref, small_ref, small_got_ref, second_ref, grad_ref, returned_ref,
-    second_out, grad_out, returned_out, small_out, own_ref, *sends
+    keep_ref, got_ref, small_ref, small_got_ref, second_ref, returned_ref,
+    second_out, returned_out, small_out, own_ref, *sends
 ):
-    grad_out[...] = grad_ref[...]
     returned_out[...] = returned_ref[...]
     end, cols = second_ref.shape
     high = small_ref.shape[0]
@@ -605,16 +630,13 @@
     gain_first = gain_one.astype(f32)[None, :]
     gain_second = gain_two.astype(f32)[None, :]
 
-    expert_ids = routes[:, 0]
-    picks = (expert_ids[:, None] == jnp.arange(experts, dtype=jnp.int32)[None, :]).astype(jnp.int32)
-    slot_index = jnp.sum((jnp.cumsum(picks, axis=0) - 1) * picks, axis=1)
-    target = expert_ids * capacity + slot_index
-    codes = jnp.arange(slots, dtype=jnp.int32)
-    turned = ((codes // capacity) ^ me) * capacity + codes % capacity if direct else codes
-    table = (turned[:, None] == target[None, :]).astype(bf16)
-    back_table = (target[:, None] == turned[None, :]).astype(bf16)
-    plain_table = (codes[:, None] == target[None, :]).astype(bf16)
-    plain_back_table = (target[:, None] == codes[None, :]).astype(bf16)
+    back_table, plain_back_table = call(
+        functools.partial(tables_kernel, experts, capacity, direct),
+        "tables",
+        [out((block_rows, slots), bf16)] * 2,
+        [ids, routes],
+        smem=1,
+    )
 
     lengths_row = lax.dynamic_slice_in_dim(doc_lengths, me, 1, 0)[0]
     ends = jnp.cumsum(lengths_row)
@@ -671,7 +693,7 @@
         slots_kernel,
         "cot_slots",
         [out((slots, width), bf16)],
-        [plain_table, cotangent, Raw(mixed_sent)],
+        [plain_back_table, cotangent, Raw(pieces[min(3, parts - 1)])],
     )[0]
     cots_own = trade_natural(cot_slots).reshape(natural)
     cots_other = across(cots_own, "core", 1)
@@ -685,20 +707,25 @@
     )[0]
     attended_got = across(attended, "tensor", 1)
     block_shapes = [out((slots // parts, width), bf16)] * parts
-    hidden, *blocks = call(
+    hidden = x_rows.astype(f32) + (attended.astype(f32) + attended_got.astype(f32))
+    blocks = call(
         dispatch_kernel,
         "dispatch",
-        [Near(out((block_rows, width), f32)), *block_shapes],
-        [Near(x_rows), attended, Near(attended_got), gain_second, Near(table)],
+        block_shapes,
+        [hidden, gain_second, back_table],
     )
     received = trade(blocks)
     cots, back_active = call(
         functools.partial(cots_kernel, parts),
         "cots",
-        [Near(out((2 * slots, width), bf16)), Near(out((2 * slots, w_down.shape[1]), f32))],
+        [Far(out((2 * slots, width), bf16)), Near(out((2 * slots, w_down.shape[1]), f32))],
         [ids, Near(cots_own), Near(cots_other), w_down, Raw(blocks[0])],
         smem=1,
-        scratch=[pltpu.VMEM((slots, width), f32)] if direct else [],
+        scratch=[
+            pltpu.VMEM((2 * slots, width), bf16),
+            pltpu.SemaphoreType.DMA((2,)),
+            *([pltpu.VMEM((slots, width), f32)] if direct else []),
+        ],
     )
     slots_own = jnp.concatenate(received)
     slots_other = across(slots_own, "core", 1)
@@ -725,7 +752,7 @@
         gather_kernel,
         "gather_grad",
         [out((block_rows, width), bf16)],
-        [Near(back_table), *grad_back],
+        [back_table, *grad_back],
     )[0]
     grad_normed_two_got = across(grad_normed_two, "tensor", 1)
 
@@ -840,18 +867,17 @@
         returned_kernel,
         "returned",
         [out(half_block, bf16), out(half_block, bf16)],
-        [ids, Near(plain_back_table), Near(out_back), Raw(grad_kept)],
+        [ids, plain_back_table, Near(out_back), Raw(grad_kept)],
         smem=1,
     )
     part = out((shard_rows, chunk), f32)
     if direct:
         tall = width // 2 + 2 * small_rows
-        second_sent, grad_sent, returned_sent, small, own_one, *send_one = call(
+        second_sent, returned_sent, small, own_one, *send_one = call(
             fold_kernel,
             "fold_first",
             [
                 out((tall, chunk), bf16),
-                out(grad_sent.shape, bf16),
                 out(returned_sent.shape, bf16),
                 out((2 * small_rows, chunk), f32),
                 out((node_rows, chunk), f32),
@@ -863,7 +889,6 @@
                 small,
                 across(small, "tensor", 1),
                 second_chunk[1],
-                grad_sent,
                 returned_sent,
             ],
         )
@@ -910,7 +935,9 @@
         "expert_grads",
         [out(w_up.shape, f32), out(w_down.shape, f32)],
         [
-            *(Near(a) for a in (slots_all, cots, active, grad_upward, chosen)),
+            Near(slots_all),
+            cots,
+            *(Near(a) for a in (active, grad_upward, chosen)),
             Raw(second_done),
         ],
     )

time: 161 us -> 160 us (level)
  waiting for transfers between devices: 41.9 us -> 36.7 us
  starting transfers between devices: 59.4 us -> 64.4 us
  Pallas kernels: 45.6 us -> 47.7 us
  local copies, waits for them, and re-layouts: 8.74 us -> 7.02 us
    ppermute x47, waiting for transfers between devices: 41.9 us -> 35.6 us  [across(): lax.ppermute(shard, axis, [(i, i ^ bits) for i in range(lax.axis_size(axi...]
    ppermute x47, starting transfers between devices: 52.1 us -> 55.5 us  [across(): lax.ppermute(shard, axis, [(i, i ^ bits) for i in range(lax.axis_size(axi...]
    pallas_call x26 -> x27, Pallas kernels: 45.6 us -> 47.7 us  [call(): pl.pallas_call(body, name=name, out_shape=[space[type(o)](x.shape, x.dtyp...]
    unnamed x81 -> x64, local copies, waits for them, and re-layouts: 7.67 us -> 6.15 us
  transfers between devices with their start and end apart: 49 -> 49, of which waited for: 18 -> 13; matrix products, arithmetic and copies ran while one was open for 2% -> 1% of each run, Pallas kernels for 18% -> 24%
where the time goes in v5:
time: 160 us; the launch traced here: 159 us
  starting transfers between devices  64.4 us (40%)
  Pallas kernels  47.7 us (30%)
  waiting for transfers between devices  36.7 us (23%)
  local copies, waits for them, and re-layouts  7.02 us (4%)
  other arithmetic  1.91 us (1%)
    ppermute x47, starting transfers between devices, across(): lax.ppermute(shard, axis, [(i, i ^ bits) for i in range(lax.axis_size(axi...  55.5 us
    pallas_call x27, Pallas kernels, call(): pl.pallas_call(body, name=name, out_shape=[space[type(o)](x.shape, x.dtyp...  47.7 us
    ppermute x47, waiting for transfers between devices, across(): lax.ppermute(shard, axis, [(i, i ^ bits) for i in range(lax.axis_size(axi...  35.6 us
    all_to_all x2, starting transfers between devices, trade_natural(): lax.all_to_all(stacked, 'node', split_axis=0, concat_axis=0, tiled=True)  8.94 us
    unnamed x64, local copies, waits for them, and re-layouts  6.15 us
  transfers between devices with their start and end apart: 49, of which 13 were waited for; matrix products, arithmetic and copies ran while one was open for 1% of the time, Pallas kernels for 24%

profile of v5, /device:TPU:0, one launch (start us, length us, event | category | flops | bytes accessed | tf_op | source)
XLA Modules:
  0.0 159.5 jit_solution(13771804646342337790)
XLA Ops:
  0.8 1.6 shares.1
  2.9 2.6 %collective-permute-start = (bf16[128,768]{1,0:T(8,128)(2,1)}, bf16[128,768]{1,0:T(8,128)(2,1)S(1)}, u32[]{:S(2)}, u32[]{:S(2)}) collective-permute-start(bf16[128,768]{1,0:T(8,128)(2,1)} %x_ref.1), channel_id=1, source_target_pairs={{0,1},{1,0},{2,3},{3,2},{4,5},{5,4},{6,7},{7,6},{8,9},{9,8},{10,11... | collective-permute-start | bytes 589832 | tf_op jit(solution)/shard_map/ppermute | solution.py:30
  5.5 1.6 collective-permute-start.2
  7.1 1.6 collective-permute-start.4
  9.5 2.6 %collective-permute-start.6 = (bf16[96,768]{1,0:T(8,128)(2,1)S(1)}, bf16[96,768]{1,0:T(8,128)(2,1)S(1)}, u32[]{:S(2)}, u32[]{:S(2)}) collective-permute-start(bf16[96,768]{1,0:T(8,128)(2,1)S(1)} %maximum_select_fusion.refs_0_), channel_id=1, source_target_pairs={{0,16},{4,20},{8,24},{12,28},{16,0},{20,4},{24,8},{28,12},{1,17},{... | collective-permute-start | bytes 442376 | tf_op jit(solution)/shard_map/ppermute | solution.py:30
  12.3 0.9 copy-done.11
  15.1 0.9 tables.1
  16.1 7.3 %collective-permute-done.6.refs_4_ = bf16[96,768]{1,0:T(8,128)(2,1)S(1)} collective-permute-done((bf16[96,768]{1,0:T(8,128)(2,1)S(1)}, bf16[96,768]{1,0:T(8,128)(2,1)S(1)}, u32[]{:S(2)}, u32[]{:S(2)}) %collective-permute-start.6) | collective-permute-done | bytes 147488 | tf_op jit(solution)/shard_map/ppermute | solution.py:30
  23.9 1.5 collective-permute-start.9
  25.4 1.1 cot_slots.1
  26.5 4.2 %all-to-all-start = ((bf16[8,40,768]{2,1,0:T(8,128)(2,1)}), bf16[8,40,768]{2,1,0:T(8,128)(2,1)S(1)}, u32[]{:S(2)}, u32[]{:S(2)}) async-start(bf16[8,40,768]{2,1,0:T(8,128)(2,1)} %bitcast.7), calls=%async_computation | async-start | bytes 983040 | tf_op jit(solution)/shard_map/all_to_all | solution.py:600
  31.2 0.9 copy-done.22
  32.1 5.6 %attend.1 = (bf16[768,768]{1,0:T(8,128)(2,1)S(1)}, bf16[768,192]{1,0:T(8,128)(2,1)S(1)}, bf16[512,768]{1,0:T(8,128)(2,1)S(1)}, bf16[512,576]{1,0:T(8,128)(2,1)S(...) custom-call(s32[3]{0:T(128)S(1)} %pad_add_fusion.ids, ...), custom_call_target="tpu_custom_call" | custom-call | tf_op jit(solution)/shard_map/attend/pallas_call | solution.py:55
  38.3 2.3 %park.1 = (bf16[768,768]{1,0:T(8,128)(2,1)}, bf16[768,192]{1,0:T(8,128)(2,1)}, bf16[512,768]{1,0:T(8,128)(2,1)}, bf16[512,576]{1,0:T(8,128)(2,1)}, bf16[512,192]...) custom-call(bf16[768,768]{1,0:T(8,128)(2,1)S(1)} %get-tuple-element.118.refs_0_, ...), custom_call_target="tpu_custom_call" | custom-call | tf_op jit(solution)/shard_map/park/pallas_call | solution.py:55
  41.1 1.2 collective-permute-start.12
  42.3 1.1 all-to-all-done.own_ref
  43.4 8.9 %collective-permute-done.12 = bf16[256,768]{1,0:T(8,128)(2,1)S(1)} collective-permute-done((bf16[256,768]{1,0:T(8,128)(2,1)S(1)}, bf16[256,768]{1,0:T(8,128)(2,1)S(1)}, u32[]{:S(2)}, u32[]{:S(2)}) %collective-permute-start.12) | collective-permute-done | bytes 393248 | tf_op jit(solution)/shard_map/ppermute | solution.py:30
  52.8 2.1 %collective-permute-start.13 = (bf16[40,768]{1,0:T(8,128)(2,1)S(1)}, bf16[40,768]{1,0:T(8,128)(2,1)S(1)}, u32[]{:S(2)}, u32[]{:S(2)}) collective-permute-start(bf16[40,768]{1,0:T(8,128)(2,1)S(1)} %get-tuple-element.129), channel_id=1, source_target_pairs={{0,4},{4,0},{8,12},{12,8},{16,20},{20,16},{24,28},{28,24},{1,5},{5... | collective-permute-start | bytes 184328 | tf_op jit(solution)/shard_map/ppermute | solution.py:30
  54.9 1.5 collective-permute-start.14
  56.4 2.8 %collective-permute-start.16 = (bf16[40,768]{1,0:T(8,128)(2,1)S(1)}, bf16[40,768]{1,0:T(8,128)(2,1)S(1)}, u32[]{:S(2)}, u32[]{:S(2)}) collective-permute-start(bf16[40,768]{1,0:T(8,128)(2,1)S(1)} %get-tuple-element.132), channel_id=1, source_target_pairs={{0,16},{4,20},{8,24},{12,28},{16,0},{20,4},{24,8},{28,12},{1,17},{... | collective-permute-start | bytes 184328 | tf_op jit(solution)/shard_map/ppermute | solution.py:30
  59.3 1.6 %collective-permute-start.17 = (bf16[40,768]{1,0:T(8,128)(2,1)S(1)}, bf16[40,768]{1,0:T(8,128)(2,1)S(1)}, u32[]{:S(2)}, u32[]{:S(2)}) collective-permute-start(bf16[40,768]{1,0:T(8,128)(2,1)S(1)} %get-tuple-element.133), channel_id=1, source_target_pairs={{0,20},{4,16},{8,28},{12,24},{16,4},{20,0},{24,12},{28,8},{1,21},{... | collective-permute-start | bytes 184328 | tf_op jit(solution)/shard_map/ppermute | solution.py:30
  60.9 3.2 %collective-permute-start.18 = (bf16[40,768]{1,0:T(8,128)(2,1)S(1)}, bf16[40,768]{1,0:T(8,128)(2,1)S(1)}, u32[]{:S(2)}, u32[]{:S(2)}) collective-permute-start(bf16[40,768]{1,0:T(8,128)(2,1)S(1)} %get-tuple-element.134), channel_id=1, source_target_pairs={{0,24},{4,28},{8,16},{12,20},{16,8},{20,12},{24,0},{28,4},{1,25},{... | collective-permute-start | bytes 184328 | tf_op jit(solution)/shard_map/ppermute | solution.py:30
  64.2 0.8 collective-permute-start.19
  65.0 3.8 %collective-permute-done.17 = bf16[40,768]{1,0:T(8,128)(2,1)S(1)} collective-permute-done((bf16[40,768]{1,0:T(8,128)(2,1)S(1)}, bf16[40,768]{1,0:T(8,128)(2,1)S(1)}, u32[]{:S(2)}, u32[]{:S(2)}) %collective-permute-start.17) | collective-permute-done | bytes 61472 | tf_op jit(solution)/shard_map/ppermute | solution.py:30
  68.9 2.4 %collective-permute-done.19 = bf16[40,768]{1,0:T(8,128)(2,1)S(1)} collective-permute-done((bf16[40,768]{1,0:T(8,128)(2,1)S(1)}, bf16[40,768]{1,0:T(8,128)(2,1)S(1)}, u32[]{:S(2)}, u32[]{:S(2)}) %collective-permute-start.19) | collective-permute-done | bytes 61472 | tf_op jit(solution)/shard_map/ppermute | solution.py:30
  71.3 1.8 %cots.1 = (bf16[640,768]{1,0:T(8,128)(2,1)}, f32[640,768]{1,0:T(8,128)S(1)}) custom-call(s32[3]{0:T(128)S(1)} %pad_add_fusion.ids, bf16[8,40,768]{2,1,0:T(8,128)(2,1)S(1)} %all-to-all-done.own_ref, bf16[8,40,768]{2,1,0:T(8,128)(2,1)S(1)} %collective-permute-done.21.other_ref, bf16[768,768]{1,0:T(8,128)(2,1)S(1)} %copy-done.1, ...), custom_call_target="tpu_custom_call" | custom-call | tf_op jit(solution)/shard_map/cots/pallas_call | solution.py:55
  73.2 5.3 %expert.1 = (bf16[640,768]{1,0:T(8,128)(2,1)S(1)}, bf16[640,768]{1,0:T(8,128)(2,1)S(1)}, f32[640,1]{1,0:T(8,128)S(1)}, f32[320,768]{1,0:T(8,128)S(1)}, bf16[320,...) custom-call(s32[3]{0:T(128)S(1)} %pad_add_fusion.ids, ...), custom_call_target="tpu_custom_call" | custom-call | tf_op jit(solution)/shard_map/expert/pallas_call | solution.py:55
  79.0 1.5 collective-permute-done.22.got_ref
  80.6 1.0 expert_out.1
  83.2 2.3 %collective-permute-start.26 = (bf16[40,768]{1,0:T(8,128)(2,1)S(1)}, bf16[40,768]{1,0:T(8,128)(2,1)S(1)}, u32[]{:S(2)}, u32[]{:S(2)}) collective-permute-start(bf16[40,768]{1,0:T(8,128)(2,1)S(1)} %get-tuple-element.147), channel_id=1, source_target_pairs={{0,12},{4,8},{8,4},{12,0},{16,28},{20,24},{24,20},{28,16},{1,13},{... | collective-permute-start | bytes 184328 | tf_op jit(solution)/shard_map/ppermute | solution.py:30
  85.5 1.3 collective-permute-start.27
  86.9 1.6 collective-permute-start.28
  88.4 1.0 collective-permute-start.29
  89.5 3.7 %collective-permute-start.30 = (bf16[40,768]{1,0:T(8,128)(2,1)S(1)}, bf16[40,768]{1,0:T(8,128)(2,1)S(1)}, u32[]{:S(2)}, u32[]{:S(2)}) collective-permute-start(bf16[40,768]{1,0:T(8,128)(2,1)S(1)} %get-tuple-element.141.held_ref), channel_id=1, source_target_pairs={{0,28},{4,24},{8,20},{12,16},{16,12},{20,8},{24,4},{28,0},{1,29},{... | collective-permute-start | bytes 184328 | tf_op jit(solution)/shard_map/ppermute | solution.py:30
  93.2 1.6 collective-permute-done.27.refs_4_
  94.7 2.4 %collective-permute-done.28.refs_5_ = bf16[40,768]{1,0:T(8,128)(2,1)S(1)} collective-permute-done((bf16[40,768]{1,0:T(8,128)(2,1)S(1)}, bf16[40,768]{1,0:T(8,128)(2,1)S(1)}, u32[]{:S(2)}, u32[]{:S(2)}) %collective-permute-start.28) | collective-permute-done | bytes 61472 | tf_op jit(solution)/shard_map/ppermute | solution.py:30
  97.5 1.2 collective-permute-start.31
  98.7 1.4 join_out.1.refs_8_
  100.2 4.7 %all-to-all-start.1 = ((bf16[8,40,768]{2,1,0:T(8,128)(2,1)}), bf16[8,40,768]{2,1,0:T(8,128)(2,1)S(1)}, u32[]{:S(2)}, u32[]{:S(2)}) async-start(bf16[8,40,768]{2,1,0:T(8,128)(2,1)} %join_out.1.refs_8_), calls=%async_computation.1 | async-start | bytes 983040 | tf_op jit(solution)/shard_map/all_to_all | solution.py:600
  104.8 2.4 %unpark.1 = (bf16[768,768]{1,0:T(8,128)(2,1)S(1)}, bf16[768,192]{1,0:T(8,128)(2,1)S(1)}, bf16[512,768]{1,0:T(8,128)(2,1)S(1)}, bf16[512,576]{1,0:T(8,128)(2,1)S(...) custom-call(bf16[768,768]{1,0:T(8,128)(2,1)} %get-tuple-element.151., ...), custom_call_target="tpu_custom_call" | custom-call | tf_op jit(solution)/shard_map/unpark/pallas_call | solution.py:55
  107.3 1.5 hidden_back.1
  109.6 1.7 %collective-permute-done.32.other_ref = bf16[256,768]{1,0:T(8,128)(2,1)S(1)} collective-permute-done((bf16[256,768]{1,0:T(8,128)(2,1)S(1)}, bf16[256,768]{1,0:T(8,128)(2,1)S(1)}, u32[]{:S(2)}, u32[]{:S(2)}) %collective-permute-start.32) | collective-permute-done | bytes 393248 | tf_op jit(solution)/shard_map/ppermute | solution.py:30
  111.3 3.8 %first_back.1 = (bf16[512,192]{1,0:T(8,128)(2,1)S(1)}, bf16[512,192]{1,0:T(8,128)(2,1)S(1)}, f32[8,1024]{1,0:T(8,128)S(1)}, bf16[512,768]{1,0:T(8,128)(2,1)S(1)}...) custom-call(s32[3]{0:T(128)S(1)} %pad_add_fusion.ids, bf16[256,768]{1,0:T(8,128)(2,1)S(1)} %get-tuple-element.159.own_ref, ...), custom_call_target="tpu_custom_call" | custom-call | tf_op jit(solution)/shard_map/first_back/pallas_call | solution.py:55
  115.9 2.0 %collective-permute-start.33 = (bf16[384,384]{1,0:T(8,128)(2,1)}, bf16[384,384]{1,0:T(8,128)(2,1)}, u32[]{:S(2)}, u32[]{:S(2)}) collective-permute-start(bf16[384,384]{1,0:T(8,128)(2,1)} %get-tuple-element.176), channel_id=1, source_target_pairs={{0,4},{4,0},{8,12},{12,8},{16,20},{20,16},{24,28},{28,24},{1,5},{5... | collective-permute-start | bytes 884744 | tf_op jit(solution)/shard_map/ppermute | solution.py:30
  118.2 5.2 %second_back.1 = (f32[256,768]{1,0:T(8,128)S(1)}, bf16[256,768]{1,0:T(8,128)(2,1)}, f32[16,768]{1,0:T(8,128)S(1)}, f32[384,384]{1,0:T(8,128)S(1)}, bf16[384,384]{1,0:T(8,128)(2,1)S(1)}) custom-call(s32[3]{0:T(128)S(1)} %pad_add_fusion.ids, bf16[512,192]{1,0:T(8,128)(2,1)S(1)} %get-tuple-element.164.gm_ref, ...), custom_call_target="tpu_custom_call" | custom-call | tf_op jit(solution)/shard_map/second_back/pallas_call | solution.py:55
  124.9 0.9 collective-permute-start.34
  125.8 0.9 copy-done.10
  126.7 0.9 returned.1
  127.7 1.4 collective-permute-done.34.small_got_ref
  129.1 1.1 fold_first.1
  130.4 3.5 %collective-permute-start.38 = (bf16[96,384]{1,0:T(8,128)(2,1)S(1)}, bf16[96,384]{1,0:T(8,128)(2,1)S(1)}, u32[]{:S(2)}, u32[]{:S(2)}) collective-permute-start(bf16[96,384]{1,0:T(8,128)(2,1)S(1)} %get-tuple-element.182.held_ref), channel_id=1, source_target_pairs={{0,8},{4,12},{8,0},{12,4},{16,24},{20,28},{24,16},{28,20},{1,9},{5... | collective-permute-start | bytes 221192 | tf_op jit(solution)/shard_map/ppermute | solution.py:30
  134.7 1.6 collective-permute-start.40
  136.3 1.2 collective-permute-start.35
  137.5 1.2 normed_sum.1
  138.7 3.4 %collective-permute-done.39.refs_2_ = bf16[96,384]{1,0:T(8,128)(2,1)S(1)} collective-permute-done((bf16[96,384]{1,0:T(8,128)(2,1)S(1)}, bf16[96,384]{1,0:T(8,128)(2,1)S(1)}, u32[]{:S(2)}, u32[]{:S(2)}) %collective-permute-start.39) | collective-permute-done | bytes 73760 | tf_op jit(solution)/shard_map/ppermute | solution.py:30
  142.8 1.2 collective-permute-start.41
  144.1 1.3 collective-permute-start.43
  145.4 1.1 collective-permute-start.44
  146.5 1.9 %collective-permute-start.45 = (bf16[128,384]{1,0:T(8,128)(2,1)S(1)}, bf16[128,384]{1,0:T(8,128)(2,1)S(1)}, u32[]{:S(2)}, u32[]{:S(2)}) collective-permute-start(bf16[128,384]{1,0:T(8,128)(2,1)S(1)} %get-tuple-element.198), channel_id=1, source_target_pairs={{0,24},{4,28},{8,16},{12,20},{16,8},{20,12},{24,0},{28,4},{1,25},{... | collective-permute-start | bytes 294920 | tf_op jit(solution)/shard_map/ppermute | solution.py:30
  148.4 1.3 activations.1.refs_5_
  149.8 3.7 %expert_grads.1 = (f32[768,768]{1,0:T(8,128)}, f32[768,768]{1,0:T(8,128)}) custom-call(bf16[640,768]{1,0:T(8,128)(2,1)S(1)} %copy-done.8, bf16[640,768]{1,0:T(8,128)(2,1)S(1)} %copy-done.4, bf16[640,768]{1,0:T(8,128)(2,1)S(1)} %get-tuple-element.137.active_ref, bf16[640,768]{1,0:T(8,128)(2,1)S(1)} %copy-done.6, f32[640,1]{1,0:T(8,128)S(1)} %get-tuple-element.138.chosen_ref, ...), custom_call_target="tpu_custom_call" | custom-call | tf_op jit(solution)/shard_map/expert_grads/pallas_call | solution.py:55
  153.5 0.9 input_grad.1.refs_6_
  156.0 0.9 collective-permute-done.42.got_one
  156.9 1.4 columns.1
  (141 shorter events, 16.5 us)
Async XLA Ops:
  0.6 15.4 %copy-start = (f32[32,12]{0,1:T(8,128)S(1)}, f32[32,12]{0,1:T(8,128)}, u32[]{:S(2)}) copy-start(f32[32,12]{0,1:T(8,128)} %param.21) | copy-start | bytes 4612
  0.7 14.1 %copy-start.24 = (s32[1023]{0:T(1024)S(1)}, s32[1023]{0:T(1024)}, u32[]{:S(2)}) copy-start(s32[1023]{0:T(1024)} %param.28) | copy-start | bytes 12280
  0.7 14.2 %copy-start.25 = (bf16[768]{0:T(1024)(128)(2,1)S(1)}, bf16[768]{0:T(1024)(128)(2,1)}, u32[]{:S(2)}) copy-start(bf16[768]{0:T(1024)(128)(2,1)} %param.16) | copy-start | bytes 4612
  0.7 14.2 %copy-start.27 = (s32[256,1]{0,1:T(1,128)S(1)}, s32[256,1]{0,1:T(1,128)}, u32[]{:S(2)}) copy-start(s32[256,1]{0,1:T(1,128)} %param.26) | copy-start | bytes 3076
  0.7 24.7 %copy-start.2 = (bf16[256,768]{1,0:T(8,128)(2,1)S(1)}, bf16[256,768]{1,0:T(8,128)(2,1)}, u32[]{:S(2)}) copy-start(bf16[256,768]{1,0:T(8,128)(2,1)} %cot_ref.1) | copy-start | bytes 1179652
  2.4 3.1 %collective-permute-start.1 = (bf16[48,768]{1,0:T(8,128)(2,1)S(1)}, bf16[48,768]{1,0:T(8,128)(2,1)S(1)}, u32[]{:S(2)}, u32[]{:S(2)}) collective-permute-start(bf16[48,768]{1,0:T(8,128)(2,1)S(1)} %get-tuple-element.114), channel_id=1, source_target_pairs={{0,2},{2,0},{1,3},{3,1},{4,6},{6,4},{5,7},{7,5},{8,10},{10,8},{9,1... | collective-permute-start | bytes 221192 | tf_op jit(solution)/shard_map/ppermute | solution.py:30
  2.9 9.5 %collective-permute-start = (bf16[128,768]{1,0:T(8,128)(2,1)}, bf16[128,768]{1,0:T(8,128)(2,1)S(1)}, u32[]{:S(2)}, u32[]{:S(2)}) collective-permute-start(bf16[128,768]{1,0:T(8,128)(2,1)} %x_ref.1), channel_id=1, source_target_pairs={{0,1},{1,0},{2,3},{3,2},{4,5},{5,4},{6,7},{7,6},{8,9},{9,8},{10,11... | collective-permute-start | bytes 589832 | tf_op jit(solution)/shard_map/ppermute | solution.py:30
  5.5 6.8 %collective-permute-start.2 = (bf16[96,768]{1,0:T(8,128)(2,1)S(1)}, bf16[96,768]{1,0:T(8,128)(2,1)S(1)}, u32[]{:S(2)}, u32[]{:S(2)}) collective-permute-start(bf16[96,768]{1,0:T(8,128)(2,1)S(1)} %maximum_select_fusion.refs_0_), channel_id=1, source_target_pairs={{0,4},{4,0},{8,12},{12,8},{16,20},{20,16},{24,28},{28,24},{1,5},{5... | collective-permute-start | bytes 442376 | tf_op jit(solution)/shard_map/ppermute | solution.py:30
  7.1 6.9 %collective-permute-start.4 = (bf16[96,768]{1,0:T(8,128)(2,1)S(1)}, bf16[96,768]{1,0:T(8,128)(2,1)S(1)}, u32[]{:S(2)}, u32[]{:S(2)}) collective-permute-start(bf16[96,768]{1,0:T(8,128)(2,1)S(1)} %maximum_select_fusion.refs_0_), channel_id=1, source_target_pairs={{0,8},{4,12},{8,0},{12,4},{16,24},{20,28},{24,16},{28,20},{1,9},{5... | collective-permute-start | bytes 442376 | tf_op jit(solution)/shard_map/ppermute | solution.py:30
  9.5 13.8 %collective-permute-start.6 = (bf16[96,768]{1,0:T(8,128)(2,1)S(1)}, bf16[96,768]{1,0:T(8,128)(2,1)S(1)}, u32[]{:S(2)}, u32[]{:S(2)}) collective-permute-start(bf16[96,768]{1,0:T(8,128)(2,1)S(1)} %maximum_select_fusion.refs_0_), channel_id=1, source_target_pairs={{0,16},{4,20},{8,24},{12,28},{16,0},{20,4},{24,8},{28,12},{1,17},{... | collective-permute-start | bytes 442376 | tf_op jit(solution)/shard_map/ppermute | solution.py:30
  12.1 11.8 %collective-permute-start.8 = (bf16[96,768]{1,0:T(8,128)(2,1)S(1)}, bf16[96,768]{1,0:T(8,128)(2,1)S(1)}, u32[]{:S(2)}, u32[]{:S(2)}) collective-permute-start(bf16[96,768]{1,0:T(8,128)(2,1)S(1)} %maximum_select_fusion.refs_0_), channel_id=1, source_target_pairs={{0,24},{4,28},{8,16},{12,20},{16,8},{20,12},{24,0},{28,4},{1,25},{... | collective-permute-start | bytes 442376 | tf_op jit(solution)/shard_map/ppermute | solution.py:30
  13.8 17.4 %collective-permute-start.3 = (bf16[256,768]{1,0:T(8,128)(2,1)S(1)}, bf16[256,768]{1,0:T(8,128)(2,1)S(1)}, u32[]{:S(2)}, u32[]{:S(2)}) collective-permute-start(bf16[256,768]{1,0:T(8,128)(2,1)S(1)} %rows.1.own_ref), channel_id=1, source_target_pairs={{0,2},{2,0},{1,3},{3,1},{4,6},{6,4},{5,7},{7,5},{8,10},{10,8},{9,1... | collective-permute-start | bytes 1179656 | tf_op jit(solution)/shard_map/ppermute | solution.py:30
  13.9 11.4 %collective-permute-start.5 = (bf16[96,768]{1,0:T(8,128)(2,1)S(1)}, bf16[96,768]{1,0:T(8,128)(2,1)S(1)}, u32[]{:S(2)}, u32[]{:S(2)}) collective-permute-start(bf16[96,768]{1,0:T(8,128)(2,1)S(1)} %collective-permute-done.4.refs_2_), channel_id=1, source_target_pairs={{0,4},{4,0},{8,12},{12,8},{16,20},{20,16},{24,28},{28,24},{1,5},{5... | collective-permute-start | bytes 442376 | tf_op jit(solution)/shard_map/ppermute | solution.py:30
  16.0 15.2 %copy-start.9 = (bf16[256,320]{1,0:T(8,128)(2,1)}, bf16[256,320]{1,0:T(8,128)(2,1)S(1)}, u32[]{:S(2)}) copy-start(bf16[256,320]{1,0:T(8,128)(2,1)S(1)} %get-tuple-element.126.table_ref) | copy-start | bytes 491524
  23.3 7.8 %collective-permute-start.7 = (bf16[96,768]{1,0:T(8,128)(2,1)S(1)}, bf16[96,768]{1,0:T(8,128)(2,1)}, u32[]{:S(2)}, u32[]{:S(2)}) collective-permute-start(bf16[96,768]{1,0:T(8,128)(2,1)S(1)} %collective-permute-done.6.refs_4_), channel_id=1, source_target_pairs={{0,4},{4,0},{8,12},{12,8},{16,20},{20,16},{24,28},{28,24},{1,5},{5... | collective-permute-start | bytes 442376 | tf_op jit(solution)/shard_map/ppermute | solution.py:30
  23.9 7.3 %copy-start.21 = (bf16[96,768]{1,0:T(8,128)(2,1)}, bf16[96,768]{1,0:T(8,128)(2,1)S(1)}, u32[]{:S(2)}) copy-start(bf16[96,768]{1,0:T(8,128)(2,1)S(1)} %collective-permute-done.8.refs_6_) | copy-start | bytes 442372
  23.9 7.3 %collective-permute-start.9 = (bf16[96,768]{1,0:T(8,128)(2,1)S(1)}, bf16[96,768]{1,0:T(8,128)(2,1)}, u32[]{:S(2)}, u32[]{:S(2)}) collective-permute-start(bf16[96,768]{1,0:T(8,128)(2,1)S(1)} %collective-permute-done.8.refs_6_), channel_id=1, source_target_pairs={{0,4},{4,0},{8,12},{12,8},{16,20},{20,16},{24,28},{28,24},{1,5},{5... | collective-permute-start | bytes 442376 | tf_op jit(solution)/shard_map/ppermute | solution.py:30
  26.5 16.9 %all-to-all-start = ((bf16[8,40,768]{2,1,0:T(8,128)(2,1)}), bf16[8,40,768]{2,1,0:T(8,128)(2,1)S(1)}, u32[]{:S(2)}, u32[]{:S(2)}) async-start(bf16[8,40,768]{2,1,0:T(8,128)(2,1)} %bitcast.7), calls=%async_computation | async-start | bytes 983040 | tf_op jit(solution)/shard_map/all_to_all | solution.py:600
  37.8 2.9 %collective-permute-start.11 = (bf16[768,192]{1,0:T(8,128)(2,1)S(1)}, bf16[768,192]{1,0:T(8,128)(2,1)S(1)}, u32[]{:S(2)}, u32[]{:S(2)}) collective-permute-start(bf16[768,192]{1,0:T(8,128)(2,1)S(1)} %get-tuple-element.117.refs_1_.wo_ref), channel_id=1, source_target_pairs={{0,2},{2,0},{1,3},{3,1},{4,6},{6,4},{5,7},{7,5},{8,10},{10,8},{9,1... | collective-permute-start | bytes 884744 | tf_op jit(solution)/shard_map/ppermute | solution.py:30
  37.9 2.8 %collective-permute-start.10 = (bf16[256,192]{1,0:T(8,128)(2,1)S(1)}, bf16[256,192]{1,0:T(8,128)(2,1)S(1)}, u32[]{:S(2)}, u32[]{:S(2)}) collective-permute-start(bf16[256,192]{1,0:T(8,128)(2,1)S(1)} %get-tuple-element.116), channel_id=1, source_target_pairs={{0,2},{2,0},{1,3},{3,1},{4,6},{6,4},{5,7},{7,5},{8,10},{10,8},{9,1... | collective-permute-start | bytes 294920 | tf_op jit(solution)/shard_map/ppermute | solution.py:30
  41.1 11.2 %collective-permute-start.12 = (bf16[256,768]{1,0:T(8,128)(2,1)S(1)}, bf16[256,768]{1,0:T(8,128)(2,1)S(1)}, u32[]{:S(2)}, u32[]{:S(2)}) collective-permute-start(bf16[256,768]{1,0:T(8,128)(2,1)S(1)} %attended.1), channel_id=1, source_target_pairs={{0,1},{1,0},{2,3},{3,2},{4,5},{5,4},{6,7},{7,6},{8,9},{9,8},{10,11... | collective-permute-start | bytes 1179656 | tf_op jit(solution)/shard_map/ppermute | solution.py:30
  43.4 27.9 %collective-permute-start.21 = (bf16[8,40,768]{2,1,0:T(8,128)(2,1)S(1)}, bf16[8,40,768]{2,1,0:T(8,128)(2,1)S(1)}, u32[]{:S(2)}, u32[]{:S(2)}) collective-permute-start(bf16[8,40,768]{2,1,0:T(8,128)(2,1)S(1)} %all-to-all-done.own_ref), channel_id=1, source_target_pairs={{0,2},{2,0},{1,3},{3,1},{4,6},{6,4},{5,7},{7,5},{8,10},{10,8},{9,1... | collective-permute-start | bytes 1474568 | tf_op jit(solution)/shard_map/ppermute | solution.py:30
  52.4 18.9 %copy-start.1 = (bf16[768,768]{1,0:T(8,128)(2,1)S(1)}, bf16[768,768]{1,0:T(8,128)(2,1)}, u32[]{:S(2)}) copy-start(bf16[768,768]{1,0:T(8,128)(2,1)} %wdown_ref.3) | copy-start | bytes 3538948
  52.8 6.5 %collective-permute-start.13 = (bf16[40,768]{1,0:T(8,128)(2,1)S(1)}, bf16[40,768]{1,0:T(8,128)(2,1)S(1)}, u32[]{:S(2)}, u32[]{:S(2)}) collective-permute-start(bf16[40,768]{1,0:T(8,128)(2,1)S(1)} %get-tuple-element.129), channel_id=1, source_target_pairs={{0,4},{4,0},{8,12},{12,8},{16,20},{20,16},{24,28},{28,24},{1,5},{5... | collective-permute-start | bytes 184328 | tf_op jit(solution)/shard_map/ppermute | solution.py:30
  54.9 6.0 %collective-permute-start.14 = (bf16[40,768]{1,0:T(8,128)(2,1)S(1)}, bf16[40,768]{1,0:T(8,128)(2,1)S(1)}, u32[]{:S(2)}, u32[]{:S(2)}) collective-permute-start(bf16[40,768]{1,0:T(8,128)(2,1)S(1)} %get-tuple-element.130), channel_id=1, source_target_pairs={{0,8},{4,12},{8,0},{12,4},{16,24},{20,28},{24,16},{28,20},{1,9},{5... | collective-permute-start | bytes 184328 | tf_op jit(solution)/shard_map/ppermute | solution.py:30
  56.4 7.8 %collective-permute-start.15 = (bf16[40,768]{1,0:T(8,128)(2,1)S(1)}, bf16[40,768]{1,0:T(8,128)(2,1)S(1)}, u32[]{:S(2)}, u32[]{:S(2)}) collective-permute-start(bf16[40,768]{1,0:T(8,128)(2,1)S(1)} %get-tuple-element.131), channel_id=1, source_target_pairs={{0,12},{4,8},{8,4},{12,0},{16,28},{20,24},{24,20},{28,16},{1,13},{... | collective-permute-start | bytes 184328 | tf_op jit(solution)/shard_map/ppermute | solution.py:30
  56.4 8.6 %collective-permute-start.16 = (bf16[40,768]{1,0:T(8,128)(2,1)S(1)}, bf16[40,768]{1,0:T(8,128)(2,1)S(1)}, u32[]{:S(2)}, u32[]{:S(2)}) collective-permute-start(bf16[40,768]{1,0:T(8,128)(2,1)S(1)} %get-tuple-element.132), channel_id=1, source_target_pairs={{0,16},{4,20},{8,24},{12,28},{16,0},{20,4},{24,8},{28,12},{1,17},{... | collective-permute-start | bytes 184328 | tf_op jit(solution)/shard_map/ppermute | solution.py:30
  59.3 9.6 %collective-permute-start.17 = (bf16[40,768]{1,0:T(8,128)(2,1)S(1)}, bf16[40,768]{1,0:T(8,128)(2,1)S(1)}, u32[]{:S(2)}, u32[]{:S(2)}) collective-permute-start(bf16[40,768]{1,0:T(8,128)(2,1)S(1)} %get-tuple-element.133), channel_id=1, source_target_pairs={{0,20},{4,16},{8,28},{12,24},{16,4},{20,0},{24,12},{28,8},{1,21},{... | collective-permute-start | bytes 184328 | tf_op jit(solution)/shard_map/ppermute | solution.py:30
  60.9 7.9 %collective-permute-start.18 = (bf16[40,768]{1,0:T(8,128)(2,1)S(1)}, bf16[40,768]{1,0:T(8,128)(2,1)S(1)}, u32[]{:S(2)}, u32[]{:S(2)}) collective-permute-start(bf16[40,768]{1,0:T(8,128)(2,1)S(1)} %get-tuple-element.134), channel_id=1, source_target_pairs={{0,24},{4,28},{8,16},{12,20},{16,8},{20,12},{24,0},{28,4},{1,25},{... | collective-permute-start | bytes 184328 | tf_op jit(solution)/shard_map/ppermute | solution.py:30
  64.2 7.1 %collective-permute-start.19 = (bf16[40,768]{1,0:T(8,128)(2,1)S(1)}, bf16[40,768]{1,0:T(8,128)(2,1)S(1)}, u32[]{:S(2)}, u32[]{:S(2)}) collective-permute-start(bf16[40,768]{1,0:T(8,128)(2,1)S(1)} %get-tuple-element.135), channel_id=1, source_target_pairs={{0,28},{4,24},{8,20},{12,16},{16,12},{20,8},{24,4},{28,0},{1,29},{... | collective-permute-start | bytes 184328 | tf_op jit(solution)/shard_map/ppermute | solution.py:30
  68.9 4.3 %copy-start.3 = (bf16[768,768]{1,0:T(8,128)(2,1)S(1)}, bf16[768,768]{1,0:T(8,128)(2,1)}, u32[]{:S(2)}) copy-start(bf16[768,768]{1,0:T(8,128)(2,1)} %wup_ref.1) | copy-start | bytes 3538948
  68.9 4.3 %copy-start.23 = (bf16[768,8]{0,1:T(8,128)(2,1)S(1)}, bf16[768,8]{0,1:T(8,128)(2,1)}, u32[]{:S(2)}) copy-start(bf16[768,8]{0,1:T(8,128)(2,1)} %param.23) | copy-start | bytes 36868
  71.3 1.9 %collective-permute-start.20 = (bf16[320,768]{1,0:T(8,128)(2,1)S(1)}, bf16[320,768]{1,0:T(8,128)(2,1)S(1)}, u32[]{:S(2)}, u32[]{:S(2)}) collective-permute-start(bf16[320,768]{1,0:T(8,128)(2,1)S(1)} %constant_dynamic-update-slice_fusion.own_ref), channel_id=1, source_target_pairs={{0,2},{2,0},{1,3},{3,1},{4,6},{6,4},{5,7},{7,5},{8,10},{10,8},{9,1... | collective-permute-start | bytes 1474568 | tf_op jit(solution)/shard_map/ppermute | solution.py:30
  78.5 2.0 %collective-permute-start.22 = (bf16[320,768]{1,0:T(8,128)(2,1)S(1)}, bf16[320,768]{1,0:T(8,128)(2,1)S(1)}, u32[]{:S(2)}, u32[]{:S(2)}) collective-permute-start(bf16[320,768]{1,0:T(8,128)(2,1)S(1)} %get-tuple-element.140), channel_id=1, source_target_pairs={{0,2},{2,0},{1,3},{3,1},{4,6},{6,4},{5,7},{7,5},{8,10},{10,8},{9,1... | collective-permute-start | bytes 1474568 | tf_op jit(solution)/shard_map/ppermute | solution.py:30
  81.6 17.1 %collective-permute-start.23 = (bf16[320,768]{1,0:T(8,128)(2,1)S(1)}, bf16[320,768]{1,0:T(8,128)(2,1)S(1)}, u32[]{:S(2)}, u32[]{:S(2)}) collective-permute-start(bf16[320,768]{1,0:T(8,128)(2,1)S(1)} %get-tuple-element.143), channel_id=1, source_target_pairs={{0,2},{2,0},{1,3},{3,1},{4,6},{6,4},{5,7},{7,5},{8,10},{10,8},{9,1... | collective-permute-start | bytes 1474568 | tf_op jit(solution)/shard_map/ppermute | solution.py:30
  82.0 4.8 %collective-permute-start.24 = (bf16[40,768]{1,0:T(8,128)(2,1)S(1)}, bf16[40,768]{1,0:T(8,128)(2,1)S(1)}, u32[]{:S(2)}, u32[]{:S(2)}) collective-permute-start(bf16[40,768]{1,0:T(8,128)(2,1)S(1)} %get-tuple-element.145), channel_id=1, source_target_pairs={{0,4},{4,0},{8,12},{12,8},{16,20},{20,16},{24,28},{28,24},{1,5},{5... | collective-permute-start | bytes 184328 | tf_op jit(solution)/shard_map/ppermute | solution.py:30
  82.6 5.9 %collective-permute-start.25 = (bf16[40,768]{1,0:T(8,128)(2,1)S(1)}, bf16[40,768]{1,0:T(8,128)(2,1)S(1)}, u32[]{:S(2)}, u32[]{:S(2)}) collective-permute-start(bf16[40,768]{1,0:T(8,128)(2,1)S(1)} %get-tuple-element.146), channel_id=1, source_target_pairs={{0,8},{4,12},{8,0},{12,4},{16,24},{20,28},{24,16},{28,20},{1,9},{5... | collective-permute-start | bytes 184328 | tf_op jit(solution)/shard_map/ppermute | solution.py:30
  83.2 6.3 %collective-permute-start.26 = (bf16[40,768]{1,0:T(8,128)(2,1)S(1)}, bf16[40,768]{1,0:T(8,128)(2,1)S(1)}, u32[]{:S(2)}, u32[]{:S(2)}) collective-permute-start(bf16[40,768]{1,0:T(8,128)(2,1)S(1)} %get-tuple-element.147), channel_id=1, source_target_pairs={{0,12},{4,8},{8,4},{12,0},{16,28},{20,24},{24,20},{28,16},{1,13},{... | collective-permute-start | bytes 184328 | tf_op jit(solution)/shard_map/ppermute | solution.py:30
  85.5 9.2 %collective-permute-start.27 = (bf16[40,768]{1,0:T(8,128)(2,1)S(1)}, bf16[40,768]{1,0:T(8,128)(2,1)S(1)}, u32[]{:S(2)}, u32[]{:S(2)}) collective-permute-start(bf16[40,768]{1,0:T(8,128)(2,1)S(1)} %get-tuple-element.148), channel_id=1, source_target_pairs={{0,16},{4,20},{8,24},{12,28},{16,0},{20,4},{24,8},{28,12},{1,17},{... | collective-permute-start | bytes 184328 | tf_op jit(solution)/shard_map/ppermute | solution.py:30
  86.9 10.2 %collective-permute-start.28 = (bf16[40,768]{1,0:T(8,128)(2,1)S(1)}, bf16[40,768]{1,0:T(8,128)(2,1)S(1)}, u32[]{:S(2)}, u32[]{:S(2)}) collective-permute-start(bf16[40,768]{1,0:T(8,128)(2,1)S(1)} %get-tuple-element.149), channel_id=1, source_target_pairs={{0,20},{4,16},{8,28},{12,24},{16,4},{20,0},{24,12},{28,8},{1,21},{... | collective-permute-start | bytes 184328 | tf_op jit(solution)/shard_map/ppermute | solution.py:30
  88.4 8.6 %collective-permute-start.29 = (bf16[40,768]{1,0:T(8,128)(2,1)S(1)}, bf16[40,768]{1,0:T(8,128)(2,1)S(1)}, u32[]{:S(2)}, u32[]{:S(2)}) collective-permute-start(bf16[40,768]{1,0:T(8,128)(2,1)S(1)} %get-tuple-element.150), channel_id=1, source_target_pairs={{0,24},{4,28},{8,16},{12,20},{16,8},{20,12},{24,0},{28,4},{1,25},{... | collective-permute-start | bytes 184328 | tf_op jit(solution)/shard_map/ppermute | solution.py:30
  89.5 7.6 %collective-permute-start.30 = (bf16[40,768]{1,0:T(8,128)(2,1)S(1)}, bf16[40,768]{1,0:T(8,128)(2,1)S(1)}, u32[]{:S(2)}, u32[]{:S(2)}) collective-permute-start(bf16[40,768]{1,0:T(8,128)(2,1)S(1)} %get-tuple-element.141.held_ref), channel_id=1, source_target_pairs={{0,28},{4,24},{8,20},{12,16},{16,12},{20,8},{24,4},{28,0},{1,29},{... | collective-permute-start | bytes 184328 | tf_op jit(solution)/shard_map/ppermute | solution.py:30
  97.5 9.8 %collective-permute-start.31 = (bf16[256,768]{1,0:T(8,128)(2,1)S(1)}, bf16[256,768]{1,0:T(8,128)(2,1)}, u32[]{:S(2)}, u32[]{:S(2)}) collective-permute-start(bf16[256,768]{1,0:T(8,128)(2,1)S(1)} %gather_grad.1.own_ref), channel_id=1, source_target_pairs={{0,1},{1,0},{2,3},{3,2},{4,5},{5,4},{6,7},{7,6},{8,9},{9,8},{10,11... | collective-permute-start | bytes 1179656 | tf_op jit(solution)/shard_map/ppermute | solution.py:30
  100.2 25.6 %all-to-all-start.1 = ((bf16[8,40,768]{2,1,0:T(8,128)(2,1)}), bf16[8,40,768]{2,1,0:T(8,128)(2,1)S(1)}, u32[]{:S(2)}, u32[]{:S(2)}) async-start(bf16[8,40,768]{2,1,0:T(8,128)(2,1)} %join_out.1.refs_8_), calls=%async_computation.1 | async-start | bytes 983040 | tf_op jit(solution)/shard_map/all_to_all | solution.py:600
  109.6 1.7 %collective-permute-start.32 = (bf16[256,768]{1,0:T(8,128)(2,1)S(1)}, bf16[256,768]{1,0:T(8,128)(2,1)S(1)}, u32[]{:S(2)}, u32[]{:S(2)}) collective-permute-start(bf16[256,768]{1,0:T(8,128)(2,1)S(1)} %get-tuple-element.159.own_ref), channel_id=1, source_target_pairs={{0,2},{2,0},{1,3},{3,1},{4,6},{6,4},{5,7},{7,5},{8,10},{10,8},{9,1... | collective-permute-start | bytes 1179656 | tf_op jit(solution)/shard_map/ppermute | solution.py:30
  115.9 13.2 %collective-permute-start.33 = (bf16[384,384]{1,0:T(8,128)(2,1)}, bf16[384,384]{1,0:T(8,128)(2,1)}, u32[]{:S(2)}, u32[]{:S(2)}) collective-permute-start(bf16[384,384]{1,0:T(8,128)(2,1)} %get-tuple-element.176), channel_id=1, source_target_pairs={{0,4},{4,0},{8,12},{12,8},{16,20},{20,16},{24,28},{28,24},{1,5},{5... | collective-permute-start | bytes 884744 | tf_op jit(solution)/shard_map/ppermute | solution.py:30
  124.9 11.4 %collective-permute-start.36 = (bf16[256,768]{1,0:T(8,128)(2,1)}, bf16[256,768]{1,0:T(8,128)(2,1)}, u32[]{:S(2)}, u32[]{:S(2)}) collective-permute-start(bf16[256,768]{1,0:T(8,128)(2,1)} %get-tuple-element.181), channel_id=1, source_target_pairs={{0,2},{2,0},{1,3},{3,1},{4,6},{6,4},{5,7},{7,5},{8,10},{10,8},{9,1... | collective-permute-start | bytes 1179656 | tf_op jit(solution)/shard_map/ppermute | solution.py:30
  124.9 4.2 %collective-permute-start.34 = (f32[16,768]{1,0:T(8,128)S(1)}, f32[16,768]{1,0:T(8,128)S(1)}, u32[]{:S(2)}, u32[]{:S(2)}) collective-permute-start(f32[16,768]{1,0:T(8,128)S(1)} %get-tuple-element.177.small_ref), channel_id=1, source_target_pairs={{0,1},{1,0},{2,3},{3,2},{4,5},{5,4},{6,7},{7,6},{8,9},{9,8},{10,11... | collective-permute-start | bytes 147464 | tf_op jit(solution)/shard_map/ppermute | solution.py:30
  129.1 13.0 %copy-start.14 = (f32[384,384]{1,0:T(8,128)S(1)}, f32[384,384]{1,0:T(8,128)}, u32[]{:S(2)}) copy-start(f32[384,384]{1,0:T(8,128)} %copy-done.13) | copy-start | bytes 1769476
  130.2 11.9 %collective-permute-start.37 = (bf16[416,384]{1,0:T(8,128)(2,1)S(1)}, bf16[416,384]{1,0:T(8,128)(2,1)S(1)}, u32[]{:S(2)}, u32[]{:S(2)}) collective-permute-start(bf16[416,384]{1,0:T(8,128)(2,1)S(1)} %get-tuple-element.185), channel_id=1, source_target_pairs={{0,4},{4,0},{8,12},{12,8},{16,20},{20,16},{24,28},{28,24},{1,5},{5... | collective-permute-start | bytes 958472 | tf_op jit(solution)/shard_map/ppermute | solution.py:30
  130.4 8.3 %collective-permute-start.38 = (bf16[96,384]{1,0:T(8,128)(2,1)S(1)}, bf16[96,384]{1,0:T(8,128)(2,1)S(1)}, u32[]{:S(2)}, u32[]{:S(2)}) collective-permute-start(bf16[96,384]{1,0:T(8,128)(2,1)S(1)} %get-tuple-element.182.held_ref), channel_id=1, source_target_pairs={{0,8},{4,12},{8,0},{12,4},{16,24},{20,28},{24,16},{28,20},{1,9},{5... | collective-permute-start | bytes 221192 | tf_op jit(solution)/shard_map/ppermute | solution.py:30
  133.9 8.2 %collective-permute-start.39 = (bf16[96,384]{1,0:T(8,128)(2,1)S(1)}, bf16[96,384]{1,0:T(8,128)(2,1)S(1)}, u32[]{:S(2)}, u32[]{:S(2)}) collective-permute-start(bf16[96,384]{1,0:T(8,128)(2,1)S(1)} %get-tuple-element.189), channel_id=1, source_target_pairs={{0,16},{4,20},{8,24},{12,28},{16,0},{20,4},{24,8},{28,12},{1,17},{... | collective-permute-start | bytes 221192 | tf_op jit(solution)/shard_map/ppermute | solution.py:30
  134.7 7.4 %collective-permute-start.40 = (bf16[96,384]{1,0:T(8,128)(2,1)S(1)}, bf16[96,384]{1,0:T(8,128)(2,1)S(1)}, u32[]{:S(2)}, u32[]{:S(2)}) collective-permute-start(bf16[96,384]{1,0:T(8,128)(2,1)S(1)} %get-tuple-element.190), channel_id=1, source_target_pairs={{0,24},{4,28},{8,16},{12,20},{16,8},{20,12},{24,0},{28,4},{1,25},{... | collective-permute-start | bytes 221192 | tf_op jit(solution)/shard_map/ppermute | solution.py:30
  136.3 12.2 %collective-permute-start.35 = (bf16[128,768]{1,0:T(8,128)(2,1)S(1)}, bf16[128,768]{1,0:T(8,128)(2,1)S(1)}, u32[]{:S(2)}, u32[]{:S(2)}) collective-permute-start(bf16[128,768]{1,0:T(8,128)(2,1)S(1)} %get-tuple-element.180), channel_id=1, source_target_pairs={{0,1},{1,0},{2,3},{3,2},{4,5},{5,4},{6,7},{7,6},{8,9},{9,8},{10,11... | collective-permute-start | bytes 589832 | tf_op jit(solution)/shard_map/ppermute | solution.py:30
  137.5 12.3 %copy-start.8 = (bf16[640,768]{1,0:T(8,128)(2,1)S(1)}, bf16[640,768]{1,0:T(8,128)(2,1)}, u32[]{:S(2)}) copy-start(bf16[640,768]{1,0:T(8,128)(2,1)} %copy-done.7) | copy-start | bytes 2949124
  142.1 7.6 %copy-start.4 = (bf16[640,768]{1,0:T(8,128)(2,1)S(1)}, bf16[640,768]{1,0:T(8,128)(2,1)}, u32[]{:S(2)}) copy-start(bf16[640,768]{1,0:T(8,128)(2,1)} %get-tuple-element.200.cots_ref) | copy-start | bytes 2949124
  142.1 7.6 %copy-start.6 = (bf16[640,768]{1,0:T(8,128)(2,1)S(1)}, bf16[640,768]{1,0:T(8,128)(2,1)}, u32[]{:S(2)}) copy-start(bf16[640,768]{1,0:T(8,128)(2,1)} %copy-done.5) | copy-start | bytes 2949124
  142.8 10.7 %collective-permute-start.41 = (bf16[128,768]{1,0:T(8,128)(2,1)S(1)}, bf16[128,768]{1,0:T(8,128)(2,1)S(1)}, u32[]{:S(2)}, u32[]{:S(2)}) collective-permute-start(bf16[128,768]{1,0:T(8,128)(2,1)S(1)} %get-tuple-element.191), channel_id=1, source_target_pairs={{0,1},{1,0},{2,3},{3,2},{4,5},{5,4},{6,7},{7,6},{8,9},{9,8},{10,11... | collective-permute-start | bytes 589832 | tf_op jit(solution)/shard_map/ppermute | solution.py:30
  144.1 10.4 %collective-permute-start.43 = (bf16[128,384]{1,0:T(8,128)(2,1)S(1)}, bf16[128,384]{1,0:T(8,128)(2,1)S(1)}, u32[]{:S(2)}, u32[]{:S(2)}) collective-permute-start(bf16[128,384]{1,0:T(8,128)(2,1)S(1)} %get-tuple-element.196.held_ref), channel_id=1, source_target_pairs={{0,8},{4,12},{8,0},{12,4},{16,24},{20,28},{24,16},{28,20},{1,9},{5... | collective-permute-start | bytes 294920 | tf_op jit(solution)/shard_map/ppermute | solution.py:30
  145.4 9.4 %collective-permute-start.44 = (bf16[128,384]{1,0:T(8,128)(2,1)S(1)}, bf16[128,384]{1,0:T(8,128)(2,1)S(1)}, u32[]{:S(2)}, u32[]{:S(2)}) collective-permute-start(bf16[128,384]{1,0:T(8,128)(2,1)S(1)} %get-tuple-element.197), channel_id=1, source_target_pairs={{0,16},{4,20},{8,24},{12,28},{16,0},{20,4},{24,8},{28,12},{1,17},{... | collective-permute-start | bytes 294920 | tf_op jit(solution)/shard_map/ppermute | solution.py:30
  146.5 8.3 %collective-permute-start.45 = (bf16[128,384]{1,0:T(8,128)(2,1)S(1)}, bf16[128,384]{1,0:T(8,128)(2,1)S(1)}, u32[]{:S(2)}, u32[]{:S(2)}) collective-permute-start(bf16[128,384]{1,0:T(8,128)(2,1)S(1)} %get-tuple-element.198), channel_id=1, source_target_pairs={{0,24},{4,28},{8,16},{12,20},{16,8},{20,12},{24,0},{28,4},{1,25},{... | collective-permute-start | bytes 294920 | tf_op jit(solution)/shard_map/ppermute | solution.py:30
  149.7 3.8 %copy-start.12 = (bf16[128,768]{1,0:T(8,128)(2,1)S(1)}, bf16[128,768]{1,0:T(8,128)(2,1)}, u32[]{:S(2)}) copy-start(bf16[128,768]{1,0:T(8,128)(2,1)} %x_ref.1) | copy-start | bytes 589828
  155.4 1.5 collective-permute-start.46
  155.5 1.4 collective-permute-start.42
  (13 other events, 22.3 us)

commit v6 on v5

--- a/solution.py
+++ b/solution.py
@@ -238,7 +238,7 @@
 def expert_kernel(ids, own_ref, other_ref, h_ref, wup_ref, wr_ref, *refs):
     active_ref, gup_ref, chosen_ref, keep_ref, send_ref, router_ref, all_ref = refs
     rows = own_ref.shape[0]
-    step = rows // 2
+    step = rows
     router = jnp.zeros(router_ref.shape, f32)
     root = 0.7978845608028654
     for i in range(0, 2 * rows, step):

time: 160 us -> 159 us (level)
  no operation moved by 1% of the time
where the time goes in v6:
time: 159 us; the launch traced here: 158 us
  starting transfers between devices  64.5 us (41%)
  Pallas kernels  46.6 us (29%)
  waiting for transfers between devices  36.7 us (23%)
  local copies, waits for them, and re-layouts  7.02 us (4%)
  other arithmetic  1.91 us (1%)
    ppermute x47, starting transfers between devices, across(): lax.ppermute(shard, axis, [(i, i ^ bits) for i in range(lax.axis_size(axi...  55.5 us
    pallas_call x27, Pallas kernels, call(): pl.pallas_call(body, name=name, out_shape=[space[type(o)](x.shape, x.dtyp...  46.6 us
    ppermute x47, waiting for transfers between devices, across(): lax.ppermute(shard, axis, [(i, i ^ bits) for i in range(lax.axis_size(axi...  35.6 us
    all_to_all x2, starting transfers between devices, trade_natural(): lax.all_to_all(stacked, 'node', split_axis=0, concat_axis=0, tiled=True)  8.91 us
    unnamed x64, local copies, waits for them, and re-layouts  6.15 us
  transfers between devices with their start and end apart: 49, of which 13 were waited for; matrix products, arithmetic and copies ran while one was open for 1% of the time, Pallas kernels for 24%

profile of v6, /device:TPU:0, one launch (start us, length us, event | category | flops | bytes accessed | tf_op | source)
XLA Modules:
  0.0 158.4 jit_solution(14018236899509930539)
XLA Ops:
  0.8 1.6 shares.1
  2.9 2.6 %collective-permute-start = (bf16[128,768]{1,0:T(8,128)(2,1)}, bf16[128,768]{1,0:T(8,128)(2,1)S(1)}, u32[]{:S(2)}, u32[]{:S(2)}) collective-permute-start(bf16[128,768]{1,0:T(8,128)(2,1)} %x_ref.1), channel_id=1, source_target_pairs={{0,1},{1,0},{2,3},{3,2},{4,5},{5,4},{6,7},{7,6},{8,9},{9,8},{10,11... | collective-permute-start | bytes 589832 | tf_op jit(solution)/shard_map/ppermute | solution.py:30
  5.5 1.6 collective-permute-start.2
  7.1 1.6 collective-permute-start.4
  9.5 2.6 %collective-permute-start.6 = (bf16[96,768]{1,0:T(8,128)(2,1)S(1)}, bf16[96,768]{1,0:T(8,128)(2,1)S(1)}, u32[]{:S(2)}, u32[]{:S(2)}) collective-permute-start(bf16[96,768]{1,0:T(8,128)(2,1)S(1)} %maximum_select_fusion.refs_0_), channel_id=1, source_target_pairs={{0,16},{4,20},{8,24},{12,28},{16,0},{20,4},{24,8},{28,12},{1,17},{... | collective-permute-start | bytes 442376 | tf_op jit(solution)/shard_map/ppermute | solution.py:30
  12.3 0.9 copy-done.11
  15.1 0.9 tables.1
  16.1 7.3 %collective-permute-done.6.refs_4_ = bf16[96,768]{1,0:T(8,128)(2,1)S(1)} collective-permute-done((bf16[96,768]{1,0:T(8,128)(2,1)S(1)}, bf16[96,768]{1,0:T(8,128)(2,1)S(1)}, u32[]{:S(2)}, u32[]{:S(2)}) %collective-permute-start.6) | collective-permute-done | bytes 147488 | tf_op jit(solution)/shard_map/ppermute | solution.py:30
  23.9 1.5 collective-permute-start.9
  25.4 1.1 cot_slots.1
  26.5 4.2 %all-to-all-start = ((bf16[8,40,768]{2,1,0:T(8,128)(2,1)}), bf16[8,40,768]{2,1,0:T(8,128)(2,1)S(1)}, u32[]{:S(2)}, u32[]{:S(2)}) async-start(bf16[8,40,768]{2,1,0:T(8,128)(2,1)} %bitcast.7), calls=%async_computation | async-start | bytes 983040 | tf_op jit(solution)/shard_map/all_to_all | solution.py:600
  31.2 0.9 copy-done.22
  32.1 5.6 %attend.1 = (bf16[768,768]{1,0:T(8,128)(2,1)S(1)}, bf16[768,192]{1,0:T(8,128)(2,1)S(1)}, bf16[512,768]{1,0:T(8,128)(2,1)S(1)}, bf16[512,576]{1,0:T(8,128)(2,1)S(...) custom-call(s32[3]{0:T(128)S(1)} %pad_add_fusion.ids, ...), custom_call_target="tpu_custom_call" | custom-call | tf_op jit(solution)/shard_map/attend/pallas_call | solution.py:55
  38.3 2.3 %park.1 = (bf16[768,768]{1,0:T(8,128)(2,1)}, bf16[768,192]{1,0:T(8,128)(2,1)}, bf16[512,768]{1,0:T(8,128)(2,1)}, bf16[512,576]{1,0:T(8,128)(2,1)}, bf16[512,192]...) custom-call(bf16[768,768]{1,0:T(8,128)(2,1)S(1)} %get-tuple-element.118.refs_0_, ...), custom_call_target="tpu_custom_call" | custom-call | tf_op jit(solution)/shard_map/park/pallas_call | solution.py:55
  41.1 1.2 collective-permute-start.12
  42.3 1.1 all-to-all-done.own_ref
  43.4 8.9 %collective-permute-done.12 = bf16[256,768]{1,0:T(8,128)(2,1)S(1)} collective-permute-done((bf16[256,768]{1,0:T(8,128)(2,1)S(1)}, bf16[256,768]{1,0:T(8,128)(2,1)S(1)}, u32[]{:S(2)}, u32[]{:S(2)}) %collective-permute-start.12) | collective-permute-done | bytes 393248 | tf_op jit(solution)/shard_map/ppermute | solution.py:30
  52.8 2.1 %collective-permute-start.13 = (bf16[40,768]{1,0:T(8,128)(2,1)S(1)}, bf16[40,768]{1,0:T(8,128)(2,1)S(1)}, u32[]{:S(2)}, u32[]{:S(2)}) collective-permute-start(bf16[40,768]{1,0:T(8,128)(2,1)S(1)} %get-tuple-element.129), channel_id=1, source_target_pairs={{0,4},{4,0},{8,12},{12,8},{16,20},{20,16},{24,28},{28,24},{1,5},{5... | collective-permute-start | bytes 184328 | tf_op jit(solution)/shard_map/ppermute | solution.py:30
  54.9 1.5 collective-permute-start.14
  56.4 2.8 %collective-permute-start.16 = (bf16[40,768]{1,0:T(8,128)(2,1)S(1)}, bf16[40,768]{1,0:T(8,128)(2,1)S(1)}, u32[]{:S(2)}, u32[]{:S(2)}) collective-permute-start(bf16[40,768]{1,0:T(8,128)(2,1)S(1)} %get-tuple-element.132), channel_id=1, source_target_pairs={{0,16},{4,20},{8,24},{12,28},{16,0},{20,4},{24,8},{28,12},{1,17},{... | collective-permute-start | bytes 184328 | tf_op jit(solution)/shard_map/ppermute | solution.py:30
  59.3 1.6 %collective-permute-start.17 = (bf16[40,768]{1,0:T(8,128)(2,1)S(1)}, bf16[40,768]{1,0:T(8,128)(2,1)S(1)}, u32[]{:S(2)}, u32[]{:S(2)}) collective-permute-start(bf16[40,768]{1,0:T(8,128)(2,1)S(1)} %get-tuple-element.133), channel_id=1, source_target_pairs={{0,20},{4,16},{8,28},{12,24},{16,4},{20,0},{24,12},{28,8},{1,21},{... | collective-permute-start | bytes 184328 | tf_op jit(solution)/shard_map/ppermute | solution.py:30
  60.9 3.2 %collective-permute-start.18 = (bf16[40,768]{1,0:T(8,128)(2,1)S(1)}, bf16[40,768]{1,0:T(8,128)(2,1)S(1)}, u32[]{:S(2)}, u32[]{:S(2)}) collective-permute-start(bf16[40,768]{1,0:T(8,128)(2,1)S(1)} %get-tuple-element.134), channel_id=1, source_target_pairs={{0,24},{4,28},{8,16},{12,20},{16,8},{20,12},{24,0},{28,4},{1,25},{... | collective-permute-start | bytes 184328 | tf_op jit(solution)/shard_map/ppermute | solution.py:30
  64.2 0.8 collective-permute-start.19
  65.0 3.8 %collective-permute-done.17 = bf16[40,768]{1,0:T(8,128)(2,1)S(1)} collective-permute-done((bf16[40,768]{1,0:T(8,128)(2,1)S(1)}, bf16[40,768]{1,0:T(8,128)(2,1)S(1)}, u32[]{:S(2)}, u32[]{:S(2)}) %collective-permute-start.17) | collective-permute-done | bytes 61472 | tf_op jit(solution)/shard_map/ppermute | solution.py:30
  68.9 2.4 %collective-permute-done.19 = bf16[40,768]{1,0:T(8,128)(2,1)S(1)} collective-permute-done((bf16[40,768]{1,0:T(8,128)(2,1)S(1)}, bf16[40,768]{1,0:T(8,128)(2,1)S(1)}, u32[]{:S(2)}, u32[]{:S(2)}) %collective-permute-start.19) | collective-permute-done | bytes 61472 | tf_op jit(solution)/shard_map/ppermute | solution.py:30
  71.3 1.8 %cots.1 = (bf16[640,768]{1,0:T(8,128)(2,1)}, f32[640,768]{1,0:T(8,128)S(1)}) custom-call(s32[3]{0:T(128)S(1)} %pad_add_fusion.ids, bf16[8,40,768]{2,1,0:T(8,128)(2,1)S(1)} %all-to-all-done.own_ref, bf16[8,40,768]{2,1,0:T(8,128)(2,1)S(1)} %collective-permute-done.21.other_ref, bf16[768,768]{1,0:T(8,128)(2,1)S(1)} %copy-done.1, ...), custom_call_target="tpu_custom_call" | custom-call | tf_op jit(solution)/shard_map/cots/pallas_call | solution.py:55
  73.2 4.2 %expert.1 = (bf16[640,768]{1,0:T(8,128)(2,1)S(1)}, bf16[640,768]{1,0:T(8,128)(2,1)S(1)}, f32[640,1]{1,0:T(8,128)S(1)}, f32[320,768]{1,0:T(8,128)S(1)}, bf16[320,...) custom-call(s32[3]{0:T(128)S(1)} %pad_add_fusion.ids, ...), custom_call_target="tpu_custom_call" | custom-call | tf_op jit(solution)/shard_map/expert/pallas_call | solution.py:55
  78.0 1.5 collective-permute-done.22.got_ref
  79.5 1.0 expert_out.1
  82.1 2.3 %collective-permute-start.26 = (bf16[40,768]{1,0:T(8,128)(2,1)S(1)}, bf16[40,768]{1,0:T(8,128)(2,1)S(1)}, u32[]{:S(2)}, u32[]{:S(2)}) collective-permute-start(bf16[40,768]{1,0:T(8,128)(2,1)S(1)} %get-tuple-element.147), channel_id=1, source_target_pairs={{0,12},{4,8},{8,4},{12,0},{16,28},{20,24},{24,20},{28,16},{1,13},{... | collective-permute-start | bytes 184328 | tf_op jit(solution)/shard_map/ppermute | solution.py:30
  84.5 1.3 collective-permute-start.27
  85.8 1.6 collective-permute-start.28
  87.4 1.0 collective-permute-start.29
  88.4 3.7 %collective-permute-start.30 = (bf16[40,768]{1,0:T(8,128)(2,1)S(1)}, bf16[40,768]{1,0:T(8,128)(2,1)S(1)}, u32[]{:S(2)}, u32[]{:S(2)}) collective-permute-start(bf16[40,768]{1,0:T(8,128)(2,1)S(1)} %get-tuple-element.141.held_ref), channel_id=1, source_target_pairs={{0,28},{4,24},{8,20},{12,16},{16,12},{20,8},{24,4},{28,0},{1,29},{... | collective-permute-start | bytes 184328 | tf_op jit(solution)/shard_map/ppermute | solution.py:30
  92.1 1.6 collective-permute-done.27.refs_4_
  93.7 2.3 %collective-permute-done.28.refs_5_ = bf16[40,768]{1,0:T(8,128)(2,1)S(1)} collective-permute-done((bf16[40,768]{1,0:T(8,128)(2,1)S(1)}, bf16[40,768]{1,0:T(8,128)(2,1)S(1)}, u32[]{:S(2)}, u32[]{:S(2)}) %collective-permute-start.28) | collective-permute-done | bytes 61472 | tf_op jit(solution)/shard_map/ppermute | solution.py:30
  96.4 1.2 collective-permute-start.31
  97.6 1.4 join_out.1.refs_8_
  99.1 4.7 %all-to-all-start.1 = ((bf16[8,40,768]{2,1,0:T(8,128)(2,1)}), bf16[8,40,768]{2,1,0:T(8,128)(2,1)S(1)}, u32[]{:S(2)}, u32[]{:S(2)}) async-start(bf16[8,40,768]{2,1,0:T(8,128)(2,1)} %join_out.1.refs_8_), calls=%async_computation.1 | async-start | bytes 983040 | tf_op jit(solution)/shard_map/all_to_all | solution.py:600
  103.7 2.4 %unpark.1 = (bf16[768,768]{1,0:T(8,128)(2,1)S(1)}, bf16[768,192]{1,0:T(8,128)(2,1)S(1)}, bf16[512,768]{1,0:T(8,128)(2,1)S(1)}, bf16[512,576]{1,0:T(8,128)(2,1)S(...) custom-call(bf16[768,768]{1,0:T(8,128)(2,1)} %get-tuple-element.151., ...), custom_call_target="tpu_custom_call" | custom-call | tf_op jit(solution)/shard_map/unpark/pallas_call | solution.py:55
  106.2 1.5 hidden_back.1
  108.5 1.7 %collective-permute-done.32.other_ref = bf16[256,768]{1,0:T(8,128)(2,1)S(1)} collective-permute-done((bf16[256,768]{1,0:T(8,128)(2,1)S(1)}, bf16[256,768]{1,0:T(8,128)(2,1)S(1)}, u32[]{:S(2)}, u32[]{:S(2)}) %collective-permute-start.32) | collective-permute-done | bytes 393248 | tf_op jit(solution)/shard_map/ppermute | solution.py:30
  110.2 3.8 %first_back.1 = (bf16[512,192]{1,0:T(8,128)(2,1)S(1)}, bf16[512,192]{1,0:T(8,128)(2,1)S(1)}, f32[8,1024]{1,0:T(8,128)S(1)}, bf16[512,768]{1,0:T(8,128)(2,1)S(1)}...) custom-call(s32[3]{0:T(128)S(1)} %pad_add_fusion.ids, bf16[256,768]{1,0:T(8,128)(2,1)S(1)} %get-tuple-element.159.own_ref, ...), custom_call_target="tpu_custom_call" | custom-call | tf_op jit(solution)/shard_map/first_back/pallas_call | solution.py:55
  114.8 2.0 %collective-permute-start.33 = (bf16[384,384]{1,0:T(8,128)(2,1)}, bf16[384,384]{1,0:T(8,128)(2,1)}, u32[]{:S(2)}, u32[]{:S(2)}) collective-permute-start(bf16[384,384]{1,0:T(8,128)(2,1)} %get-tuple-element.176), channel_id=1, source_target_pairs={{0,4},{4,0},{8,12},{12,8},{16,20},{20,16},{24,28},{28,24},{1,5},{5... | collective-permute-start | bytes 884744 | tf_op jit(solution)/shard_map/ppermute | solution.py:30
  117.1 5.2 %second_back.1 = (f32[256,768]{1,0:T(8,128)S(1)}, bf16[256,768]{1,0:T(8,128)(2,1)}, f32[16,768]{1,0:T(8,128)S(1)}, f32[384,384]{1,0:T(8,128)S(1)}, bf16[384,384]{1,0:T(8,128)(2,1)S(1)}) custom-call(s32[3]{0:T(128)S(1)} %pad_add_fusion.ids, bf16[512,192]{1,0:T(8,128)(2,1)S(1)} %get-tuple-element.164.gm_ref, ...), custom_call_target="tpu_custom_call" | custom-call | tf_op jit(solution)/shard_map/second_back/pallas_call | solution.py:55
  123.8 0.9 collective-permute-start.34
  124.7 0.9 copy-done.10
  125.6 0.9 returned.1
  126.6 1.4 collective-permute-done.34.small_got_ref
  128.0 1.1 fold_first.1
  129.3 3.6 %collective-permute-start.38 = (bf16[96,384]{1,0:T(8,128)(2,1)S(1)}, bf16[96,384]{1,0:T(8,128)(2,1)S(1)}, u32[]{:S(2)}, u32[]{:S(2)}) collective-permute-start(bf16[96,384]{1,0:T(8,128)(2,1)S(1)} %get-tuple-element.182.held_ref), channel_id=1, source_target_pairs={{0,8},{4,12},{8,0},{12,4},{16,24},{20,28},{24,16},{28,20},{1,9},{5... | collective-permute-start | bytes 221192 | tf_op jit(solution)/shard_map/ppermute | solution.py:30
  133.6 1.6 %collective-permute-start.40 = (bf16[96,384]{1,0:T(8,128)(2,1)S(1)}, bf16[96,384]{1,0:T(8,128)(2,1)S(1)}, u32[]{:S(2)}, u32[]{:S(2)}) collective-permute-start(bf16[96,384]{1,0:T(8,128)(2,1)S(1)} %get-tuple-element.190), channel_id=1, source_target_pairs={{0,24},{4,28},{8,16},{12,20},{16,8},{20,12},{24,0},{28,4},{1,25},{... | collective-permute-start | bytes 221192 | tf_op jit(solution)/shard_map/ppermute | solution.py:30
  135.2 1.2 collective-permute-start.35
  136.4 1.2 normed_sum.1
  137.7 3.4 %collective-permute-done.39.refs_2_ = bf16[96,384]{1,0:T(8,128)(2,1)S(1)} collective-permute-done((bf16[96,384]{1,0:T(8,128)(2,1)S(1)}, bf16[96,384]{1,0:T(8,128)(2,1)S(1)}, u32[]{:S(2)}, u32[]{:S(2)}) %collective-permute-start.39) | collective-permute-done | bytes 73760 | tf_op jit(solution)/shard_map/ppermute | solution.py:30
  141.8 1.2 collective-permute-start.41
  143.0 1.3 collective-permute-start.43
  144.3 1.1 collective-permute-start.44
  145.5 1.9 %collective-permute-start.45 = (bf16[128,384]{1,0:T(8,128)(2,1)S(1)}, bf16[128,384]{1,0:T(8,128)(2,1)S(1)}, u32[]{:S(2)}, u32[]{:S(2)}) collective-permute-start(bf16[128,384]{1,0:T(8,128)(2,1)S(1)} %get-tuple-element.198), channel_id=1, source_target_pairs={{0,24},{4,28},{8,16},{12,20},{16,8},{20,12},{24,0},{28,4},{1,25},{... | collective-permute-start | bytes 294920 | tf_op jit(solution)/shard_map/ppermute | solution.py:30
  147.4 1.3 activations.1.refs_5_
  148.7 3.7 %expert_grads.1 = (f32[768,768]{1,0:T(8,128)}, f32[768,768]{1,0:T(8,128)}) custom-call(bf16[640,768]{1,0:T(8,128)(2,1)S(1)} %copy-done.8, bf16[640,768]{1,0:T(8,128)(2,1)S(1)} %copy-done.4, bf16[640,768]{1,0:T(8,128)(2,1)S(1)} %get-tuple-element.137.active_ref, bf16[640,768]{1,0:T(8,128)(2,1)S(1)} %copy-done.6, f32[640,1]{1,0:T(8,128)S(1)} %get-tuple-element.138.chosen_ref, ...), custom_call_target="tpu_custom_call" | custom-call | tf_op jit(solution)/shard_map/expert_grads/pallas_call | solution.py:55
  152.5 0.9 input_grad.1.refs_6_
  154.9 0.9 collective-permute-done.42.got_one
  155.9 1.4 columns.1
  (141 shorter events, 16.5 us)
Async XLA Ops:
  0.6 15.4 %copy-start = (f32[32,12]{0,1:T(8,128)S(1)}, f32[32,12]{0,1:T(8,128)}, u32[]{:S(2)}) copy-start(f32[32,12]{0,1:T(8,128)} %param.21) | copy-start | bytes 4612
  0.7 14.1 %copy-start.24 = (s32[1023]{0:T(1024)S(1)}, s32[1023]{0:T(1024)}, u32[]{:S(2)}) copy-start(s32[1023]{0:T(1024)} %param.28) | copy-start | bytes 12280
  0.7 14.2 %copy-start.25 = (bf16[768]{0:T(1024)(128)(2,1)S(1)}, bf16[768]{0:T(1024)(128)(2,1)}, u32[]{:S(2)}) copy-start(bf16[768]{0:T(1024)(128)(2,1)} %param.16) | copy-start | bytes 4612
  0.7 14.2 %copy-start.27 = (s32[256,1]{0,1:T(1,128)S(1)}, s32[256,1]{0,1:T(1,128)}, u32[]{:S(2)}) copy-start(s32[256,1]{0,1:T(1,128)} %param.26) | copy-start | bytes 3076
  0.7 24.7 %copy-start.2 = (bf16[256,768]{1,0:T(8,128)(2,1)S(1)}, bf16[256,768]{1,0:T(8,128)(2,1)}, u32[]{:S(2)}) copy-start(bf16[256,768]{1,0:T(8,128)(2,1)} %cot_ref.1) | copy-start | bytes 1179652
  2.4 3.1 %collective-permute-start.1 = (bf16[48,768]{1,0:T(8,128)(2,1)S(1)}, bf16[48,768]{1,0:T(8,128)(2,1)S(1)}, u32[]{:S(2)}, u32[]{:S(2)}) collective-permute-start(bf16[48,768]{1,0:T(8,128)(2,1)S(1)} %get-tuple-element.114), channel_id=1, source_target_pairs={{0,2},{2,0},{1,3},{3,1},{4,6},{6,4},{5,7},{7,5},{8,10},{10,8},{9,1... | collective-permute-start | bytes 221192 | tf_op jit(solution)/shard_map/ppermute | solution.py:30
  2.9 9.5 %collective-permute-start = (bf16[128,768]{1,0:T(8,128)(2,1)}, bf16[128,768]{1,0:T(8,128)(2,1)S(1)}, u32[]{:S(2)}, u32[]{:S(2)}) collective-permute-start(bf16[128,768]{1,0:T(8,128)(2,1)} %x_ref.1), channel_id=1, source_target_pairs={{0,1},{1,0},{2,3},{3,2},{4,5},{5,4},{6,7},{7,6},{8,9},{9,8},{10,11... | collective-permute-start | bytes 589832 | tf_op jit(solution)/shard_map/ppermute | solution.py:30
  5.5 6.8 %collective-permute-start.2 = (bf16[96,768]{1,0:T(8,128)(2,1)S(1)}, bf16[96,768]{1,0:T(8,128)(2,1)S(1)}, u32[]{:S(2)}, u32[]{:S(2)}) collective-permute-start(bf16[96,768]{1,0:T(8,128)(2,1)S(1)} %maximum_select_fusion.refs_0_), channel_id=1, source_target_pairs={{0,4},{4,0},{8,12},{12,8},{16,20},{20,16},{24,28},{28,24},{1,5},{5... | collective-permute-start | bytes 442376 | tf_op jit(solution)/shard_map/ppermute | solution.py:30
  7.1 6.9 %collective-permute-start.4 = (bf16[96,768]{1,0:T(8,128)(2,1)S(1)}, bf16[96,768]{1,0:T(8,128)(2,1)S(1)}, u32[]{:S(2)}, u32[]{:S(2)}) collective-permute-start(bf16[96,768]{1,0:T(8,128)(2,1)S(1)} %maximum_select_fusion.refs_0_), channel_id=1, source_target_pairs={{0,8},{4,12},{8,0},{12,4},{16,24},{20,28},{24,16},{28,20},{1,9},{5... | collective-permute-start | bytes 442376 | tf_op jit(solution)/shard_map/ppermute | solution.py:30
  9.5 13.8 %collective-permute-start.6 = (bf16[96,768]{1,0:T(8,128)(2,1)S(1)}, bf16[96,768]{1,0:T(8,128)(2,1)S(1)}, u32[]{:S(2)}, u32[]{:S(2)}) collective-permute-start(bf16[96,768]{1,0:T(8,128)(2,1)S(1)} %maximum_select_fusion.refs_0_), channel_id=1, source_target_pairs={{0,16},{4,20},{8,24},{12,28},{16,0},{20,4},{24,8},{28,12},{1,17},{... | collective-permute-start | bytes 442376 | tf_op jit(solution)/shard_map/ppermute | solution.py:30
  12.1 11.8 %collective-permute-start.8 = (bf16[96,768]{1,0:T(8,128)(2,1)S(1)}, bf16[96,768]{1,0:T(8,128)(2,1)S(1)}, u32[]{:S(2)}, u32[]{:S(2)}) collective-permute-start(bf16[96,768]{1,0:T(8,128)(2,1)S(1)} %maximum_select_fusion.refs_0_), channel_id=1, source_target_pairs={{0,24},{4,28},{8,16},{12,20},{16,8},{20,12},{24,0},{28,4},{1,25},{... | collective-permute-start | bytes 442376 | tf_op jit(solution)/shard_map/ppermute | solution.py:30
  13.8 17.4 %collective-permute-start.3 = (bf16[256,768]{1,0:T(8,128)(2,1)S(1)}, bf16[256,768]{1,0:T(8,128)(2,1)S(1)}, u32[]{:S(2)}, u32[]{:S(2)}) collective-permute-start(bf16[256,768]{1,0:T(8,128)(2,1)S(1)} %rows.1.own_ref), channel_id=1, source_target_pairs={{0,2},{2,0},{1,3},{3,1},{4,6},{6,4},{5,7},{7,5},{8,10},{10,8},{9,1... | collective-permute-start | bytes 1179656 | tf_op jit(solution)/shard_map/ppermute | solution.py:30
  13.9 11.4 %collective-permute-start.5 = (bf16[96,768]{1,0:T(8,128)(2,1)S(1)}, bf16[96,768]{1,0:T(8,128)(2,1)S(1)}, u32[]{:S(2)}, u32[]{:S(2)}) collective-permute-start(bf16[96,768]{1,0:T(8,128)(2,1)S(1)} %collective-permute-done.4.refs_2_), channel_id=1, source_target_pairs={{0,4},{4,0},{8,12},{12,8},{16,20},{20,16},{24,28},{28,24},{1,5},{5... | collective-permute-start | bytes 442376 | tf_op jit(solution)/shard_map/ppermute | solution.py:30
  16.0 15.2 %copy-start.9 = (bf16[256,320]{1,0:T(8,128)(2,1)}, bf16[256,320]{1,0:T(8,128)(2,1)S(1)}, u32[]{:S(2)}) copy-start(bf16[256,320]{1,0:T(8,128)(2,1)S(1)} %get-tuple-element.126.table_ref) | copy-start | bytes 491524
  23.3 7.8 %collective-permute-start.7 = (bf16[96,768]{1,0:T(8,128)(2,1)S(1)}, bf16[96,768]{1,0:T(8,128)(2,1)}, u32[]{:S(2)}, u32[]{:S(2)}) collective-permute-start(bf16[96,768]{1,0:T(8,128)(2,1)S(1)} %collective-permute-done.6.refs_4_), channel_id=1, source_target_pairs={{0,4},{4,0},{8,12},{12,8},{16,20},{20,16},{24,28},{28,24},{1,5},{5... | collective-permute-start | bytes 442376 | tf_op jit(solution)/shard_map/ppermute | solution.py:30
  23.9 7.3 %copy-start.21 = (bf16[96,768]{1,0:T(8,128)(2,1)}, bf16[96,768]{1,0:T(8,128)(2,1)S(1)}, u32[]{:S(2)}) copy-start(bf16[96,768]{1,0:T(8,128)(2,1)S(1)} %collective-permute-done.8.refs_6_) | copy-start | bytes 442372
  23.9 7.3 %collective-permute-start.9 = (bf16[96,768]{1,0:T(8,128)(2,1)S(1)}, bf16[96,768]{1,0:T(8,128)(2,1)}, u32[]{:S(2)}, u32[]{:S(2)}) collective-permute-start(bf16[96,768]{1,0:T(8,128)(2,1)S(1)} %collective-permute-done.8.refs_6_), channel_id=1, source_target_pairs={{0,4},{4,0},{8,12},{12,8},{16,20},{20,16},{24,28},{28,24},{1,5},{5... | collective-permute-start | bytes 442376 | tf_op jit(solution)/shard_map/ppermute | solution.py:30
  26.5 16.9 %all-to-all-start = ((bf16[8,40,768]{2,1,0:T(8,128)(2,1)}), bf16[8,40,768]{2,1,0:T(8,128)(2,1)S(1)}, u32[]{:S(2)}, u32[]{:S(2)}) async-start(bf16[8,40,768]{2,1,0:T(8,128)(2,1)} %bitcast.7), calls=%async_computation | async-start | bytes 983040 | tf_op jit(solution)/shard_map/all_to_all | solution.py:600
  37.8 2.9 %collective-permute-start.11 = (bf16[768,192]{1,0:T(8,128)(2,1)S(1)}, bf16[768,192]{1,0:T(8,128)(2,1)S(1)}, u32[]{:S(2)}, u32[]{:S(2)}) collective-permute-start(bf16[768,192]{1,0:T(8,128)(2,1)S(1)} %get-tuple-element.117.refs_1_.wo_ref), channel_id=1, source_target_pairs={{0,2},{2,0},{1,3},{3,1},{4,6},{6,4},{5,7},{7,5},{8,10},{10,8},{9,1... | collective-permute-start | bytes 884744 | tf_op jit(solution)/shard_map/ppermute | solution.py:30
  37.9 2.8 %collective-permute-start.10 = (bf16[256,192]{1,0:T(8,128)(2,1)S(1)}, bf16[256,192]{1,0:T(8,128)(2,1)S(1)}, u32[]{:S(2)}, u32[]{:S(2)}) collective-permute-start(bf16[256,192]{1,0:T(8,128)(2,1)S(1)} %get-tuple-element.116), channel_id=1, source_target_pairs={{0,2},{2,0},{1,3},{3,1},{4,6},{6,4},{5,7},{7,5},{8,10},{10,8},{9,1... | collective-permute-start | bytes 294920 | tf_op jit(solution)/shard_map/ppermute | solution.py:30
  41.1 11.2 %collective-permute-start.12 = (bf16[256,768]{1,0:T(8,128)(2,1)S(1)}, bf16[256,768]{1,0:T(8,128)(2,1)S(1)}, u32[]{:S(2)}, u32[]{:S(2)}) collective-permute-start(bf16[256,768]{1,0:T(8,128)(2,1)S(1)} %attended.1), channel_id=1, source_target_pairs={{0,1},{1,0},{2,3},{3,2},{4,5},{5,4},{6,7},{7,6},{8,9},{9,8},{10,11... | collective-permute-start | bytes 1179656 | tf_op jit(solution)/shard_map/ppermute | solution.py:30
  43.4 27.9 %collective-permute-start.21 = (bf16[8,40,768]{2,1,0:T(8,128)(2,1)S(1)}, bf16[8,40,768]{2,1,0:T(8,128)(2,1)S(1)}, u32[]{:S(2)}, u32[]{:S(2)}) collective-permute-start(bf16[8,40,768]{2,1,0:T(8,128)(2,1)S(1)} %all-to-all-done.own_ref), channel_id=1, source_target_pairs={{0,2},{2,0},{1,3},{3,1},{4,6},{6,4},{5,7},{7,5},{8,10},{10,8},{9,1... | collective-permute-start | bytes 1474568 | tf_op jit(solution)/shard_map/ppermute | solution.py:30
  52.4 18.9 %copy-start.1 = (bf16[768,768]{1,0:T(8,128)(2,1)S(1)}, bf16[768,768]{1,0:T(8,128)(2,1)}, u32[]{:S(2)}) copy-start(bf16[768,768]{1,0:T(8,128)(2,1)} %wdown_ref.3) | copy-start | bytes 3538948
  52.8 6.5 %collective-permute-start.13 = (bf16[40,768]{1,0:T(8,128)(2,1)S(1)}, bf16[40,768]{1,0:T(8,128)(2,1)S(1)}, u32[]{:S(2)}, u32[]{:S(2)}) collective-permute-start(bf16[40,768]{1,0:T(8,128)(2,1)S(1)} %get-tuple-element.129), channel_id=1, source_target_pairs={{0,4},{4,0},{8,12},{12,8},{16,20},{20,16},{24,28},{28,24},{1,5},{5... | collective-permute-start | bytes 184328 | tf_op jit(solution)/shard_map/ppermute | solution.py:30
  54.9 6.0 %collective-permute-start.14 = (bf16[40,768]{1,0:T(8,128)(2,1)S(1)}, bf16[40,768]{1,0:T(8,128)(2,1)S(1)}, u32[]{:S(2)}, u32[]{:S(2)}) collective-permute-start(bf16[40,768]{1,0:T(8,128)(2,1)S(1)} %get-tuple-element.130), channel_id=1, source_target_pairs={{0,8},{4,12},{8,0},{12,4},{16,24},{20,28},{24,16},{28,20},{1,9},{5... | collective-permute-start | bytes 184328 | tf_op jit(solution)/shard_map/ppermute | solution.py:30
  56.4 7.8 %collective-permute-start.15 = (bf16[40,768]{1,0:T(8,128)(2,1)S(1)}, bf16[40,768]{1,0:T(8,128)(2,1)S(1)}, u32[]{:S(2)}, u32[]{:S(2)}) collective-permute-start(bf16[40,768]{1,0:T(8,128)(2,1)S(1)} %get-tuple-element.131), channel_id=1, source_target_pairs={{0,12},{4,8},{8,4},{12,0},{16,28},{20,24},{24,20},{28,16},{1,13},{... | collective-permute-start | bytes 184328 | tf_op jit(solution)/shard_map/ppermute | solution.py:30
  56.4 8.6 %collective-permute-start.16 = (bf16[40,768]{1,0:T(8,128)(2,1)S(1)}, bf16[40,768]{1,0:T(8,128)(2,1)S(1)}, u32[]{:S(2)}, u32[]{:S(2)}) collective-permute-start(bf16[40,768]{1,0:T(8,128)(2,1)S(1)} %get-tuple-element.132), channel_id=1, source_target_pairs={{0,16},{4,20},{8,24},{12,28},{16,0},{20,4},{24,8},{28,12},{1,17},{... | collective-permute-start | bytes 184328 | tf_op jit(solution)/shard_map/ppermute | solution.py:30
  59.3 9.6 %collective-permute-start.17 = (bf16[40,768]{1,0:T(8,128)(2,1)S(1)}, bf16[40,768]{1,0:T(8,128)(2,1)S(1)}, u32[]{:S(2)}, u32[]{:S(2)}) collective-permute-start(bf16[40,768]{1,0:T(8,128)(2,1)S(1)} %get-tuple-element.133), channel_id=1, source_target_pairs={{0,20},{4,16},{8,28},{12,24},{16,4},{20,0},{24,12},{28,8},{1,21},{... | collective-permute-start | bytes 184328 | tf_op jit(solution)/shard_map/ppermute | solution.py:30
  60.9 7.9 %collective-permute-start.18 = (bf16[40,768]{1,0:T(8,128)(2,1)S(1)}, bf16[40,768]{1,0:T(8,128)(2,1)S(1)}, u32[]{:S(2)}, u32[]{:S(2)}) collective-permute-start(bf16[40,768]{1,0:T(8,128)(2,1)S(1)} %get-tuple-element.134), channel_id=1, source_target_pairs={{0,24},{4,28},{8,16},{12,20},{16,8},{20,12},{24,0},{28,4},{1,25},{... | collective-permute-start | bytes 184328 | tf_op jit(solution)/shard_map/ppermute | solution.py:30
  64.2 7.1 %collective-permute-start.19 = (bf16[40,768]{1,0:T(8,128)(2,1)S(1)}, bf16[40,768]{1,0:T(8,128)(2,1)S(1)}, u32[]{:S(2)}, u32[]{:S(2)}) collective-permute-start(bf16[40,768]{1,0:T(8,128)(2,1)S(1)} %get-tuple-element.135), channel_id=1, source_target_pairs={{0,28},{4,24},{8,20},{12,16},{16,12},{20,8},{24,4},{28,0},{1,29},{... | collective-permute-start | bytes 184328 | tf_op jit(solution)/shard_map/ppermute | solution.py:30
  68.9 4.3 %copy-start.3 = (bf16[768,768]{1,0:T(8,128)(2,1)S(1)}, bf16[768,768]{1,0:T(8,128)(2,1)}, u32[]{:S(2)}) copy-start(bf16[768,768]{1,0:T(8,128)(2,1)} %wup_ref.1) | copy-start | bytes 3538948
  68.9 4.3 %copy-start.23 = (bf16[768,8]{0,1:T(8,128)(2,1)S(1)}, bf16[768,8]{0,1:T(8,128)(2,1)}, u32[]{:S(2)}) copy-start(bf16[768,8]{0,1:T(8,128)(2,1)} %param.23) | copy-start | bytes 36868
  71.3 1.9 %collective-permute-start.20 = (bf16[320,768]{1,0:T(8,128)(2,1)S(1)}, bf16[320,768]{1,0:T(8,128)(2,1)S(1)}, u32[]{:S(2)}, u32[]{:S(2)}) collective-permute-start(bf16[320,768]{1,0:T(8,128)(2,1)S(1)} %constant_dynamic-update-slice_fusion.own_ref), channel_id=1, source_target_pairs={{0,2},{2,0},{1,3},{3,1},{4,6},{6,4},{5,7},{7,5},{8,10},{10,8},{9,1... | collective-permute-start | bytes 1474568 | tf_op jit(solution)/shard_map/ppermute | solution.py:30
  77.4 2.0 %collective-permute-start.22 = (bf16[320,768]{1,0:T(8,128)(2,1)S(1)}, bf16[320,768]{1,0:T(8,128)(2,1)S(1)}, u32[]{:S(2)}, u32[]{:S(2)}) collective-permute-start(bf16[320,768]{1,0:T(8,128)(2,1)S(1)} %get-tuple-element.140), channel_id=1, source_target_pairs={{0,2},{2,0},{1,3},{3,1},{4,6},{6,4},{5,7},{7,5},{8,10},{10,8},{9,1... | collective-permute-start | bytes 1474568 | tf_op jit(solution)/shard_map/ppermute | solution.py:30
  80.5 17.1 %collective-permute-start.23 = (bf16[320,768]{1,0:T(8,128)(2,1)S(1)}, bf16[320,768]{1,0:T(8,128)(2,1)S(1)}, u32[]{:S(2)}, u32[]{:S(2)}) collective-permute-start(bf16[320,768]{1,0:T(8,128)(2,1)S(1)} %get-tuple-element.143), channel_id=1, source_target_pairs={{0,2},{2,0},{1,3},{3,1},{4,6},{6,4},{5,7},{7,5},{8,10},{10,8},{9,1... | collective-permute-start | bytes 1474568 | tf_op jit(solution)/shard_map/ppermute | solution.py:30
  81.0 4.8 %collective-permute-start.24 = (bf16[40,768]{1,0:T(8,128)(2,1)S(1)}, bf16[40,768]{1,0:T(8,128)(2,1)S(1)}, u32[]{:S(2)}, u32[]{:S(2)}) collective-permute-start(bf16[40,768]{1,0:T(8,128)(2,1)S(1)} %get-tuple-element.145), channel_id=1, source_target_pairs={{0,4},{4,0},{8,12},{12,8},{16,20},{20,16},{24,28},{28,24},{1,5},{5... | collective-permute-start | bytes 184328 | tf_op jit(solution)/shard_map/ppermute | solution.py:30
  81.5 5.9 %collective-permute-start.25 = (bf16[40,768]{1,0:T(8,128)(2,1)S(1)}, bf16[40,768]{1,0:T(8,128)(2,1)S(1)}, u32[]{:S(2)}, u32[]{:S(2)}) collective-permute-start(bf16[40,768]{1,0:T(8,128)(2,1)S(1)} %get-tuple-element.146), channel_id=1, source_target_pairs={{0,8},{4,12},{8,0},{12,4},{16,24},{20,28},{24,16},{28,20},{1,9},{5... | collective-permute-start | bytes 184328 | tf_op jit(solution)/shard_map/ppermute | solution.py:30
  82.1 6.3 %collective-permute-start.26 = (bf16[40,768]{1,0:T(8,128)(2,1)S(1)}, bf16[40,768]{1,0:T(8,128)(2,1)S(1)}, u32[]{:S(2)}, u32[]{:S(2)}) collective-permute-start(bf16[40,768]{1,0:T(8,128)(2,1)S(1)} %get-tuple-element.147), channel_id=1, source_target_pairs={{0,12},{4,8},{8,4},{12,0},{16,28},{20,24},{24,20},{28,16},{1,13},{... | collective-permute-start | bytes 184328 | tf_op jit(solution)/shard_map/ppermute | solution.py:30
  84.5 9.2 %collective-permute-start.27 = (bf16[40,768]{1,0:T(8,128)(2,1)S(1)}, bf16[40,768]{1,0:T(8,128)(2,1)S(1)}, u32[]{:S(2)}, u32[]{:S(2)}) collective-permute-start(bf16[40,768]{1,0:T(8,128)(2,1)S(1)} %get-tuple-element.148), channel_id=1, source_target_pairs={{0,16},{4,20},{8,24},{12,28},{16,0},{20,4},{24,8},{28,12},{1,17},{... | collective-permute-start | bytes 184328 | tf_op jit(solution)/shard_map/ppermute | solution.py:30
  85.8 10.2 %collective-permute-start.28 = (bf16[40,768]{1,0:T(8,128)(2,1)S(1)}, bf16[40,768]{1,0:T(8,128)(2,1)S(1)}, u32[]{:S(2)}, u32[]{:S(2)}) collective-permute-start(bf16[40,768]{1,0:T(8,128)(2,1)S(1)} %get-tuple-element.149), channel_id=1, source_target_pairs={{0,20},{4,16},{8,28},{12,24},{16,4},{20,0},{24,12},{28,8},{1,21},{... | collective-permute-start | bytes 184328 | tf_op jit(solution)/shard_map/ppermute | solution.py:30
  87.4 8.6 %collective-permute-start.29 = (bf16[40,768]{1,0:T(8,128)(2,1)S(1)}, bf16[40,768]{1,0:T(8,128)(2,1)S(1)}, u32[]{:S(2)}, u32[]{:S(2)}) collective-permute-start(bf16[40,768]{1,0:T(8,128)(2,1)S(1)} %get-tuple-element.150), channel_id=1, source_target_pairs={{0,24},{4,28},{8,16},{12,20},{16,8},{20,12},{24,0},{28,4},{1,25},{... | collective-permute-start | bytes 184328 | tf_op jit(solution)/shard_map/ppermute | solution.py:30
  88.4 7.6 %collective-permute-start.30 = (bf16[40,768]{1,0:T(8,128)(2,1)S(1)}, bf16[40,768]{1,0:T(8,128)(2,1)S(1)}, u32[]{:S(2)}, u32[]{:S(2)}) collective-permute-start(bf16[40,768]{1,0:T(8,128)(2,1)S(1)} %get-tuple-element.141.held_ref), channel_id=1, source_target_pairs={{0,28},{4,24},{8,20},{12,16},{16,12},{20,8},{24,4},{28,0},{1,29},{... | collective-permute-start | bytes 184328 | tf_op jit(solution)/shard_map/ppermute | solution.py:30
  96.4 9.8 %collective-permute-start.31 = (bf16[256,768]{1,0:T(8,128)(2,1)S(1)}, bf16[256,768]{1,0:T(8,128)(2,1)}, u32[]{:S(2)}, u32[]{:S(2)}) collective-permute-start(bf16[256,768]{1,0:T(8,128)(2,1)S(1)} %gather_grad.1.own_ref), channel_id=1, source_target_pairs={{0,1},{1,0},{2,3},{3,2},{4,5},{5,4},{6,7},{7,6},{8,9},{9,8},{10,11... | collective-permute-start | bytes 1179656 | tf_op jit(solution)/shard_map/ppermute | solution.py:30
  99.1 25.6 %all-to-all-start.1 = ((bf16[8,40,768]{2,1,0:T(8,128)(2,1)}), bf16[8,40,768]{2,1,0:T(8,128)(2,1)S(1)}, u32[]{:S(2)}, u32[]{:S(2)}) async-start(bf16[8,40,768]{2,1,0:T(8,128)(2,1)} %join_out.1.refs_8_), calls=%async_computation.1 | async-start | bytes 983040 | tf_op jit(solution)/shard_map/all_to_all | solution.py:600
  108.5 1.7 %collective-permute-start.32 = (bf16[256,768]{1,0:T(8,128)(2,1)S(1)}, bf16[256,768]{1,0:T(8,128)(2,1)S(1)}, u32[]{:S(2)}, u32[]{:S(2)}) collective-permute-start(bf16[256,768]{1,0:T(8,128)(2,1)S(1)} %get-tuple-element.159.own_ref), channel_id=1, source_target_pairs={{0,2},{2,0},{1,3},{3,1},{4,6},{6,4},{5,7},{7,5},{8,10},{10,8},{9,1... | collective-permute-start | bytes 1179656 | tf_op jit(solution)/shard_map/ppermute | solution.py:30
  114.8 13.2 %collective-permute-start.33 = (bf16[384,384]{1,0:T(8,128)(2,1)}, bf16[384,384]{1,0:T(8,128)(2,1)}, u32[]{:S(2)}, u32[]{:S(2)}) collective-permute-start(bf16[384,384]{1,0:T(8,128)(2,1)} %get-tuple-element.176), channel_id=1, source_target_pairs={{0,4},{4,0},{8,12},{12,8},{16,20},{20,16},{24,28},{28,24},{1,5},{5... | collective-permute-start | bytes 884744 | tf_op jit(solution)/shard_map/ppermute | solution.py:30
  123.8 11.4 %collective-permute-start.36 = (bf16[256,768]{1,0:T(8,128)(2,1)}, bf16[256,768]{1,0:T(8,128)(2,1)}, u32[]{:S(2)}, u32[]{:S(2)}) collective-permute-start(bf16[256,768]{1,0:T(8,128)(2,1)} %get-tuple-element.181), channel_id=1, source_target_pairs={{0,2},{2,0},{1,3},{3,1},{4,6},{6,4},{5,7},{7,5},{8,10},{10,8},{9,1... | collective-permute-start | bytes 1179656 | tf_op jit(solution)/shard_map/ppermute | solution.py:30
  123.8 4.2 %collective-permute-start.34 = (f32[16,768]{1,0:T(8,128)S(1)}, f32[16,768]{1,0:T(8,128)S(1)}, u32[]{:S(2)}, u32[]{:S(2)}) collective-permute-start(f32[16,768]{1,0:T(8,128)S(1)} %get-tuple-element.177.small_ref), channel_id=1, source_target_pairs={{0,1},{1,0},{2,3},{3,2},{4,5},{5,4},{6,7},{7,6},{8,9},{9,8},{10,11... | collective-permute-start | bytes 147464 | tf_op jit(solution)/shard_map/ppermute | solution.py:30
  128.0 13.1 %copy-start.14 = (f32[384,384]{1,0:T(8,128)S(1)}, f32[384,384]{1,0:T(8,128)}, u32[]{:S(2)}) copy-start(f32[384,384]{1,0:T(8,128)} %copy-done.13) | copy-start | bytes 1769476
  129.1 11.9 %collective-permute-start.37 = (bf16[416,384]{1,0:T(8,128)(2,1)S(1)}, bf16[416,384]{1,0:T(8,128)(2,1)S(1)}, u32[]{:S(2)}, u32[]{:S(2)}) collective-permute-start(bf16[416,384]{1,0:T(8,128)(2,1)S(1)} %get-tuple-element.185), channel_id=1, source_target_pairs={{0,4},{4,0},{8,12},{12,8},{16,20},{20,16},{24,28},{28,24},{1,5},{5... | collective-permute-start | bytes 958472 | tf_op jit(solution)/shard_map/ppermute | solution.py:30
  129.3 8.4 %collective-permute-start.38 = (bf16[96,384]{1,0:T(8,128)(2,1)S(1)}, bf16[96,384]{1,0:T(8,128)(2,1)S(1)}, u32[]{:S(2)}, u32[]{:S(2)}) collective-permute-start(bf16[96,384]{1,0:T(8,128)(2,1)S(1)} %get-tuple-element.182.held_ref), channel_id=1, source_target_pairs={{0,8},{4,12},{8,0},{12,4},{16,24},{20,28},{24,16},{28,20},{1,9},{5... | collective-permute-start | bytes 221192 | tf_op jit(solution)/shard_map/ppermute | solution.py:30
  132.9 8.2 %collective-permute-start.39 = (bf16[96,384]{1,0:T(8,128)(2,1)S(1)}, bf16[96,384]{1,0:T(8,128)(2,1)S(1)}, u32[]{:S(2)}, u32[]{:S(2)}) collective-permute-start(bf16[96,384]{1,0:T(8,128)(2,1)S(1)} %get-tuple-element.189), channel_id=1, source_target_pairs={{0,16},{4,20},{8,24},{12,28},{16,0},{20,4},{24,8},{28,12},{1,17},{... | collective-permute-start | bytes 221192 | tf_op jit(solution)/shard_map/ppermute | solution.py:30
  133.6 7.5 %collective-permute-start.40 = (bf16[96,384]{1,0:T(8,128)(2,1)S(1)}, bf16[96,384]{1,0:T(8,128)(2,1)S(1)}, u32[]{:S(2)}, u32[]{:S(2)}) collective-permute-start(bf16[96,384]{1,0:T(8,128)(2,1)S(1)} %get-tuple-element.190), channel_id=1, source_target_pairs={{0,24},{4,28},{8,16},{12,20},{16,8},{20,12},{24,0},{28,4},{1,25},{... | collective-permute-start | bytes 221192 | tf_op jit(solution)/shard_map/ppermute | solution.py:30
  135.2 12.2 %collective-permute-start.35 = (bf16[128,768]{1,0:T(8,128)(2,1)S(1)}, bf16[128,768]{1,0:T(8,128)(2,1)S(1)}, u32[]{:S(2)}, u32[]{:S(2)}) collective-permute-start(bf16[128,768]{1,0:T(8,128)(2,1)S(1)} %get-tuple-element.180), channel_id=1, source_target_pairs={{0,1},{1,0},{2,3},{3,2},{4,5},{5,4},{6,7},{7,6},{8,9},{9,8},{10,11... | collective-permute-start | bytes 589832 | tf_op jit(solution)/shard_map/ppermute | solution.py:30
  136.4 12.3 %copy-start.8 = (bf16[640,768]{1,0:T(8,128)(2,1)S(1)}, bf16[640,768]{1,0:T(8,128)(2,1)}, u32[]{:S(2)}) copy-start(bf16[640,768]{1,0:T(8,128)(2,1)} %copy-done.7) | copy-start | bytes 2949124
  141.1 7.6 %copy-start.4 = (bf16[640,768]{1,0:T(8,128)(2,1)S(1)}, bf16[640,768]{1,0:T(8,128)(2,1)}, u32[]{:S(2)}) copy-start(bf16[640,768]{1,0:T(8,128)(2,1)} %get-tuple-element.200.cots_ref) | copy-start | bytes 2949124
  141.1 7.6 %copy-start.6 = (bf16[640,768]{1,0:T(8,128)(2,1)S(1)}, bf16[640,768]{1,0:T(8,128)(2,1)}, u32[]{:S(2)}) copy-start(bf16[640,768]{1,0:T(8,128)(2,1)} %copy-done.5) | copy-start | bytes 2949124
  141.8 10.7 %collective-permute-start.41 = (bf16[128,768]{1,0:T(8,128)(2,1)S(1)}, bf16[128,768]{1,0:T(8,128)(2,1)S(1)}, u32[]{:S(2)}, u32[]{:S(2)}) collective-permute-start(bf16[128,768]{1,0:T(8,128)(2,1)S(1)} %get-tuple-element.191), channel_id=1, source_target_pairs={{0,1},{1,0},{2,3},{3,2},{4,5},{5,4},{6,7},{7,6},{8,9},{9,8},{10,11... | collective-permute-start | bytes 589832 | tf_op jit(solution)/shard_map/ppermute | solution.py:30
  143.0 10.4 %collective-permute-start.43 = (bf16[128,384]{1,0:T(8,128)(2,1)S(1)}, bf16[128,384]{1,0:T(8,128)(2,1)S(1)}, u32[]{:S(2)}, u32[]{:S(2)}) collective-permute-start(bf16[128,384]{1,0:T(8,128)(2,1)S(1)} %get-tuple-element.196.held_ref), channel_id=1, source_target_pairs={{0,8},{4,12},{8,0},{12,4},{16,24},{20,28},{24,16},{28,20},{1,9},{5... | collective-permute-start | bytes 294920 | tf_op jit(solution)/shard_map/ppermute | solution.py:30
  144.3 9.4 %collective-permute-start.44 = (bf16[128,384]{1,0:T(8,128)(2,1)S(1)}, bf16[128,384]{1,0:T(8,128)(2,1)S(1)}, u32[]{:S(2)}, u32[]{:S(2)}) collective-permute-start(bf16[128,384]{1,0:T(8,128)(2,1)S(1)} %get-tuple-element.197), channel_id=1, source_target_pairs={{0,16},{4,20},{8,24},{12,28},{16,0},{20,4},{24,8},{28,12},{1,17},{... | collective-permute-start | bytes 294920 | tf_op jit(solution)/shard_map/ppermute | solution.py:30
  145.5 8.3 %collective-permute-start.45 = (bf16[128,384]{1,0:T(8,128)(2,1)S(1)}, bf16[128,384]{1,0:T(8,128)(2,1)S(1)}, u32[]{:S(2)}, u32[]{:S(2)}) collective-permute-start(bf16[128,384]{1,0:T(8,128)(2,1)S(1)} %get-tuple-element.198), channel_id=1, source_target_pairs={{0,24},{4,28},{8,16},{12,20},{16,8},{20,12},{24,0},{28,4},{1,25},{... | collective-permute-start | bytes 294920 | tf_op jit(solution)/shard_map/ppermute | solution.py:30
  148.7 3.8 %copy-start.12 = (bf16[128,768]{1,0:T(8,128)(2,1)S(1)}, bf16[128,768]{1,0:T(8,128)(2,1)}, u32[]{:S(2)}) copy-start(bf16[128,768]{1,0:T(8,128)(2,1)} %x_ref.1) | copy-start | bytes 589828
  154.3 1.5 collective-permute-start.46
  154.4 1.4 collective-permute-start.42
  (13 other events, 22.3 us)

commit v7 on v6

--- a/solution.py
+++ b/solution.py
@@ -68,7 +68,7 @@
 
 
 def is_plain(array):
-    return array.dtype in (bf16, f32, jnp.int32)
+    return getattr(array, "dtype", None) in (bf16, f32, jnp.int32)
 
 
 def padded_bytes(array):
@@ -384,14 +384,14 @@
         ).astype(bf16)
 
 
-def send_rows(parts, me, gw_ref, outs):
+def send_rows(parts, me, gw_ref, outs, keep_ref):
     if parts == 1:
         outs[0][...] = gw_ref[...].astype(bf16)
         return
     rows = gw_ref.shape[0] // parts
     for i in range(parts // 2):
         at = slice(i * rows, (i + 1) * rows)
-        outs[0][at, :] = gw_ref[pl.ds(pl.multiple_of((me ^ 2 * i) * rows, rows), rows), :]
+        keep_ref[at, :] = gw_ref[pl.ds(pl.multiple_of((me ^ 2 * i) * rows, rows), rows), :]
         there = pl.ds(pl.multiple_of((me ^ 2 * i ^ 1) * rows, rows), rows)
         outs[1][at, :] = gw_ref[there, :].astype(bf16)
 
@@ -411,7 +411,7 @@
     seq_ref[...] = (unit_rows(x_ref[...]) * gain_ref[...]).astype(bf16)
     gw_ref[:, :cut] = mm_at(seq_ref[...], dqkv_ref[...])
     gw_ref[:, cut:] = mm_at(ga_ref[...], mixed_ref[...])
-    send_rows(parts, ids[1], gw_ref, outs)
+    send_rows(parts, ids[1], gw_ref, outs, outs[0])
 
 
 def second_back_kernel(
@@ -420,14 +420,18 @@
     count = heads + 2
     qkv_ref, *probs, x_ref, w_ref = refs[:count]
     refs = refs[count:]
-    keep_ref, send_ref, small_ref, *outs = refs[:-5]
-    diag_ref, dqkv_ref, all_ref, ds_ref, gw_ref = refs[-5:]
+    keep_ref, send_ref, small_ref, *outs = refs[:-7]
+    diag_ref, dqkv_ref, all_ref, ds_ref, gw_ref, near_ref, sem = refs[-7:]
     core, me, side = ids[0], ids[1], ids[2]
     half = keep_ref.shape[0]
     diag_ref[...] = diag_in_ref[...]
     heads_back(heads, 1, qkv_ref, gm_ref, probs, dqkv_ref, diag_ref, ds_ref)
     gw_ref[...] = mm_at(seq_ref[...], dqkv_ref[...])
-    send_rows(parts, me, gw_ref, outs)
+    send_rows(parts, me, gw_ref, outs, near_ref)
+    copy = None
+    if parts > 1:
+        copy = pltpu.make_async_copy(near_ref, outs[0], sem)
+        copy.start()
     rest = (heads - 1) * HD
     for i in range(3):
         at = i * heads * HD
@@ -453,6 +457,8 @@
         small_ref[2 + experts : 2 + experts + heads, i * lanes : (i + 1) * lanes] = jnp.where(
             side * GROUP + core == i, bias[:heads, :], 0.0
         )
+    if copy is not None:
+        copy.wait()
 
 
 def fold_kernel(
@@ -802,7 +808,7 @@
     small_rows = -(-(2 + experts + heads) // 16) * 16
     if direct:
         first_shapes = [out((width // 2, chunk), t) for t in (f32, bf16)]
-        second_shapes = [out((width // 2, other_chunk), t) for t in (f32, bf16)]
+        second_shapes = [Far(out((width // 2, other_chunk), f32)), out((width // 2, other_chunk), bf16)]
     else:
         first_shapes = [out((width, chunk), bf16)]
         second_shapes = [out((width, other_chunk), bf16)]
@@ -859,6 +865,8 @@
             pltpu.VMEM((seq, 3 * cols), bf16),
             pltpu.VMEM((seq, seq), bf16),
             pltpu.VMEM((width, other_chunk), f32),
+            pltpu.VMEM((width // 2, other_chunk), f32),
+            pltpu.SemaphoreType.DMA,
         ],
     )
 

time: 159 us -> 158 us (level)
  local copies, waits for them, and re-layouts: 7.02 us -> 5.38 us
    unnamed x64 -> x62, local copies, waits for them, and re-layouts: 6.15 us -> 4.51 us
  transfers between devices with their start and end apart: 49 -> 49, of which waited for: 13 -> 13; matrix products, arithmetic and copies ran while one was open for 1% -> 1% of each run, Pallas kernels for 24% -> 25%
where the time goes in v7:
time: 158 us
  starting transfers between devices  64.4 us (41%)
  Pallas kernels  47.4 us (30%)
  waiting for transfers between devices  36.7 us (23%)
  local copies, waits for them, and re-layouts  5.38 us (3%)
  other arithmetic  1.91 us (1%)
    ppermute x47, starting transfers between devices, across(): lax.ppermute(shard, axis, [(i, i ^ bits) for i in range(lax.axis_size(axi...  55.5 us
    pallas_call x27, Pallas kernels, call(): pl.pallas_call(body, name=name, out_shape=[space[type(o)](x.shape, x.dtyp...  47.4 us
    ppermute x47, waiting for transfers between devices, across(): lax.ppermute(shard, axis, [(i, i ^ bits) for i in range(lax.axis_size(axi...  35.7 us
    all_to_all x2, starting transfers between devices, trade_natural(): lax.all_to_all(stacked, 'node', split_axis=0, concat_axis=0, tiled=True)  8.92 us
    unnamed x62, local copies, waits for them, and re-layouts  4.51 us
  transfers between devices with their start and end apart: 49, of which 13 were waited for; matrix products, arithmetic and copies ran while one was open for 1% of the time, Pallas kernels for 25%

profile of v7, /device:TPU:0, one launch (start us, length us, event | category | flops | bytes accessed | tf_op | source)
XLA Modules:
  0.0 157.6 jit_solution(15087486732165032287)
XLA Ops:
  0.8 1.6 shares.1
  2.9 2.6 %collective-permute-start = (bf16[128,768]{1,0:T(8,128)(2,1)}, bf16[128,768]{1,0:T(8,128)(2,1)S(1)}, u32[]{:S(2)}, u32[]{:S(2)}) collective-permute-start(bf16[128,768]{1,0:T(8,128)(2,1)} %x_ref.1), channel_id=1, source_target_pairs={{0,1},{1,0},{2,3},{3,2},{4,5},{5,4},{6,7},{7,6},{8,9},{9,8},{10,11... | collective-permute-start | bytes 589832 | tf_op jit(solution)/shard_map/ppermute | solution.py:30
  5.5 1.6 collective-permute-start.2
  7.1 1.6 %collective-permute-start.4 = (bf16[96,768]{1,0:T(8,128)(2,1)S(1)}, bf16[96,768]{1,0:T(8,128)(2,1)S(1)}, u32[]{:S(2)}, u32[]{:S(2)}) collective-permute-start(bf16[96,768]{1,0:T(8,128)(2,1)S(1)} %maximum_select_fusion.refs_0_), channel_id=1, source_target_pairs={{0,8},{4,12},{8,0},{12,4},{16,24},{20,28},{24,16},{28,20},{1,9},{5... | collective-permute-start | bytes 442376 | tf_op jit(solution)/shard_map/ppermute | solution.py:30
  9.5 2.6 %collective-permute-start.6 = (bf16[96,768]{1,0:T(8,128)(2,1)S(1)}, bf16[96,768]{1,0:T(8,128)(2,1)S(1)}, u32[]{:S(2)}, u32[]{:S(2)}) collective-permute-start(bf16[96,768]{1,0:T(8,128)(2,1)S(1)} %maximum_select_fusion.refs_0_), channel_id=1, source_target_pairs={{0,16},{4,20},{8,24},{12,28},{16,0},{20,4},{24,8},{28,12},{1,17},{... | collective-permute-start | bytes 442376 | tf_op jit(solution)/shard_map/ppermute | solution.py:30
  12.3 0.9 copy-done.11
  15.1 0.9 tables.1
  16.1 7.3 %collective-permute-done.6.refs_4_ = bf16[96,768]{1,0:T(8,128)(2,1)S(1)} collective-permute-done((bf16[96,768]{1,0:T(8,128)(2,1)S(1)}, bf16[96,768]{1,0:T(8,128)(2,1)S(1)}, u32[]{:S(2)}, u32[]{:S(2)}) %collective-permute-start.6) | collective-permute-done | bytes 147488 | tf_op jit(solution)/shard_map/ppermute | solution.py:30
  23.9 1.5 collective-permute-start.9
  25.4 1.1 cot_slots.1
  26.5 4.2 %all-to-all-start = ((bf16[8,40,768]{2,1,0:T(8,128)(2,1)}), bf16[8,40,768]{2,1,0:T(8,128)(2,1)S(1)}, u32[]{:S(2)}, u32[]{:S(2)}) async-start(bf16[8,40,768]{2,1,0:T(8,128)(2,1)} %bitcast.7), calls=%async_computation | async-start | bytes 983040 | tf_op jit(solution)/shard_map/all_to_all | solution.py:606
  31.2 0.9 copy-done.21
  32.1 5.6 %attend.1 = (bf16[768,768]{1,0:T(8,128)(2,1)S(1)}, bf16[768,192]{1,0:T(8,128)(2,1)S(1)}, bf16[512,768]{1,0:T(8,128)(2,1)S(1)}, bf16[512,576]{1,0:T(8,128)(2,1)S(...) custom-call(s32[3]{0:T(128)S(1)} %pad_add_fusion.ids, ...), custom_call_target="tpu_custom_call" | custom-call | tf_op jit(solution)/shard_map/attend/pallas_call | solution.py:55
  38.3 2.3 %park.1 = (bf16[768,768]{1,0:T(8,128)(2,1)}, bf16[768,192]{1,0:T(8,128)(2,1)}, bf16[512,768]{1,0:T(8,128)(2,1)}, bf16[512,576]{1,0:T(8,128)(2,1)}, bf16[512,192]...) custom-call(bf16[768,768]{1,0:T(8,128)(2,1)S(1)} %get-tuple-element.118.refs_0_, ...), custom_call_target="tpu_custom_call" | custom-call | tf_op jit(solution)/shard_map/park/pallas_call | solution.py:55
  41.1 1.2 collective-permute-start.12
  42.3 1.1 all-to-all-done.own_ref
  43.4 8.9 %collective-permute-done.12 = bf16[256,768]{1,0:T(8,128)(2,1)S(1)} collective-permute-done((bf16[256,768]{1,0:T(8,128)(2,1)S(1)}, bf16[256,768]{1,0:T(8,128)(2,1)S(1)}, u32[]{:S(2)}, u32[]{:S(2)}) %collective-permute-start.12) | collective-permute-done | bytes 393248 | tf_op jit(solution)/shard_map/ppermute | solution.py:30
  52.8 2.1 %collective-permute-start.13 = (bf16[40,768]{1,0:T(8,128)(2,1)S(1)}, bf16[40,768]{1,0:T(8,128)(2,1)S(1)}, u32[]{:S(2)}, u32[]{:S(2)}) collective-permute-start(bf16[40,768]{1,0:T(8,128)(2,1)S(1)} %get-tuple-element.129), channel_id=1, source_target_pairs={{0,4},{4,0},{8,12},{12,8},{16,20},{20,16},{24,28},{28,24},{1,5},{5... | collective-permute-start | bytes 184328 | tf_op jit(solution)/shard_map/ppermute | solution.py:30
  54.9 1.5 collective-permute-start.14
  56.4 2.8 %collective-permute-start.16 = (bf16[40,768]{1,0:T(8,128)(2,1)S(1)}, bf16[40,768]{1,0:T(8,128)(2,1)S(1)}, u32[]{:S(2)}, u32[]{:S(2)}) collective-permute-start(bf16[40,768]{1,0:T(8,128)(2,1)S(1)} %get-tuple-element.132), channel_id=1, source_target_pairs={{0,16},{4,20},{8,24},{12,28},{16,0},{20,4},{24,8},{28,12},{1,17},{... | collective-permute-start | bytes 184328 | tf_op jit(solution)/shard_map/ppermute | solution.py:30
  59.3 1.6 %collective-permute-start.17 = (bf16[40,768]{1,0:T(8,128)(2,1)S(1)}, bf16[40,768]{1,0:T(8,128)(2,1)S(1)}, u32[]{:S(2)}, u32[]{:S(2)}) collective-permute-start(bf16[40,768]{1,0:T(8,128)(2,1)S(1)} %get-tuple-element.133), channel_id=1, source_target_pairs={{0,20},{4,16},{8,28},{12,24},{16,4},{20,0},{24,12},{28,8},{1,21},{... | collective-permute-start | bytes 184328 | tf_op jit(solution)/shard_map/ppermute | solution.py:30
  60.9 3.2 %collective-permute-start.18 = (bf16[40,768]{1,0:T(8,128)(2,1)S(1)}, bf16[40,768]{1,0:T(8,128)(2,1)S(1)}, u32[]{:S(2)}, u32[]{:S(2)}) collective-permute-start(bf16[40,768]{1,0:T(8,128)(2,1)S(1)} %get-tuple-element.134), channel_id=1, source_target_pairs={{0,24},{4,28},{8,16},{12,20},{16,8},{20,12},{24,0},{28,4},{1,25},{... | collective-permute-start | bytes 184328 | tf_op jit(solution)/shard_map/ppermute | solution.py:30
  64.2 0.8 collective-permute-start.19
  65.0 3.8 %collective-permute-done.17 = bf16[40,768]{1,0:T(8,128)(2,1)S(1)} collective-permute-done((bf16[40,768]{1,0:T(8,128)(2,1)S(1)}, bf16[40,768]{1,0:T(8,128)(2,1)S(1)}, u32[]{:S(2)}, u32[]{:S(2)}) %collective-permute-start.17) | collective-permute-done | bytes 61472 | tf_op jit(solution)/shard_map/ppermute | solution.py:30
  68.9 2.4 %collective-permute-done.19 = bf16[40,768]{1,0:T(8,128)(2,1)S(1)} collective-permute-done((bf16[40,768]{1,0:T(8,128)(2,1)S(1)}, bf16[40,768]{1,0:T(8,128)(2,1)S(1)}, u32[]{:S(2)}, u32[]{:S(2)}) %collective-permute-start.19) | collective-permute-done | bytes 61472 | tf_op jit(solution)/shard_map/ppermute | solution.py:30
  71.3 1.8 %cots.1 = (bf16[640,768]{1,0:T(8,128)(2,1)}, f32[640,768]{1,0:T(8,128)S(1)}) custom-call(s32[3]{0:T(128)S(1)} %pad_add_fusion.ids, bf16[8,40,768]{2,1,0:T(8,128)(2,1)S(1)} %all-to-all-done.own_ref, bf16[8,40,768]{2,1,0:T(8,128)(2,1)S(1)} %collective-permute-done.21.other_ref, bf16[768,768]{1,0:T(8,128)(2,1)S(1)} %copy-done.1, ...), custom_call_target="tpu_custom_call" | custom-call | tf_op jit(solution)/shard_map/cots/pallas_call | solution.py:55
  73.2 4.2 %expert.1 = (bf16[640,768]{1,0:T(8,128)(2,1)S(1)}, bf16[640,768]{1,0:T(8,128)(2,1)S(1)}, f32[640,1]{1,0:T(8,128)S(1)}, f32[320,768]{1,0:T(8,128)S(1)}, bf16[320,...) custom-call(s32[3]{0:T(128)S(1)} %pad_add_fusion.ids, ...), custom_call_target="tpu_custom_call" | custom-call | tf_op jit(solution)/shard_map/expert/pallas_call | solution.py:55
  78.0 1.5 collective-permute-done.22.got_ref
  79.5 1.0 expert_out.1
  82.2 2.3 %collective-permute-start.26 = (bf16[40,768]{1,0:T(8,128)(2,1)S(1)}, bf16[40,768]{1,0:T(8,128)(2,1)S(1)}, u32[]{:S(2)}, u32[]{:S(2)}) collective-permute-start(bf16[40,768]{1,0:T(8,128)(2,1)S(1)} %get-tuple-element.147), channel_id=1, source_target_pairs={{0,12},{4,8},{8,4},{12,0},{16,28},{20,24},{24,20},{28,16},{1,13},{... | collective-permute-start | bytes 184328 | tf_op jit(solution)/shard_map/ppermute | solution.py:30
  84.5 1.3 collective-permute-start.27
  85.8 1.6 %collective-permute-start.28 = (bf16[40,768]{1,0:T(8,128)(2,1)S(1)}, bf16[40,768]{1,0:T(8,128)(2,1)S(1)}, u32[]{:S(2)}, u32[]{:S(2)}) collective-permute-start(bf16[40,768]{1,0:T(8,128)(2,1)S(1)} %get-tuple-element.149), channel_id=1, source_target_pairs={{0,20},{4,16},{8,28},{12,24},{16,4},{20,0},{24,12},{28,8},{1,21},{... | collective-permute-start | bytes 184328 | tf_op jit(solution)/shard_map/ppermute | solution.py:30
  87.4 1.0 collective-permute-start.29
  88.4 3.7 %collective-permute-start.30 = (bf16[40,768]{1,0:T(8,128)(2,1)S(1)}, bf16[40,768]{1,0:T(8,128)(2,1)S(1)}, u32[]{:S(2)}, u32[]{:S(2)}) collective-permute-start(bf16[40,768]{1,0:T(8,128)(2,1)S(1)} %get-tuple-element.141.held_ref), channel_id=1, source_target_pairs={{0,28},{4,24},{8,20},{12,16},{16,12},{20,8},{24,4},{28,0},{1,29},{... | collective-permute-start | bytes 184328 | tf_op jit(solution)/shard_map/ppermute | solution.py:30
  92.1 1.6 collective-permute-done.27.refs_4_
  93.7 2.4 %collective-permute-done.28.refs_5_ = bf16[40,768]{1,0:T(8,128)(2,1)S(1)} collective-permute-done((bf16[40,768]{1,0:T(8,128)(2,1)S(1)}, bf16[40,768]{1,0:T(8,128)(2,1)S(1)}, u32[]{:S(2)}, u32[]{:S(2)}) %collective-permute-start.28) | collective-permute-done | bytes 61472 | tf_op jit(solution)/shard_map/ppermute | solution.py:30
  96.4 1.2 collective-permute-start.31
  97.7 1.4 join_out.1.refs_8_
  99.1 4.7 %all-to-all-start.1 = ((bf16[8,40,768]{2,1,0:T(8,128)(2,1)}), bf16[8,40,768]{2,1,0:T(8,128)(2,1)S(1)}, u32[]{:S(2)}, u32[]{:S(2)}) async-start(bf16[8,40,768]{2,1,0:T(8,128)(2,1)} %join_out.1.refs_8_), calls=%async_computation.1 | async-start | bytes 983040 | tf_op jit(solution)/shard_map/all_to_all | solution.py:606
  103.8 2.4 %unpark.1 = (bf16[768,768]{1,0:T(8,128)(2,1)S(1)}, bf16[768,192]{1,0:T(8,128)(2,1)S(1)}, bf16[512,768]{1,0:T(8,128)(2,1)S(1)}, bf16[512,576]{1,0:T(8,128)(2,1)S(...) custom-call(bf16[768,768]{1,0:T(8,128)(2,1)} %get-tuple-element.151., ...), custom_call_target="tpu_custom_call" | custom-call | tf_op jit(solution)/shard_map/unpark/pallas_call | solution.py:55
  106.2 1.5 hidden_back.1
  108.5 1.7 %collective-permute-done.32.other_ref = bf16[256,768]{1,0:T(8,128)(2,1)S(1)} collective-permute-done((bf16[256,768]{1,0:T(8,128)(2,1)S(1)}, bf16[256,768]{1,0:T(8,128)(2,1)S(1)}, u32[]{:S(2)}, u32[]{:S(2)}) %collective-permute-start.32) | collective-permute-done | bytes 393248 | tf_op jit(solution)/shard_map/ppermute | solution.py:30
  110.2 3.8 %first_back.1 = (bf16[512,192]{1,0:T(8,128)(2,1)S(1)}, bf16[512,192]{1,0:T(8,128)(2,1)S(1)}, f32[8,1024]{1,0:T(8,128)S(1)}, bf16[512,768]{1,0:T(8,128)(2,1)S(1)}...) custom-call(s32[3]{0:T(128)S(1)} %pad_add_fusion.ids, bf16[256,768]{1,0:T(8,128)(2,1)S(1)} %get-tuple-element.159.own_ref, ...), custom_call_target="tpu_custom_call" | custom-call | tf_op jit(solution)/shard_map/first_back/pallas_call | solution.py:55
  114.1 2.0 %collective-permute-start.33 = (bf16[384,384]{1,0:T(8,128)(2,1)}, bf16[384,384]{1,0:T(8,128)(2,1)}, u32[]{:S(2)}, u32[]{:S(2)}) collective-permute-start(bf16[384,384]{1,0:T(8,128)(2,1)} %get-tuple-element.176), channel_id=1, source_target_pairs={{0,4},{4,0},{8,12},{12,8},{16,20},{20,16},{24,28},{28,24},{1,5},{5... | collective-permute-start | bytes 884744 | tf_op jit(solution)/shard_map/ppermute | solution.py:30
  116.3 6.0 %second_back.1 = (f32[256,768]{1,0:T(8,128)S(1)}, bf16[256,768]{1,0:T(8,128)(2,1)}, f32[16,768]{1,0:T(8,128)S(1)}, f32[384,384]{1,0:T(8,128)}, bf16[384,384]{1,0:T(8,128)(2,1)S(1)}) custom-call(s32[3]{0:T(128)S(1)} %pad_add_fusion.ids, bf16[512,192]{1,0:T(8,128)(2,1)S(1)} %get-tuple-element.164.gm_ref, bf16[512,192]{1,0:T(8,128)(2,1)S(1)} %get-tuple-element.165.first_ref, ...), custom_call_target="tpu_custom_call" | custom-call | tf_op jit(solution)/shard_map/second_back/pallas_call | solution.py:55
  123.0 0.9 collective-permute-start.34
  123.9 0.9 copy-done.10
  124.8 0.9 returned.1
  125.7 1.5 collective-permute-done.34.small_got_ref
  127.2 1.1 fold_first.1
  128.5 3.5 %collective-permute-start.38 = (bf16[96,384]{1,0:T(8,128)(2,1)S(1)}, bf16[96,384]{1,0:T(8,128)(2,1)S(1)}, u32[]{:S(2)}, u32[]{:S(2)}) collective-permute-start(bf16[96,384]{1,0:T(8,128)(2,1)S(1)} %get-tuple-element.182.held_ref), channel_id=1, source_target_pairs={{0,8},{4,12},{8,0},{12,4},{16,24},{20,28},{24,16},{28,20},{1,9},{5... | collective-permute-start | bytes 221192 | tf_op jit(solution)/shard_map/ppermute | solution.py:30
  132.8 1.6 %collective-permute-start.40 = (bf16[96,384]{1,0:T(8,128)(2,1)S(1)}, bf16[96,384]{1,0:T(8,128)(2,1)S(1)}, u32[]{:S(2)}, u32[]{:S(2)}) collective-permute-start(bf16[96,384]{1,0:T(8,128)(2,1)S(1)} %get-tuple-element.190), channel_id=1, source_target_pairs={{0,24},{4,28},{8,16},{12,20},{16,8},{20,12},{24,0},{28,4},{1,25},{... | collective-permute-start | bytes 221192 | tf_op jit(solution)/shard_map/ppermute | solution.py:30
  134.4 1.2 collective-permute-start.35
  135.5 1.2 normed_sum.1
  136.8 3.4 %collective-permute-done.39.refs_2_ = bf16[96,384]{1,0:T(8,128)(2,1)S(1)} collective-permute-done((bf16[96,384]{1,0:T(8,128)(2,1)S(1)}, bf16[96,384]{1,0:T(8,128)(2,1)S(1)}, u32[]{:S(2)}, u32[]{:S(2)}) %collective-permute-start.39) | collective-permute-done | bytes 73760 | tf_op jit(solution)/shard_map/ppermute | solution.py:30
  140.9 1.2 collective-permute-start.41
  142.1 1.3 collective-permute-start.43
  143.5 1.1 collective-permute-start.44
  144.6 1.9 %collective-permute-start.45 = (bf16[128,384]{1,0:T(8,128)(2,1)S(1)}, bf16[128,384]{1,0:T(8,128)(2,1)S(1)}, u32[]{:S(2)}, u32[]{:S(2)}) collective-permute-start(bf16[128,384]{1,0:T(8,128)(2,1)S(1)} %get-tuple-element.198), channel_id=1, source_target_pairs={{0,24},{4,28},{8,16},{12,20},{16,8},{20,12},{24,0},{28,4},{1,25},{... | collective-permute-start | bytes 294920 | tf_op jit(solution)/shard_map/ppermute | solution.py:30
  146.5 1.3 activations.1.refs_5_
  147.8 3.7 %expert_grads.1 = (f32[768,768]{1,0:T(8,128)}, f32[768,768]{1,0:T(8,128)}) custom-call(bf16[640,768]{1,0:T(8,128)(2,1)S(1)} %copy-done.8, bf16[640,768]{1,0:T(8,128)(2,1)S(1)} %copy-done.4, bf16[640,768]{1,0:T(8,128)(2,1)S(1)} %get-tuple-element.137.active_ref, bf16[640,768]{1,0:T(8,128)(2,1)S(1)} %copy-done.6, f32[640,1]{1,0:T(8,128)S(1)} %get-tuple-element.138.chosen_ref, ...), custom_call_target="tpu_custom_call" | custom-call | tf_op jit(solution)/shard_map/expert_grads/pallas_call | solution.py:55
  151.6 0.9 input_grad.1.refs_6_
  154.1 0.9 collective-permute-done.42.got_one
  155.0 1.4 columns.1
  (139 shorter events, 14.9 us)
Async XLA Ops:
  0.6 15.4 %copy-start = (f32[32,12]{0,1:T(8,128)S(1)}, f32[32,12]{0,1:T(8,128)}, u32[]{:S(2)}) copy-start(f32[32,12]{0,1:T(8,128)} %param.21) | copy-start | bytes 4612
  0.7 14.1 %copy-start.23 = (s32[1023]{0:T(1024)S(1)}, s32[1023]{0:T(1024)}, u32[]{:S(2)}) copy-start(s32[1023]{0:T(1024)} %param.28) | copy-start | bytes 12280
  0.7 14.2 %copy-start.24 = (bf16[768]{0:T(1024)(128)(2,1)S(1)}, bf16[768]{0:T(1024)(128)(2,1)}, u32[]{:S(2)}) copy-start(bf16[768]{0:T(1024)(128)(2,1)} %param.16) | copy-start | bytes 4612
  0.7 14.2 %copy-start.26 = (s32[256,1]{0,1:T(1,128)S(1)}, s32[256,1]{0,1:T(1,128)}, u32[]{:S(2)}) copy-start(s32[256,1]{0,1:T(1,128)} %param.26) | copy-start | bytes 3076
  0.7 24.7 %copy-start.2 = (bf16[256,768]{1,0:T(8,128)(2,1)S(1)}, bf16[256,768]{1,0:T(8,128)(2,1)}, u32[]{:S(2)}) copy-start(bf16[256,768]{1,0:T(8,128)(2,1)} %cot_ref.1) | copy-start | bytes 1179652
  2.4 3.1 %collective-permute-start.1 = (bf16[48,768]{1,0:T(8,128)(2,1)S(1)}, bf16[48,768]{1,0:T(8,128)(2,1)S(1)}, u32[]{:S(2)}, u32[]{:S(2)}) collective-permute-start(bf16[48,768]{1,0:T(8,128)(2,1)S(1)} %get-tuple-element.114), channel_id=1, source_target_pairs={{0,2},{2,0},{1,3},{3,1},{4,6},{6,4},{5,7},{7,5},{8,10},{10,8},{9,1... | collective-permute-start | bytes 221192 | tf_op jit(solution)/shard_map/ppermute | solution.py:30
  2.9 9.5 %collective-permute-start = (bf16[128,768]{1,0:T(8,128)(2,1)}, bf16[128,768]{1,0:T(8,128)(2,1)S(1)}, u32[]{:S(2)}, u32[]{:S(2)}) collective-permute-start(bf16[128,768]{1,0:T(8,128)(2,1)} %x_ref.1), channel_id=1, source_target_pairs={{0,1},{1,0},{2,3},{3,2},{4,5},{5,4},{6,7},{7,6},{8,9},{9,8},{10,11... | collective-permute-start | bytes 589832 | tf_op jit(solution)/shard_map/ppermute | solution.py:30
  5.5 6.8 %collective-permute-start.2 = (bf16[96,768]{1,0:T(8,128)(2,1)S(1)}, bf16[96,768]{1,0:T(8,128)(2,1)S(1)}, u32[]{:S(2)}, u32[]{:S(2)}) collective-permute-start(bf16[96,768]{1,0:T(8,128)(2,1)S(1)} %maximum_select_fusion.refs_0_), channel_id=1, source_target_pairs={{0,4},{4,0},{8,12},{12,8},{16,20},{20,16},{24,28},{28,24},{1,5},{5... | collective-permute-start | bytes 442376 | tf_op jit(solution)/shard_map/ppermute | solution.py:30
  7.1 6.9 %collective-permute-start.4 = (bf16[96,768]{1,0:T(8,128)(2,1)S(1)}, bf16[96,768]{1,0:T(8,128)(2,1)S(1)}, u32[]{:S(2)}, u32[]{:S(2)}) collective-permute-start(bf16[96,768]{1,0:T(8,128)(2,1)S(1)} %maximum_select_fusion.refs_0_), channel_id=1, source_target_pairs={{0,8},{4,12},{8,0},{12,4},{16,24},{20,28},{24,16},{28,20},{1,9},{5... | collective-permute-start | bytes 442376 | tf_op jit(solution)/shard_map/ppermute | solution.py:30
  9.5 13.8 %collective-permute-start.6 = (bf16[96,768]{1,0:T(8,128)(2,1)S(1)}, bf16[96,768]{1,0:T(8,128)(2,1)S(1)}, u32[]{:S(2)}, u32[]{:S(2)}) collective-permute-start(bf16[96,768]{1,0:T(8,128)(2,1)S(1)} %maximum_select_fusion.refs_0_), channel_id=1, source_target_pairs={{0,16},{4,20},{8,24},{12,28},{16,0},{20,4},{24,8},{28,12},{1,17},{... | collective-permute-start | bytes 442376 | tf_op jit(solution)/shard_map/ppermute | solution.py:30
  12.1 11.8 %collective-permute-start.8 = (bf16[96,768]{1,0:T(8,128)(2,1)S(1)}, bf16[96,768]{1,0:T(8,128)(2,1)S(1)}, u32[]{:S(2)}, u32[]{:S(2)}) collective-permute-start(bf16[96,768]{1,0:T(8,128)(2,1)S(1)} %maximum_select_fusion.refs_0_), channel_id=1, source_target_pairs={{0,24},{4,28},{8,16},{12,20},{16,8},{20,12},{24,0},{28,4},{1,25},{... | collective-permute-start | bytes 442376 | tf_op jit(solution)/shard_map/ppermute | solution.py:30
  13.8 17.4 %collective-permute-start.3 = (bf16[256,768]{1,0:T(8,128)(2,1)S(1)}, bf16[256,768]{1,0:T(8,128)(2,1)S(1)}, u32[]{:S(2)}, u32[]{:S(2)}) collective-permute-start(bf16[256,768]{1,0:T(8,128)(2,1)S(1)} %rows.1.own_ref), channel_id=1, source_target_pairs={{0,2},{2,0},{1,3},{3,1},{4,6},{6,4},{5,7},{7,5},{8,10},{10,8},{9,1... | collective-permute-start | bytes 1179656 | tf_op jit(solution)/shard_map/ppermute | solution.py:30
  13.9 11.4 %collective-permute-start.5 = (bf16[96,768]{1,0:T(8,128)(2,1)S(1)}, bf16[96,768]{1,0:T(8,128)(2,1)S(1)}, u32[]{:S(2)}, u32[]{:S(2)}) collective-permute-start(bf16[96,768]{1,0:T(8,128)(2,1)S(1)} %collective-permute-done.4.refs_2_), channel_id=1, source_target_pairs={{0,4},{4,0},{8,12},{12,8},{16,20},{20,16},{24,28},{28,24},{1,5},{5... | collective-permute-start | bytes 442376 | tf_op jit(solution)/shard_map/ppermute | solution.py:30
  16.0 15.2 %copy-start.9 = (bf16[256,320]{1,0:T(8,128)(2,1)}, bf16[256,320]{1,0:T(8,128)(2,1)S(1)}, u32[]{:S(2)}) copy-start(bf16[256,320]{1,0:T(8,128)(2,1)S(1)} %get-tuple-element.126.table_ref) | copy-start | bytes 491524
  23.3 7.8 %collective-permute-start.7 = (bf16[96,768]{1,0:T(8,128)(2,1)S(1)}, bf16[96,768]{1,0:T(8,128)(2,1)}, u32[]{:S(2)}, u32[]{:S(2)}) collective-permute-start(bf16[96,768]{1,0:T(8,128)(2,1)S(1)} %collective-permute-done.6.refs_4_), channel_id=1, source_target_pairs={{0,4},{4,0},{8,12},{12,8},{16,20},{20,16},{24,28},{28,24},{1,5},{5... | collective-permute-start | bytes 442376 | tf_op jit(solution)/shard_map/ppermute | solution.py:30
  23.9 7.3 %copy-start.20 = (bf16[96,768]{1,0:T(8,128)(2,1)}, bf16[96,768]{1,0:T(8,128)(2,1)S(1)}, u32[]{:S(2)}) copy-start(bf16[96,768]{1,0:T(8,128)(2,1)S(1)} %collective-permute-done.8.refs_6_) | copy-start | bytes 442372
  23.9 7.3 %collective-permute-start.9 = (bf16[96,768]{1,0:T(8,128)(2,1)S(1)}, bf16[96,768]{1,0:T(8,128)(2,1)}, u32[]{:S(2)}, u32[]{:S(2)}) collective-permute-start(bf16[96,768]{1,0:T(8,128)(2,1)S(1)} %collective-permute-done.8.refs_6_), channel_id=1, source_target_pairs={{0,4},{4,0},{8,12},{12,8},{16,20},{20,16},{24,28},{28,24},{1,5},{5... | collective-permute-start | bytes 442376 | tf_op jit(solution)/shard_map/ppermute | solution.py:30
  26.5 16.9 %all-to-all-start = ((bf16[8,40,768]{2,1,0:T(8,128)(2,1)}), bf16[8,40,768]{2,1,0:T(8,128)(2,1)S(1)}, u32[]{:S(2)}, u32[]{:S(2)}) async-start(bf16[8,40,768]{2,1,0:T(8,128)(2,1)} %bitcast.7), calls=%async_computation | async-start | bytes 983040 | tf_op jit(solution)/shard_map/all_to_all | solution.py:606
  37.8 2.9 %collective-permute-start.11 = (bf16[768,192]{1,0:T(8,128)(2,1)S(1)}, bf16[768,192]{1,0:T(8,128)(2,1)S(1)}, u32[]{:S(2)}, u32[]{:S(2)}) collective-permute-start(bf16[768,192]{1,0:T(8,128)(2,1)S(1)} %get-tuple-element.117.refs_1_.wo_ref), channel_id=1, source_target_pairs={{0,2},{2,0},{1,3},{3,1},{4,6},{6,4},{5,7},{7,5},{8,10},{10,8},{9,1... | collective-permute-start | bytes 884744 | tf_op jit(solution)/shard_map/ppermute | solution.py:30
  37.9 2.8 %collective-permute-start.10 = (bf16[256,192]{1,0:T(8,128)(2,1)S(1)}, bf16[256,192]{1,0:T(8,128)(2,1)S(1)}, u32[]{:S(2)}, u32[]{:S(2)}) collective-permute-start(bf16[256,192]{1,0:T(8,128)(2,1)S(1)} %get-tuple-element.116), channel_id=1, source_target_pairs={{0,2},{2,0},{1,3},{3,1},{4,6},{6,4},{5,7},{7,5},{8,10},{10,8},{9,1... | collective-permute-start | bytes 294920 | tf_op jit(solution)/shard_map/ppermute | solution.py:30
  41.1 11.2 %collective-permute-start.12 = (bf16[256,768]{1,0:T(8,128)(2,1)S(1)}, bf16[256,768]{1,0:T(8,128)(2,1)S(1)}, u32[]{:S(2)}, u32[]{:S(2)}) collective-permute-start(bf16[256,768]{1,0:T(8,128)(2,1)S(1)} %attended.1), channel_id=1, source_target_pairs={{0,1},{1,0},{2,3},{3,2},{4,5},{5,4},{6,7},{7,6},{8,9},{9,8},{10,11... | collective-permute-start | bytes 1179656 | tf_op jit(solution)/shard_map/ppermute | solution.py:30
  43.4 27.9 %collective-permute-start.21 = (bf16[8,40,768]{2,1,0:T(8,128)(2,1)S(1)}, bf16[8,40,768]{2,1,0:T(8,128)(2,1)S(1)}, u32[]{:S(2)}, u32[]{:S(2)}) collective-permute-start(bf16[8,40,768]{2,1,0:T(8,128)(2,1)S(1)} %all-to-all-done.own_ref), channel_id=1, source_target_pairs={{0,2},{2,0},{1,3},{3,1},{4,6},{6,4},{5,7},{7,5},{8,10},{10,8},{9,1... | collective-permute-start | bytes 1474568 | tf_op jit(solution)/shard_map/ppermute | solution.py:30
  52.4 18.9 %copy-start.1 = (bf16[768,768]{1,0:T(8,128)(2,1)S(1)}, bf16[768,768]{1,0:T(8,128)(2,1)}, u32[]{:S(2)}) copy-start(bf16[768,768]{1,0:T(8,128)(2,1)} %wdown_ref.3) | copy-start | bytes 3538948
  52.8 6.5 %collective-permute-start.13 = (bf16[40,768]{1,0:T(8,128)(2,1)S(1)}, bf16[40,768]{1,0:T(8,128)(2,1)S(1)}, u32[]{:S(2)}, u32[]{:S(2)}) collective-permute-start(bf16[40,768]{1,0:T(8,128)(2,1)S(1)} %get-tuple-element.129), channel_id=1, source_target_pairs={{0,4},{4,0},{8,12},{12,8},{16,20},{20,16},{24,28},{28,24},{1,5},{5... | collective-permute-start | bytes 184328 | tf_op jit(solution)/shard_map/ppermute | solution.py:30
  54.9 6.0 %collective-permute-start.14 = (bf16[40,768]{1,0:T(8,128)(2,1)S(1)}, bf16[40,768]{1,0:T(8,128)(2,1)S(1)}, u32[]{:S(2)}, u32[]{:S(2)}) collective-permute-start(bf16[40,768]{1,0:T(8,128)(2,1)S(1)} %get-tuple-element.130), channel_id=1, source_target_pairs={{0,8},{4,12},{8,0},{12,4},{16,24},{20,28},{24,16},{28,20},{1,9},{5... | collective-permute-start | bytes 184328 | tf_op jit(solution)/shard_map/ppermute | solution.py:30
  56.4 7.8 %collective-permute-start.15 = (bf16[40,768]{1,0:T(8,128)(2,1)S(1)}, bf16[40,768]{1,0:T(8,128)(2,1)S(1)}, u32[]{:S(2)}, u32[]{:S(2)}) collective-permute-start(bf16[40,768]{1,0:T(8,128)(2,1)S(1)} %get-tuple-element.131), channel_id=1, source_target_pairs={{0,12},{4,8},{8,4},{12,0},{16,28},{20,24},{24,20},{28,16},{1,13},{... | collective-permute-start | bytes 184328 | tf_op jit(solution)/shard_map/ppermute | solution.py:30
  56.4 8.6 %collective-permute-start.16 = (bf16[40,768]{1,0:T(8,128)(2,1)S(1)}, bf16[40,768]{1,0:T(8,128)(2,1)S(1)}, u32[]{:S(2)}, u32[]{:S(2)}) collective-permute-start(bf16[40,768]{1,0:T(8,128)(2,1)S(1)} %get-tuple-element.132), channel_id=1, source_target_pairs={{0,16},{4,20},{8,24},{12,28},{16,0},{20,4},{24,8},{28,12},{1,17},{... | collective-permute-start | bytes 184328 | tf_op jit(solution)/shard_map/ppermute | solution.py:30
  59.3 9.6 %collective-permute-start.17 = (bf16[40,768]{1,0:T(8,128)(2,1)S(1)}, bf16[40,768]{1,0:T(8,128)(2,1)S(1)}, u32[]{:S(2)}, u32[]{:S(2)}) collective-permute-start(bf16[40,768]{1,0:T(8,128)(2,1)S(1)} %get-tuple-element.133), channel_id=1, source_target_pairs={{0,20},{4,16},{8,28},{12,24},{16,4},{20,0},{24,12},{28,8},{1,21},{... | collective-permute-start | bytes 184328 | tf_op jit(solution)/shard_map/ppermute | solution.py:30
  60.9 7.9 %collective-permute-start.18 = (bf16[40,768]{1,0:T(8,128)(2,1)S(1)}, bf16[40,768]{1,0:T(8,128)(2,1)S(1)}, u32[]{:S(2)}, u32[]{:S(2)}) collective-permute-start(bf16[40,768]{1,0:T(8,128)(2,1)S(1)} %get-tuple-element.134), channel_id=1, source_target_pairs={{0,24},{4,28},{8,16},{12,20},{16,8},{20,12},{24,0},{28,4},{1,25},{... | collective-permute-start | bytes 184328 | tf_op jit(solution)/shard_map/ppermute | solution.py:30
  64.2 7.1 %collective-permute-start.19 = (bf16[40,768]{1,0:T(8,128)(2,1)S(1)}, bf16[40,768]{1,0:T(8,128)(2,1)S(1)}, u32[]{:S(2)}, u32[]{:S(2)}) collective-permute-start(bf16[40,768]{1,0:T(8,128)(2,1)S(1)} %get-tuple-element.135), channel_id=1, source_target_pairs={{0,28},{4,24},{8,20},{12,16},{16,12},{20,8},{24,4},{28,0},{1,29},{... | collective-permute-start | bytes 184328 | tf_op jit(solution)/shard_map/ppermute | solution.py:30
  68.9 4.3 %copy-start.3 = (bf16[768,768]{1,0:T(8,128)(2,1)S(1)}, bf16[768,768]{1,0:T(8,128)(2,1)}, u32[]{:S(2)}) copy-start(bf16[768,768]{1,0:T(8,128)(2,1)} %wup_ref.1) | copy-start | bytes 3538948
  68.9 4.3 %copy-start.22 = (bf16[768,8]{0,1:T(8,128)(2,1)S(1)}, bf16[768,8]{0,1:T(8,128)(2,1)}, u32[]{:S(2)}) copy-start(bf16[768,8]{0,1:T(8,128)(2,1)} %param.23) | copy-start | bytes 36868
  71.3 1.9 %collective-permute-start.20 = (bf16[320,768]{1,0:T(8,128)(2,1)S(1)}, bf16[320,768]{1,0:T(8,128)(2,1)S(1)}, u32[]{:S(2)}, u32[]{:S(2)}) collective-permute-start(bf16[320,768]{1,0:T(8,128)(2,1)S(1)} %constant_dynamic-update-slice_fusion.own_ref), channel_id=1, source_target_pairs={{0,2},{2,0},{1,3},{3,1},{4,6},{6,4},{5,7},{7,5},{8,10},{10,8},{9,1... | collective-permute-start | bytes 1474568 | tf_op jit(solution)/shard_map/ppermute | solution.py:30
  77.4 2.0 %collective-permute-start.22 = (bf16[320,768]{1,0:T(8,128)(2,1)S(1)}, bf16[320,768]{1,0:T(8,128)(2,1)S(1)}, u32[]{:S(2)}, u32[]{:S(2)}) collective-permute-start(bf16[320,768]{1,0:T(8,128)(2,1)S(1)} %get-tuple-element.140), channel_id=1, source_target_pairs={{0,2},{2,0},{1,3},{3,1},{4,6},{6,4},{5,7},{7,5},{8,10},{10,8},{9,1... | collective-permute-start | bytes 1474568 | tf_op jit(solution)/shard_map/ppermute | solution.py:30
  80.5 17.1 %collective-permute-start.23 = (bf16[320,768]{1,0:T(8,128)(2,1)S(1)}, bf16[320,768]{1,0:T(8,128)(2,1)S(1)}, u32[]{:S(2)}, u32[]{:S(2)}) collective-permute-start(bf16[320,768]{1,0:T(8,128)(2,1)S(1)} %get-tuple-element.143), channel_id=1, source_target_pairs={{0,2},{2,0},{1,3},{3,1},{4,6},{6,4},{5,7},{7,5},{8,10},{10,8},{9,1... | collective-permute-start | bytes 1474568 | tf_op jit(solution)/shard_map/ppermute | solution.py:30
  81.0 4.8 %collective-permute-start.24 = (bf16[40,768]{1,0:T(8,128)(2,1)S(1)}, bf16[40,768]{1,0:T(8,128)(2,1)S(1)}, u32[]{:S(2)}, u32[]{:S(2)}) collective-permute-start(bf16[40,768]{1,0:T(8,128)(2,1)S(1)} %get-tuple-element.145), channel_id=1, source_target_pairs={{0,4},{4,0},{8,12},{12,8},{16,20},{20,16},{24,28},{28,24},{1,5},{5... | collective-permute-start | bytes 184328 | tf_op jit(solution)/shard_map/ppermute | solution.py:30
  81.5 5.9 %collective-permute-start.25 = (bf16[40,768]{1,0:T(8,128)(2,1)S(1)}, bf16[40,768]{1,0:T(8,128)(2,1)S(1)}, u32[]{:S(2)}, u32[]{:S(2)}) collective-permute-start(bf16[40,768]{1,0:T(8,128)(2,1)S(1)} %get-tuple-element.146), channel_id=1, source_target_pairs={{0,8},{4,12},{8,0},{12,4},{16,24},{20,28},{24,16},{28,20},{1,9},{5... | collective-permute-start | bytes 184328 | tf_op jit(solution)/shard_map/ppermute | solution.py:30
  82.2 6.3 %collective-permute-start.26 = (bf16[40,768]{1,0:T(8,128)(2,1)S(1)}, bf16[40,768]{1,0:T(8,128)(2,1)S(1)}, u32[]{:S(2)}, u32[]{:S(2)}) collective-permute-start(bf16[40,768]{1,0:T(8,128)(2,1)S(1)} %get-tuple-element.147), channel_id=1, source_target_pairs={{0,12},{4,8},{8,4},{12,0},{16,28},{20,24},{24,20},{28,16},{1,13},{... | collective-permute-start | bytes 184328 | tf_op jit(solution)/shard_map/ppermute | solution.py:30
  84.5 9.2 %collective-permute-start.27 = (bf16[40,768]{1,0:T(8,128)(2,1)S(1)}, bf16[40,768]{1,0:T(8,128)(2,1)S(1)}, u32[]{:S(2)}, u32[]{:S(2)}) collective-permute-start(bf16[40,768]{1,0:T(8,128)(2,1)S(1)} %get-tuple-element.148), channel_id=1, source_target_pairs={{0,16},{4,20},{8,24},{12,28},{16,0},{20,4},{24,8},{28,12},{1,17},{... | collective-permute-start | bytes 184328 | tf_op jit(solution)/shard_map/ppermute | solution.py:30
  85.8 10.3 %collective-permute-start.28 = (bf16[40,768]{1,0:T(8,128)(2,1)S(1)}, bf16[40,768]{1,0:T(8,128)(2,1)S(1)}, u32[]{:S(2)}, u32[]{:S(2)}) collective-permute-start(bf16[40,768]{1,0:T(8,128)(2,1)S(1)} %get-tuple-element.149), channel_id=1, source_target_pairs={{0,20},{4,16},{8,28},{12,24},{16,4},{20,0},{24,12},{28,8},{1,21},{... | collective-permute-start | bytes 184328 | tf_op jit(solution)/shard_map/ppermute | solution.py:30
  87.4 8.7 %collective-permute-start.29 = (bf16[40,768]{1,0:T(8,128)(2,1)S(1)}, bf16[40,768]{1,0:T(8,128)(2,1)S(1)}, u32[]{:S(2)}, u32[]{:S(2)}) collective-permute-start(bf16[40,768]{1,0:T(8,128)(2,1)S(1)} %get-tuple-element.150), channel_id=1, source_target_pairs={{0,24},{4,28},{8,16},{12,20},{16,8},{20,12},{24,0},{28,4},{1,25},{... | collective-permute-start | bytes 184328 | tf_op jit(solution)/shard_map/ppermute | solution.py:30
  88.4 7.6 %collective-permute-start.30 = (bf16[40,768]{1,0:T(8,128)(2,1)S(1)}, bf16[40,768]{1,0:T(8,128)(2,1)S(1)}, u32[]{:S(2)}, u32[]{:S(2)}) collective-permute-start(bf16[40,768]{1,0:T(8,128)(2,1)S(1)} %get-tuple-element.141.held_ref), channel_id=1, source_target_pairs={{0,28},{4,24},{8,20},{12,16},{16,12},{20,8},{24,4},{28,0},{1,29},{... | collective-permute-start | bytes 184328 | tf_op jit(solution)/shard_map/ppermute | solution.py:30
  96.4 9.8 %collective-permute-start.31 = (bf16[256,768]{1,0:T(8,128)(2,1)S(1)}, bf16[256,768]{1,0:T(8,128)(2,1)}, u32[]{:S(2)}, u32[]{:S(2)}) collective-permute-start(bf16[256,768]{1,0:T(8,128)(2,1)S(1)} %gather_grad.1.own_ref), channel_id=1, source_target_pairs={{0,1},{1,0},{2,3},{3,2},{4,5},{5,4},{6,7},{7,6},{8,9},{9,8},{10,11... | collective-permute-start | bytes 1179656 | tf_op jit(solution)/shard_map/ppermute | solution.py:30
  99.1 24.8 %all-to-all-start.1 = ((bf16[8,40,768]{2,1,0:T(8,128)(2,1)}), bf16[8,40,768]{2,1,0:T(8,128)(2,1)S(1)}, u32[]{:S(2)}, u32[]{:S(2)}) async-start(bf16[8,40,768]{2,1,0:T(8,128)(2,1)} %join_out.1.refs_8_), calls=%async_computation.1 | async-start | bytes 983040 | tf_op jit(solution)/shard_map/all_to_all | solution.py:606
  108.5 1.7 %collective-permute-start.32 = (bf16[256,768]{1,0:T(8,128)(2,1)S(1)}, bf16[256,768]{1,0:T(8,128)(2,1)S(1)}, u32[]{:S(2)}, u32[]{:S(2)}) collective-permute-start(bf16[256,768]{1,0:T(8,128)(2,1)S(1)} %get-tuple-element.159.own_ref), channel_id=1, source_target_pairs={{0,2},{2,0},{1,3},{3,1},{4,6},{6,4},{5,7},{7,5},{8,10},{10,8},{9,1... | collective-permute-start | bytes 1179656 | tf_op jit(solution)/shard_map/ppermute | solution.py:30
  114.1 8.2 %copy-start.14 = (f32[384,384]{1,0:T(8,128)}, f32[384,384]{1,0:T(8,128)S(1)}, u32[]{:S(2)}) copy-start(f32[384,384]{1,0:T(8,128)S(1)} %get-tuple-element.175.keep_ref) | copy-start | bytes 1769476
  114.1 13.1 %collective-permute-start.33 = (bf16[384,384]{1,0:T(8,128)(2,1)}, bf16[384,384]{1,0:T(8,128)(2,1)}, u32[]{:S(2)}, u32[]{:S(2)}) collective-permute-start(bf16[384,384]{1,0:T(8,128)(2,1)} %get-tuple-element.176), channel_id=1, source_target_pairs={{0,4},{4,0},{8,12},{12,8},{16,20},{20,16},{24,28},{28,24},{1,5},{5... | collective-permute-start | bytes 884744 | tf_op jit(solution)/shard_map/ppermute | solution.py:30
  123.0 11.3 %collective-permute-start.36 = (bf16[256,768]{1,0:T(8,128)(2,1)}, bf16[256,768]{1,0:T(8,128)(2,1)}, u32[]{:S(2)}, u32[]{:S(2)}) collective-permute-start(bf16[256,768]{1,0:T(8,128)(2,1)} %get-tuple-element.181), channel_id=1, source_target_pairs={{0,2},{2,0},{1,3},{3,1},{4,6},{6,4},{5,7},{7,5},{8,10},{10,8},{9,1... | collective-permute-start | bytes 1179656 | tf_op jit(solution)/shard_map/ppermute | solution.py:30
  123.0 4.2 %collective-permute-start.34 = (f32[16,768]{1,0:T(8,128)S(1)}, f32[16,768]{1,0:T(8,128)S(1)}, u32[]{:S(2)}, u32[]{:S(2)}) collective-permute-start(f32[16,768]{1,0:T(8,128)S(1)} %get-tuple-element.177.small_ref), channel_id=1, source_target_pairs={{0,1},{1,0},{2,3},{3,2},{4,5},{5,4},{6,7},{7,6},{8,9},{9,8},{10,11... | collective-permute-start | bytes 147464 | tf_op jit(solution)/shard_map/ppermute | solution.py:30
  127.2 13.0 %copy-start.13 = (f32[384,384]{1,0:T(8,128)S(1)}, f32[384,384]{1,0:T(8,128)}, u32[]{:S(2)}) copy-start(f32[384,384]{1,0:T(8,128)} %get-tuple-element.184.keep_ref) | copy-start | bytes 1769476
  128.3 11.9 %collective-permute-start.37 = (bf16[416,384]{1,0:T(8,128)(2,1)S(1)}, bf16[416,384]{1,0:T(8,128)(2,1)S(1)}, u32[]{:S(2)}, u32[]{:S(2)}) collective-permute-start(bf16[416,384]{1,0:T(8,128)(2,1)S(1)} %get-tuple-element.185), channel_id=1, source_target_pairs={{0,4},{4,0},{8,12},{12,8},{16,20},{20,16},{24,28},{28,24},{1,5},{5... | collective-permute-start | bytes 958472 | tf_op jit(solution)/shard_map/ppermute | solution.py:30
  128.5 8.3 %collective-permute-start.38 = (bf16[96,384]{1,0:T(8,128)(2,1)S(1)}, bf16[96,384]{1,0:T(8,128)(2,1)S(1)}, u32[]{:S(2)}, u32[]{:S(2)}) collective-permute-start(bf16[96,384]{1,0:T(8,128)(2,1)S(1)} %get-tuple-element.182.held_ref), channel_id=1, source_target_pairs={{0,8},{4,12},{8,0},{12,4},{16,24},{20,28},{24,16},{28,20},{1,9},{5... | collective-permute-start | bytes 221192 | tf_op jit(solution)/shard_map/ppermute | solution.py:30
  132.0 8.2 %collective-permute-start.39 = (bf16[96,384]{1,0:T(8,128)(2,1)S(1)}, bf16[96,384]{1,0:T(8,128)(2,1)S(1)}, u32[]{:S(2)}, u32[]{:S(2)}) collective-permute-start(bf16[96,384]{1,0:T(8,128)(2,1)S(1)} %get-tuple-element.189), channel_id=1, source_target_pairs={{0,16},{4,20},{8,24},{12,28},{16,0},{20,4},{24,8},{28,12},{1,17},{... | collective-permute-start | bytes 221192 | tf_op jit(solution)/shard_map/ppermute | solution.py:30
  132.8 7.4 %collective-permute-start.40 = (bf16[96,384]{1,0:T(8,128)(2,1)S(1)}, bf16[96,384]{1,0:T(8,128)(2,1)S(1)}, u32[]{:S(2)}, u32[]{:S(2)}) collective-permute-start(bf16[96,384]{1,0:T(8,128)(2,1)S(1)} %get-tuple-element.190), channel_id=1, source_target_pairs={{0,24},{4,28},{8,16},{12,20},{16,8},{20,12},{24,0},{28,4},{1,25},{... | collective-permute-start | bytes 221192 | tf_op jit(solution)/shard_map/ppermute | solution.py:30
  134.4 12.2 %collective-permute-start.35 = (bf16[128,768]{1,0:T(8,128)(2,1)S(1)}, bf16[128,768]{1,0:T(8,128)(2,1)S(1)}, u32[]{:S(2)}, u32[]{:S(2)}) collective-permute-start(bf16[128,768]{1,0:T(8,128)(2,1)S(1)} %get-tuple-element.180), channel_id=1, source_target_pairs={{0,1},{1,0},{2,3},{3,2},{4,5},{5,4},{6,7},{7,6},{8,9},{9,8},{10,11... | collective-permute-start | bytes 589832 | tf_op jit(solution)/shard_map/ppermute | solution.py:30
  135.5 12.3 %copy-start.8 = (bf16[640,768]{1,0:T(8,128)(2,1)S(1)}, bf16[640,768]{1,0:T(8,128)(2,1)}, u32[]{:S(2)}) copy-start(bf16[640,768]{1,0:T(8,128)(2,1)} %copy-done.7) | copy-start | bytes 2949124
  140.2 7.6 %copy-start.4 = (bf16[640,768]{1,0:T(8,128)(2,1)S(1)}, bf16[640,768]{1,0:T(8,128)(2,1)}, u32[]{:S(2)}) copy-start(bf16[640,768]{1,0:T(8,128)(2,1)} %get-tuple-element.200.cots_ref) | copy-start | bytes 2949124
  140.2 7.6 %copy-start.6 = (bf16[640,768]{1,0:T(8,128)(2,1)S(1)}, bf16[640,768]{1,0:T(8,128)(2,1)}, u32[]{:S(2)}) copy-start(bf16[640,768]{1,0:T(8,128)(2,1)} %copy-done.5) | copy-start | bytes 2949124
  140.9 10.7 %collective-permute-start.41 = (bf16[128,768]{1,0:T(8,128)(2,1)S(1)}, bf16[128,768]{1,0:T(8,128)(2,1)S(1)}, u32[]{:S(2)}, u32[]{:S(2)}) collective-permute-start(bf16[128,768]{1,0:T(8,128)(2,1)S(1)} %get-tuple-element.191), channel_id=1, source_target_pairs={{0,1},{1,0},{2,3},{3,2},{4,5},{5,4},{6,7},{7,6},{8,9},{9,8},{10,11... | collective-permute-start | bytes 589832 | tf_op jit(solution)/shard_map/ppermute | solution.py:30
  142.1 10.4 %collective-permute-start.43 = (bf16[128,384]{1,0:T(8,128)(2,1)S(1)}, bf16[128,384]{1,0:T(8,128)(2,1)S(1)}, u32[]{:S(2)}, u32[]{:S(2)}) collective-permute-start(bf16[128,384]{1,0:T(8,128)(2,1)S(1)} %get-tuple-element.196.held_ref), channel_id=1, source_target_pairs={{0,8},{4,12},{8,0},{12,4},{16,24},{20,28},{24,16},{28,20},{1,9},{5... | collective-permute-start | bytes 294920 | tf_op jit(solution)/shard_map/ppermute | solution.py:30
  143.5 9.4 %collective-permute-start.44 = (bf16[128,384]{1,0:T(8,128)(2,1)S(1)}, bf16[128,384]{1,0:T(8,128)(2,1)S(1)}, u32[]{:S(2)}, u32[]{:S(2)}) collective-permute-start(bf16[128,384]{1,0:T(8,128)(2,1)S(1)} %get-tuple-element.197), channel_id=1, source_target_pairs={{0,16},{4,20},{8,24},{12,28},{16,0},{20,4},{24,8},{28,12},{1,17},{... | collective-permute-start | bytes 294920 | tf_op jit(solution)/shard_map/ppermute | solution.py:30
  144.6 8.3 %collective-permute-start.45 = (bf16[128,384]{1,0:T(8,128)(2,1)S(1)}, bf16[128,384]{1,0:T(8,128)(2,1)S(1)}, u32[]{:S(2)}, u32[]{:S(2)}) collective-permute-start(bf16[128,384]{1,0:T(8,128)(2,1)S(1)} %get-tuple-element.198), channel_id=1, source_target_pairs={{0,24},{4,28},{8,16},{12,20},{16,8},{20,12},{24,0},{28,4},{1,25},{... | collective-permute-start | bytes 294920 | tf_op jit(solution)/shard_map/ppermute | solution.py:30
  153.5 1.5 collective-permute-start.46
  153.6 1.4 collective-permute-start.42
  (12 other events, 24.5 us)

commit v8 on v7

--- a/solution.py
+++ b/solution.py
@@ -312,18 +312,21 @@
     refs[-1][...] = mm(back_table_ref[...], slots).astype(bf16)
 
 
-def hidden_back_kernel(ids, hidden_ref, own_ref, got_ref, cot_ref, gain_ref, held_ref, grad_ref, low_ref, dgain_ref, all_ref):
+def hidden_back_kernel(ids, hidden_ref, own_ref, got_ref, cot_ref, gain_ref, held_ref, grad_ref, low_ref, dgain_ref, all_ref, sem):
     hidden = hidden_ref[...]
     grad_normed = own_ref[...].astype(f32) + got_ref[...].astype(f32)
     scale = lax.rsqrt(jnp.mean(hidden * hidden, axis=1, keepdims=True) + norm_eps)
-    dgain_ref[...] = jnp.sum(grad_normed * hidden * scale, axis=0, keepdims=True)
     pulled = gain_ref[...] * grad_normed
     inner = jnp.mean(pulled * hidden, axis=1, keepdims=True)
     grad = cot_ref[...].astype(f32) + scale * pulled - hidden * (scale * scale * scale) * inner
-    low_ref[...] = grad.astype(bf16)
     all_ref[...] = grad
     rows = grad_ref.shape[0]
-    grad_ref[...] = all_ref[pl.ds(pl.multiple_of(ids[2] * rows, rows), rows), :]
+    mine = all_ref.at[pl.ds(pl.multiple_of(ids[2] * rows, rows), rows)]
+    copy = pltpu.make_async_copy(mine, grad_ref, sem)
+    copy.start()
+    low_ref[...] = grad.astype(bf16)
+    dgain_ref[...] = jnp.sum(grad_normed * hidden * scale, axis=0, keepdims=True)
+    copy.wait()
 
 
 def returned_kernel(ids, table_ref, slots_ref, held_ref, keep_ref, send_ref):
@@ -789,7 +792,7 @@
     grad_hidden, grad_attended, gain_two_part = call(
         hidden_back_kernel,
         "hidden_back",
-        [Near(out(half_block, f32)), out((block_rows, width), bf16), Near(out((1, width), f32))],
+        [Far(out(half_block, f32)), out((block_rows, width), bf16), Near(out((1, width), f32))],
         [
             ids,
             Near(hidden),
@@ -800,7 +803,7 @@
             Raw(mixed),
         ],
         smem=1,
-        scratch=[pltpu.VMEM((block_rows, width), f32)],
+        scratch=[pltpu.VMEM((block_rows, width), f32), pltpu.SemaphoreType.DMA],
     )
     grad_attended_other = across(grad_attended, "core", 1)
     chunk = 3 * HD + cols

time: 158 us -> 158 us (level)
    unnamed x62 -> x60, local copies, waits for them, and re-layouts: 4.51 us -> 3.75 us
where the time goes in v8:
time: 158 us
  starting transfers between devices  64.5 us (41%)
  Pallas kernels  48.1 us (30%)
  waiting for transfers between devices  36.7 us (23%)
  local copies, waits for them, and re-layouts  4.62 us (3%)
  other arithmetic  1.91 us (1%)
    ppermute x47, starting transfers between devices, across(): lax.ppermute(shard, axis, [(i, i ^ bits) for i in range(lax.axis_size(axi...  55.6 us
    pallas_call x27, Pallas kernels, call(): pl.pallas_call(body, name=name, out_shape=[space[type(o)](x.shape, x.dtyp...  48.1 us
    ppermute x47, waiting for transfers between devices, across(): lax.ppermute(shard, axis, [(i, i ^ bits) for i in range(lax.axis_size(axi...  35.6 us
    all_to_all x2, starting transfers between devices, trade_natural(): lax.all_to_all(stacked, 'node', split_axis=0, concat_axis=0, tiled=True)  8.93 us
    unnamed x60, local copies, waits for them, and re-layouts  3.75 us
  transfers between devices with their start and end apart: 49, of which 13 were waited for; matrix products, arithmetic and copies ran while one was open for 1% of the time, Pallas kernels for 25%

profile of v8, /device:TPU:0, one launch (start us, length us, event | category | flops | bytes accessed | tf_op | source)
XLA Modules:
  0.0 157.6 jit_solution(13044920937281399941)
XLA Ops:
  0.8 1.6 shares.1
  2.9 2.6 %collective-permute-start = (bf16[128,768]{1,0:T(8,128)(2,1)}, bf16[128,768]{1,0:T(8,128)(2,1)S(1)}, u32[]{:S(2)}, u32[]{:S(2)}) collective-permute-start(bf16[128,768]{1,0:T(8,128)(2,1)} %x_ref.1), channel_id=1, source_target_pairs={{0,1},{1,0},{2,3},{3,2},{4,5},{5,4},{6,7},{7,6},{8,9},{9,8},{10,11... | collective-permute-start | bytes 589832 | tf_op jit(solution)/shard_map/ppermute | solution.py:30
  5.5 1.6 collective-permute-start.2
  7.1 1.6 %collective-permute-start.4 = (bf16[96,768]{1,0:T(8,128)(2,1)S(1)}, bf16[96,768]{1,0:T(8,128)(2,1)S(1)}, u32[]{:S(2)}, u32[]{:S(2)}) collective-permute-start(bf16[96,768]{1,0:T(8,128)(2,1)S(1)} %maximum_select_fusion.refs_0_), channel_id=1, source_target_pairs={{0,8},{4,12},{8,0},{12,4},{16,24},{20,28},{24,16},{28,20},{1,9},{5... | collective-permute-start | bytes 442376 | tf_op jit(solution)/shard_map/ppermute | solution.py:30
  9.5 2.6 %collective-permute-start.6 = (bf16[96,768]{1,0:T(8,128)(2,1)S(1)}, bf16[96,768]{1,0:T(8,128)(2,1)S(1)}, u32[]{:S(2)}, u32[]{:S(2)}) collective-permute-start(bf16[96,768]{1,0:T(8,128)(2,1)S(1)} %maximum_select_fusion.refs_0_), channel_id=1, source_target_pairs={{0,16},{4,20},{8,24},{12,28},{16,0},{20,4},{24,8},{28,12},{1,17},{... | collective-permute-start | bytes 442376 | tf_op jit(solution)/shard_map/ppermute | solution.py:30
  12.3 0.9 copy-done.11
  15.1 0.9 tables.1
  16.1 7.3 %collective-permute-done.6.refs_4_ = bf16[96,768]{1,0:T(8,128)(2,1)S(1)} collective-permute-done((bf16[96,768]{1,0:T(8,128)(2,1)S(1)}, bf16[96,768]{1,0:T(8,128)(2,1)S(1)}, u32[]{:S(2)}, u32[]{:S(2)}) %collective-permute-start.6) | collective-permute-done | bytes 147488 | tf_op jit(solution)/shard_map/ppermute | solution.py:30
  23.9 1.5 collective-permute-start.9
  25.4 1.1 cot_slots.1
  26.5 4.2 %all-to-all-start = ((bf16[8,40,768]{2,1,0:T(8,128)(2,1)}), bf16[8,40,768]{2,1,0:T(8,128)(2,1)S(1)}, u32[]{:S(2)}, u32[]{:S(2)}) async-start(bf16[8,40,768]{2,1,0:T(8,128)(2,1)} %bitcast.7), calls=%async_computation | async-start | bytes 983040 | tf_op jit(solution)/shard_map/all_to_all | solution.py:609
  31.2 0.9 copy-done.20
  32.1 5.6 %attend.1 = (bf16[768,768]{1,0:T(8,128)(2,1)S(1)}, bf16[768,192]{1,0:T(8,128)(2,1)S(1)}, bf16[512,768]{1,0:T(8,128)(2,1)S(1)}, bf16[512,576]{1,0:T(8,128)(2,1)S(...) custom-call(s32[3]{0:T(128)S(1)} %pad_add_fusion.ids, ...), custom_call_target="tpu_custom_call" | custom-call | tf_op jit(solution)/shard_map/attend/pallas_call | solution.py:55
  38.3 2.3 %park.1 = (bf16[768,768]{1,0:T(8,128)(2,1)}, bf16[768,192]{1,0:T(8,128)(2,1)}, bf16[512,768]{1,0:T(8,128)(2,1)}, bf16[512,576]{1,0:T(8,128)(2,1)}, bf16[512,192]...) custom-call(bf16[768,768]{1,0:T(8,128)(2,1)S(1)} %get-tuple-element.118.refs_0_, ...), custom_call_target="tpu_custom_call" | custom-call | tf_op jit(solution)/shard_map/park/pallas_call | solution.py:55
  41.1 1.2 collective-permute-start.12
  42.3 1.1 all-to-all-done.own_ref
  43.4 8.8 %collective-permute-done.12 = bf16[256,768]{1,0:T(8,128)(2,1)S(1)} collective-permute-done((bf16[256,768]{1,0:T(8,128)(2,1)S(1)}, bf16[256,768]{1,0:T(8,128)(2,1)S(1)}, u32[]{:S(2)}, u32[]{:S(2)}) %collective-permute-start.12) | collective-permute-done | bytes 393248 | tf_op jit(solution)/shard_map/ppermute | solution.py:30
  52.8 2.1 %collective-permute-start.13 = (bf16[40,768]{1,0:T(8,128)(2,1)S(1)}, bf16[40,768]{1,0:T(8,128)(2,1)S(1)}, u32[]{:S(2)}, u32[]{:S(2)}) collective-permute-start(bf16[40,768]{1,0:T(8,128)(2,1)S(1)} %get-tuple-element.129), channel_id=1, source_target_pairs={{0,4},{4,0},{8,12},{12,8},{16,20},{20,16},{24,28},{28,24},{1,5},{5... | collective-permute-start | bytes 184328 | tf_op jit(solution)/shard_map/ppermute | solution.py:30
  54.9 1.5 collective-permute-start.14
  56.4 2.8 %collective-permute-start.16 = (bf16[40,768]{1,0:T(8,128)(2,1)S(1)}, bf16[40,768]{1,0:T(8,128)(2,1)S(1)}, u32[]{:S(2)}, u32[]{:S(2)}) collective-permute-start(bf16[40,768]{1,0:T(8,128)(2,1)S(1)} %get-tuple-element.132), channel_id=1, source_target_pairs={{0,16},{4,20},{8,24},{12,28},{16,0},{20,4},{24,8},{28,12},{1,17},{... | collective-permute-start | bytes 184328 | tf_op jit(solution)/shard_map/ppermute | solution.py:30
  59.3 1.6 %collective-permute-start.17 = (bf16[40,768]{1,0:T(8,128)(2,1)S(1)}, bf16[40,768]{1,0:T(8,128)(2,1)S(1)}, u32[]{:S(2)}, u32[]{:S(2)}) collective-permute-start(bf16[40,768]{1,0:T(8,128)(2,1)S(1)} %get-tuple-element.133), channel_id=1, source_target_pairs={{0,20},{4,16},{8,28},{12,24},{16,4},{20,0},{24,12},{28,8},{1,21},{... | collective-permute-start | bytes 184328 | tf_op jit(solution)/shard_map/ppermute | solution.py:30
  60.9 3.2 %collective-permute-start.18 = (bf16[40,768]{1,0:T(8,128)(2,1)S(1)}, bf16[40,768]{1,0:T(8,128)(2,1)S(1)}, u32[]{:S(2)}, u32[]{:S(2)}) collective-permute-start(bf16[40,768]{1,0:T(8,128)(2,1)S(1)} %get-tuple-element.134), channel_id=1, source_target_pairs={{0,24},{4,28},{8,16},{12,20},{16,8},{20,12},{24,0},{28,4},{1,25},{... | collective-permute-start | bytes 184328 | tf_op jit(solution)/shard_map/ppermute | solution.py:30
  64.2 0.8 collective-permute-start.19
  65.0 3.8 %collective-permute-done.17 = bf16[40,768]{1,0:T(8,128)(2,1)S(1)} collective-permute-done((bf16[40,768]{1,0:T(8,128)(2,1)S(1)}, bf16[40,768]{1,0:T(8,128)(2,1)S(1)}, u32[]{:S(2)}, u32[]{:S(2)}) %collective-permute-start.17) | collective-permute-done | bytes 61472 | tf_op jit(solution)/shard_map/ppermute | solution.py:30
  68.9 2.4 %collective-permute-done.19 = bf16[40,768]{1,0:T(8,128)(2,1)S(1)} collective-permute-done((bf16[40,768]{1,0:T(8,128)(2,1)S(1)}, bf16[40,768]{1,0:T(8,128)(2,1)S(1)}, u32[]{:S(2)}, u32[]{:S(2)}) %collective-permute-start.19) | collective-permute-done | bytes 61472 | tf_op jit(solution)/shard_map/ppermute | solution.py:30
  71.3 1.8 %cots.1 = (bf16[640,768]{1,0:T(8,128)(2,1)}, f32[640,768]{1,0:T(8,128)S(1)}) custom-call(s32[3]{0:T(128)S(1)} %pad_add_fusion.ids, bf16[8,40,768]{2,1,0:T(8,128)(2,1)S(1)} %all-to-all-done.own_ref, bf16[8,40,768]{2,1,0:T(8,128)(2,1)S(1)} %collective-permute-done.21.other_ref, bf16[768,768]{1,0:T(8,128)(2,1)S(1)} %copy-done.1, ...), custom_call_target="tpu_custom_call" | custom-call | tf_op jit(solution)/shard_map/cots/pallas_call | solution.py:55
  73.2 4.2 %expert.1 = (bf16[640,768]{1,0:T(8,128)(2,1)S(1)}, bf16[640,768]{1,0:T(8,128)(2,1)S(1)}, f32[640,1]{1,0:T(8,128)S(1)}, f32[320,768]{1,0:T(8,128)S(1)}, bf16[320,...) custom-call(s32[3]{0:T(128)S(1)} %pad_add_fusion.ids, ...), custom_call_target="tpu_custom_call" | custom-call | tf_op jit(solution)/shard_map/expert/pallas_call | solution.py:55
  78.0 1.5 collective-permute-done.22.got_ref
  79.5 1.0 expert_out.1
  82.1 2.3 %collective-permute-start.26 = (bf16[40,768]{1,0:T(8,128)(2,1)S(1)}, bf16[40,768]{1,0:T(8,128)(2,1)S(1)}, u32[]{:S(2)}, u32[]{:S(2)}) collective-permute-start(bf16[40,768]{1,0:T(8,128)(2,1)S(1)} %get-tuple-element.147), channel_id=1, source_target_pairs={{0,12},{4,8},{8,4},{12,0},{16,28},{20,24},{24,20},{28,16},{1,13},{... | collective-permute-start | bytes 184328 | tf_op jit(solution)/shard_map/ppermute | solution.py:30
  84.5 1.3 collective-permute-start.27
  85.8 1.6 %collective-permute-start.28 = (bf16[40,768]{1,0:T(8,128)(2,1)S(1)}, bf16[40,768]{1,0:T(8,128)(2,1)S(1)}, u32[]{:S(2)}, u32[]{:S(2)}) collective-permute-start(bf16[40,768]{1,0:T(8,128)(2,1)S(1)} %get-tuple-element.149), channel_id=1, source_target_pairs={{0,20},{4,16},{8,28},{12,24},{16,4},{20,0},{24,12},{28,8},{1,21},{... | collective-permute-start | bytes 184328 | tf_op jit(solution)/shard_map/ppermute | solution.py:30
  87.4 1.0 collective-permute-start.29
  88.4 3.7 %collective-permute-start.30 = (bf16[40,768]{1,0:T(8,128)(2,1)S(1)}, bf16[40,768]{1,0:T(8,128)(2,1)S(1)}, u32[]{:S(2)}, u32[]{:S(2)}) collective-permute-start(bf16[40,768]{1,0:T(8,128)(2,1)S(1)} %get-tuple-element.141.held_ref), channel_id=1, source_target_pairs={{0,28},{4,24},{8,20},{12,16},{16,12},{20,8},{24,4},{28,0},{1,29},{... | collective-permute-start | bytes 184328 | tf_op jit(solution)/shard_map/ppermute | solution.py:30
  92.1 1.6 collective-permute-done.27.refs_4_
  93.7 2.4 %collective-permute-done.28.refs_5_ = bf16[40,768]{1,0:T(8,128)(2,1)S(1)} collective-permute-done((bf16[40,768]{1,0:T(8,128)(2,1)S(1)}, bf16[40,768]{1,0:T(8,128)(2,1)S(1)}, u32[]{:S(2)}, u32[]{:S(2)}) %collective-permute-start.28) | collective-permute-done | bytes 61472 | tf_op jit(solution)/shard_map/ppermute | solution.py:30
  96.4 1.2 collective-permute-start.31
  97.7 1.4 join_out.1.refs_8_
  99.1 4.7 %all-to-all-start.1 = ((bf16[8,40,768]{2,1,0:T(8,128)(2,1)}), bf16[8,40,768]{2,1,0:T(8,128)(2,1)S(1)}, u32[]{:S(2)}, u32[]{:S(2)}) async-start(bf16[8,40,768]{2,1,0:T(8,128)(2,1)} %join_out.1.refs_8_), calls=%async_computation.1 | async-start | bytes 983040 | tf_op jit(solution)/shard_map/all_to_all | solution.py:609
  103.8 2.4 %unpark.1 = (bf16[768,768]{1,0:T(8,128)(2,1)S(1)}, bf16[768,192]{1,0:T(8,128)(2,1)S(1)}, bf16[512,768]{1,0:T(8,128)(2,1)S(1)}, bf16[512,576]{1,0:T(8,128)(2,1)S(...) custom-call(bf16[768,768]{1,0:T(8,128)(2,1)} %get-tuple-element.151., ...), custom_call_target="tpu_custom_call" | custom-call | tf_op jit(solution)/shard_map/unpark/pallas_call | solution.py:55
  106.2 2.3 %hidden_back.1 = (f32[128,768]{1,0:T(8,128)}, bf16[256,768]{1,0:T(8,128)(2,1)S(1)}, f32[1,768]{1,0:T(1,128)S(1)}) custom-call(s32[3]{0:T(128)S(1)} %pad_add_fusion.ids, f32[256,768]{1,0:T(8,128)S(1)} %add_add_fusion.hidden_ref, bf16[256,768]{1,0:T(8,128)(2,1)S(1)} %gather_grad.1.own_ref, bf16[256,768]{1,0:T(8,128)(2,1)} %collective-permute-done.31.got_ref, ...), custom_call_target="tpu_custom_call" | custom-call | tf_op jit(solution)/shard_map/hidden_back/pallas_call | solution.py:55
  108.6 1.7 %collective-permute-done.32.other_ref = bf16[256,768]{1,0:T(8,128)(2,1)S(1)} collective-permute-done((bf16[256,768]{1,0:T(8,128)(2,1)S(1)}, bf16[256,768]{1,0:T(8,128)(2,1)S(1)}, u32[]{:S(2)}, u32[]{:S(2)}) %collective-permute-start.32) | collective-permute-done | bytes 393248 | tf_op jit(solution)/shard_map/ppermute | solution.py:30
  110.3 3.8 %first_back.1 = (bf16[512,192]{1,0:T(8,128)(2,1)S(1)}, bf16[512,192]{1,0:T(8,128)(2,1)S(1)}, f32[8,1024]{1,0:T(8,128)S(1)}, bf16[512,768]{1,0:T(8,128)(2,1)S(1)}...) custom-call(s32[3]{0:T(128)S(1)} %pad_add_fusion.ids, bf16[256,768]{1,0:T(8,128)(2,1)S(1)} %get-tuple-element.159.own_ref, ...), custom_call_target="tpu_custom_call" | custom-call | tf_op jit(solution)/shard_map/first_back/pallas_call | solution.py:55
  114.1 2.0 %collective-permute-start.33 = (bf16[384,384]{1,0:T(8,128)(2,1)}, bf16[384,384]{1,0:T(8,128)(2,1)}, u32[]{:S(2)}, u32[]{:S(2)}) collective-permute-start(bf16[384,384]{1,0:T(8,128)(2,1)} %get-tuple-element.176), channel_id=1, source_target_pairs={{0,4},{4,0},{8,12},{12,8},{16,20},{20,16},{24,28},{28,24},{1,5},{5... | collective-permute-start | bytes 884744 | tf_op jit(solution)/shard_map/ppermute | solution.py:30
  116.3 6.0 %second_back.1 = (f32[256,768]{1,0:T(8,128)S(1)}, bf16[256,768]{1,0:T(8,128)(2,1)}, f32[16,768]{1,0:T(8,128)S(1)}, f32[384,384]{1,0:T(8,128)}, bf16[384,384]{1,0:T(8,128)(2,1)S(1)}) custom-call(s32[3]{0:T(128)S(1)} %pad_add_fusion.ids, bf16[512,192]{1,0:T(8,128)(2,1)S(1)} %get-tuple-element.164.gm_ref, bf16[512,192]{1,0:T(8,128)(2,1)S(1)} %get-tuple-element.165.first_ref, ...), custom_call_target="tpu_custom_call" | custom-call | tf_op jit(solution)/shard_map/second_back/pallas_call | solution.py:55
  123.1 0.9 collective-permute-start.34
  123.9 0.9 copy-done.10
  124.8 0.9 returned.1
  125.8 1.4 collective-permute-done.34.small_got_ref
  127.2 1.1 fold_first.1
  128.5 3.5 %collective-permute-start.38 = (bf16[96,384]{1,0:T(8,128)(2,1)S(1)}, bf16[96,384]{1,0:T(8,128)(2,1)S(1)}, u32[]{:S(2)}, u32[]{:S(2)}) collective-permute-start(bf16[96,384]{1,0:T(8,128)(2,1)S(1)} %get-tuple-element.182.held_ref), channel_id=1, source_target_pairs={{0,8},{4,12},{8,0},{12,4},{16,24},{20,28},{24,16},{28,20},{1,9},{5... | collective-permute-start | bytes 221192 | tf_op jit(solution)/shard_map/ppermute | solution.py:30
  132.8 1.6 %collective-permute-start.40 = (bf16[96,384]{1,0:T(8,128)(2,1)S(1)}, bf16[96,384]{1,0:T(8,128)(2,1)S(1)}, u32[]{:S(2)}, u32[]{:S(2)}) collective-permute-start(bf16[96,384]{1,0:T(8,128)(2,1)S(1)} %get-tuple-element.190), channel_id=1, source_target_pairs={{0,24},{4,28},{8,16},{12,20},{16,8},{20,12},{24,0},{28,4},{1,25},{... | collective-permute-start | bytes 221192 | tf_op jit(solution)/shard_map/ppermute | solution.py:30
  134.4 1.2 collective-permute-start.35
  135.6 1.2 normed_sum.1
  136.8 3.4 %collective-permute-done.39.refs_2_ = bf16[96,384]{1,0:T(8,128)(2,1)S(1)} collective-permute-done((bf16[96,384]{1,0:T(8,128)(2,1)S(1)}, bf16[96,384]{1,0:T(8,128)(2,1)S(1)}, u32[]{:S(2)}, u32[]{:S(2)}) %collective-permute-start.39) | collective-permute-done | bytes 73760 | tf_op jit(solution)/shard_map/ppermute | solution.py:30
  140.9 1.2 collective-permute-start.41
  142.2 1.3 collective-permute-start.43
  143.5 1.1 collective-permute-start.44
  144.6 1.9 %collective-permute-start.45 = (bf16[128,384]{1,0:T(8,128)(2,1)S(1)}, bf16[128,384]{1,0:T(8,128)(2,1)S(1)}, u32[]{:S(2)}, u32[]{:S(2)}) collective-permute-start(bf16[128,384]{1,0:T(8,128)(2,1)S(1)} %get-tuple-element.198), channel_id=1, source_target_pairs={{0,24},{4,28},{8,16},{12,20},{16,8},{20,12},{24,0},{28,4},{1,25},{... | collective-permute-start | bytes 294920 | tf_op jit(solution)/shard_map/ppermute | solution.py:30
  146.6 1.3 activations.1.refs_5_
  147.9 3.7 %expert_grads.1 = (f32[768,768]{1,0:T(8,128)}, f32[768,768]{1,0:T(8,128)}) custom-call(bf16[640,768]{1,0:T(8,128)(2,1)S(1)} %copy-done.8, bf16[640,768]{1,0:T(8,128)(2,1)S(1)} %copy-done.4, bf16[640,768]{1,0:T(8,128)(2,1)S(1)} %get-tuple-element.137.active_ref, bf16[640,768]{1,0:T(8,128)(2,1)S(1)} %copy-done.6, f32[640,1]{1,0:T(8,128)S(1)} %get-tuple-element.138.chosen_ref, ...), custom_call_target="tpu_custom_call" | custom-call | tf_op jit(solution)/shard_map/expert_grads/pallas_call | solution.py:55
  151.6 0.9 input_grad.1.refs_6_
  154.1 0.9 collective-permute-done.42.got_one
  155.0 1.4 columns.1
  (137 shorter events, 14.2 us)
Async XLA Ops:
  0.6 15.4 %copy-start = (f32[32,12]{0,1:T(8,128)S(1)}, f32[32,12]{0,1:T(8,128)}, u32[]{:S(2)}) copy-start(f32[32,12]{0,1:T(8,128)} %param.21) | copy-start | bytes 4612
  0.7 14.1 %copy-start.22 = (s32[1023]{0:T(1024)S(1)}, s32[1023]{0:T(1024)}, u32[]{:S(2)}) copy-start(s32[1023]{0:T(1024)} %param.28) | copy-start | bytes 12280
  0.7 14.2 %copy-start.23 = (bf16[768]{0:T(1024)(128)(2,1)S(1)}, bf16[768]{0:T(1024)(128)(2,1)}, u32[]{:S(2)}) copy-start(bf16[768]{0:T(1024)(128)(2,1)} %param.16) | copy-start | bytes 4612
  0.7 14.2 %copy-start.25 = (s32[256,1]{0,1:T(1,128)S(1)}, s32[256,1]{0,1:T(1,128)}, u32[]{:S(2)}) copy-start(s32[256,1]{0,1:T(1,128)} %param.26) | copy-start | bytes 3076
  0.7 24.7 %copy-start.2 = (bf16[256,768]{1,0:T(8,128)(2,1)S(1)}, bf16[256,768]{1,0:T(8,128)(2,1)}, u32[]{:S(2)}) copy-start(bf16[256,768]{1,0:T(8,128)(2,1)} %cot_ref.1) | copy-start | bytes 1179652
  2.4 3.1 %collective-permute-start.1 = (bf16[48,768]{1,0:T(8,128)(2,1)S(1)}, bf16[48,768]{1,0:T(8,128)(2,1)S(1)}, u32[]{:S(2)}, u32[]{:S(2)}) collective-permute-start(bf16[48,768]{1,0:T(8,128)(2,1)S(1)} %get-tuple-element.114), channel_id=1, source_target_pairs={{0,2},{2,0},{1,3},{3,1},{4,6},{6,4},{5,7},{7,5},{8,10},{10,8},{9,1... | collective-permute-start | bytes 221192 | tf_op jit(solution)/shard_map/ppermute | solution.py:30
  2.9 9.5 %collective-permute-start = (bf16[128,768]{1,0:T(8,128)(2,1)}, bf16[128,768]{1,0:T(8,128)(2,1)S(1)}, u32[]{:S(2)}, u32[]{:S(2)}) collective-permute-start(bf16[128,768]{1,0:T(8,128)(2,1)} %x_ref.1), channel_id=1, source_target_pairs={{0,1},{1,0},{2,3},{3,2},{4,5},{5,4},{6,7},{7,6},{8,9},{9,8},{10,11... | collective-permute-start | bytes 589832 | tf_op jit(solution)/shard_map/ppermute | solution.py:30
  5.5 6.8 %collective-permute-start.2 = (bf16[96,768]{1,0:T(8,128)(2,1)S(1)}, bf16[96,768]{1,0:T(8,128)(2,1)S(1)}, u32[]{:S(2)}, u32[]{:S(2)}) collective-permute-start(bf16[96,768]{1,0:T(8,128)(2,1)S(1)} %maximum_select_fusion.refs_0_), channel_id=1, source_target_pairs={{0,4},{4,0},{8,12},{12,8},{16,20},{20,16},{24,28},{28,24},{1,5},{5... | collective-permute-start | bytes 442376 | tf_op jit(solution)/shard_map/ppermute | solution.py:30
  7.1 6.9 %collective-permute-start.4 = (bf16[96,768]{1,0:T(8,128)(2,1)S(1)}, bf16[96,768]{1,0:T(8,128)(2,1)S(1)}, u32[]{:S(2)}, u32[]{:S(2)}) collective-permute-start(bf16[96,768]{1,0:T(8,128)(2,1)S(1)} %maximum_select_fusion.refs_0_), channel_id=1, source_target_pairs={{0,8},{4,12},{8,0},{12,4},{16,24},{20,28},{24,16},{28,20},{1,9},{5... | collective-permute-start | bytes 442376 | tf_op jit(solution)/shard_map/ppermute | solution.py:30
  9.5 13.8 %collective-permute-start.6 = (bf16[96,768]{1,0:T(8,128)(2,1)S(1)}, bf16[96,768]{1,0:T(8,128)(2,1)S(1)}, u32[]{:S(2)}, u32[]{:S(2)}) collective-permute-start(bf16[96,768]{1,0:T(8,128)(2,1)S(1)} %maximum_select_fusion.refs_0_), channel_id=1, source_target_pairs={{0,16},{4,20},{8,24},{12,28},{16,0},{20,4},{24,8},{28,12},{1,17},{... | collective-permute-start | bytes 442376 | tf_op jit(solution)/shard_map/ppermute | solution.py:30
  12.1 11.8 %collective-permute-start.8 = (bf16[96,768]{1,0:T(8,128)(2,1)S(1)}, bf16[96,768]{1,0:T(8,128)(2,1)S(1)}, u32[]{:S(2)}, u32[]{:S(2)}) collective-permute-start(bf16[96,768]{1,0:T(8,128)(2,1)S(1)} %maximum_select_fusion.refs_0_), channel_id=1, source_target_pairs={{0,24},{4,28},{8,16},{12,20},{16,8},{20,12},{24,0},{28,4},{1,25},{... | collective-permute-start | bytes 442376 | tf_op jit(solution)/shard_map/ppermute | solution.py:30
  13.8 17.4 %collective-permute-start.3 = (bf16[256,768]{1,0:T(8,128)(2,1)S(1)}, bf16[256,768]{1,0:T(8,128)(2,1)S(1)}, u32[]{:S(2)}, u32[]{:S(2)}) collective-permute-start(bf16[256,768]{1,0:T(8,128)(2,1)S(1)} %rows.1.own_ref), channel_id=1, source_target_pairs={{0,2},{2,0},{1,3},{3,1},{4,6},{6,4},{5,7},{7,5},{8,10},{10,8},{9,1... | collective-permute-start | bytes 1179656 | tf_op jit(solution)/shard_map/ppermute | solution.py:30
  13.9 11.4 %collective-permute-start.5 = (bf16[96,768]{1,0:T(8,128)(2,1)S(1)}, bf16[96,768]{1,0:T(8,128)(2,1)S(1)}, u32[]{:S(2)}, u32[]{:S(2)}) collective-permute-start(bf16[96,768]{1,0:T(8,128)(2,1)S(1)} %collective-permute-done.4.refs_2_), channel_id=1, source_target_pairs={{0,4},{4,0},{8,12},{12,8},{16,20},{20,16},{24,28},{28,24},{1,5},{5... | collective-permute-start | bytes 442376 | tf_op jit(solution)/shard_map/ppermute | solution.py:30
  16.0 15.2 %copy-start.9 = (bf16[256,320]{1,0:T(8,128)(2,1)}, bf16[256,320]{1,0:T(8,128)(2,1)S(1)}, u32[]{:S(2)}) copy-start(bf16[256,320]{1,0:T(8,128)(2,1)S(1)} %get-tuple-element.126.table_ref) | copy-start | bytes 491524
  23.3 7.8 %collective-permute-start.7 = (bf16[96,768]{1,0:T(8,128)(2,1)S(1)}, bf16[96,768]{1,0:T(8,128)(2,1)}, u32[]{:S(2)}, u32[]{:S(2)}) collective-permute-start(bf16[96,768]{1,0:T(8,128)(2,1)S(1)} %collective-permute-done.6.refs_4_), channel_id=1, source_target_pairs={{0,4},{4,0},{8,12},{12,8},{16,20},{20,16},{24,28},{28,24},{1,5},{5... | collective-permute-start | bytes 442376 | tf_op jit(solution)/shard_map/ppermute | solution.py:30
  23.9 7.3 %copy-start.19 = (bf16[96,768]{1,0:T(8,128)(2,1)}, bf16[96,768]{1,0:T(8,128)(2,1)S(1)}, u32[]{:S(2)}) copy-start(bf16[96,768]{1,0:T(8,128)(2,1)S(1)} %collective-permute-done.8.refs_6_) | copy-start | bytes 442372
  23.9 7.3 %collective-permute-start.9 = (bf16[96,768]{1,0:T(8,128)(2,1)S(1)}, bf16[96,768]{1,0:T(8,128)(2,1)}, u32[]{:S(2)}, u32[]{:S(2)}) collective-permute-start(bf16[96,768]{1,0:T(8,128)(2,1)S(1)} %collective-permute-done.8.refs_6_), channel_id=1, source_target_pairs={{0,4},{4,0},{8,12},{12,8},{16,20},{20,16},{24,28},{28,24},{1,5},{5... | collective-permute-start | bytes 442376 | tf_op jit(solution)/shard_map/ppermute | solution.py:30
  26.5 16.9 %all-to-all-start = ((bf16[8,40,768]{2,1,0:T(8,128)(2,1)}), bf16[8,40,768]{2,1,0:T(8,128)(2,1)S(1)}, u32[]{:S(2)}, u32[]{:S(2)}) async-start(bf16[8,40,768]{2,1,0:T(8,128)(2,1)} %bitcast.7), calls=%async_computation | async-start | bytes 983040 | tf_op jit(solution)/shard_map/all_to_all | solution.py:609
  37.8 2.9 %collective-permute-start.11 = (bf16[768,192]{1,0:T(8,128)(2,1)S(1)}, bf16[768,192]{1,0:T(8,128)(2,1)S(1)}, u32[]{:S(2)}, u32[]{:S(2)}) collective-permute-start(bf16[768,192]{1,0:T(8,128)(2,1)S(1)} %get-tuple-element.117.refs_1_.wo_ref), channel_id=1, source_target_pairs={{0,2},{2,0},{1,3},{3,1},{4,6},{6,4},{5,7},{7,5},{8,10},{10,8},{9,1... | collective-permute-start | bytes 884744 | tf_op jit(solution)/shard_map/ppermute | solution.py:30
  37.9 2.8 %collective-permute-start.10 = (bf16[256,192]{1,0:T(8,128)(2,1)S(1)}, bf16[256,192]{1,0:T(8,128)(2,1)S(1)}, u32[]{:S(2)}, u32[]{:S(2)}) collective-permute-start(bf16[256,192]{1,0:T(8,128)(2,1)S(1)} %get-tuple-element.116), channel_id=1, source_target_pairs={{0,2},{2,0},{1,3},{3,1},{4,6},{6,4},{5,7},{7,5},{8,10},{10,8},{9,1... | collective-permute-start | bytes 294920 | tf_op jit(solution)/shard_map/ppermute | solution.py:30
  41.1 11.2 %collective-permute-start.12 = (bf16[256,768]{1,0:T(8,128)(2,1)S(1)}, bf16[256,768]{1,0:T(8,128)(2,1)S(1)}, u32[]{:S(2)}, u32[]{:S(2)}) collective-permute-start(bf16[256,768]{1,0:T(8,128)(2,1)S(1)} %attended.1), channel_id=1, source_target_pairs={{0,1},{1,0},{2,3},{3,2},{4,5},{5,4},{6,7},{7,6},{8,9},{9,8},{10,11... | collective-permute-start | bytes 1179656 | tf_op jit(solution)/shard_map/ppermute | solution.py:30
  43.4 27.9 %collective-permute-start.21 = (bf16[8,40,768]{2,1,0:T(8,128)(2,1)S(1)}, bf16[8,40,768]{2,1,0:T(8,128)(2,1)S(1)}, u32[]{:S(2)}, u32[]{:S(2)}) collective-permute-start(bf16[8,40,768]{2,1,0:T(8,128)(2,1)S(1)} %all-to-all-done.own_ref), channel_id=1, source_target_pairs={{0,2},{2,0},{1,3},{3,1},{4,6},{6,4},{5,7},{7,5},{8,10},{10,8},{9,1... | collective-permute-start | bytes 1474568 | tf_op jit(solution)/shard_map/ppermute | solution.py:30
  52.4 18.9 %copy-start.1 = (bf16[768,768]{1,0:T(8,128)(2,1)S(1)}, bf16[768,768]{1,0:T(8,128)(2,1)}, u32[]{:S(2)}) copy-start(bf16[768,768]{1,0:T(8,128)(2,1)} %wdown_ref.3) | copy-start | bytes 3538948
  52.8 6.5 %collective-permute-start.13 = (bf16[40,768]{1,0:T(8,128)(2,1)S(1)}, bf16[40,768]{1,0:T(8,128)(2,1)S(1)}, u32[]{:S(2)}, u32[]{:S(2)}) collective-permute-start(bf16[40,768]{1,0:T(8,128)(2,1)S(1)} %get-tuple-element.129), channel_id=1, source_target_pairs={{0,4},{4,0},{8,12},{12,8},{16,20},{20,16},{24,28},{28,24},{1,5},{5... | collective-permute-start | bytes 184328 | tf_op jit(solution)/shard_map/ppermute | solution.py:30
  54.9 6.0 %collective-permute-start.14 = (bf16[40,768]{1,0:T(8,128)(2,1)S(1)}, bf16[40,768]{1,0:T(8,128)(2,1)S(1)}, u32[]{:S(2)}, u32[]{:S(2)}) collective-permute-start(bf16[40,768]{1,0:T(8,128)(2,1)S(1)} %get-tuple-element.130), channel_id=1, source_target_pairs={{0,8},{4,12},{8,0},{12,4},{16,24},{20,28},{24,16},{28,20},{1,9},{5... | collective-permute-start | bytes 184328 | tf_op jit(solution)/shard_map/ppermute | solution.py:30
  56.4 7.8 %collective-permute-start.15 = (bf16[40,768]{1,0:T(8,128)(2,1)S(1)}, bf16[40,768]{1,0:T(8,128)(2,1)S(1)}, u32[]{:S(2)}, u32[]{:S(2)}) collective-permute-start(bf16[40,768]{1,0:T(8,128)(2,1)S(1)} %get-tuple-element.131), channel_id=1, source_target_pairs={{0,12},{4,8},{8,4},{12,0},{16,28},{20,24},{24,20},{28,16},{1,13},{... | collective-permute-start | bytes 184328 | tf_op jit(solution)/shard_map/ppermute | solution.py:30
  56.4 8.6 %collective-permute-start.16 = (bf16[40,768]{1,0:T(8,128)(2,1)S(1)}, bf16[40,768]{1,0:T(8,128)(2,1)S(1)}, u32[]{:S(2)}, u32[]{:S(2)}) collective-permute-start(bf16[40,768]{1,0:T(8,128)(2,1)S(1)} %get-tuple-element.132), channel_id=1, source_target_pairs={{0,16},{4,20},{8,24},{12,28},{16,0},{20,4},{24,8},{28,12},{1,17},{... | collective-permute-start | bytes 184328 | tf_op jit(solution)/shard_map/ppermute | solution.py:30
  59.3 9.6 %collective-permute-start.17 = (bf16[40,768]{1,0:T(8,128)(2,1)S(1)}, bf16[40,768]{1,0:T(8,128)(2,1)S(1)}, u32[]{:S(2)}, u32[]{:S(2)}) collective-permute-start(bf16[40,768]{1,0:T(8,128)(2,1)S(1)} %get-tuple-element.133), channel_id=1, source_target_pairs={{0,20},{4,16},{8,28},{12,24},{16,4},{20,0},{24,12},{28,8},{1,21},{... | collective-permute-start | bytes 184328 | tf_op jit(solution)/shard_map/ppermute | solution.py:30
  60.9 7.9 %collective-permute-start.18 = (bf16[40,768]{1,0:T(8,128)(2,1)S(1)}, bf16[40,768]{1,0:T(8,128)(2,1)S(1)}, u32[]{:S(2)}, u32[]{:S(2)}) collective-permute-start(bf16[40,768]{1,0:T(8,128)(2,1)S(1)} %get-tuple-element.134), channel_id=1, source_target_pairs={{0,24},{4,28},{8,16},{12,20},{16,8},{20,12},{24,0},{28,4},{1,25},{... | collective-permute-start | bytes 184328 | tf_op jit(solution)/shard_map/ppermute | solution.py:30
  64.2 7.1 %collective-permute-start.19 = (bf16[40,768]{1,0:T(8,128)(2,1)S(1)}, bf16[40,768]{1,0:T(8,128)(2,1)S(1)}, u32[]{:S(2)}, u32[]{:S(2)}) collective-permute-start(bf16[40,768]{1,0:T(8,128)(2,1)S(1)} %get-tuple-element.135), channel_id=1, source_target_pairs={{0,28},{4,24},{8,20},{12,16},{16,12},{20,8},{24,4},{28,0},{1,29},{... | collective-permute-start | bytes 184328 | tf_op jit(solution)/shard_map/ppermute | solution.py:30
  68.9 4.3 %copy-start.3 = (bf16[768,768]{1,0:T(8,128)(2,1)S(1)}, bf16[768,768]{1,0:T(8,128)(2,1)}, u32[]{:S(2)}) copy-start(bf16[768,768]{1,0:T(8,128)(2,1)} %wup_ref.1) | copy-start | bytes 3538948
  68.9 4.3 %copy-start.21 = (bf16[768,8]{0,1:T(8,128)(2,1)S(1)}, bf16[768,8]{0,1:T(8,128)(2,1)}, u32[]{:S(2)}) copy-start(bf16[768,8]{0,1:T(8,128)(2,1)} %param.23) | copy-start | bytes 36868
  71.3 1.9 %collective-permute-start.20 = (bf16[320,768]{1,0:T(8,128)(2,1)S(1)}, bf16[320,768]{1,0:T(8,128)(2,1)S(1)}, u32[]{:S(2)}, u32[]{:S(2)}) collective-permute-start(bf16[320,768]{1,0:T(8,128)(2,1)S(1)} %constant_dynamic-update-slice_fusion.own_ref), channel_id=1, source_target_pairs={{0,2},{2,0},{1,3},{3,1},{4,6},{6,4},{5,7},{7,5},{8,10},{10,8},{9,1... | collective-permute-start | bytes 1474568 | tf_op jit(solution)/shard_map/ppermute | solution.py:30
  77.4 2.0 %collective-permute-start.22 = (bf16[320,768]{1,0:T(8,128)(2,1)S(1)}, bf16[320,768]{1,0:T(8,128)(2,1)S(1)}, u32[]{:S(2)}, u32[]{:S(2)}) collective-permute-start(bf16[320,768]{1,0:T(8,128)(2,1)S(1)} %get-tuple-element.140), channel_id=1, source_target_pairs={{0,2},{2,0},{1,3},{3,1},{4,6},{6,4},{5,7},{7,5},{8,10},{10,8},{9,1... | collective-permute-start | bytes 1474568 | tf_op jit(solution)/shard_map/ppermute | solution.py:30
  80.5 17.1 %collective-permute-start.23 = (bf16[320,768]{1,0:T(8,128)(2,1)S(1)}, bf16[320,768]{1,0:T(8,128)(2,1)S(1)}, u32[]{:S(2)}, u32[]{:S(2)}) collective-permute-start(bf16[320,768]{1,0:T(8,128)(2,1)S(1)} %get-tuple-element.143), channel_id=1, source_target_pairs={{0,2},{2,0},{1,3},{3,1},{4,6},{6,4},{5,7},{7,5},{8,10},{10,8},{9,1... | collective-permute-start | bytes 1474568 | tf_op jit(solution)/shard_map/ppermute | solution.py:30
  81.0 4.8 %collective-permute-start.24 = (bf16[40,768]{1,0:T(8,128)(2,1)S(1)}, bf16[40,768]{1,0:T(8,128)(2,1)S(1)}, u32[]{:S(2)}, u32[]{:S(2)}) collective-permute-start(bf16[40,768]{1,0:T(8,128)(2,1)S(1)} %get-tuple-element.145), channel_id=1, source_target_pairs={{0,4},{4,0},{8,12},{12,8},{16,20},{20,16},{24,28},{28,24},{1,5},{5... | collective-permute-start | bytes 184328 | tf_op jit(solution)/shard_map/ppermute | solution.py:30
  81.5 5.9 %collective-permute-start.25 = (bf16[40,768]{1,0:T(8,128)(2,1)S(1)}, bf16[40,768]{1,0:T(8,128)(2,1)S(1)}, u32[]{:S(2)}, u32[]{:S(2)}) collective-permute-start(bf16[40,768]{1,0:T(8,128)(2,1)S(1)} %get-tuple-element.146), channel_id=1, source_target_pairs={{0,8},{4,12},{8,0},{12,4},{16,24},{20,28},{24,16},{28,20},{1,9},{5... | collective-permute-start | bytes 184328 | tf_op jit(solution)/shard_map/ppermute | solution.py:30
  82.1 6.3 %collective-permute-start.26 = (bf16[40,768]{1,0:T(8,128)(2,1)S(1)}, bf16[40,768]{1,0:T(8,128)(2,1)S(1)}, u32[]{:S(2)}, u32[]{:S(2)}) collective-permute-start(bf16[40,768]{1,0:T(8,128)(2,1)S(1)} %get-tuple-element.147), channel_id=1, source_target_pairs={{0,12},{4,8},{8,4},{12,0},{16,28},{20,24},{24,20},{28,16},{1,13},{... | collective-permute-start | bytes 184328 | tf_op jit(solution)/shard_map/ppermute | solution.py:30
  84.5 9.2 %collective-permute-start.27 = (bf16[40,768]{1,0:T(8,128)(2,1)S(1)}, bf16[40,768]{1,0:T(8,128)(2,1)S(1)}, u32[]{:S(2)}, u32[]{:S(2)}) collective-permute-start(bf16[40,768]{1,0:T(8,128)(2,1)S(1)} %get-tuple-element.148), channel_id=1, source_target_pairs={{0,16},{4,20},{8,24},{12,28},{16,0},{20,4},{24,8},{28,12},{1,17},{... | collective-permute-start | bytes 184328 | tf_op jit(solution)/shard_map/ppermute | solution.py:30
  85.8 10.3 %collective-permute-start.28 = (bf16[40,768]{1,0:T(8,128)(2,1)S(1)}, bf16[40,768]{1,0:T(8,128)(2,1)S(1)}, u32[]{:S(2)}, u32[]{:S(2)}) collective-permute-start(bf16[40,768]{1,0:T(8,128)(2,1)S(1)} %get-tuple-element.149), channel_id=1, source_target_pairs={{0,20},{4,16},{8,28},{12,24},{16,4},{20,0},{24,12},{28,8},{1,21},{... | collective-permute-start | bytes 184328 | tf_op jit(solution)/shard_map/ppermute | solution.py:30
  87.4 8.7 %collective-permute-start.29 = (bf16[40,768]{1,0:T(8,128)(2,1)S(1)}, bf16[40,768]{1,0:T(8,128)(2,1)S(1)}, u32[]{:S(2)}, u32[]{:S(2)}) collective-permute-start(bf16[40,768]{1,0:T(8,128)(2,1)S(1)} %get-tuple-element.150), channel_id=1, source_target_pairs={{0,24},{4,28},{8,16},{12,20},{16,8},{20,12},{24,0},{28,4},{1,25},{... | collective-permute-start | bytes 184328 | tf_op jit(solution)/shard_map/ppermute | solution.py:30
  88.4 7.6 %collective-permute-start.30 = (bf16[40,768]{1,0:T(8,128)(2,1)S(1)}, bf16[40,768]{1,0:T(8,128)(2,1)S(1)}, u32[]{:S(2)}, u32[]{:S(2)}) collective-permute-start(bf16[40,768]{1,0:T(8,128)(2,1)S(1)} %get-tuple-element.141.held_ref), channel_id=1, source_target_pairs={{0,28},{4,24},{8,20},{12,16},{16,12},{20,8},{24,4},{28,0},{1,29},{... | collective-permute-start | bytes 184328 | tf_op jit(solution)/shard_map/ppermute | solution.py:30
  96.4 9.8 %collective-permute-start.31 = (bf16[256,768]{1,0:T(8,128)(2,1)S(1)}, bf16[256,768]{1,0:T(8,128)(2,1)}, u32[]{:S(2)}, u32[]{:S(2)}) collective-permute-start(bf16[256,768]{1,0:T(8,128)(2,1)S(1)} %gather_grad.1.own_ref), channel_id=1, source_target_pairs={{0,1},{1,0},{2,3},{3,2},{4,5},{5,4},{6,7},{7,6},{8,9},{9,8},{10,11... | collective-permute-start | bytes 1179656 | tf_op jit(solution)/shard_map/ppermute | solution.py:30
  99.1 24.8 %all-to-all-start.1 = ((bf16[8,40,768]{2,1,0:T(8,128)(2,1)}), bf16[8,40,768]{2,1,0:T(8,128)(2,1)S(1)}, u32[]{:S(2)}, u32[]{:S(2)}) async-start(bf16[8,40,768]{2,1,0:T(8,128)(2,1)} %join_out.1.refs_8_), calls=%async_computation.1 | async-start | bytes 983040 | tf_op jit(solution)/shard_map/all_to_all | solution.py:609
  108.5 1.8 %collective-permute-start.32 = (bf16[256,768]{1,0:T(8,128)(2,1)S(1)}, bf16[256,768]{1,0:T(8,128)(2,1)S(1)}, u32[]{:S(2)}, u32[]{:S(2)}) collective-permute-start(bf16[256,768]{1,0:T(8,128)(2,1)S(1)} %get-tuple-element.159.own_ref), channel_id=1, source_target_pairs={{0,2},{2,0},{1,3},{3,1},{4,6},{6,4},{5,7},{7,5},{8,10},{10,8},{9,1... | collective-permute-start | bytes 1179656 | tf_op jit(solution)/shard_map/ppermute | solution.py:30
  114.1 8.2 %copy-start.14 = (f32[384,384]{1,0:T(8,128)}, f32[384,384]{1,0:T(8,128)S(1)}, u32[]{:S(2)}) copy-start(f32[384,384]{1,0:T(8,128)S(1)} %get-tuple-element.175.keep_ref) | copy-start | bytes 1769476
  114.1 13.1 %collective-permute-start.33 = (bf16[384,384]{1,0:T(8,128)(2,1)}, bf16[384,384]{1,0:T(8,128)(2,1)}, u32[]{:S(2)}, u32[]{:S(2)}) collective-permute-start(bf16[384,384]{1,0:T(8,128)(2,1)} %get-tuple-element.176), channel_id=1, source_target_pairs={{0,4},{4,0},{8,12},{12,8},{16,20},{20,16},{24,28},{28,24},{1,5},{5... | collective-permute-start | bytes 884744 | tf_op jit(solution)/shard_map/ppermute | solution.py:30
  123.1 11.4 %collective-permute-start.36 = (bf16[256,768]{1,0:T(8,128)(2,1)}, bf16[256,768]{1,0:T(8,128)(2,1)}, u32[]{:S(2)}, u32[]{:S(2)}) collective-permute-start(bf16[256,768]{1,0:T(8,128)(2,1)} %get-tuple-element.181), channel_id=1, source_target_pairs={{0,2},{2,0},{1,3},{3,1},{4,6},{6,4},{5,7},{7,5},{8,10},{10,8},{9,1... | collective-permute-start | bytes 1179656 | tf_op jit(solution)/shard_map/ppermute | solution.py:30
  123.1 4.2 %collective-permute-start.34 = (f32[16,768]{1,0:T(8,128)S(1)}, f32[16,768]{1,0:T(8,128)S(1)}, u32[]{:S(2)}, u32[]{:S(2)}) collective-permute-start(f32[16,768]{1,0:T(8,128)S(1)} %get-tuple-element.177.small_ref), channel_id=1, source_target_pairs={{0,1},{1,0},{2,3},{3,2},{4,5},{5,4},{6,7},{7,6},{8,9},{9,8},{10,11... | collective-permute-start | bytes 147464 | tf_op jit(solution)/shard_map/ppermute | solution.py:30
  127.2 13.0 %copy-start.13 = (f32[384,384]{1,0:T(8,128)S(1)}, f32[384,384]{1,0:T(8,128)}, u32[]{:S(2)}) copy-start(f32[384,384]{1,0:T(8,128)} %get-tuple-element.184.keep_ref) | copy-start | bytes 1769476
  128.4 11.9 %collective-permute-start.37 = (bf16[416,384]{1,0:T(8,128)(2,1)S(1)}, bf16[416,384]{1,0:T(8,128)(2,1)S(1)}, u32[]{:S(2)}, u32[]{:S(2)}) collective-permute-start(bf16[416,384]{1,0:T(8,128)(2,1)S(1)} %get-tuple-element.185), channel_id=1, source_target_pairs={{0,4},{4,0},{8,12},{12,8},{16,20},{20,16},{24,28},{28,24},{1,5},{5... | collective-permute-start | bytes 958472 | tf_op jit(solution)/shard_map/ppermute | solution.py:30
  128.5 8.3 %collective-permute-start.38 = (bf16[96,384]{1,0:T(8,128)(2,1)S(1)}, bf16[96,384]{1,0:T(8,128)(2,1)S(1)}, u32[]{:S(2)}, u32[]{:S(2)}) collective-permute-start(bf16[96,384]{1,0:T(8,128)(2,1)S(1)} %get-tuple-element.182.held_ref), channel_id=1, source_target_pairs={{0,8},{4,12},{8,0},{12,4},{16,24},{20,28},{24,16},{28,20},{1,9},{5... | collective-permute-start | bytes 221192 | tf_op jit(solution)/shard_map/ppermute | solution.py:30
  132.0 8.2 %collective-permute-start.39 = (bf16[96,384]{1,0:T(8,128)(2,1)S(1)}, bf16[96,384]{1,0:T(8,128)(2,1)S(1)}, u32[]{:S(2)}, u32[]{:S(2)}) collective-permute-start(bf16[96,384]{1,0:T(8,128)(2,1)S(1)} %get-tuple-element.189), channel_id=1, source_target_pairs={{0,16},{4,20},{8,24},{12,28},{16,0},{20,4},{24,8},{28,12},{1,17},{... | collective-permute-start | bytes 221192 | tf_op jit(solution)/shard_map/ppermute | solution.py:30
  132.8 7.4 %collective-permute-start.40 = (bf16[96,384]{1,0:T(8,128)(2,1)S(1)}, bf16[96,384]{1,0:T(8,128)(2,1)S(1)}, u32[]{:S(2)}, u32[]{:S(2)}) collective-permute-start(bf16[96,384]{1,0:T(8,128)(2,1)S(1)} %get-tuple-element.190), channel_id=1, source_target_pairs={{0,24},{4,28},{8,16},{12,20},{16,8},{20,12},{24,0},{28,4},{1,25},{... | collective-permute-start | bytes 221192 | tf_op jit(solution)/shard_map/ppermute | solution.py:30
  134.4 12.2 %collective-permute-start.35 = (bf16[128,768]{1,0:T(8,128)(2,1)S(1)}, bf16[128,768]{1,0:T(8,128)(2,1)S(1)}, u32[]{:S(2)}, u32[]{:S(2)}) collective-permute-start(bf16[128,768]{1,0:T(8,128)(2,1)S(1)} %get-tuple-element.180), channel_id=1, source_target_pairs={{0,1},{1,0},{2,3},{3,2},{4,5},{5,4},{6,7},{7,6},{8,9},{9,8},{10,11... | collective-permute-start | bytes 589832 | tf_op jit(solution)/shard_map/ppermute | solution.py:30
  135.6 12.3 %copy-start.8 = (bf16[640,768]{1,0:T(8,128)(2,1)S(1)}, bf16[640,768]{1,0:T(8,128)(2,1)}, u32[]{:S(2)}) copy-start(bf16[640,768]{1,0:T(8,128)(2,1)} %copy-done.7) | copy-start | bytes 2949124
  140.2 7.6 %copy-start.4 = (bf16[640,768]{1,0:T(8,128)(2,1)S(1)}, bf16[640,768]{1,0:T(8,128)(2,1)}, u32[]{:S(2)}) copy-start(bf16[640,768]{1,0:T(8,128)(2,1)} %get-tuple-element.200.cots_ref) | copy-start | bytes 2949124
  140.2 7.6 %copy-start.6 = (bf16[640,768]{1,0:T(8,128)(2,1)S(1)}, bf16[640,768]{1,0:T(8,128)(2,1)}, u32[]{:S(2)}) copy-start(bf16[640,768]{1,0:T(8,128)(2,1)} %copy-done.5) | copy-start | bytes 2949124
  140.9 10.7 %collective-permute-start.41 = (bf16[128,768]{1,0:T(8,128)(2,1)S(1)}, bf16[128,768]{1,0:T(8,128)(2,1)S(1)}, u32[]{:S(2)}, u32[]{:S(2)}) collective-permute-start(bf16[128,768]{1,0:T(8,128)(2,1)S(1)} %get-tuple-element.191), channel_id=1, source_target_pairs={{0,1},{1,0},{2,3},{3,2},{4,5},{5,4},{6,7},{7,6},{8,9},{9,8},{10,11... | collective-permute-start | bytes 589832 | tf_op jit(solution)/shard_map/ppermute | solution.py:30
  142.2 10.4 %collective-permute-start.43 = (bf16[128,384]{1,0:T(8,128)(2,1)S(1)}, bf16[128,384]{1,0:T(8,128)(2,1)S(1)}, u32[]{:S(2)}, u32[]{:S(2)}) collective-permute-start(bf16[128,384]{1,0:T(8,128)(2,1)S(1)} %get-tuple-element.196.held_ref), channel_id=1, source_target_pairs={{0,8},{4,12},{8,0},{12,4},{16,24},{20,28},{24,16},{28,20},{1,9},{5... | collective-permute-start | bytes 294920 | tf_op jit(solution)/shard_map/ppermute | solution.py:30
  143.5 9.4 %collective-permute-start.44 = (bf16[128,384]{1,0:T(8,128)(2,1)S(1)}, bf16[128,384]{1,0:T(8,128)(2,1)S(1)}, u32[]{:S(2)}, u32[]{:S(2)}) collective-permute-start(bf16[128,384]{1,0:T(8,128)(2,1)S(1)} %get-tuple-element.197), channel_id=1, source_target_pairs={{0,16},{4,20},{8,24},{12,28},{16,0},{20,4},{24,8},{28,12},{1,17},{... | collective-permute-start | bytes 294920 | tf_op jit(solution)/shard_map/ppermute | solution.py:30
  144.6 8.3 %collective-permute-start.45 = (bf16[128,384]{1,0:T(8,128)(2,1)S(1)}, bf16[128,384]{1,0:T(8,128)(2,1)S(1)}, u32[]{:S(2)}, u32[]{:S(2)}) collective-permute-start(bf16[128,384]{1,0:T(8,128)(2,1)S(1)} %get-tuple-element.198), channel_id=1, source_target_pairs={{0,24},{4,28},{8,16},{12,20},{16,8},{20,12},{24,0},{28,4},{1,25},{... | collective-permute-start | bytes 294920 | tf_op jit(solution)/shard_map/ppermute | solution.py:30
  153.5 1.5 collective-permute-start.46
  153.6 1.4 collective-permute-start.42
  (11 other events, 23.7 us)
